TPU v7x, 32 devices: a whole 2x2x4 slice. The times are simulated.
32 devices in a mesh: fsdp: 2 (over y), ctx: 4 (over x, core), tp: 4 (over z).
Axes of the slice: x: 2, y: 2, z: 4, core: 2. Of those that a mesh axis runs over, the one named last changes fastest.
Arguments:
- tokens: bfloat16 [2, 4096, 1536], P('fsdp', 'ctx'), may hold values from -6 to 6
- teacher: bfloat16 [2, 4096, 1536], P('fsdp', 'ctx'), may hold values from -6 to 6
- segment_ids: int32 [2, 4096], P('fsdp', 'ctx'), may hold values from 0 to 4095, as said below
- positions: int32 [2, 4096], P('fsdp', 'ctx'), may hold values from 0 to 6143, as said below
- valid_mask: int32 [2, 4096], P('fsdp', 'ctx'), may hold values 0 or 1
- valid_count: int32 [], replicated, may hold values from 8192 to 32767
- gain_attn: bfloat16 [1536], P(('fsdp', 'ctx')), may hold values from 0.5 to 1.5
- w_query: bfloat16 [1536, 1536], P(('fsdp', 'ctx'), 'tp'), may hold values from -0.15625 to 0.15625
- w_key: bfloat16 [1536, 768], P(('fsdp', 'ctx'), 'tp'), may hold values from -0.15625 to 0.15625
- w_value: bfloat16 [1536, 768], P(('fsdp', 'ctx'), 'tp'), may hold values from -0.15625 to 0.15625
- w_out: bfloat16 [1536, 1536], P('tp', ('fsdp', 'ctx')), may hold values from -6 to 6
- gain_ffn: bfloat16 [1536], P(('fsdp', 'ctx')), may hold values from 0.5 to 1.5
- w_gate: bfloat16 [1536, 4096], P(('fsdp', 'ctx'), 'tp'), may hold values from -0.15625 to 0.15625
- w_up: bfloat16 [1536, 4096], P(('fsdp', 'ctx'), 'tp'), may hold values from -0.15625 to 0.15625
- w_down: bfloat16 [4096, 1536], P('tp', ('fsdp', 'ctx')), may hold values from -0.09375 to 0.09375
Outputs:
- mixed: bfloat16 [2, 4096, 1536], P('fsdp', 'ctx')
- loss: float32 [], replicated
- grad_tokens: float32 [2, 4096, 1536], P('fsdp', 'ctx')
- grad_gain_attn: float32 [1536], P(('fsdp', 'ctx'))
- grad_w_query: float32 [1536, 1536], P(('fsdp', 'ctx'), 'tp')
- grad_w_key: float32 [1536, 768], P(('fsdp', 'ctx'), 'tp')
- grad_w_value: float32 [1536, 768], P(('fsdp', 'ctx'), 'tp')
- grad_w_out: float32 [1536, 1536], P('tp', ('fsdp', 'ctx'))
- grad_gain_ffn: float32 [1536], P(('fsdp', 'ctx'))
- grad_w_gate: float32 [1536, 4096], P(('fsdp', 'ctx'), 'tp')
- grad_w_up: float32 [1536, 4096], P(('fsdp', 'ctx'), 'tp')
- grad_w_down: float32 [4096, 1536], P('tp', ('fsdp', 'ctx'))
Inputs may be any that keep to these rules, and one draw needn't show every extreme that they name: `segment_ids`: along each sequence the ids start at 0 and never fall; a run of equal ids is one document, and the last document of every sequence has the id 4096 - 1. In every sequence one document begins within its first 1024 tokens and ends within its last 1024. `positions`: inside a document the position rises by one from token to token.
All inputs are finite; a program needn't handle non-finite values. No bound on the sum of `valid_mask` on one device may be relied on, other than what follows from the above.
Results may differ from a plain program's by a relative error of at most 0.02.
Values may be sent and summed in bfloat16 or wider, within the bound.
No kernel may reach another device: no remote copies, remote signals or barrier semaphores. Data moves between devices by JAX's collectives and lax.ppermute only.
A program may use at most 192 MiB of HBM per device.

v0:
```python
import math

import jax
import jax.numpy as jnp
from jax import lax
from jax.sharding import PartitionSpec as P

HD = 96


EPSILON = 1e-05
ROPE_BASE = 100000.0
MASKED = -1e30


def as_sent(array):

    def short(part):
        return part.astype(jnp.bfloat16) if part.dtype == jnp.float32 else part

    return jax.tree.map(short, array)


def rope_tables(places):
    half_dim = HD // 2
    frequency = jnp.exp(
        jnp.arange(half_dim).astype(jnp.float32) * (-2.0 * math.log(ROPE_BASE) / HD)
    )
    angles = places.astype(jnp.float32)[..., None] * frequency
    return (jnp.cos(angles), jnp.sin(angles))


def rotate(values, cos_table, sin_table):
    half_dim = values.shape[-1] // 2
    lower_half = values[..., :half_dim]
    upper_half = values[..., half_dim:]
    return jnp.concatenate(
        [
            lower_half * cos_table - upper_half * sin_table,
            upper_half * cos_table + lower_half * sin_table,
        ],
        axis=-1,
    )


def unrotate(values, cos_table, sin_table):
    half_dim = values.shape[-1] // 2
    lower_half = values[..., :half_dim]
    upper_half = values[..., half_dim:]
    return jnp.concatenate(
        [
            lower_half * cos_table + upper_half * sin_table,
            upper_half * cos_table - lower_half * sin_table,
        ],
        axis=-1,
    )


def rotate_keys(values, cos_table, sin_table):
    half_dim = values.shape[1] // 2
    lower_half = values[:, :half_dim]
    upper_half = values[:, half_dim:]
    return jnp.concatenate(
        [
            lower_half * cos_table - upper_half * sin_table,
            upper_half * cos_table + lower_half * sin_table,
        ],
        axis=1,
    )


def unrotate_keys(values, cos_table, sin_table):
    half_dim = values.shape[1] // 2
    lower_half = values[:, :half_dim]
    upper_half = values[:, half_dim:]
    return jnp.concatenate(
        [
            lower_half * cos_table + upper_half * sin_table,
            upper_half * cos_table - lower_half * sin_table,
        ],
        axis=1,
    )


def norm_parts(values):
    factor = lax.rsqrt(jnp.mean(values * values, axis=-1, keepdims=True) + EPSILON)
    return (factor, values * factor)


def norm_back(grad_normed_in, normed, factor, gain_vec):
    grad_normed = grad_normed_in * gain_vec
    return factor * (grad_normed - normed * jnp.mean(grad_normed * normed, axis=-1, keepdims=True))


def block_width():
    return 1024


def sweep_keys(total_len, block_step, initial):
    block_len = block_width()

    def turn(turn_index, running):
        return block_step(turn_index * block_len, block_len, running)

    return lax.fori_loop(0, total_len // block_len, turn, initial)


def keep_state(running):
    return running


def contract_rows(left_op, right_op):
    return lax.dot_general(
        left_op, right_op, (((0,), (0,)), ((), ())), preferred_element_type=jnp.float32
    )


def contract_cols(left_op, right_op):
    return lax.dot_general(
        left_op, right_op, (((1,), (1,)), ((), ())), preferred_element_type=jnp.float32
    )


def on_device(
    tokens,
    teacher,
    segment_ids,
    positions,
    valid_mask,
    valid_count,
    gain_attn,
    w_query,
    w_key,
    w_value,
    w_out,
    gain_ffn,
    w_gate,
    w_up,
    w_down,
):
    rows_f = tokens[0].astype(jnp.float32)
    target = teacher[0].astype(jnp.float32)
    seg_local = segment_ids[0]
    valid_rows = valid_mask[0].astype(jnp.float32)[:, None]
    tok_rows, model_width = rows_f.shape
    share_rows = tok_rows // lax.axis_size("tp")
    share_start = lax.axis_index("tp") * share_rows
    first_row = lax.axis_index("ctx") * tok_rows
    row_query = first_row + jnp.arange(tok_rows, dtype=jnp.int32)
    last_row = first_row + tok_rows - 1
    seg_low = seg_local[0]
    att_scale = HD ** (-0.5)
    cos_table, sin_table = rope_tables(positions[0])
    cos_keys = cos_table.T
    sin_keys = sin_table.T

    def own_rows(values):
        return lax.dynamic_slice_in_dim(values, share_start, share_rows, 0)

    q_weight, k_weight, v_weight, o_weight, g_weight, u_weight, d_weight, gain_att, gain_mlp = (
        lax.all_gather(w_query, ("fsdp", "ctx"), axis=0, tiled=True),
        lax.all_gather(w_key, ("fsdp", "ctx"), axis=0, tiled=True),
        lax.all_gather(w_value, ("fsdp", "ctx"), axis=0, tiled=True),
        lax.all_gather(w_out, ("fsdp", "ctx"), axis=1, tiled=True),
        lax.all_gather(w_gate, ("fsdp", "ctx"), axis=0, tiled=True),
        lax.all_gather(w_up, ("fsdp", "ctx"), axis=0, tiled=True),
        lax.all_gather(w_down, ("fsdp", "ctx"), axis=1, tiled=True),
        lax.all_gather(gain_attn, ("fsdp", "ctx"), axis=0, tiled=True),
        lax.all_gather(gain_ffn, ("fsdp", "ctx"), axis=0, tiled=True),
    )
    gain_att = gain_att.astype(jnp.float32)
    gain_mlp = gain_mlp.astype(jnp.float32)
    q_cols = q_weight.shape[1]
    kv_cols = k_weight.shape[1]
    heads_q = q_cols // HD
    heads_k = kv_cols // HD
    group_size = heads_q // heads_k
    scale_a, normed_a = norm_parts(rows_f)
    hidden_a = (normed_a * gain_att).astype(jnp.bfloat16)
    query_lin = jnp.dot(hidden_a, q_weight, preferred_element_type=jnp.float32).reshape(
        tok_rows, heads_q, HD
    )
    query_rot = rotate(query_lin, cos_table[:, None, :], sin_table[:, None, :]).astype(jnp.bfloat16)
    grouped_q = query_rot.reshape(tok_rows, heads_k, group_size, HD)
    w_kv = jnp.concatenate([k_weight, v_weight], axis=1)
    kv_lin = lax.dot_general(
        w_kv, hidden_a, (((0,), (1,)), ((), ())), preferred_element_type=jnp.float32
    )
    key_rot = rotate_keys(kv_lin[:kv_cols].reshape(heads_k, HD, tok_rows), cos_keys, sin_keys)
    kv_send = jnp.concatenate(
        [key_rot.reshape(kv_cols, tok_rows), kv_lin[kv_cols:]], axis=0
    ).astype(jnp.bfloat16)
    kv_all, seg_all = (
        lax.all_gather(kv_send, "ctx", axis=1, tiled=True),
        lax.all_gather(seg_local, "ctx", axis=0, tiled=True),
    )
    total_keys = kv_all.shape[1]
    keys_all = kv_all[:kv_cols].reshape(heads_k, HD, total_keys)
    values_all = kv_all[kv_cols:].reshape(heads_k, HD, total_keys)

    def scores_at(key_start, block_len):
        keys_block = lax.dynamic_slice_in_dim(keys_all, key_start, block_len, 2)
        seg_block = lax.dynamic_slice_in_dim(seg_all, key_start, block_len, 0)
        raw_scores = (
            jnp.einsum("qkgd,kdn->kgqn", grouped_q, keys_block, preferred_element_type=jnp.float32)
            * att_scale
        )
        columns = key_start + jnp.arange(block_len, dtype=jnp.int32)
        allowed = (seg_local[:, None] == seg_block[None, :]) & (
            columns[None, :] <= row_query[:, None]
        )
        return jnp.where(allowed, raw_scores, MASKED)

    def is_live(key_start, block_len):
        return (key_start <= last_row) & (seg_all[key_start + block_len - 1] >= seg_low)

    def forward_step(key_start, block_len, running):

        def forward_compute_block(state_in):
            row_max, row_sum, accum = state_in
            scores = scores_at(key_start, block_len)
            new_max = jnp.maximum(row_max, jnp.max(scores, axis=-1))
            shrink = jnp.exp(row_max - new_max)
            exp_scores = jnp.exp(scores - new_max[..., None])
            row_sum = row_sum * shrink + jnp.sum(exp_scores, axis=-1)
            values_block = lax.dynamic_slice_in_dim(values_all, key_start, block_len, 2)
            added = jnp.einsum(
                "kgqn,kdn->qkgd",
                exp_scores.astype(jnp.bfloat16),
                values_block,
                preferred_element_type=jnp.float32,
            )
            accum = accum * jnp.transpose(shrink, (2, 0, 1))[..., None] + added
            return (new_max, row_sum, accum)

        return lax.cond(is_live(key_start, block_len), forward_compute_block, keep_state, running)

    stat_shape = (heads_k, group_size, tok_rows)
    row_max, row_sum, accum = sweep_keys(
        total_keys,
        forward_step,
        (
            jnp.full(stat_shape, MASKED, jnp.float32),
            jnp.zeros(stat_shape, jnp.float32),
            jnp.zeros((tok_rows, heads_k, group_size, HD), jnp.float32),
        ),
    )
    attended_full = accum / jnp.transpose(row_sum, (2, 0, 1))[..., None]
    attended = attended_full.reshape(tok_rows, q_cols).astype(jnp.bfloat16)

    def probs_at(key_start, block_len):
        scores = scores_at(key_start, block_len)
        return jnp.exp(scores - row_max[..., None]) / row_sum[..., None]

    attn_share = lax.psum_scatter(
        jnp.dot(attended, o_weight, preferred_element_type=jnp.float32).astype(jnp.bfloat16),
        "tp",
        scatter_dimension=0,
        tiled=True,
    ).astype(jnp.float32)
    resid_share = own_rows(rows_f) + attn_share
    scale_f, normed_f = norm_parts(resid_share)
    hidden_share = (normed_f * gain_mlp).astype(jnp.bfloat16)
    hidden_f = lax.all_gather(hidden_share, "tp", axis=0, tiled=True)
    gate_lin = jnp.dot(hidden_f, g_weight, preferred_element_type=jnp.float32)
    up_lin = jnp.dot(hidden_f, u_weight, preferred_element_type=jnp.float32)
    sig_gate = jax.nn.sigmoid(gate_lin)
    act_gate = gate_lin * sig_gate
    inner_act = (act_gate * up_lin).astype(jnp.bfloat16)
    ffn_share = lax.psum_scatter(
        jnp.dot(inner_act, d_weight, preferred_element_type=jnp.float32).astype(jnp.bfloat16),
        "tp",
        scatter_dimension=0,
        tiled=True,
    ).astype(jnp.float32)
    result_rows = lax.all_gather(
        (resid_share + ffn_share).astype(jnp.bfloat16), "tp", axis=0, tiled=True
    ).astype(jnp.float32)
    error_rows = result_rows - target
    grad_out = valid_rows * error_rows
    loss_part = jnp.sum(grad_out * error_rows)
    loss_spread = jnp.full((lax.axis_size(("fsdp", "ctx")),), 1.0, jnp.float32) * loss_part
    grad_ffn = grad_out.astype(jnp.bfloat16)
    grad_inner = contract_cols(grad_ffn, d_weight)
    part_down = contract_rows(inner_act, grad_ffn)
    silu_slope = sig_gate * (1.0 + gate_lin * (1.0 - sig_gate))
    grad_gate = (grad_inner * up_lin * silu_slope).astype(jnp.bfloat16)
    grad_up = (grad_inner * act_gate).astype(jnp.bfloat16)
    part_gate = contract_rows(hidden_f, grad_gate)
    part_up = contract_rows(hidden_f, grad_up)
    grad_hidden_f = lax.psum_scatter(
        (contract_cols(grad_gate, g_weight) + contract_cols(grad_up, u_weight)).astype(
            jnp.bfloat16
        ),
        "tp",
        scatter_dimension=0,
        tiled=True,
    ).astype(jnp.float32)
    part_gain_mlp = jnp.sum(grad_hidden_f * normed_f, axis=0)
    grad_mid = own_rows(grad_out) + norm_back(grad_hidden_f, normed_f, scale_f, gain_mlp)
    grad_attn = lax.all_gather(grad_mid.astype(jnp.bfloat16), "tp", axis=0, tiled=True)
    part_out = contract_rows(attended, grad_attn)
    grad_heads = (
        contract_cols(grad_attn, o_weight)
        .astype(jnp.bfloat16)
        .reshape(tok_rows, heads_k, group_size, HD)
    )
    delta_rows = jnp.transpose(
        jnp.sum(grad_heads.astype(jnp.float32) * attended_full, axis=-1), (1, 2, 0)
    )

    def grad_step(key_start, block_len, running):

        def grad_compute_block(carried):
            grad_query, grad_keys = carried
            prob_rows = probs_at(key_start, block_len)
            prob_low = prob_rows.astype(jnp.bfloat16)
            keys_block = lax.dynamic_slice_in_dim(keys_all, key_start, block_len, 2)
            values_block = lax.dynamic_slice_in_dim(values_all, key_start, block_len, 2)
            grad_probs = jnp.einsum(
                "qkgd,kdn->kgqn", grad_heads, values_block, preferred_element_type=jnp.float32
            )
            grad_scores = (prob_rows * (grad_probs - delta_rows[..., None])).astype(jnp.bfloat16)
            grad_query = grad_query + jnp.einsum(
                "kgqn,kdn->qkgd", grad_scores, keys_block, preferred_element_type=jnp.float32
            )
            key_part = jnp.einsum(
                "kgqn,qkgd->kdn", grad_scores, grouped_q, preferred_element_type=jnp.float32
            )
            value_part = jnp.einsum(
                "kgqn,qkgd->kdn", prob_low, grad_heads, preferred_element_type=jnp.float32
            )
            block_grads = jnp.concatenate([key_part, value_part], axis=0)
            grad_keys = lax.dynamic_update_slice_in_dim(grad_keys, block_grads, key_start, 2)
            return (grad_query, grad_keys)

        return lax.cond(is_live(key_start, block_len), grad_compute_block, keep_state, running)

    grad_query, grad_keys = sweep_keys(
        total_keys,
        grad_step,
        (
            jnp.zeros((tok_rows, heads_k, group_size, HD), jnp.float32),
            jnp.zeros((2 * heads_k, HD, total_keys), jnp.float32),
        ),
    )
    kv_grad_local = lax.psum_scatter(
        grad_keys.reshape(2 * kv_cols, total_keys).astype(jnp.bfloat16),
        "ctx",
        scatter_dimension=1,
        tiled=True,
    ).astype(jnp.float32)
    grad_key_rot = kv_grad_local[:kv_cols].reshape(heads_k, HD, tok_rows) * att_scale
    grad_key_lin = unrotate_keys(grad_key_rot, cos_keys, sin_keys).reshape(kv_cols, tok_rows)
    grad_kv = jnp.concatenate([grad_key_lin, kv_grad_local[kv_cols:]], axis=0).astype(jnp.bfloat16)
    grad_query_lin = unrotate(
        grad_query.reshape(tok_rows, heads_q, HD) * att_scale,
        cos_table[:, None, :],
        sin_table[:, None, :],
    )
    grad_query_lin = grad_query_lin.reshape(tok_rows, q_cols).astype(jnp.bfloat16)
    part_query = contract_rows(hidden_a, grad_query_lin)
    part_kv = lax.dot_general(
        hidden_a, grad_kv, (((0,), (1,)), ((), ())), preferred_element_type=jnp.float32
    )
    part_key = part_kv[:, :kv_cols]
    part_value = part_kv[:, kv_cols:]
    grad_hidden_a = lax.psum_scatter(
        (
            contract_cols(grad_query_lin, q_weight)
            + lax.dot_general(
                grad_kv, w_kv, (((0,), (1,)), ((), ())), preferred_element_type=jnp.float32
            )
        ).astype(jnp.bfloat16),
        "tp",
        scatter_dimension=0,
        tiled=True,
    ).astype(jnp.float32)
    normed_a_share = own_rows(normed_a)
    part_gain_att = jnp.sum(grad_hidden_a * normed_a_share, axis=0)
    grad_share = grad_mid + norm_back(grad_hidden_a, normed_a_share, own_rows(scale_a), gain_att)
    gain_stack = jnp.stack([part_gain_att, part_gain_mlp], axis=0)
    grad_rows, gain_rows = (
        lax.all_gather(as_sent(grad_share), "tp", axis=0, tiled=True).astype(grad_share.dtype),
        lax.all_gather(gain_stack.astype(jnp.bfloat16), "tp", axis=0, tiled=True).astype(
            gain_stack.dtype
        ),
    )
    gain_total = jnp.sum(gain_rows.reshape(-1, 2, model_width), axis=0)
    total_gain_att = gain_total[0]
    total_gain_mlp = gain_total[1]
    (
        shard_query,
        shard_key,
        shard_value,
        shard_out,
        shard_gate,
        shard_up,
        shard_down,
        shard_gain_att,
        shard_gain_mlp,
        shard_loss,
    ) = (
        lax.psum_scatter(
            part_query.astype(jnp.bfloat16), ("fsdp", "ctx"), scatter_dimension=0, tiled=True
        ).astype(jnp.float32),
        lax.psum_scatter(
            part_key.astype(jnp.bfloat16), ("fsdp", "ctx"), scatter_dimension=0, tiled=True
        ).astype(jnp.float32),
        lax.psum_scatter(
            part_value.astype(jnp.bfloat16), ("fsdp", "ctx"), scatter_dimension=0, tiled=True
        ).astype(jnp.float32),
        lax.psum_scatter(
            part_out.astype(jnp.bfloat16), ("fsdp", "ctx"), scatter_dimension=1, tiled=True
        ).astype(jnp.float32),
        lax.psum_scatter(
            part_gate.astype(jnp.bfloat16), ("fsdp", "ctx"), scatter_dimension=0, tiled=True
        ).astype(jnp.float32),
        lax.psum_scatter(
            part_up.astype(jnp.bfloat16), ("fsdp", "ctx"), scatter_dimension=0, tiled=True
        ).astype(jnp.float32),
        lax.psum_scatter(
            part_down.astype(jnp.bfloat16), ("fsdp", "ctx"), scatter_dimension=1, tiled=True
        ).astype(jnp.float32),
        lax.psum_scatter(
            total_gain_att.astype(jnp.bfloat16), ("fsdp", "ctx"), scatter_dimension=0, tiled=True
        ).astype(jnp.float32),
        lax.psum_scatter(
            total_gain_mlp.astype(jnp.bfloat16), ("fsdp", "ctx"), scatter_dimension=0, tiled=True
        ).astype(jnp.float32),
        lax.psum_scatter(
            loss_spread.astype(jnp.bfloat16), ("fsdp", "ctx"), scatter_dimension=0, tiled=True
        ).astype(jnp.float32),
    )
    loss_value = shard_loss[0] / (valid_count.astype(jnp.float32) * model_width)
    return (
        result_rows.astype(jnp.bfloat16)[None],
        loss_value,
        grad_rows[None],
        shard_gain_att,
        shard_query,
        shard_key,
        shard_value,
        shard_out,
        shard_gain_mlp,
        shard_gate,
        shard_up,
        shard_down,
    )


def solution(mesh):
    placed = (
        P("fsdp", "ctx", None),
        P("fsdp", "ctx", None),
        P("fsdp", "ctx"),
        P("fsdp", "ctx"),
        P("fsdp", "ctx"),
        P(),
        P(("fsdp", "ctx")),
        P(("fsdp", "ctx"), "tp"),
        P(("fsdp", "ctx"), "tp"),
        P(("fsdp", "ctx"), "tp"),
        P("tp", ("fsdp", "ctx")),
        P(("fsdp", "ctx")),
        P(("fsdp", "ctx"), "tp"),
        P(("fsdp", "ctx"), "tp"),
        P("tp", ("fsdp", "ctx")),
    )
    return jax.shard_map(
        on_device,
        mesh=mesh,
        in_specs=placed,
        out_specs=(
            P("fsdp", "ctx", None),
            P(),
            P("fsdp", "ctx", None),
            P(("fsdp", "ctx")),
            P(("fsdp", "ctx"), "tp"),
            P(("fsdp", "ctx"), "tp"),
            P(("fsdp", "ctx"), "tp"),
            P("tp", ("fsdp", "ctx")),
            P(("fsdp", "ctx")),
            P(("fsdp", "ctx"), "tp"),
            P(("fsdp", "ctx"), "tp"),
            P("tp", ("fsdp", "ctx")),
        ),
        check_vma=False,
    )
```

profile of v0, /device:TPU:0, one launch (start us, length us, event | category | flops | bytes accessed | tf_op | source)
XLA Modules:
  0.0 1321.6 jit_solution(12397779929093032033)
XLA Ops:
  11.8 16.0 %all-reduce.6 = (bf16[1536]{0:T(1024)(128)(2,1)S(1)}, bf16[1536]{0:T(1024)(128)(2,1)}) all-reduce(bf16[1536]{0:T(1024)(128)(2,1)S(1)} %dynamic-update-slice, bf16[1536]{0:T(1024)(128)(2,1)S(1)} %dynamic-update-slice.1), channel_id=1, replica_groups=mesh['fsdp'=2,'ctx'=4,'tp'=4] {'fsdp','ctx'}, use_global_device_ids=true, to_apply=%add | all-reduce | flops 3072 | bytes 12288
  27.8 11.0 all_gather.49
  38.8 10.1 all_gather.50
  48.9 2.9 fusion.41
  57.7 5.6 all-gather
  64.8 2.6 copy.38
  67.4 2.8 fusion.44
  70.6 14.8 %all-gather.13.cloned.1.call-done = bf16[384,4096]{1,0:T(8,128)(2,1)} async-done(((bf16[384,1024]{1,0:T(8,128)(2,1)}), bf16[384,4096]{1,0:T(8,128)(2,1)}) %all-gather.13.cloned.1.call-update) | async-done | bytes 3145744 | tf_op jit(solution)/shard_map/all_gather | solution.py:194
  85.4 3.9 fusion.75
  89.5 23.3 %while.42 = (s32[]{:T(128)}, f32[2,2,1024]{2,1,0:T(2,128)S(1)}, f32[2,2,1024]{2,1,0:T(2,128)S(1)}, f32[1024,2,2,96]{0,3,2,1:T(8,128)S(1)}, s32[]{:T(128)}, /*ind...) while((s32[]{:T(128)}, f32[2,2,1024]{2,1,0:T(2,128)S(1)}, ...), condition=%wide.region_6.7_spmd.clone, body=%wide.region_1.6_spmd.clone.sunk | while | flops 1660696576 | bytes 59548096 | solution.py:105
  91.4 15.7 %conditional.6 = ((f32[2,2,1024]{2,1,0:T(2,128)S(1)}, f32[2,2,1024]{2,1,0:T(2,128)S(1)}, f32[1024,2,2,96]{0,3,2,1:T(8,128)S(1)})) conditional(s32[]{:T(128)} %convert_element_type.421, (f32[2,2,1024]{2,1,0:T(2,128)S(1)}, f32[2,2,1024]{2,1,0:T(2,128)S(1)}, f32[1024,2,2,96]{0,3,2,1:T(8,128)S(1)}) %tuple.137, (s32[1,1024]{1,0:T(1,128)S(1)}, s32[]{:T(128)}, ...), branch_computations={%region_2.0_spmd, %region_3.5_spmd} | conditional | flops 1660696576 | bytes 59543636 | solution.py:236
  92.6 4.6 fusion.6
  97.2 6.1 bitcast_add_fusion
  103.4 3.7 fusion.5
  113.9 5.0 convolution_convert_fusion
  119.6 5.5 convert_element_type.244
  125.1 101.3 %reduce-scatter.17.cloned.1.call-done = bf16[256,1536]{1,0:T(8,128)(2,1)} async-done(((bf16[1024,1536]{1,0:T(8,128)(2,1)}), bf16[256,1536]{1,0:T(8,128)(2,1)}) %reduce-scatter.17.cloned.1.call-update) | async-done | bytes 786448 | tf_op jit(solution)/shard_map/reduce_scatter | solution.py:255
  231.3 29.3 %all-gather.21.cloned.1.call-done = bf16[1536,1024]{1,0:T(8,128)(2,1)} async-done(((bf16[192,1024]{1,0:T(8,128)(2,1)}), bf16[1536,1024]{1,0:T(8,128)(2,1)}) %all-gather.21.cloned.1.call-update) | async-done | bytes 3145744 | tf_op jit(solution)/shard_map/all_gather | solution.py:165
  260.6 65.5 %all-gather.19.cloned.1.call-done = bf16[1024,1536]{1,0:T(8,128)(2,1)} async-done(((bf16[256,1536]{1,0:T(8,128)(2,1)}), bf16[1024,1536]{1,0:T(8,128)(2,1)}) %all-gather.19.cloned.1.call-update) | async-done | bytes 3145744 | tf_op jit(solution)/shard_map/all_gather | solution.py:264
  326.1 8.3 fusion.78
  334.4 24.6 %all-gather.23.cloned.1.call-done = bf16[1536,1024]{1,0:T(8,128)(2,1)} async-done(((bf16[192,1024]{1,0:T(8,128)(2,1)}), bf16[1536,1024]{1,0:T(8,128)(2,1)}) %all-gather.23.cloned.1.call-update) | async-done | bytes 3145744 | tf_op jit(solution)/shard_map/all_gather | solution.py:166
  359.0 10.4 multiply_convert_fusion.4
  369.4 23.8 %all-gather.25.cloned.1.call-done = bf16[1024,1536]{0,1:T(8,128)(2,1)} async-done(((bf16[1024,192]{0,1:T(8,128)(2,1)}), bf16[1024,1536]{0,1:T(8,128)(2,1)}) %all-gather.25.cloned.1.call-update) | async-done | bytes 3145744 | tf_op jit(solution)/shard_map/all_gather | solution.py:167
  393.2 7.6 convolution_convert_fusion.4
  400.9 60.4 %reduce-scatter.19.cloned.1.call-done = bf16[256,1536]{1,0:T(8,128)(2,1)} async-done(((bf16[1024,1536]{1,0:T(8,128)(2,1)}), bf16[256,1536]{1,0:T(8,128)(2,1)}) %reduce-scatter.19.cloned.1.call-update) | async-done | bytes 786448 | tf_op jit(solution)/shard_map/reduce_scatter | solution.py:270
  464.0 63.2 %all-gather.27.cloned.1.call-done = bf16[1024,1536]{1,0:T(8,128)(2,1)} async-done(((bf16[256,1536]{1,0:T(8,128)(2,1)}), bf16[1024,1536]{1,0:T(8,128)(2,1)}) %all-gather.27.cloned.1.call-update) | async-done | bytes 3145744 | tf_op jit(solution)/shard_map/all_gather | solution.py:276
  527.2 11.0 multiply_convert_fusion.2
  538.3 3.4 fusion.79
  541.8 4.9 add_convert_fusion.1
  546.8 7.5 fusion.42
  554.2 51.5 %reduce-scatter.21.cloned.1.call-done = bf16[256,1536]{1,0:T(8,128)(2,1)} async-done(((bf16[1024,1536]{1,0:T(8,128)(2,1)}), bf16[256,1536]{1,0:T(8,128)(2,1)}) %reduce-scatter.21.cloned.1.call-update) | async-done | bytes 786448 | tf_op jit(solution)/shard_map/reduce_scatter | solution.py:291
  608.1 3.0 fusion.72
  611.3 63.5 %all-gather.29.cloned.1.call-done = bf16[1024,1536]{1,0:T(8,128)(2,1)} async-done(((bf16[256,1536]{1,0:T(8,128)(2,1)}), bf16[1024,1536]{1,0:T(8,128)(2,1)}) %all-gather.29.cloned.1.call-update) | async-done | bytes 3145744 | tf_op jit(solution)/shard_map/all_gather | solution.py:301
  674.8 3.6 convolution_convert_fusion.7
  681.0 42.8 %while.43 = (s32[]{:T(128)}, f32[1024,2,2,96]{0,3,2,1:T(8,128)S(1)}, bf16[4,96,4096]{2,1,0:T(8,128)(2,1)}, s32[]{:T(128)}, s32[4096]{0:T(1024)S(1)}, /*index=5*/...) while((s32[]{:T(128)}, ...), condition=%wide.region_18.19_spmd.clone, body=%wide.region_15.18_spmd.clone.sunk | while | flops 4065200128 | bytes 87515624 | solution.py:105
  682.8 35.2 %conditional.7 = ((f32[1024,2,2,96]{0,3,2,1:T(8,128)S(1)}, bf16[4,96,4096]{2,1,0:T(8,128)(2,1)})) conditional(s32[]{:T(128)} %convert_element_type.422, (f32[1024,2,2,96]{0,3,2,1:T(8,128)S(1)}, bf16[4,96,4096]{2,1,0:T(8,128)(2,1)}) %tuple.140, (s32[]{:T(128)}, bf16[2,96,4096]{2,1,0:T(8,128)(2,1)}, s32[1,1024]{1,0:T(1,128)S(1)}, ...), branch_computations={%region_16.16_spmd, %region_17.17_spmd} | conditional | flops 4065200128 | bytes 87511128 | solution.py:337
  684.1 9.4 fusion.26
  693.5 8.5 fusion.29
  702.0 8.4 fusion.23
  710.4 3.9 convolution_bitcast_fusion
  714.3 2.8 bitcast_add_fusion.1
  726.0 4.5 fusion.80
  730.5 135.1 %reduce-scatter.23.cloned.1.call-done = bf16[384,1024]{1,0:T(8,128)(2,1)} async-done(((bf16[384,4096]{1,0:T(8,128)(2,1)}), bf16[384,1024]{1,0:T(8,128)(2,1)}) %reduce-scatter.23.cloned.1.call-update) | async-done | bytes 786448 | tf_op jit(solution)/shard_map/reduce_scatter | solution.py:347
  867.8 6.4 add_convert_fusion
  876.1 7.9 convolution_convert_fusion.1
  885.9 6.5 convolution_convert_fusion.2
  892.4 6.5 convolution_convert_fusion.3
  899.3 5.2 convolution_convert_fusion.6
  904.6 4.3 fusion.48
  909.0 2.5 convolution_convert_fusion.5
  915.0 3.1 bitcast_multiply_fusion
  920.7 14.0 %reduce-scatter.25.cloned.1.call-done = bf16[256,1536]{1,0:T(8,128)(2,1)} async-done(((bf16[1024,1536]{1,0:T(8,128)(2,1)}), bf16[256,1536]{1,0:T(8,128)(2,1)}) %reduce-scatter.25.cloned.1.call-update) | async-done | bytes 786448 | tf_op jit(solution)/shard_map/reduce_scatter | solution.py:368
  936.8 3.7 fusion.58
  941.9 42.7 %reduce-scatter.35.cloned.1.call-done = bf16[1024,192]{0,1:T(8,128)(2,1)} async-done(((bf16[1024,1536]{0,1:T(8,128)(2,1)}), bf16[1024,192]{0,1:T(8,128)(2,1)}) %reduce-scatter.35.cloned.1.call-update) | async-done | bytes 393232 | tf_op jit(solution)/shard_map/reduce_scatter | solution.py:422
  986.5 47.5 %reduce-scatter.33.cloned.1.call-done = bf16[192,1024]{1,0:T(8,128)(2,1)} async-done(((bf16[1536,1024]{1,0:T(8,128)(2,1)}), bf16[192,1024]{1,0:T(8,128)(2,1)}) %reduce-scatter.33.cloned.1.call-update) | async-done | bytes 393232 | tf_op jit(solution)/shard_map/reduce_scatter | solution.py:419
  1036.0 47.9 %reduce-scatter.31.cloned.1.call-done = bf16[192,1024]{1,0:T(8,128)(2,1)} async-done(((bf16[1536,1024]{1,0:T(8,128)(2,1)}), bf16[192,1024]{1,0:T(8,128)(2,1)}) %reduce-scatter.31.cloned.1.call-update) | async-done | bytes 393232 | tf_op jit(solution)/shard_map/reduce_scatter | solution.py:416
  1085.9 37.9 %reduce-scatter.29.cloned.1.call-done = bf16[384,192]{0,1:T(8,128)(2,1)} async-done(((bf16[384,1536]{0,1:T(8,128)(2,1)}), bf16[384,192]{0,1:T(8,128)(2,1)}) %reduce-scatter.29.cloned.1.call-update) | async-done | bytes 147472 | tf_op jit(solution)/shard_map/reduce_scatter | solution.py:413
  1125.5 38.7 %reduce-scatter.27.cloned.1.call-done = bf16[192,384]{1,0:T(8,128)(2,1)} async-done(((bf16[1536,384]{1,0:T(8,128)(2,1)}), bf16[192,384]{1,0:T(8,128)(2,1)}) %reduce-scatter.27.cloned.1.call-update) | async-done | bytes 147472 | tf_op jit(solution)/shard_map/reduce_scatter | solution.py:404
  1165.8 36.3 %reduce-scatter.39.cloned.1.call-done = bf16[192,192]{1,0:T(8,128)(2,1)} async-done(((bf16[1536,192]{1,0:T(8,128)(2,1)}), bf16[192,192]{1,0:T(8,128)(2,1)}) %reduce-scatter.39.cloned.1.call-update) | async-done | bytes 73744
  1204.0 36.4 %reduce-scatter.37.cloned.1.call-done = bf16[192,192]{1,0:T(8,128)(2,1)} async-done(((bf16[1536,192]{1,0:T(8,128)(2,1)}), bf16[192,192]{1,0:T(8,128)(2,1)}) %reduce-scatter.37.cloned.1.call-update) | async-done | bytes 73744
  1242.1 13.3 %all-gather.1 = bf16[4,2,1536]{2,1,0:T(2,128)(2,1)S(1)} all-gather(bf16[1,2,1536]{2,1,0:T(2,128)(2,1)S(1)} %maximum_bitcast_fusion), channel_id=1, replica_groups=mesh['fsdp'=2,'ctx'=4,'tp'=4] {'tp'}, dimensions={0}, use_global_device_ids=true | all-gather | bytes 30720 | tf_op jit(solution)/shard_map/all_gather | solution.py:385
  1256.2 13.2 all-reduce.5
  1271.9 34.2 %all-gather.31.cloned.1.call-done = bf16[1024,1536]{1,0:T(8,128)(2,1)} async-done(((bf16[256,1536]{1,0:T(8,128)(2,1)}), bf16[1024,1536]{1,0:T(8,128)(2,1)}) %all-gather.31.cloned.1.call-update) | async-done | bytes 3145744 | tf_op jit(solution)/shard_map/all_gather | solution.py:384
  1306.1 5.5 bitcast_convert_fusion
  (240 shorter events, 68.1 us)
Async XLA Ops:
  7.2 44.6 %copy-start.3 = (bf16[1,1024,1536]{2,1,0:T(8,128)(2,1)S(1)}, bf16[1,1024,1536]{2,1,0:T(8,128)(2,1)}, u32[]{:S(2)}) copy-start(bf16[1,1024,1536]{2,1,0:T(8,128)(2,1)} %param.23) | copy-start | bytes 9437188
  7.2 57.6 %all-gather.15.cloned.1.call-start = ((), (), s32[]{:S(2)}) async-start(), calls=%async_computation.13 | async-start | bytes 1327104 | tf_op jit(solution)/shard_map/all_gather | solution.py:161
  7.9 77.5 %all-gather.13.cloned.1.call-start = ((), (), s32[]{:S(2)}) async-start(), calls=%async_computation.12 | async-start | bytes 3932160 | tf_op jit(solution)/shard_map/all_gather | solution.py:194
  27.8 39.6 %copy-start.28 = (f32[1536]{0:T(1024)}, f32[1536]{0:T(1024)S(1)}, u32[]{:S(2)}) copy-start(f32[1536]{0:T(1024)S(1)} %convert_element_type.246) | copy-start | bytes 18436
  38.8 14.9 %copy-start.10 = (bf16[1536,192]{1,0:T(8,128)(2,1)}, bf16[1536,192]{1,0:T(8,128)(2,1)S(1)}, u32[]{:S(2)}) copy-start(bf16[1536,192]{1,0:T(8,128)(2,1)S(1)} %all_gather.49) | copy-start | bytes 1769476
  48.9 4.8 copy-start.12
  51.7 2.0 copy-start.32
  51.8 2.1 copy-start.40
  53.8 3.4 copy-start.24
  53.9 3.8 copy-start.42
  56.4 57.5 %all-gather.17.cloned.1.call-start = ((), (), s32[]{:S(2)}) async-start(), calls=%async_computation.14 | async-start | bytes 1327104 | tf_op jit(solution)/shard_map/all_gather | solution.py:164
  57.1 169.3 %reduce-scatter.17.cloned.1.call-start = ((), (), s32[]{:S(2)}) async-start(), calls=%async_computation.15 | async-start | bytes 3932160 | tf_op jit(solution)/shard_map/reduce_scatter | solution.py:255
  64.7 5.5 copy-start.18
  64.8 5.5 copy-start.20
  70.6 19.0 %copy-start.27 = (s32[1,4096]{1,0:T(1,128)S(1)}, s32[1,4096]{1,0:T(1,128)}, u32[]{:S(2)}) copy-start(s32[1,4096]{1,0:T(1,128)} %all-gather) | copy-start | bytes 49156
  112.8 12.3 copy-start.2
  119.0 141.6 %all-gather.21.cloned.1.call-start = ((), (), s32[]{:S(2)}) async-start(), calls=%async_computation.17 | async-start | bytes 3538944 | tf_op jit(solution)/shard_map/all_gather | solution.py:165
  119.6 206.5 %all-gather.19.cloned.1.call-start = ((), (), s32[]{:S(2)}) async-start(), calls=%async_computation.16 | async-start | bytes 3932160 | tf_op jit(solution)/shard_map/all_gather | solution.py:264
  119.6 5.5 copy-start.39
  125.1 483.0 %copy-start.25 = (f32[1536]{0:T(1024)}, f32[1536]{0:T(1024)S(1)}, u32[]{:S(2)}) copy-start(f32[1536]{0:T(1024)S(1)} %convert_element_type.257) | copy-start | bytes 18436
  228.4 379.7 %copy-start = (f32[256,1536]{1,0:T(8,128)}, f32[256,1536]{1,0:T(8,128)S(1)}, u32[]{:S(2)}) copy-start(f32[256,1536]{1,0:T(8,128)S(1)} %get-tuple-element.1140) | copy-start | bytes 4718596
  228.4 379.7 %copy-start.30 = (f32[256]{0:T(256)}, f32[256]{0:T(256)S(1)}, u32[]{:S(2)}) copy-start(f32[256]{0:T(256)S(1)} %add_rsqrt_fusion.1) | copy-start | bytes 3076
  229.7 129.3 %all-gather.23.cloned.1.call-start = ((), (), s32[]{:S(2)}) async-start(), calls=%async_computation.18 | async-start | bytes 3538944 | tf_op jit(solution)/shard_map/all_gather | solution.py:166
  230.5 162.7 %all-gather.25.cloned.1.call-start = ((), (), s32[]{:S(2)}) async-start(), calls=%async_computation.19 | async-start | bytes 3538944 | tf_op jit(solution)/shard_map/all_gather | solution.py:167
  231.2 230.1 %reduce-scatter.19.cloned.1.call-start = ((), (), s32[]{:S(2)}) async-start(), calls=%async_computation.20 | async-start | bytes 3932160 | tf_op jit(solution)/shard_map/reduce_scatter | solution.py:270
  400.9 63.1 %copy-start.41 = (s32[1,1024]{1,0:T(1,128)S(1)}, s32[1,1024]{1,0:T(1,128)}, u32[]{:S(2)}) copy-start(s32[1,1024]{1,0:T(1,128)} %param.27) | copy-start | bytes 12292
  400.9 126.3 %all-gather.27.cloned.1.call-start = ((), (), s32[]{:S(2)}) async-start(), calls=%async_computation.21 | async-start | bytes 3932160 | tf_op jit(solution)/shard_map/all_gather | solution.py:276
  463.5 142.3 %reduce-scatter.21.cloned.1.call-start = ((), (), s32[]{:S(2)}) async-start(), calls=%async_computation.22 | async-start | bytes 3932160 | tf_op jit(solution)/shard_map/reduce_scatter | solution.py:291
  464.0 82.8 %copy-start.35 = (f32[1,1024]{1,0:T(1,128)}, f32[1,1024]{1,0:T(1,128)S(1)}, u32[]{:S(2)}) copy-start(f32[1,1024]{1,0:T(1,128)S(1)} %convert_element_type.263) | copy-start | bytes 12292
  527.2 11.0 copy-start.44
  538.2 3.5 copy-start.46
  538.2 3.5 copy-start.47
  538.3 3.5 copy-start.45
  546.7 128.1 %all-gather.29.cloned.1.call-start = ((), (), s32[]{:S(2)}) async-start(), calls=%async_computation.23 | async-start | bytes 3932160 | tf_op jit(solution)/shard_map/all_gather | solution.py:301
  608.1 70.4 %copy-start.37 = (f32[256]{0:T(256)}, f32[256]{0:T(256)S(1)}, u32[]{:S(2)}) copy-start(f32[256]{0:T(256)S(1)} %broadcast_multiply_fusion.2) | copy-start | bytes 3076
  611.1 254.5 %reduce-scatter.23.cloned.1.call-start = ((), (), s32[]{:S(2)}) async-start(), calls=%async_computation.24 | async-start | bytes 3932160 | tf_op jit(solution)/shard_map/reduce_scatter | solution.py:347
  723.8 210.8 %reduce-scatter.25.cloned.1.call-start = ((), (), s32[]{:S(2)}) async-start(), calls=%async_computation.25 | async-start | bytes 3932160 | tf_op jit(solution)/shard_map/reduce_scatter | solution.py:368
  724.1 1.9 copy-start.8
  726.0 140.8 %copy-start.15 = (f32[48,1024]{1,0:T(8,128)S(1)}, f32[48,1024]{1,0:T(8,128)}, u32[]{:S(2)}) copy-start(f32[48,1024]{1,0:T(8,128)} %copy-done.14) | copy-start | bytes 589828
  726.0 140.8 %copy-start.17 = (f32[48,1024]{1,0:T(8,128)S(1)}, f32[48,1024]{1,0:T(8,128)}, u32[]{:S(2)}) copy-start(f32[48,1024]{1,0:T(8,128)} %copy-done.16) | copy-start | bytes 589828
  730.5 137.3 %copy-start.11 = (bf16[1536,192]{1,0:T(8,128)(2,1)S(1)}, bf16[1536,192]{1,0:T(8,128)(2,1)}, u32[]{:S(2)}) copy-start(bf16[1536,192]{1,0:T(8,128)(2,1)} %copy-done.10) | copy-start | bytes 1769476
  730.5 137.3 %copy-start.13 = (bf16[1536,192]{1,0:T(8,128)(2,1)S(1)}, bf16[1536,192]{1,0:T(8,128)(2,1)}, u32[]{:S(2)}) copy-start(bf16[1536,192]{1,0:T(8,128)(2,1)} %copy-done.12) | copy-start | bytes 1769476
  865.6 1.3 copy-start.23
  867.8 6.5 copy-start.36
  874.2 1.9 copy-start.5
  874.2 110.4 %reduce-scatter.35.cloned.1.call-start = ((), (), s32[]{:S(2)}) async-start(), calls=%async_computation.31 | async-start | bytes 3538944 | tf_op jit(solution)/shard_map/reduce_scatter | solution.py:422
  884.0 1.9 copy-start.43
  884.0 150.0 %reduce-scatter.33.cloned.1.call-start = ((), (), s32[]{:S(2)}) async-start(), calls=%async_computation.30 | async-start | bytes 3538944 | tf_op jit(solution)/shard_map/reduce_scatter | solution.py:419
  892.4 191.5 %reduce-scatter.31.cloned.1.call-start = ((), (), s32[]{:S(2)}) async-start(), calls=%async_computation.29 | async-start | bytes 3538944 | tf_op jit(solution)/shard_map/reduce_scatter | solution.py:416
  899.0 5.6 copy-start.4
  899.0 5.6 copy-start.29
  899.0 5.6 copy-start.33
  899.0 224.8 %reduce-scatter.29.cloned.1.call-start = ((), (), s32[]{:S(2)}) async-start(), calls=%async_computation.28 | async-start | bytes 1327104 | tf_op jit(solution)/shard_map/reduce_scatter | solution.py:413
  904.5 259.7 %reduce-scatter.27.cloned.1.call-start = ((), (), s32[]{:S(2)}) async-start(), calls=%async_computation.27 | async-start | bytes 1327104 | tf_op jit(solution)/shard_map/reduce_scatter | solution.py:404
  908.9 293.2 %reduce-scatter.39.cloned.1.call-start = ((), (), s32[]{:S(2)}) async-start(), calls=%async_computation.33 | async-start | bytes 884736
  914.9 325.5 %reduce-scatter.37.cloned.1.call-start = ((), (), s32[]{:S(2)}) async-start(), calls=%async_computation.32 | async-start | bytes 884736
  918.1 18.6 %copy-start.1 = (f32[256,1536]{1,0:T(8,128)S(1)}, f32[256,1536]{1,0:T(8,128)}, u32[]{:S(2)}) copy-start(f32[256,1536]{1,0:T(8,128)} %copy-done) | copy-start | bytes 4718596
  918.1 18.6 %copy-start.7 = (bf16[256,1536]{1,0:T(8,128)(2,1)S(1)}, bf16[256,1536]{1,0:T(8,128)(2,1)}, u32[]{:S(2)}) copy-start(bf16[256,1536]{1,0:T(8,128)(2,1)} %reduce-scatter.21.cloned.1.call-done) | copy-start | bytes 2359300
  918.1 18.6 %copy-start.26 = (f32[1536]{0:T(1024)S(1)}, f32[1536]{0:T(1024)}, u32[]{:S(2)}) copy-start(f32[1536]{0:T(1024)} %copy-done.25) | copy-start | bytes 18436
  918.1 18.7 %copy-start.31 = (f32[256]{0:T(256)S(1)}, f32[256]{0:T(256)}, u32[]{:S(2)}) copy-start(f32[256]{0:T(256)} %copy-done.30) | copy-start | bytes 3076
  918.1 18.7 %copy-start.38 = (f32[256]{0:T(256)S(1)}, f32[256]{0:T(256)}, u32[]{:S(2)}) copy-start(f32[256]{0:T(256)} %copy-done.37) | copy-start | bytes 3076
  920.6 385.5 %all-gather.31.cloned.1.call-start = ((), (), s32[]{:S(2)}) async-start(), calls=%async_computation.26 | async-start | bytes 3932160 | tf_op jit(solution)/shard_map/all_gather | solution.py:384
  940.6 145.3 %copy-start.34 = (bf16[1536]{0:T(1024)(128)(2,1)S(1)}, bf16[1536]{0:T(1024)(128)(2,1)}, u32[]{:S(2)}) copy-start(bf16[1536]{0:T(1024)(128)(2,1)} %get-tuple-element.1074) | copy-start | bytes 9220
  1271.9 39.6 %copy-start.6 = (bf16[1024,1536]{1,0:T(8,128)(2,1)S(1)}, bf16[1024,1536]{1,0:T(8,128)(2,1)}, u32[]{:S(2)}) copy-start(bf16[1024,1536]{1,0:T(8,128)(2,1)} %all-gather.27.cloned.1.call-done) | copy-start | bytes 9437188
  (6 other events, 5.0 us)
Sparse Core Ops, SparseCore 0:
  9.9 27.7 all-gather.14
  56.5 28.8 all-gather.12
  87.3 24.0 all-gather.16
  119.1 107.3 reduce-scatter.16
  228.2 32.3 all-gather.20
  262.6 63.4 all-gather.18
  328.0 30.9 all-gather.22
  360.9 32.3 all-gather.24
  401.0 60.2 reduce-scatter.18
  463.6 63.5 all-gather.26
  546.8 58.8 reduce-scatter.20
  611.2 63.5 all-gather.28
  723.9 141.6 reduce-scatter.22
  874.3 60.2 reduce-scatter.24
  938.2 46.2 reduce-scatter.34
  987.8 46.1 reduce-scatter.32
  1037.6 46.2 reduce-scatter.30
  1087.0 36.7 reduce-scatter.28
  1127.4 36.7 reduce-scatter.26
  1167.2 34.9 reduce-scatter.38
  1205.3 34.9 reduce-scatter.36
  1242.5 63.5 all-gather.30
where the time goes:
time: 1330 us; the launch traced here: 1320 us
  waiting for transfers between devices  972 us (73%)
  matrix products  147 us (11%)
  blocking collectives  69.1 us (5%)
  other arithmetic  64.7 us (5%)
  local copies, waits for them, and re-layouts  37.3 us (3%)
  between operations  19.4 us (1%)
    reduce_scatter x1, waiting for transfers between devices, on_device(): lax.psum_scatter(grad_keys.reshape(2 * kv_cols, total_keys).astype(jnp.bf...  135 us
    reduce_scatter x1, waiting for transfers between devices, on_device(): lax.psum_scatter(jnp.dot(attended, o_weight, preferred_element_type=jnp.f...  101 us
    unnamed x24, waiting for transfers between devices  76.1 us
    all_gather x1, waiting for transfers between devices, on_device(): hidden_f = lax.all_gather(hidden_share, 'tp', axis=0, tiled=True)  65.5 us
    all_gather x1, waiting for transfers between devices, on_device(): lax.all_gather(grad_mid.astype(jnp.bfloat16), 'tp', axis=0, tiled=True)  63.5 us
    all_gather x1, waiting for transfers between devices, on_device(): lax.all_gather((resid_share + ffn_share).astype(jnp.bfloat16), 'tp', axis...  63.2 us
    reduce_scatter x1, waiting for transfers between devices, on_device(): lax.psum_scatter(jnp.dot(inner_act, d_weight, preferred_element_type=jnp....  60.4 us
    reduce_scatter x1, waiting for transfers between devices, on_device(): lax.psum_scatter((contract_cols(grad_gate, g_weight) + contract_cols(grad...  51.5 us
  transfers between devices with their start and end apart: 22, of which 20 were waited for; matrix products, arithmetic and copies ran while one was open for 11% of the time, Pallas kernels for 0%

commit v1 on v0

v1 whole, which is shorter than its diff:
```python
import functools
import math

import jax
import jax.numpy as jnp
from jax import lax
from jax.experimental import pallas as pl
from jax.experimental.pallas import tpu as pltpu
from jax.sharding import Mesh
from jax.sharding import PartitionSpec as P

HD=96
NEG=-1e30
F32=jnp.float32; BF=jnp.bfloat16
def dot(a,b,ca,cb):
    return lax.dot_general(a,b,(((ca,),(cb,)),((),())),preferred_element_type=F32)

def fwd_kernel(scale2, tq, tk, group, bounds, q_ref, k_ref, v_ref, st_ref, qp_ref, o_ref, of_ref, lse_ref, ks, m_s, l_s, acc):
    i = pl.program_id(1)
    @pl.when(i == 0)
    def _():
        ks[...] = k_ref[...].astype(F32).T.astype(BF)
    q2 = jnp.concatenate([q_ref[h*HD:(h+1)*HD, :] for h in range(group)], axis=1)
    st = jnp.concatenate([st_ref[...]]*group, axis=1)
    qp = jnp.concatenate([qp_ref[...]]*group, axis=1)
    m_s[...] = jnp.full_like(m_s, NEG)
    l_s[...] = jnp.zeros_like(l_s)
    acc[...] = jnp.zeros_like(acc)
    def step(masked, j, _):
        off = pl.multiple_of(j*tk, tk)
        s = dot(ks[pl.ds(off, tk), :], q2, 1, 0)
        if masked:
            kid = off + lax.broadcasted_iota(jnp.int32, s.shape, 0)
            s = jnp.where((kid >= st) & (kid <= qp), s, NEG)
        m_old = m_s[...]
        m_new = jnp.maximum(m_old, jnp.max(s, axis=0, keepdims=True))
        p = jnp.exp2((s - m_new)*scale2)
        al = jnp.exp2((m_old - m_new)*scale2)
        l_s[...] = l_s[...]*al + jnp.sum(p, axis=0, keepdims=True)
        m_s[...] = m_new
        acc[...] = acc[...]*al + dot(v_ref[:, pl.ds(off, tk)], p.astype(BF), 1, 0)
        return 0
    lo, a, b, hi = bounds[i,0], bounds[i,1], bounds[i,2], bounds[i,3]
    lax.fori_loop(lo, a, functools.partial(step, True), 0)
    lax.fori_loop(a, b, functools.partial(step, False), 0)
    lax.fori_loop(b, hi, functools.partial(step, True), 0)
    o = acc[...]/l_s[...]
    lse = m_s[...]*scale2 + jnp.log2(l_s[...])
    for h in range(group):
        oh = o[:, h*tq:(h+1)*tq]
        of_ref[h*HD:(h+1)*HD, :] = oh
        o_ref[h*HD:(h+1)*HD, :] = oh.astype(BF)
        lse_ref[0, h:h+1, :] = lse[:, h*tq:(h+1)*tq]

def attn_fwd(qT, kT, vT, start, qpos, bounds, tq=256, tk=512):
    T = qT.shape[1]; N = kT.shape[1]; kv = kT.shape[0]//HD; group = qT.shape[0]//kT.shape[0]
    scale2 = HD**-0.5*math.log2(math.e)
    qs = pl.BlockSpec((group*HD, tq), lambda g,i,b:(g,i))
    ksp = pl.BlockSpec((HD, N), lambda g,i,b:(g,0))
    row = pl.BlockSpec((1, tq), lambda g,i,b:(0,i))
    return pl.pallas_call(
        functools.partial(fwd_kernel, scale2, tq, tk, group),
        out_shape=(jax.ShapeDtypeStruct(qT.shape, BF), jax.ShapeDtypeStruct(qT.shape, F32), jax.ShapeDtypeStruct((kv, group, T), F32)),
        grid_spec=pltpu.PrefetchScalarGridSpec(num_scalar_prefetch=1, grid=(kv, T//tq),
            in_specs=[qs, ksp, ksp, row, row],
            out_specs=[qs, qs, pl.BlockSpec((1, group, tq), lambda g,i,b:(g,0,i))],
            scratch_shapes=[pltpu.VMEM((N,HD),BF), pltpu.VMEM((1,group*tq),F32), pltpu.VMEM((1,group*tq),F32), pltpu.VMEM((HD,group*tq),F32)]),
        compiler_params=pltpu.CompilerParams(vmem_limit_bytes=48*2**20),
        name="attend",
    )(bounds, qT, kT, vT, start, qpos)

def bwd_kernel(scale2, tq, tk, group, bounds, q_ref, k_ref, v_ref, st_ref, qp_ref, g_ref, of_ref, lse_ref, dq_ref, dk_ref, dv_ref, ks, vs, dks, dvs, dqs):
    i = pl.program_id(1)
    @pl.when(i == 0)
    def _():
        ks[...] = k_ref[...].astype(F32).T.astype(BF)
        vs[...] = v_ref[...].astype(F32).T.astype(BF)
        dks[...] = jnp.zeros_like(dks)
        dvs[...] = jnp.zeros_like(dvs)
    cat = lambda f: jnp.concatenate([f(h) for h in range(group)], axis=1)
    q2 = cat(lambda h: q_ref[h*HD:(h+1)*HD, :])
    g2 = cat(lambda h: g_ref[h*HD:(h+1)*HD, :])
    lse = cat(lambda h: lse_ref[0, h:h+1, :])
    delta = cat(lambda h: jnp.sum(g_ref[h*HD:(h+1)*HD, :].astype(F32)*of_ref[h*HD:(h+1)*HD, :], axis=0, keepdims=True))
    st = cat(lambda h: st_ref[...])
    qp = cat(lambda h: qp_ref[...])
    dqs[...] = jnp.zeros_like(dqs)
    def step(masked, j, _):
        off = pl.multiple_of(j*tk, tk)
        s = dot(ks[pl.ds(off, tk), :], q2, 1, 0)
        if masked:
            kid = off + lax.broadcasted_iota(jnp.int32, s.shape, 0)
            s = jnp.where((kid >= st) & (kid <= qp), s, NEG)
        p = jnp.exp2(s*scale2 - lse)
        dp = dot(vs[pl.ds(off, tk), :], g2, 1, 0)
        ds = (p*(dp - delta)).astype(BF)
        dvs[:, pl.ds(off, tk)] += dot(g2, p.astype(BF), 1, 1)
        dks[:, pl.ds(off, tk)] += dot(q2, ds, 1, 1)
        dqs[...] += dot(k_ref[:, pl.ds(off, tk)], ds, 1, 0)
        return 0
    lo, a, b, hi = bounds[i,0], bounds[i,1], bounds[i,2], bounds[i,3]
    lax.fori_loop(lo, a, functools.partial(step, True), 0)
    lax.fori_loop(a, b, functools.partial(step, False), 0)
    lax.fori_loop(b, hi, functools.partial(step, True), 0)
    for h in range(group):
        dq_ref[h*HD:(h+1)*HD, :] = dqs[:, h*tq:(h+1)*tq]
    @pl.when(i == pl.num_programs(1)-1)
    def _():
        dk_ref[...] = dks[...].astype(BF)
        dv_ref[...] = dvs[...].astype(BF)

def attn_bwd(qT, kT, vT, start, qpos, bounds, gT, of, lse, tq=256, tk=512):
    T = qT.shape[1]; N = kT.shape[1]; kv = kT.shape[0]//HD; group = qT.shape[0]//kT.shape[0]
    scale2 = HD**-0.5*math.log2(math.e)
    qs = pl.BlockSpec((group*HD, tq), lambda g,i,b:(g,i))
    ksp = pl.BlockSpec((HD, N), lambda g,i,b:(g,0))
    row = pl.BlockSpec((1, tq), lambda g,i,b:(0,i))
    return pl.pallas_call(
        functools.partial(bwd_kernel, scale2, tq, tk, group),
        out_shape=(jax.ShapeDtypeStruct(qT.shape, F32), jax.ShapeDtypeStruct(kT.shape, BF), jax.ShapeDtypeStruct(kT.shape, BF)),
        grid_spec=pltpu.PrefetchScalarGridSpec(num_scalar_prefetch=1, grid=(kv, T//tq),
            in_specs=[qs, ksp, ksp, row, row, qs, qs, pl.BlockSpec((1, group, tq), lambda g,i,b:(g,0,i))],
            out_specs=[qs, ksp, ksp],
            scratch_shapes=[pltpu.VMEM((N,HD),BF), pltpu.VMEM((N,HD),BF), pltpu.VMEM((HD,N),F32), pltpu.VMEM((HD,N),F32), pltpu.VMEM((HD,group*tq),F32)]),
        compiler_params=pltpu.CompilerParams(vmem_limit_bytes=56*2**20),
        name="attend_back",
    )(bounds, qT, kT, vT, start, qpos, gT, of, lse)

def make_bounds(start, q_first, T, tq, tk):
    s = start.reshape(-1, tq)
    first = q_first + jnp.arange(T//tq, dtype=jnp.int32)*tq
    lo = s[:,0]//tk
    hi = (first + tq - 1)//tk + 1
    a = jnp.minimum((s[:,-1] + tk - 1)//tk, hi)
    b = jnp.maximum(first//tk, a)
    return jnp.stack([lo,a,b,hi],axis=1).astype(jnp.int32)

EPSILON = 1e-05
ROPE_BASE = 100000.0
AXES = ("fsdp", "cx", "cc", "tp")


def swap(values, axis, step=1):
    size = lax.axis_size(axis)
    return lax.ppermute(values, axis, [(i, i ^ step) for i in range(size)])


def ordered(parts, index):
    if len(parts) == 1:
        return list(parts)
    if len(parts) == 2:
        first = index == 0
        return [jnp.where(first, parts[0], parts[1]), jnp.where(first, parts[1], parts[0])]
    stacked = jnp.stack(parts)
    return [
        lax.dynamic_index_in_dim(stacked, jnp.bitwise_xor(index, a), 0, keepdims=False)
        for a in range(len(parts))
    ]


def everyone(values, axis):
    return [values] + [swap(values, axis, k) for k in range(1, lax.axis_size(axis))]


def place_kernel(count, width, place, *refs):
    sources, out, sems = refs[:-2], refs[-2], refs[-1]
    copies = []
    n = 0
    for source in sources:
        for b in range(source.shape[0]):
            copies.append(
                pltpu.make_async_copy(source.at[b], out.at[place[n]], sems.at[n])
            )
            n += 1
    for copy in copies:
        copy.start()
    for copy in copies:
        copy.wait()


def put_blocks(sources, place):
    count = sum(s.shape[0] for s in sources)
    shape = sources[0].shape[1:]
    return pl.pallas_call(
        functools.partial(place_kernel, count, None),
        out_shape=jax.ShapeDtypeStruct((count,) + shape, sources[0].dtype),
        in_specs=[pl.BlockSpec(memory_space=pltpu.SMEM)]
        + [pl.BlockSpec(memory_space=pl.ANY)] * len(sources),
        out_specs=pl.BlockSpec(memory_space=pl.ANY),
        scratch_shapes=[pltpu.SemaphoreType.DMA((count,))],
        name="put_blocks",
    )(jnp.stack(place).astype(jnp.int32), *sources)


def gather_rows(shard):
    rows, width = shard.shape
    nf, nx, nc = (lax.axis_size(a) for a in ("fsdp", "cx", "cc"))
    y, x, c = (lax.axis_index(a) for a in ("fsdp", "cx", "cc"))
    half = rows // 2
    if nf == 2 and nx == 2:
        from_x = swap(shard, "cx")
        from_y = swap(shard, "fsdp")
        top = swap(from_y[:half], "cx")
        low = swap(from_x[half:], "fsdp")
        near = jnp.concatenate([shard, from_x, from_y, top, low], axis=0)
    else:
        near = jnp.concatenate(everyone(shard, "cx"), axis=0)
        near = jnp.concatenate(everyone(near, "fsdp"), axis=0)
    sources = [v.reshape(nf * nx, rows, width) for v in everyone(near, "cc")]
    place = [
        ((y ^ dy) * nc + (c ^ dc)) * nx + (x ^ dx)
        for dc in range(nc)
        for dy in range(nf)
        for dx in range(nx)
    ]
    return put_blocks(sources, place).reshape(nf * nc * nx * rows, width)


def scatter_rows(part):
    nf, nx, nc = (lax.axis_size(a) for a in ("fsdp", "cx", "cc"))
    y, x, c = (lax.axis_index(a) for a in ("fsdp", "cx", "cc"))
    width = part.shape[1]
    total = part.reshape(nf, nc, -1, width)
    total = summed(total, 1, "cc", c)
    total = summed(total.astype(jnp.bfloat16), 0, "fsdp", y)
    total = summed(total.astype(jnp.bfloat16).reshape(nx, -1, width), 0, "cx", x)
    return total


def summed(part, dim, axis, index):
    take = lambda k: lax.dynamic_index_in_dim(part, index ^ k, dim, keepdims=False)
    total = take(0).astype(jnp.float32)
    for k in range(1, lax.axis_size(axis)):
        total = total + swap(take(k), axis, k).astype(jnp.float32)
    return total


def reordered(values, nf, first, second):
    width = values.shape[1] // (nf * first * second)
    blocks = [
        (f * first + a) * second + b
        for f in range(nf)
        for b in range(second)
        for a in range(first)
    ]
    return jnp.concatenate([values[:, b * width : (b + 1) * width] for b in blocks], axis=1)


def norm_parts(values):
    factor = lax.rsqrt(jnp.mean(values * values, axis=-1, keepdims=True) + EPSILON)
    return (factor, values * factor)


def norm_back(grad_normed_in, normed, factor, gain_vec):
    grad_normed = grad_normed_in * gain_vec
    return factor * (grad_normed - normed * jnp.mean(grad_normed * normed, axis=-1, keepdims=True))


def turned(values, cos_table, sin_table):
    half = values.shape[1] // 2
    low, high = values[:, :half], values[:, half:]
    return jnp.concatenate(
        [low * cos_table - high * sin_table, high * cos_table + low * sin_table], axis=1
    )


def whole_block(ref):
    block = ref[...]
    return block.reshape(block.shape[1] * block.shape[3], block.shape[4])


def ffn_forward_kernel(own, h_ref, wg_ref, wu_ref, wd_ref, slope_ref, act_ref, inner_ref, out_ref, send_ref, acc):
    z = pl.program_id(0)
    hidden = h_ref[...]
    gate = dot(hidden, whole_block(wg_ref), 1, 0)
    up = dot(hidden, whole_block(wu_ref), 1, 0)
    sig = jax.nn.sigmoid(gate)
    act = gate * sig
    slope_ref[...] = up * (sig * (1.0 + gate * (1.0 - sig)))
    act_ref[...] = act
    inner = (act * up).astype(BF)
    inner_ref[...] = inner
    added = dot(inner, whole_block(wd_ref), 1, 1)

    @pl.when(z == 0)
    def _():
        acc[...] = added

    @pl.when(z > 0)
    def _():
        acc[...] += added

    @pl.when(z == pl.num_programs(0) - 1)
    def _():
        out_ref[...] = acc[:own, :]
        if send_ref.shape[0] == acc.shape[0] - own:
            send_ref[...] = acc[own:, :].astype(BF)


def ffn_forward(hidden, weights, own):
    rows, width = hidden.shape
    nz, nb, _, nr, hs = weights.shape
    wspec = lambda m: pl.BlockSpec((1, nb, 1, nr, hs), lambda z: (z, 0, m, 0, 0))
    full = lambda n: pl.BlockSpec((n, width), lambda z: (0, 0))
    col = pl.BlockSpec((rows, hs), lambda z: (0, z))
    shape = jax.ShapeDtypeStruct
    return pl.pallas_call(
        functools.partial(ffn_forward_kernel, own),
        out_shape=(
            shape((rows, nz * hs), F32),
            shape((rows, nz * hs), F32),
            shape((rows, nz * hs), BF),
            shape((own, width), F32),
            shape((max(rows - own, 16), width), BF),
        ),
        grid=(nz,),
        in_specs=[full(rows), wspec(0), wspec(1), wspec(2)],
        out_specs=[col, col, col, full(own), full(max(rows - own, 16))],
        scratch_shapes=[pltpu.VMEM((rows, width), F32)],
        compiler_params=pltpu.CompilerParams(vmem_limit_bytes=56 * 2**20),
        name="feed_forward",
    )(hidden, weights, weights, weights)


def ffn_backward_kernel(own, g_ref, wg_ref, wu_ref, wd_ref, slope_ref, act_ref, gg_ref, gu_ref, out_ref, send_ref, acc):
    z = pl.program_id(0)
    grad_inner = dot(g_ref[...], whole_block(wd_ref), 1, 0)
    gg = (grad_inner * slope_ref[...]).astype(BF)
    gu = (grad_inner * act_ref[...]).astype(BF)
    gg_ref[...] = gg
    gu_ref[...] = gu
    added = dot(gg, whole_block(wg_ref), 1, 1) + dot(gu, whole_block(wu_ref), 1, 1)

    @pl.when(z == 0)
    def _():
        acc[...] = added

    @pl.when(z > 0)
    def _():
        acc[...] += added

    @pl.when(z == pl.num_programs(0) - 1)
    def _():
        out_ref[...] = acc[:own, :]
        if send_ref.shape[0] == acc.shape[0] - own:
            send_ref[...] = acc[own:, :].astype(BF)


def ffn_backward(grad, weights, slope, act, own):
    rows, width = grad.shape
    nz, nb, _, nr, hs = weights.shape
    wspec = lambda m: pl.BlockSpec((1, nb, 1, nr, hs), lambda z: (z, 0, m, 0, 0))
    full = lambda n: pl.BlockSpec((n, width), lambda z: (0, 0))
    col = pl.BlockSpec((rows, hs), lambda z: (0, z))
    shape = jax.ShapeDtypeStruct
    return pl.pallas_call(
        functools.partial(ffn_backward_kernel, own),
        out_shape=(
            shape((rows, nz * hs), BF),
            shape((rows, nz * hs), BF),
            shape((own, width), F32),
            shape((max(rows - own, 16), width), BF),
        ),
        grid=(nz,),
        in_specs=[full(rows), wspec(0), wspec(1), wspec(2), col, col],
        out_specs=[col, col, full(own), full(max(rows - own, 16))],
        scratch_shapes=[pltpu.VMEM((rows, width), F32)],
        compiler_params=pltpu.CompilerParams(vmem_limit_bytes=56 * 2**20),
        name="feed_forward_back",
    )(grad, weights, weights, weights, slope, act)


def weight_grad_kernel(count, *refs):
    left, rights, outs, flipped = refs[0], refs[1 : 1 + count], refs[1 + count : 1 + 2 * count], refs[-1]

    @pl.when(pl.program_id(0) == 0)
    def _():
        flipped[...] = left[...].astype(F32).T.astype(BF)

    for right, out in zip(rights, outs):
        out[0] = dot(flipped[...], right[...], 1, 0).astype(BF)


def weight_grad(left, rights, nz):
    rows, width = left.shape
    hs = rights[0].shape[1] // nz
    count = len(rights)
    return pl.pallas_call(
        functools.partial(weight_grad_kernel, count),
        out_shape=(jax.ShapeDtypeStruct((nz, width, hs), BF),) * count,
        grid=(nz,),
        in_specs=[pl.BlockSpec((rows, width), lambda z: (0, 0))]
        + [pl.BlockSpec((rows, hs), lambda z: (0, z))] * count,
        out_specs=[pl.BlockSpec((1, width, hs), lambda z: (z, 0, 0))] * count,
        scratch_shapes=[pltpu.VMEM((width, rows), BF)],
        compiler_params=pltpu.CompilerParams(vmem_limit_bytes=56 * 2**20),
        name="weight_grad",
    )(left, *rights)


def on_device(
    tokens, teacher, segment_ids, positions, valid_mask, valid_count, gain_attn, w_query, w_key,
    w_value, w_out, gain_ffn, w_gate, w_up, w_down,
):
    nf, nx, nc, nz = (lax.axis_size(a) for a in AXES)
    y, x, c, z = (lax.axis_index(a) for a in AXES)
    place = x * nc + c
    rows, width = tokens.shape[1:]
    share = rows // nz
    feat = w_query.shape[0]
    q_cols, kv_cols = w_query.shape[1], w_key.shape[1]
    heads_k = kv_cols // HD
    hidden_dev = w_gate.shape[1]
    hs = hidden_dev // nx
    own_rows = lambda v: lax.dynamic_slice_in_dim(v, z * share, share, 0)
    att_scale = HD ** (-0.5)

    gains = jnp.stack([gain_attn, gain_ffn], axis=1)
    gains = jnp.pad(gains, ((0, 0), (0, 126)))
    in_weights = gather_rows(jnp.concatenate([w_query, w_key, w_value, gains], axis=1))
    w_qkv = in_weights[:, : q_cols + 2 * kv_cols]
    gain_att, gain_mlp = (
        in_weights[:, q_cols + 2 * kv_cols + i][None].astype(F32) for i in range(2)
    )

    ffn_stack = jnp.stack([w_gate, w_up, w_down.T])
    hidden_part = lambda k: lax.dynamic_slice_in_dim(ffn_stack, (x ^ k) * hs, hs, 2)
    pieces = [hidden_part(0)] + [swap(hidden_part(k), "cx", k) for k in range(1, nx)]
    ffn_shard = jnp.stack(ordered(pieces, x), axis=1).reshape(3 * nx * feat, hs)
    ffn_weights = lax.all_gather(ffn_shard, ("tp", "fsdp", "cc"), axis=0, tiled=True)
    ffn_weights = ffn_weights.reshape(nz, nf * nc, 3, nx * feat, hs)

    seg_own = segment_ids[0]
    seg_parts = everyone(seg_own[None], "cx")
    seg_near = jnp.concatenate(ordered(seg_parts, x), axis=0)
    seg_all = jnp.stack(ordered(everyone(seg_near, "cc"), c), axis=1).reshape(1, -1)
    doc_start = jnp.sum((seg_all < seg_own[:, None]).astype(jnp.int32), axis=1)[None]
    query_place = place * rows + jnp.arange(rows, dtype=jnp.int32)[None]
    half = HD // 2
    frequency = jnp.exp(
        jnp.arange(half).astype(F32) * (-2.0 * math.log(ROPE_BASE) / HD)
    )
    angles = frequency[:, None] * positions[0].astype(F32)[None]
    cos_table, sin_table = jnp.cos(angles)[None], jnp.sin(angles)[None]

    rows_bf = reordered(tokens[0], nf, nx, nc)
    rows_f = rows_bf.astype(F32)
    scale_a, normed_a = norm_parts(rows_f)
    hidden_a = (normed_a * gain_att).astype(BF)
    kv_lin = dot(w_qkv[:, q_cols:], hidden_a, 0, 1)
    k_rot = turned(kv_lin[:kv_cols].reshape(heads_k, HD, rows), cos_table, sin_table)
    kv_own = jnp.concatenate([k_rot.reshape(kv_cols, rows), kv_lin[kv_cols:]], axis=0).astype(BF)
    q_lin = dot(w_qkv[:, :q_cols], hidden_a, 0, 1)
    q_rot = turned(q_lin.reshape(-1, HD, rows), cos_table, sin_table).reshape(q_cols, rows).astype(BF)
    kv_near = jnp.stack(everyone(kv_own, "cx"))
    kv_all = put_blocks(
        everyone(kv_near, "cc"),
        [(x ^ dx) * nc + (c ^ dc) for dc in range(nc) for dx in range(nx)],
    )
    kv_all = jnp.concatenate([kv_all[i] for i in range(nx * nc)], axis=1)
    k_all, v_all = kv_all[:kv_cols], kv_all[kv_cols:]

    out_weights = gather_rows(jnp.concatenate(everyone(w_out.T, "tp"), axis=1))

    first_row = place * rows
    o_t, o_f, lse = attn_fwd(
        q_rot, k_all, v_all, doc_start, query_place,
        make_bounds(doc_start, first_row, rows, FWD_TQ, FWD_TK), FWD_TQ, FWD_TK,
    )

    chunk = lambda v, k: lax.dynamic_slice_in_dim(v, (z ^ k) * share, share, 1)
    att_t = jnp.concatenate(
        [chunk(o_t, 0)] + [swap(chunk(o_t, k), "tp", k) for k in range(1, nz)], axis=0
    )
    resid = own_rows(rows_f) + dot(att_t, out_weights, 0, 1)
    scale_f, normed_f = norm_parts(resid)
    hidden_own = (normed_f * gain_mlp).astype(BF)
    hidden_f = jnp.concatenate(everyone(hidden_own, "cx"), axis=0)
    slope, act, inner, ffn_own, ffn_send = ffn_forward(hidden_f, ffn_weights, share)

    def returned(own, send):
        for k in range(1, nx):
            own = own + swap(send[(k - 1) * share : k * share], "cx", k).astype(F32)
        return own

    result = resid + returned(ffn_own, ffn_send)
    target = reordered(own_rows(teacher[0]), nf, nx, nc).astype(F32)
    valid = own_rows(valid_mask[0].astype(F32)[:, None])
    error = result - target
    grad_out = valid * error
    loss_part = jnp.sum(grad_out * error)
    grad_ffn = jnp.concatenate(everyone(grad_out.astype(BF), "cx"), axis=0)
    (part_down,) = weight_grad(grad_ffn, [inner], nz)
    mixed_all = jnp.concatenate(ordered(everyone(result.astype(BF), "tp"), z), axis=0)
    mixed = reordered(mixed_all, nf, nc, nx)

    def scattered(parts):
        count = len(parts)
        stacked = jnp.stack([p.reshape(nz * nf * nc, nx * feat, hs) for p in parts], axis=1)
        done = lax.psum_scatter(
            stacked.reshape(nz * nf * nc * count * nx * feat, hs),
            ("tp", "fsdp", "cc"), scatter_dimension=0, tiled=True,
        ).reshape(count, nx, feat, hs)
        piece = lambda k: lax.dynamic_index_in_dim(done, x ^ k, 1, keepdims=False)
        pieces = [piece(0)] + [swap(piece(k), "cx", k) for k in range(1, nx)]
        whole = jnp.concatenate(ordered(pieces, x), axis=2).astype(F32)
        return [whole[i] for i in range(count)]

    (shard_down_t,) = scattered([part_down])
    grad_gate, grad_up, gh_own, gh_send = ffn_backward(grad_ffn, ffn_weights, slope, act, share)
    part_gate, part_up = weight_grad(hidden_f, [grad_gate, grad_up], nz)
    shard_gate, shard_up = scattered([part_gate, part_up])

    grad_hidden_f = returned(gh_own, gh_send)
    part_gain_mlp = jnp.sum(grad_hidden_f * normed_f, axis=0)
    grad_mid = grad_out + norm_back(grad_hidden_f, normed_f, scale_f, gain_mlp)
    grad_attn = grad_mid.astype(BF)
    g_att = dot(out_weights, grad_attn, 0, 1).astype(BF).reshape(nz, q_cols, share)
    g_parts = [g_att[0]] + [swap(g_att[k], "tp", k) for k in range(1, nz)]
    grad_heads = jnp.concatenate(ordered(g_parts, z), axis=1)
    part_out = dot(grad_attn, att_t, 0, 1).astype(BF)

    dq, dk, dv = attn_bwd(
        q_rot, k_all, v_all, doc_start, query_place,
        make_bounds(doc_start, first_row, rows, BWD_TQ, BWD_TK), grad_heads, o_f, lse, BWD_TQ, BWD_TK,
    )
    kv_grad = jnp.concatenate([dk, dv], axis=0).reshape(2 * kv_cols, nx, nc, rows)
    kv_grad = summed(kv_grad, 2, "cc", c).astype(BF)
    kv_grad = summed(kv_grad, 1, "cx", x)
    gk = turned(kv_grad[:kv_cols].reshape(heads_k, HD, rows) * att_scale, cos_table, -sin_table)
    gq = turned(dq.reshape(-1, HD, rows) * att_scale, cos_table, -sin_table)
    grad_qkv = jnp.concatenate(
        [gq.reshape(q_cols, rows), gk.reshape(kv_cols, rows), kv_grad[kv_cols:]], axis=0
    ).astype(BF)
    part_h1 = dot(grad_qkv, w_qkv, 0, 1).astype(BF).reshape(nz, share, width)
    part_qkv = dot(hidden_a, grad_qkv, 0, 1).astype(BF)
    grad_hidden_a = summed(part_h1, 0, "tp", z)
    normed_share = own_rows(normed_a)
    part_gain_att = jnp.sum(grad_hidden_a * normed_share, axis=0)
    grad_share = grad_mid + norm_back(grad_hidden_a, normed_share, own_rows(scale_a), gain_att)
    grad_all = jnp.concatenate(ordered(everyone(grad_share.astype(BF), "tp"), z), axis=0)
    grad_tokens = reordered(grad_all, nf, nc, nx).astype(F32)

    small = jnp.stack([part_gain_att, part_gain_mlp, jnp.broadcast_to(loss_part, (width,))])
    for axis in AXES:
        step = 1
        while step < lax.axis_size(axis):
            small = small + swap(small, axis, step)
            step *= 2
    small_own = lax.dynamic_slice_in_dim(small[:2], ((y * nc + c) * nx + x) * feat, feat, 1)
    loss = small[2, 0] / (valid_count.astype(F32) * width)

    shard_qkv = scatter_rows(part_qkv)
    shard_out_t = scatter_rows(part_out)
    shard_out_t = summed(
        shard_out_t.astype(BF).reshape(feat, nz, q_cols), 1, "tp", 0
    )
    return (
        mixed[None],
        loss,
        grad_tokens[None],
        small_own[0],
        shard_qkv[:, :q_cols],
        shard_qkv[:, q_cols : q_cols + kv_cols],
        shard_qkv[:, q_cols + kv_cols :],
        shard_out_t.T,
        small_own[1],
        shard_gate,
        shard_up,
        shard_down_t.T,
    )


FWD_TQ, FWD_TK = 256, 1024
BWD_TQ, BWD_TK = 256, 512


def solution(mesh):
    nf, nctx, nz = (mesh.shape[a] for a in ("fsdp", "ctx", "tp"))
    nc = 2 if nctx % 2 == 0 else 1
    fine = Mesh(mesh.devices.reshape(nf, nctx // nc, nc, nz), AXES)
    ctx = ("cx", "cc")
    rows = ("fsdp", "cx", "cc")
    return jax.shard_map(
        on_device,
        mesh=fine,
        in_specs=(
            P("fsdp", ctx, None),
            P("fsdp", ctx, None),
            P("fsdp", ctx),
            P("fsdp", ctx),
            P("fsdp", ctx),
            P(),
            P(rows),
            P(rows, "tp"),
            P(rows, "tp"),
            P(rows, "tp"),
            P("tp", rows),
            P(rows),
            P(rows, "tp"),
            P(rows, "tp"),
            P("tp", rows),
        ),
        out_specs=(
            P("fsdp", ctx, None),
            P(),
            P("fsdp", ctx, None),
            P(rows),
            P(rows, "tp"),
            P(rows, "tp"),
            P(rows, "tp"),
            P("tp", rows),
            P(rows),
            P(rows, "tp"),
            P(rows, "tp"),
            P("tp", rows),
        ),
        check_vma=False,
    )
```

time: 1330 us -> 1110 us (0.83)
  waiting for transfers between devices: 972 us -> 286 us
  Pallas kernels: 0 us -> 410 us
  starting transfers between devices: 2.15 us -> 164 us
  matrix products: 147 us -> 21.8 us
  local copies, waits for them, and re-layouts: 37.3 us -> 113 us
  blocking collectives: 69.1 us -> 0 us
  other arithmetic: 64.7 us -> 85.6 us
    reduce_scatter x10 -> x2, waiting for transfers between devices: 577 us -> 0.02 us  [scattered(): lax.psum_scatter(stacked.reshape(nz * nf * nc * count * nx * feat, hs), (...]
    pallas_call x0 -> x9, Pallas kernels: none -> 410 us  [the longest x3 327 us: put_blocks(): pl.pallas_call(functools.partial(place_kernel, count, None), out_shape=ja...]
    all_gather x10 -> x1, waiting for transfers between devices: 319 us -> 0.01 us  [on_device(): lax.all_gather(ffn_shard, ('tp', 'fsdp', 'cc'), axis=0, tiled=True)]
    ppermute x0 -> x55, waiting for transfers between devices: none -> 286 us  [swap(): return lax.ppermute(values, axis, [(i, i ^ step) for i in range(size)])]
    ppermute x0 -> x55, starting transfers between devices: none -> 164 us  [swap(): return lax.ppermute(values, axis, [(i, i ^ step) for i in range(size)])]
    dot_general x25 -> x7, matrix products: 147 us -> 21.8 us  [dot(): lax.dot_general(a, b, (((ca,), (cb,)), ((), ())), preferred_element_type=...]
    unnamed x24 -> x3, waiting for transfers between devices: 76.1 us -> 0.05 us
    all_gather x4 -> x0, blocking collectives: 39.9 us -> none  [the longest x1 13.3 us: on_device(): lax.all_gather(gain_stack.astype(jnp.bfloat16), 'tp', axis=0, tiled=True)]
  transfers between devices with their start and end apart: 22 -> 58, of which waited for: 20 -> 22; matrix products, arithmetic and copies ran while one was open for 11% -> 18% of each run, Pallas kernels for 0% -> 35%
where the time goes in v1:
time: 1110 us; the launch traced here: 1100 us
  Pallas kernels  410 us (37%)
  waiting for transfers between devices  286 us (26%)
  starting transfers between devices  164 us (15%)
  local copies, waits for them, and re-layouts  113 us (10%)
  other arithmetic  85.6 us (8%)
  matrix products  21.8 us (2%)
  between operations  17.8 us (2%)
    pallas_call x3, Pallas kernels, put_blocks(): pl.pallas_call(functools.partial(place_kernel, count, None), out_shape=ja...  327 us
    ppermute x55, waiting for transfers between devices, swap(): return lax.ppermute(values, axis, [(i, i ^ step) for i in range(size)])  286 us
    ppermute x55, starting transfers between devices, swap(): return lax.ppermute(values, axis, [(i, i ^ step) for i in range(size)])  164 us
    unnamed x142, local copies, waits for them, and re-layouts  31.6 us
    concatenate x6, local copies, waits for them, and re-layouts, reordered(): jnp.concatenate([values[:, b * width:(b + 1) * width] for b in blocks], a...  24.2 us
  transfers between devices with their start and end apart: 58, of which 22 were waited for; matrix products, arithmetic and copies ran while one was open for 18% of the time, Pallas kernels for 35%

profile of v1, /device:TPU:0, one launch (start us, length us, event | category | flops | bytes accessed | tf_op | source)
XLA Modules:
  0.0 1098.8 jit_solution(13853026278020304158)
XLA Ops:
  10.6 2.9 collective-permute-start.21
  13.6 13.6 %collective-permute-done.21 = bf16[3,192,512]{2,1,0:T(8,128)(2,1)} collective-permute-done((bf16[3,192,512]{2,1,0:T(8,128)(2,1)}, bf16[3,192,512]{2,1,0:T(8,128)(2,1)}, u32[]{:S(2)}, u32[]{:S(2)}) %collective-permute-start.21) | collective-permute-done | bytes 589856 | tf_op jit(solution)/shard_map/ppermute | solution.py:145
  36.0 2.6 collective-permute-start.13
  38.8 2.4 slice.307
  41.2 4.4 fusion.57
  45.7 7.1 concatenate.126
  53.4 2.6 multiply_reduce_fusion
  66.5 3.6 collective-permute-done.5
  75.5 2.5 convert_reduce_fusion
  82.8 85.2 %put_blocks.3 = bf16[8,192,896]{2,1,0:T(8,128)(2,1)} custom-call(s32[8]{0:T(128)} %stack.177.place, bf16[4,192,896]{2,1,0:T(8,128)(2,1)} %bitcast.12.refs_0_, bf16[4,192,896]{2,1,0:T(8,128)(2,1)} %bitcast.13.refs_1_), custom_call_target="tpu_custom_call" | custom-call | tf_op jit(solution)/shard_map/put_blocks/pallas_call | solution.py:184
  172.7 3.9 fusion.8
  185.0 13.4 %collective-permute-done.7 = bf16[384,1024]{1,0:T(8,128)(2,1)S(1)} collective-permute-done((bf16[384,1024]{1,0:T(8,128)(2,1)S(1)}, bf16[384,1024]{1,0:T(8,128)(2,1)S(1)}, u32[]{:S(2)}, u32[]{:S(2)}) %collective-permute-start.7) | collective-permute-done | bytes 786464 | tf_op jit(solution)/shard_map/ppermute | solution.py:145
  198.5 2.6 constant_dynamic-update-slice_fusion.7
  204.7 2.9 fusion.10
  208.8 97.1 %put_blocks.4 = bf16[4,384,1024]{2,1,0:T(8,128)(2,1)} custom-call(s32[4]{0:T(128)} %pad_add_fusion.4.place, bf16[2,384,1024]{2,1,0:T(8,128)(2,1)} %copy-done.21, bf16[2,384,1024]{2,1,0:T(8,128)(2,1)} %collective-permute-done.8.refs_1_), custom_call_target="tpu_custom_call" | custom-call | tf_op jit(solution)/shard_map/put_blocks/pallas_call | solution.py:184
  309.9 12.8 %attend.1 = (bf16[384,1024]{1,0:T(8,128)(2,1)S(1)}, f32[384,1024]{1,0:T(8,128)S(1)}, f32[2,2,1024]{2,1,0:T(2,128)S(1)}) custom-call(s32[4,4]{1,0:T(4,128)S(1)} %pad_add_fusion.2.bounds, bf16[384,1024]{1,0:T(8,128)(2,1)S(1)} %bitcast.233, bf16[192,4096]{1,0:T(8,128)(2,1)S(1)} %get-tuple-element.87.k_ref, bf16[192,4096]{1,0:T(8,128)(2,1)} %get-tuple-element.86.v_ref, ...), custom_call_target="tpu_custom_call" | custom-call | tf_op jit(solution)/shard_map/attend/pallas_call | solution.py:61
  323.8 3.3 collective-permute-start.11
  327.7 3.6 convert_element_type.238
  333.7 144.8 %put_blocks.5 = bf16[8,192,1536]{2,1,0:T(8,128)(2,1)} custom-call(s32[8]{0:T(128)} %stack.177.place, bf16[4,192,1536]{2,1,0:T(8,128)(2,1)} %bitcast.33.refs_0_, bf16[4,192,1536]{2,1,0:T(8,128)(2,1)} %bitcast.34.refs_1_), custom_call_target="tpu_custom_call" | custom-call | tf_op jit(solution)/shard_map/put_blocks/pallas_call | solution.py:184
  478.6 4.7 multiply_reduce_fusion.5
  484.7 16.9 %collective-permute-start.20 = (bf16[256,1536]{1,0:T(8,128)(2,1)S(1)}, bf16[256,1536]{1,0:T(8,128)(2,1)S(1)}, u32[]{:S(2)}, u32[]{:S(2)}) collective-permute-start(bf16[256,1536]{1,0:T(8,128)(2,1)S(1)} %multiply_convert_fusion.2), channel_id=1, source_target_pairs={{0,8},{8,0},{1,9},{9,1},{2,10},{10,2},{3,11},{11,3},{4,12},{12,4},... | collective-permute-start | bytes 2359304 | tf_op jit(solution)/shard_map/ppermute | solution.py:145
  501.6 17.0 %collective-permute-done.20 = bf16[256,1536]{1,0:T(8,128)(2,1)S(1)} collective-permute-done((bf16[256,1536]{1,0:T(8,128)(2,1)S(1)}, bf16[256,1536]{1,0:T(8,128)(2,1)S(1)}, u32[]{:S(2)}, u32[]{:S(2)}) %collective-permute-start.20) | collective-permute-done | bytes 786464 | tf_op jit(solution)/shard_map/ppermute | solution.py:145
  519.9 17.7 %feed_forward.1 = (f32[512,2048]{1,0:T(8,128)}, f32[512,2048]{1,0:T(8,128)}, bf16[512,2048]{1,0:T(8,128)(2,1)}, f32[256,1536]{1,0:T(8,128)}, bf16[256,1536]{1,0:T(8,128)(2,1)}) custom-call(bf16[512,1536]{1,0:T(8,128)(2,1)} %pad_maximum_fusion.8.h_ref.refs_0_, bf16[4,4,3,384,512]{4,3,2,1,0:T(8,128)(2,1)} %bitcast.236, bf16[4,4,3,384,512]{4,3,2,1,0:T(8,128)(2,1)} %bitcast.237, ...), custom_call_target="tpu_custom_call" | custom-call | tf_op jit(solution)/shard_map/feed_forward/pallas_call | solution.py:307
  542.3 16.2 %collective-permute-done.22 = bf16[256,1536]{1,0:T(8,128)(2,1)} collective-permute-done((bf16[256,1536]{1,0:T(8,128)(2,1)}, bf16[256,1536]{1,0:T(8,128)(2,1)}, u32[]{:S(2)}, u32[]{:S(2)}) %collective-permute-start.22) | collective-permute-done | bytes 786464 | tf_op jit(solution)/shard_map/ppermute | solution.py:145
  558.5 3.1 fusion.5
  564.9 17.7 %collective-permute-done.26 = bf16[256,1536]{1,0:T(8,128)(2,1)S(1)} collective-permute-done((bf16[256,1536]{1,0:T(8,128)(2,1)S(1)}, bf16[256,1536]{1,0:T(8,128)(2,1)S(1)}, u32[]{:S(2)}, u32[]{:S(2)}) %collective-permute-start.26) | collective-permute-done | bytes 786464 | tf_op jit(solution)/shard_map/ppermute | solution.py:145
  583.9 7.9 weight_grad.3
  591.8 18.5 %feed_forward_back.1 = (bf16[512,2048]{1,0:T(8,128)(2,1)}, bf16[512,2048]{1,0:T(8,128)(2,1)}, f32[256,1536]{1,0:T(8,128)}, bf16[256,1536]{1,0:T(8,128)(2,1)}) custom-call(bf16[512,1536]{1,0:T(8,128)(2,1)} %pad_maximum_fusion.9.g_ref.refs_0_, bf16[4,4,3,384,512]{4,3,2,1,0:T(8,128)(2,1)} %bitcast.239, bf16[4,4,3,384,512]{4,3,2,1,0:T(8,128)(2,1)} %bitcast.240, ...), custom_call_target="tpu_custom_call" | custom-call | tf_op jit(solution)/shard_map/feed_forward_back/pallas_call | solution.py:356
  612.1 10.9 weight_grad.2
  623.0 10.5 pad_maximum_fusion
  637.4 2.9 multiply_add_fusion
  648.1 14.4 %collective-permute-done.28 = bf16[384,256]{0,1:T(8,128)(2,1)S(1)} collective-permute-done((bf16[384,256]{0,1:T(8,128)(2,1)}, bf16[384,256]{0,1:T(8,128)(2,1)S(1)}, u32[]{:S(2)}, u32[]{:S(2)}) %collective-permute-start.28) | collective-permute-done | bytes 196640 | tf_op jit(solution)/shard_map/ppermute | solution.py:145
  662.5 5.8 collective-permute-done.29
  670.1 15.4 %attend_back.1 = (f32[384,1024]{1,0:T(8,128)}, bf16[192,4096]{1,0:T(8,128)(2,1)}, bf16[192,4096]{1,0:T(8,128)(2,1)}) custom-call(s32[4,4]{1,0:T(4,128)} %pad_add_fusion.3.bounds, bf16[384,1024]{1,0:T(8,128)(2,1)} %bitcast.232, bf16[192,4096]{1,0:T(8,128)(2,1)} %copy-done.2, bf16[192,4096]{1,0:T(8,128)(2,1)} %get-tuple-element.86.v_ref, s32[1,1024]{1,0:T(1,128)} %bitcast.235, ...), custom_call_target="tpu_custom_call" | custom-call | tf_op jit(solution)/shard_map/attend_back/pallas_call | solution.py:118
  685.6 3.9 pad_maximum_fusion.4
  689.5 4.9 reshape.626
  694.4 8.2 constant_dynamic-slice_fusion.2
  704.7 6.3 collective-permute-start.31
  711.0 3.3 broadcast_multiply_fusion
  716.9 5.6 collective-permute-start.23
  724.8 3.0 convolution_convert_fusion
  734.9 2.6 fusion.1
  737.6 17.0 %collective-permute-start.32 = (bf16[384,1024]{1,0:T(8,128)(2,1)S(1)}, bf16[384,1024]{1,0:T(8,128)(2,1)S(1)}, u32[]{:S(2)}, u32[]{:S(2)}) collective-permute-start(bf16[384,1024]{1,0:T(8,128)(2,1)S(1)} %dynamic-slice_bitcast_fusion.10), channel_id=1, source_target_pairs={{0,8},{8,0},{1,9},{9,1},{2,10},{10,2},{3,11},{11,3},{4,12},{12,4},... | collective-permute-start | bytes 2359304 | tf_op jit(solution)/shard_map/ppermute | solution.py:145
  754.7 25.5 %collective-permute-done.23 = bf16[256,1536]{1,0:T(8,128)(2,1)S(1)} collective-permute-done((bf16[256,1536]{1,0:T(8,128)(2,1)}, bf16[256,1536]{1,0:T(8,128)(2,1)S(1)}, u32[]{:S(2)}, u32[]{:S(2)}) %collective-permute-start.23) | collective-permute-done | bytes 786464 | tf_op jit(solution)/shard_map/ppermute | solution.py:145
  780.1 4.6 collective-permute-done.24
  784.7 31.6 %collective-permute-done.25 = bf16[256,1536]{1,0:T(8,128)(2,1)S(1)} collective-permute-done((bf16[256,1536]{1,0:T(8,128)(2,1)}, bf16[256,1536]{1,0:T(8,128)(2,1)S(1)}, u32[]{:S(2)}, u32[]{:S(2)}) %collective-permute-start.25) | collective-permute-done | bytes 786464 | tf_op jit(solution)/shard_map/ppermute | solution.py:145
  820.9 2.9 convolution_convert_fusion.1
  826.3 29.0 %collective-permute-start.33 = (bf16[256,1536]{1,0:T(8,128)(2,1)}, bf16[256,1536]{1,0:T(8,128)(2,1)}, u32[]{:S(2)}, u32[]{:S(2)}) collective-permute-start(bf16[256,1536]{1,0:T(8,128)(2,1)} %get-tuple-element.71), channel_id=1, source_target_pairs={{0,1},{1,0},{2,3},{3,2},{4,5},{5,4},{6,7},{7,6},{8,9},{9,8},{10,11... | collective-permute-start | bytes 2359304 | tf_op jit(solution)/shard_map/ppermute | solution.py:145
  857.7 2.5 fusion.55
  860.2 6.9 concatenate.142
  867.2 3.0 fusion
  870.2 42.0 %collective-permute-done.33 = bf16[256,1536]{1,0:T(8,128)(2,1)} collective-permute-done((bf16[256,1536]{1,0:T(8,128)(2,1)}, bf16[256,1536]{1,0:T(8,128)(2,1)}, u32[]{:S(2)}, u32[]{:S(2)}) %collective-permute-start.33) | collective-permute-done | bytes 786464 | tf_op jit(solution)/shard_map/ppermute | solution.py:145
  912.1 23.9 %collective-permute-done.34 = bf16[256,1536]{1,0:T(8,128)(2,1)} collective-permute-done((bf16[256,1536]{1,0:T(8,128)(2,1)}, bf16[256,1536]{1,0:T(8,128)(2,1)}, u32[]{:S(2)}, u32[]{:S(2)}) %collective-permute-start.34) | collective-permute-done | bytes 786464 | tf_op jit(solution)/shard_map/ppermute | solution.py:145
  936.1 3.1 multiply_reduce_fusion.1
  943.5 5.3 collective-permute-start.37
  948.8 3.0 convolution_convert_fusion.2
  953.5 16.4 %collective-permute-start.39 = (f32[3,1536]{1,0:T(4,128)S(1)}, f32[3,1536]{1,0:T(4,128)S(1)}, u32[]{:S(2)}, u32[]{:S(2)}) collective-permute-start(f32[3,1536]{1,0:T(4,128)S(1)} %add.493), channel_id=1, source_target_pairs={{0,1},{1,0},{2,3},{3,2},{4,5},{5,4},{6,7},{7,6},{8,9},{9,8},{10,11... | collective-permute-start | bytes 55304 | tf_op jit(solution)/shard_map/ppermute | solution.py:145
  975.9 2.7 add_convert_fusion
  978.6 15.1 %collective-permute-start.41 = (bf16[256,1536]{1,0:T(8,128)(2,1)}, bf16[256,1536]{1,0:T(8,128)(2,1)}, u32[]{:S(2)}, u32[]{:S(2)}) collective-permute-start(bf16[256,1536]{1,0:T(8,128)(2,1)} %add_convert_fusion), channel_id=1, source_target_pairs={{0,1},{1,0},{2,3},{3,2},{4,5},{5,4},{6,7},{7,6},{8,9},{9,8},{10,11... | collective-permute-start | bytes 2359304 | tf_op jit(solution)/shard_map/ppermute | solution.py:145
  1010.0 17.1 %collective-permute-done.41 = bf16[256,1536]{1,0:T(8,128)(2,1)} collective-permute-done((bf16[256,1536]{1,0:T(8,128)(2,1)}, bf16[256,1536]{1,0:T(8,128)(2,1)}, u32[]{:S(2)}, u32[]{:S(2)}) %collective-permute-start.41) | collective-permute-done | bytes 786464 | tf_op jit(solution)/shard_map/ppermute | solution.py:145
  1027.2 26.6 %collective-permute-done.42 = bf16[256,1536]{1,0:T(8,128)(2,1)} collective-permute-done((bf16[256,1536]{1,0:T(8,128)(2,1)}, bf16[256,1536]{1,0:T(8,128)(2,1)}, u32[]{:S(2)}, u32[]{:S(2)}) %collective-permute-start.42) | collective-permute-done | bytes 786464 | tf_op jit(solution)/shard_map/ppermute | solution.py:145
  1064.2 5.3 concatenate.158
  1069.5 3.6 convert_element_type.273
  1085.1 3.2 collective-permute-done.53
  (360 shorter events, 161.9 us)
Async XLA Ops:
  7.2 532.8 %copy-start = (bf16[1,1024,1536]{2,1,0:T(8,128)(2,1)S(1)}, bf16[1,1024,1536]{2,1,0:T(8,128)(2,1)}, u32[]{:S(2)}) copy-start(bf16[1,1024,1536]{2,1,0:T(8,128)(2,1)} %param.16) | copy-start | bytes 9437188
  7.2 512.7 %all-gather.2.cloned.1.call-start = ((), (), s32[]{:S(2)}) async-start(), calls=%async_computation.2 | async-start | bytes 20054016 | tf_op jit(solution)/shard_map/all_gather | solution.py:430
  10.6 16.6 %collective-permute-start.21 = (bf16[3,192,512]{2,1,0:T(8,128)(2,1)}, bf16[3,192,512]{2,1,0:T(8,128)(2,1)}, u32[]{:S(2)}, u32[]{:S(2)}) collective-permute-start(bf16[3,192,512]{2,1,0:T(8,128)(2,1)} %constant_dynamic-slice_fusion.8), channel_id=1, source_target_pairs={{0,8},{8,0},{1,9},{9,1},{2,10},{10,2},{3,11},{11,3},{4,12},{12,4},... | collective-permute-start | bytes 1769480 | tf_op jit(solution)/shard_map/ppermute | solution.py:145
  29.9 1046.9 %reduce-scatter.5.cloned.1.call-start = ((), (), s32[]{:S(2)}) async-start(), calls=%async_computation.4 | async-start | bytes 6684672 | tf_op jit(solution)/shard_map/reduce_scatter | solution.py:500
  31.1 28.2 %collective-permute-start.2 = (bf16[192,896]{1,0:T(8,128)(2,1)}, bf16[192,896]{1,0:T(8,128)(2,1)}, u32[]{:S(2)}, u32[]{:S(2)}) collective-permute-start(bf16[192,896]{1,0:T(8,128)(2,1)} %get-tuple-element.58), channel_id=1, source_target_pairs={{0,8},{8,0},{1,9},{9,1},{2,10},{10,2},{3,11},{11,3},{4,12},{12,4},... | collective-permute-start | bytes 1032200 | tf_op jit(solution)/shard_map/ppermute | solution.py:145
  32.9 24.6 %collective-permute-start.3 = (bf16[192,896]{1,0:T(8,128)(2,1)}, bf16[192,896]{1,0:T(8,128)(2,1)}, u32[]{:S(2)}, u32[]{:S(2)}) collective-permute-start(bf16[192,896]{1,0:T(8,128)(2,1)} %get-tuple-element.58), channel_id=1, source_target_pairs={{0,16},{16,0},{1,17},{17,1},{2,18},{18,2},{3,19},{19,3},{4,20},{20... | collective-permute-start | bytes 1032200 | tf_op jit(solution)/shard_map/ppermute | solution.py:145
  34.4 44.3 %collective-permute-start.12 = (bf16[192,384]{1,0:T(8,128)(2,1)}, bf16[192,384]{1,0:T(8,128)(2,1)}, u32[]{:S(2)}, u32[]{:S(2)}) collective-permute-start(bf16[192,384]{1,0:T(8,128)(2,1)} %bitcast.32), channel_id=1, source_target_pairs={{0,1},{1,0},{2,3},{3,2},{4,5},{5,4},{6,7},{7,6},{8,9},{9,8},{10,11... | collective-permute-start | bytes 442376 | tf_op jit(solution)/shard_map/ppermute | solution.py:145
  36.0 42.7 %collective-permute-start.13 = (bf16[192,384]{1,0:T(8,128)(2,1)}, bf16[192,384]{1,0:T(8,128)(2,1)}, u32[]{:S(2)}, u32[]{:S(2)}) collective-permute-start(bf16[192,384]{1,0:T(8,128)(2,1)} %bitcast.32), channel_id=1, source_target_pairs={{0,2},{1,3},{2,0},{3,1},{4,6},{5,7},{6,4},{7,5},{8,10},{9,11},{10,... | collective-permute-start | bytes 442376 | tf_op jit(solution)/shard_map/ppermute | solution.py:145
  38.6 40.1 %collective-permute-start.14 = (bf16[192,384]{1,0:T(8,128)(2,1)}, bf16[192,384]{1,0:T(8,128)(2,1)}, u32[]{:S(2)}, u32[]{:S(2)}) collective-permute-start(bf16[192,384]{1,0:T(8,128)(2,1)} %bitcast.32), channel_id=1, source_target_pairs={{0,3},{1,2},{2,1},{3,0},{4,7},{5,6},{6,5},{7,4},{8,11},{9,10},{10,... | collective-permute-start | bytes 442376 | tf_op jit(solution)/shard_map/ppermute | solution.py:145
  53.4 256.5 %copy-start.5 = (s32[1,1024]{1,0:T(1,128)}, s32[1,1024]{1,0:T(1,128)S(1)}, u32[]{:S(2)}) copy-start(s32[1,1024]{1,0:T(1,128)S(1)} %iota_add_fusion.qp_ref) | copy-start | bytes 12292
  58.4 5.5 collective-permute-start.4
  60.3 9.9 collective-permute-start.5
  63.9 7.0 collective-permute-start
  70.8 12.0 %collective-permute-start.6 = (bf16[768,896]{1,0:T(8,128)(2,1)}, bf16[768,896]{1,0:T(8,128)(2,1)}, u32[]{:S(2)}, u32[]{:S(2)}) collective-permute-start(bf16[768,896]{1,0:T(8,128)(2,1)} %constant_dynamic-update-slice_fusion), channel_id=1, source_target_pairs={{0,4},{4,0},{1,5},{5,1},{2,6},{6,2},{3,7},{7,3},{8,12},{12,8},{9,1... | collective-permute-start | bytes 4128776 | tf_op jit(solution)/shard_map/ppermute | solution.py:145
  71.5 3.3 collective-permute-start.1
  78.0 231.9 %copy-start.6 = (s32[1024]{0:T(1024)}, s32[1024]{0:T(1024)S(1)}, u32[]{:S(2)}) copy-start(s32[1024]{0:T(1024)S(1)} %convert_reduce_fusion) | copy-start | bytes 12292
  80.9 100.1 %collective-permute-start.15 = (bf16[192,1536]{1,0:T(8,128)(2,1)}, bf16[192,1536]{1,0:T(8,128)(2,1)}, u32[]{:S(2)}, u32[]{:S(2)}) collective-permute-start(bf16[192,1536]{1,0:T(8,128)(2,1)} %get-tuple-element.142), channel_id=1, source_target_pairs={{0,8},{8,0},{1,9},{9,1},{2,10},{10,2},{3,11},{11,3},{4,12},{12,4},... | collective-permute-start | bytes 1769480 | tf_op jit(solution)/shard_map/ppermute | solution.py:145
  81.7 96.8 %collective-permute-start.16 = (bf16[192,1536]{1,0:T(8,128)(2,1)}, bf16[192,1536]{1,0:T(8,128)(2,1)}, u32[]{:S(2)}, u32[]{:S(2)}) collective-permute-start(bf16[192,1536]{1,0:T(8,128)(2,1)} %get-tuple-element.142), channel_id=1, source_target_pairs={{0,16},{16,0},{1,17},{17,1},{2,18},{18,2},{3,19},{19,3},{4,20},{20... | collective-permute-start | bytes 1769480 | tf_op jit(solution)/shard_map/ppermute | solution.py:145
  177.8 20.5 %collective-permute-start.7 = (bf16[384,1024]{1,0:T(8,128)(2,1)S(1)}, bf16[384,1024]{1,0:T(8,128)(2,1)S(1)}, u32[]{:S(2)}, u32[]{:S(2)}) collective-permute-start(bf16[384,1024]{1,0:T(8,128)(2,1)S(1)} %pad_maximum_fusion.14), channel_id=1, source_target_pairs={{0,8},{8,0},{1,9},{9,1},{2,10},{10,2},{3,11},{11,3},{4,12},{12,4},... | collective-permute-start | bytes 2359304 | tf_op jit(solution)/shard_map/ppermute | solution.py:145
  179.4 23.8 %collective-permute-start.17 = (bf16[96,1536]{1,0:T(8,128)(2,1)S(1)}, bf16[96,1536]{1,0:T(8,128)(2,1)S(1)}, u32[]{:S(2)}, u32[]{:S(2)}) collective-permute-start(bf16[96,1536]{1,0:T(8,128)(2,1)S(1)} %slice.330), channel_id=1, source_target_pairs={{0,8},{8,0},{1,9},{9,1},{2,10},{10,2},{3,11},{11,3},{4,12},{12,4},... | collective-permute-start | bytes 884744 | tf_op jit(solution)/shard_map/ppermute | solution.py:145
  182.1 21.9 %collective-permute-start.18 = (bf16[96,1536]{1,0:T(8,128)(2,1)S(1)}, bf16[96,1536]{1,0:T(8,128)(2,1)S(1)}, u32[]{:S(2)}, u32[]{:S(2)}) collective-permute-start(bf16[96,1536]{1,0:T(8,128)(2,1)S(1)} %slice.331), channel_id=1, source_target_pairs={{0,16},{16,0},{1,17},{17,1},{2,18},{18,2},{3,19},{19,3},{4,20},{20... | collective-permute-start | bytes 884744 | tf_op jit(solution)/shard_map/ppermute | solution.py:145
  198.5 10.3 collective-permute-start.8
  204.7 129.1 %collective-permute-start.19 = (bf16[768,1536]{1,0:T(8,128)(2,1)}, bf16[768,1536]{1,0:T(8,128)(2,1)}, u32[]{:S(2)}, u32[]{:S(2)}) collective-permute-start(bf16[768,1536]{1,0:T(8,128)(2,1)} %constant_dynamic-update-slice_fusion.5), channel_id=1, source_target_pairs={{0,4},{4,0},{1,5},{5,1},{2,6},{6,2},{3,7},{7,3},{8,12},{12,8},{9,1... | collective-permute-start | bytes 7077896 | tf_op jit(solution)/shard_map/ppermute | solution.py:145
  323.8 154.8 %collective-permute-start.10 = (bf16[384,256]{1,0:T(8,128)(2,1)}, bf16[384,256]{1,0:T(8,128)(2,1)}, u32[]{:S(2)}, u32[]{:S(2)}) collective-permute-start(bf16[384,256]{1,0:T(8,128)(2,1)} %get-tuple-element.126), channel_id=1, source_target_pairs={{0,2},{1,3},{2,0},{3,1},{4,6},{5,7},{6,4},{7,5},{8,10},{9,11},{10,... | collective-permute-start | bytes 589832 | tf_op jit(solution)/shard_map/ppermute | solution.py:145
  323.8 154.8 %collective-permute-start.11 = (bf16[384,256]{1,0:T(8,128)(2,1)}, bf16[384,256]{1,0:T(8,128)(2,1)}, u32[]{:S(2)}, u32[]{:S(2)}) collective-permute-start(bf16[384,256]{1,0:T(8,128)(2,1)} %get-tuple-element.125), channel_id=1, source_target_pairs={{0,3},{1,2},{2,1},{3,0},{4,7},{5,6},{6,5},{7,4},{8,11},{9,10},{10,... | collective-permute-start | bytes 589832 | tf_op jit(solution)/shard_map/ppermute | solution.py:145
  327.1 151.5 %collective-permute-start.9 = (bf16[384,256]{1,0:T(8,128)(2,1)}, bf16[384,256]{1,0:T(8,128)(2,1)}, u32[]{:S(2)}, u32[]{:S(2)}) collective-permute-start(bf16[384,256]{1,0:T(8,128)(2,1)} %get-tuple-element.127), channel_id=1, source_target_pairs={{0,1},{1,0},{2,3},{3,2},{4,5},{5,4},{6,7},{7,6},{8,9},{9,8},{10,11... | collective-permute-start | bytes 589832 | tf_op jit(solution)/shard_map/ppermute | solution.py:145
  484.7 33.9 %collective-permute-start.20 = (bf16[256,1536]{1,0:T(8,128)(2,1)S(1)}, bf16[256,1536]{1,0:T(8,128)(2,1)S(1)}, u32[]{:S(2)}, u32[]{:S(2)}) collective-permute-start(bf16[256,1536]{1,0:T(8,128)(2,1)S(1)} %multiply_convert_fusion.2), channel_id=1, source_target_pairs={{0,8},{8,0},{1,9},{9,1},{2,10},{10,2},{3,11},{11,3},{4,12},{12,4},... | collective-permute-start | bytes 2359304 | tf_op jit(solution)/shard_map/ppermute | solution.py:145
  537.6 20.9 %collective-permute-start.22 = (bf16[256,1536]{1,0:T(8,128)(2,1)}, bf16[256,1536]{1,0:T(8,128)(2,1)}, u32[]{:S(2)}, u32[]{:S(2)}) collective-permute-start(bf16[256,1536]{1,0:T(8,128)(2,1)} %get-tuple-element.31), channel_id=1, source_target_pairs={{0,8},{8,0},{1,9},{9,1},{2,10},{10,2},{3,11},{11,3},{4,12},{12,4},... | collective-permute-start | bytes 2359304 | tf_op jit(solution)/shard_map/ppermute | solution.py:145
  562.8 19.9 %collective-permute-start.26 = (bf16[256,1536]{1,0:T(8,128)(2,1)S(1)}, bf16[256,1536]{1,0:T(8,128)(2,1)S(1)}, u32[]{:S(2)}, u32[]{:S(2)}) collective-permute-start(bf16[256,1536]{1,0:T(8,128)(2,1)S(1)} %multiply_convert_fusion.1), channel_id=1, source_target_pairs={{0,8},{8,0},{1,9},{9,1},{2,10},{10,2},{3,11},{11,3},{4,12},{12,4},... | collective-permute-start | bytes 2359304 | tf_op jit(solution)/shard_map/ppermute | solution.py:145
  591.8 487.3 %reduce-scatter.3.cloned.1.call-start = ((), (), s32[]{:S(2)}) async-start(), calls=%async_computation.3 | async-start | bytes 13369344 | tf_op jit(solution)/shard_map/reduce_scatter | solution.py:500
  610.3 23.2 %collective-permute-start.27 = (bf16[256,1536]{1,0:T(8,128)(2,1)}, bf16[256,1536]{1,0:T(8,128)(2,1)}, u32[]{:S(2)}, u32[]{:S(2)}) collective-permute-start(bf16[256,1536]{1,0:T(8,128)(2,1)} %get-tuple-element.35), channel_id=1, source_target_pairs={{0,8},{8,0},{1,9},{9,1},{2,10},{10,2},{3,11},{11,3},{4,12},{12,4},... | collective-permute-start | bytes 2359304 | tf_op jit(solution)/shard_map/ppermute | solution.py:145
  642.5 20.1 %collective-permute-start.28 = (bf16[384,256]{0,1:T(8,128)(2,1)}, bf16[384,256]{0,1:T(8,128)(2,1)S(1)}, u32[]{:S(2)}, u32[]{:S(2)}) collective-permute-start(bf16[384,256]{0,1:T(8,128)(2,1)} %get-tuple-element.123), channel_id=1, source_target_pairs={{0,1},{1,0},{2,3},{3,2},{4,5},{5,4},{6,7},{7,6},{8,9},{9,8},{10,11... | collective-permute-start | bytes 589832 | tf_op jit(solution)/shard_map/ppermute | solution.py:145
  644.0 24.3 %collective-permute-start.29 = (bf16[384,256]{0,1:T(8,128)(2,1)S(1)}, bf16[384,256]{0,1:T(8,128)(2,1)S(1)}, u32[]{:S(2)}, u32[]{:S(2)}) collective-permute-start(bf16[384,256]{0,1:T(8,128)(2,1)S(1)} %get-tuple-element.122), channel_id=1, source_target_pairs={{0,2},{1,3},{2,0},{3,1},{4,6},{5,7},{6,4},{7,5},{8,10},{9,11},{10,... | collective-permute-start | bytes 589832 | tf_op jit(solution)/shard_map/ppermute | solution.py:145
  646.0 22.3 %collective-permute-start.30 = (bf16[384,256]{0,1:T(8,128)(2,1)S(1)}, bf16[384,256]{0,1:T(8,128)(2,1)S(1)}, u32[]{:S(2)}, u32[]{:S(2)}) collective-permute-start(bf16[384,256]{0,1:T(8,128)(2,1)S(1)} %get-tuple-element.121), channel_id=1, source_target_pairs={{0,3},{1,2},{2,1},{3,0},{4,7},{5,6},{6,5},{7,4},{8,11},{9,10},{10,... | collective-permute-start | bytes 589832 | tf_op jit(solution)/shard_map/ppermute | solution.py:145
  704.7 28.4 %collective-permute-start.31 = (bf16[384,2,1024]{2,0,1:T(8,128)(2,1)}, bf16[384,2,1024]{2,0,1:T(8,128)(2,1)}, u32[]{:S(2)}, u32[]{:S(2)}) collective-permute-start(bf16[384,2,1024]{2,0,1:T(8,128)(2,1)} %bitcast.227), channel_id=1, source_target_pairs={{0,4},{4,0},{1,5},{5,1},{2,6},{6,2},{3,7},{7,3},{8,12},{12,8},{9,1... | collective-permute-start | bytes 4718600 | tf_op jit(solution)/shard_map/ppermute | solution.py:145
  716.9 63.3 %collective-permute-start.23 = (bf16[256,1536]{1,0:T(8,128)(2,1)}, bf16[256,1536]{1,0:T(8,128)(2,1)S(1)}, u32[]{:S(2)}, u32[]{:S(2)}) collective-permute-start(bf16[256,1536]{1,0:T(8,128)(2,1)} %get-tuple-element.109), channel_id=1, source_target_pairs={{0,1},{1,0},{2,3},{3,2},{4,5},{5,4},{6,7},{7,6},{8,9},{9,8},{10,11... | collective-permute-start | bytes 2359304 | tf_op jit(solution)/shard_map/ppermute | solution.py:145
  722.5 62.3 %collective-permute-start.24 = (bf16[256,1536]{1,0:T(8,128)(2,1)}, bf16[256,1536]{1,0:T(8,128)(2,1)S(1)}, u32[]{:S(2)}, u32[]{:S(2)}) collective-permute-start(bf16[256,1536]{1,0:T(8,128)(2,1)} %get-tuple-element.109), channel_id=1, source_target_pairs={{0,2},{1,3},{2,0},{3,1},{4,6},{5,7},{6,4},{7,5},{8,10},{9,11},{10,... | collective-permute-start | bytes 2359304 | tf_op jit(solution)/shard_map/ppermute | solution.py:145
  722.5 93.8 %collective-permute-start.25 = (bf16[256,1536]{1,0:T(8,128)(2,1)}, bf16[256,1536]{1,0:T(8,128)(2,1)S(1)}, u32[]{:S(2)}, u32[]{:S(2)}) collective-permute-start(bf16[256,1536]{1,0:T(8,128)(2,1)} %get-tuple-element.109), channel_id=1, source_target_pairs={{0,3},{1,2},{2,1},{3,0},{4,7},{5,6},{6,5},{7,4},{8,11},{9,10},{10,... | collective-permute-start | bytes 2359304 | tf_op jit(solution)/shard_map/ppermute | solution.py:145
  731.6 135.6 %collective-permute-start.47 = (bf16[2,384,1536]{2,1,0:T(8,128)(2,1)}, bf16[2,384,1536]{2,1,0:T(8,128)(2,1)}, u32[]{:S(2)}, u32[]{:S(2)}) collective-permute-start(bf16[2,384,1536]{2,1,0:T(8,128)(2,1)} %dynamic-slice_bitcast_fusion), channel_id=1, source_target_pairs={{0,4},{4,0},{1,5},{5,1},{2,6},{6,2},{3,7},{7,3},{8,12},{12,8},{9,1... | collective-permute-start | bytes 7077896 | tf_op jit(solution)/shard_map/ppermute | solution.py:145
  733.1 86.1 %copy-start.35 = (bf16[4,96,1024]{2,1,0:T(8,128)(2,1)}, bf16[4,96,1024]{2,1,0:T(8,128)(2,1)S(1)}, u32[]{:S(2)}) copy-start(bf16[4,96,1024]{2,1,0:T(8,128)(2,1)S(1)} %pad_maximum_fusion.18) | copy-start | bytes 2359300
  737.5 78.8 %copy-start.28 = (bf16[256,1536]{1,0:T(8,128)(2,1)S(1)}, bf16[256,1536]{1,0:T(8,128)(2,1)}, u32[]{:S(2)}) copy-start(bf16[256,1536]{1,0:T(8,128)(2,1)} %get-tuple-element.109) | copy-start | bytes 2359300
  737.6 80.9 %collective-permute-start.32 = (bf16[384,1024]{1,0:T(8,128)(2,1)S(1)}, bf16[384,1024]{1,0:T(8,128)(2,1)S(1)}, u32[]{:S(2)}, u32[]{:S(2)}) collective-permute-start(bf16[384,1024]{1,0:T(8,128)(2,1)S(1)} %dynamic-slice_bitcast_fusion.10), channel_id=1, source_target_pairs={{0,8},{8,0},{1,9},{9,1},{2,10},{10,2},{3,11},{11,3},{4,12},{12,4},... | collective-permute-start | bytes 2359304 | tf_op jit(solution)/shard_map/ppermute | solution.py:145
  826.3 85.8 %collective-permute-start.33 = (bf16[256,1536]{1,0:T(8,128)(2,1)}, bf16[256,1536]{1,0:T(8,128)(2,1)}, u32[]{:S(2)}, u32[]{:S(2)}) collective-permute-start(bf16[256,1536]{1,0:T(8,128)(2,1)} %get-tuple-element.71), channel_id=1, source_target_pairs={{0,1},{1,0},{2,3},{3,2},{4,5},{5,4},{6,7},{7,6},{8,9},{9,8},{10,11... | collective-permute-start | bytes 2359304 | tf_op jit(solution)/shard_map/ppermute | solution.py:145
  855.4 80.7 %collective-permute-start.34 = (bf16[256,1536]{1,0:T(8,128)(2,1)}, bf16[256,1536]{1,0:T(8,128)(2,1)}, u32[]{:S(2)}, u32[]{:S(2)}) collective-permute-start(bf16[256,1536]{1,0:T(8,128)(2,1)} %get-tuple-element.73), channel_id=1, source_target_pairs={{0,2},{1,3},{2,0},{3,1},{4,6},{5,7},{6,4},{7,5},{8,10},{9,11},{10,... | collective-permute-start | bytes 2359304 | tf_op jit(solution)/shard_map/ppermute | solution.py:145
  855.4 80.7 %collective-permute-start.35 = (bf16[256,1536]{1,0:T(8,128)(2,1)}, bf16[256,1536]{1,0:T(8,128)(2,1)}, u32[]{:S(2)}, u32[]{:S(2)}) collective-permute-start(bf16[256,1536]{1,0:T(8,128)(2,1)} %get-tuple-element.72), channel_id=1, source_target_pairs={{0,3},{1,2},{2,1},{3,0},{4,7},{5,6},{6,5},{7,4},{8,11},{9,10},{10,... | collective-permute-start | bytes 2359304 | tf_op jit(solution)/shard_map/ppermute | solution.py:145
  870.2 69.0 %copy-start.44 = (f32[1,1536]{1,0:T(1,128)S(1)}, f32[1,1536]{1,0:T(1,128)}, u32[]{:S(2)}) copy-start(f32[1,1536]{1,0:T(1,128)} %stack.206) | copy-start | bytes 18436
  939.3 4.2 collective-permute-start.36
  939.4 34.5 %collective-permute-start.48 = (bf16[384,1536]{1,0:T(8,128)(2,1)S(1)}, bf16[384,1536]{1,0:T(8,128)(2,1)S(1)}, u32[]{:S(2)}, u32[]{:S(2)}) collective-permute-start(bf16[384,1536]{1,0:T(8,128)(2,1)S(1)} %dynamic-slice_bitcast_fusion.1), channel_id=1, source_target_pairs={{0,16},{16,0},{1,17},{17,1},{2,18},{18,2},{3,19},{19,3},{4,20},{20... | collective-permute-start | bytes 3538952 | tf_op jit(solution)/shard_map/ppermute | solution.py:145
  943.5 8.3 collective-permute-start.37
  951.9 1.6 collective-permute-start.38
  953.2 44.7 %collective-permute-start.44 = (bf16[2,384,768]{2,1,0:T(8,128)(2,1)}, bf16[2,384,768]{2,1,0:T(8,128)(2,1)}, u32[]{:S(2)}, u32[]{:S(2)}) collective-permute-start(bf16[2,384,768]{2,1,0:T(8,128)(2,1)} %dynamic-slice_bitcast_fusion.2), channel_id=1, source_target_pairs={{0,4},{4,0},{1,5},{5,1},{2,6},{6,2},{3,7},{7,3},{8,12},{12,8},{9,1... | collective-permute-start | bytes 3538952 | tf_op jit(solution)/shard_map/ppermute | solution.py:145
  953.5 18.2 %collective-permute-start.39 = (f32[3,1536]{1,0:T(4,128)S(1)}, f32[3,1536]{1,0:T(4,128)S(1)}, u32[]{:S(2)}, u32[]{:S(2)}) collective-permute-start(f32[3,1536]{1,0:T(4,128)S(1)} %add.493), channel_id=1, source_target_pairs={{0,1},{1,0},{2,3},{3,2},{4,5},{5,4},{6,7},{7,6},{8,9},{9,8},{10,11... | collective-permute-start | bytes 55304 | tf_op jit(solution)/shard_map/ppermute | solution.py:145
  971.8 21.9 %collective-permute-start.40 = (f32[3,1536]{1,0:T(4,128)S(1)}, f32[3,1536]{1,0:T(4,128)S(1)}, u32[]{:S(2)}, u32[]{:S(2)}) collective-permute-start(f32[3,1536]{1,0:T(4,128)S(1)} %add.494), channel_id=1, source_target_pairs={{0,2},{1,3},{2,0},{3,1},{4,6},{5,7},{6,4},{7,5},{8,10},{9,11},{10,... | collective-permute-start | bytes 55304 | tf_op jit(solution)/shard_map/ppermute | solution.py:145
  975.1 26.6 %collective-permute-start.49 = (bf16[192,1536]{1,0:T(8,128)(2,1)}, bf16[192,1536]{1,0:T(8,128)(2,1)}, u32[]{:S(2)}, u32[]{:S(2)}) collective-permute-start(bf16[192,1536]{1,0:T(8,128)(2,1)} %dynamic-slice_bitcast_fusion.16), channel_id=1, source_target_pairs={{0,8},{8,0},{1,9},{9,1},{2,10},{10,2},{3,11},{11,3},{4,12},{12,4},... | collective-permute-start | bytes 1769480 | tf_op jit(solution)/shard_map/ppermute | solution.py:145
  978.6 48.6 %collective-permute-start.41 = (bf16[256,1536]{1,0:T(8,128)(2,1)}, bf16[256,1536]{1,0:T(8,128)(2,1)}, u32[]{:S(2)}, u32[]{:S(2)}) collective-permute-start(bf16[256,1536]{1,0:T(8,128)(2,1)} %add_convert_fusion), channel_id=1, source_target_pairs={{0,1},{1,0},{2,3},{3,2},{4,5},{5,4},{6,7},{7,6},{8,9},{9,8},{10,11... | collective-permute-start | bytes 2359304 | tf_op jit(solution)/shard_map/ppermute | solution.py:145
  993.7 60.1 %collective-permute-start.42 = (bf16[256,1536]{1,0:T(8,128)(2,1)}, bf16[256,1536]{1,0:T(8,128)(2,1)}, u32[]{:S(2)}, u32[]{:S(2)}) collective-permute-start(bf16[256,1536]{1,0:T(8,128)(2,1)} %add_convert_fusion), channel_id=1, source_target_pairs={{0,2},{1,3},{2,0},{3,1},{4,6},{5,7},{6,4},{7,5},{8,10},{9,11},{10,... | collective-permute-start | bytes 2359304 | tf_op jit(solution)/shard_map/ppermute | solution.py:145
  993.7 61.6 %collective-permute-start.43 = (bf16[256,1536]{1,0:T(8,128)(2,1)}, bf16[256,1536]{1,0:T(8,128)(2,1)}, u32[]{:S(2)}, u32[]{:S(2)}) collective-permute-start(bf16[256,1536]{1,0:T(8,128)(2,1)} %add_convert_fusion), channel_id=1, source_target_pairs={{0,3},{1,2},{2,1},{3,0},{4,7},{5,6},{6,5},{7,4},{8,11},{9,10},{10,... | collective-permute-start | bytes 2359304 | tf_op jit(solution)/shard_map/ppermute | solution.py:145
  1000.8 59.5 %collective-permute-start.45 = (bf16[384,768]{1,0:T(8,128)(2,1)}, bf16[384,768]{1,0:T(8,128)(2,1)}, u32[]{:S(2)}, u32[]{:S(2)}) collective-permute-start(bf16[384,768]{1,0:T(8,128)(2,1)} %dynamic-slice_bitcast_fusion.17), channel_id=1, source_target_pairs={{0,16},{16,0},{1,17},{17,1},{2,18},{18,2},{3,19},{19,3},{4,20},{20... | collective-permute-start | bytes 1769480 | tf_op jit(solution)/shard_map/ppermute | solution.py:145
  1007.1 66.0 %collective-permute-start.50 = (bf16[192,384]{1,0:T(8,128)(2,1)}, bf16[192,384]{1,0:T(8,128)(2,1)}, u32[]{:S(2)}, u32[]{:S(2)}) collective-permute-start(bf16[192,384]{1,0:T(8,128)(2,1)} %bitcast.230), channel_id=1, source_target_pairs={{0,1},{1,0},{2,3},{3,2},{4,5},{5,4},{6,7},{7,6},{8,9},{9,8},{10,11... | collective-permute-start | bytes 442376 | tf_op jit(solution)/shard_map/ppermute | solution.py:145
  1027.2 46.8 %collective-permute-start.51 = (bf16[192,384]{1,0:T(8,128)(2,1)}, bf16[192,384]{1,0:T(8,128)(2,1)}, u32[]{:S(2)}, u32[]{:S(2)}) collective-permute-start(bf16[192,384]{1,0:T(8,128)(2,1)} %bitcast.229), channel_id=1, source_target_pairs={{0,2},{1,3},{2,0},{3,1},{4,6},{5,7},{6,4},{7,5},{8,10},{9,11},{10,... | collective-permute-start | bytes 442376 | tf_op jit(solution)/shard_map/ppermute | solution.py:145
  1053.8 20.1 %collective-permute-start.52 = (bf16[192,384]{1,0:T(8,128)(2,1)}, bf16[192,384]{1,0:T(8,128)(2,1)}, u32[]{:S(2)}, u32[]{:S(2)}) collective-permute-start(bf16[192,384]{1,0:T(8,128)(2,1)} %bitcast.228), channel_id=1, source_target_pairs={{0,3},{1,2},{2,1},{3,0},{4,7},{5,6},{6,5},{7,4},{8,11},{9,10},{10,... | collective-permute-start | bytes 442376 | tf_op jit(solution)/shard_map/ppermute | solution.py:145
  1063.0 12.8 %collective-permute-start.46 = (bf16[192,768]{1,0:T(8,128)(2,1)}, bf16[192,768]{1,0:T(8,128)(2,1)}, u32[]{:S(2)}, u32[]{:S(2)}) collective-permute-start(bf16[192,768]{1,0:T(8,128)(2,1)} %dynamic-slice_bitcast_fusion.19), channel_id=1, source_target_pairs={{0,8},{8,0},{1,9},{9,1},{2,10},{10,2},{3,11},{11,3},{4,12},{12,4},... | collective-permute-start | bytes 884744 | tf_op jit(solution)/shard_map/ppermute | solution.py:145
  1077.8 6.3 collective-permute-start.54
  1080.2 8.2 collective-permute-start.53
  (58 other events, 450.0 us)
Sparse Core Ops, SparseCore 0:
  30.0 118.2 all-gather.1
  591.9 97.8 reduce-scatter.4
  694.4 242.1 reduce-scatter.2

commit v2 on v1

v2 whole, which is shorter than its diff:
```python
import functools
import math

import jax
import jax.numpy as jnp
from jax import lax
from jax.experimental import pallas as pl
from jax.experimental.pallas import tpu as pltpu
from jax.sharding import Mesh
from jax.sharding import PartitionSpec as P

HD=96
NEG=-1e30
F32=jnp.float32; BF=jnp.bfloat16
def dot(a,b,ca,cb):
    return lax.dot_general(a,b,(((ca,),(cb,)),((),())),preferred_element_type=F32)

def load_blocks(place, sources, keys_t, keys, values_t, values):
    n = 0
    for source in sources:
        width = source.shape[3]
        for b in range(source.shape[0]):
            at = pl.ds(pl.multiple_of(place[n]*width, width), width)
            n += 1
            if keys_t is not None:
                keys_t[:, at] = source[b, 0]
            keys[at, :] = source[b, 0].astype(F32).T.astype(BF)
            if values_t is not None:
                values_t[:, at] = source[b, 1]
            if values is not None:
                values[at, :] = source[b, 1].astype(F32).T.astype(BF)

def fwd_kernel(scale2, tq, tk, group, count, bounds, place, q_ref, *refs):
    sources, (st_ref, qp_ref, o_ref, of_ref, lse_ref, ks, v_ref, m_s, l_s, acc) = refs[:count], refs[count:]
    i = pl.program_id(1)
    @pl.when(i == 0)
    def _():
        load_blocks(place, sources, None, ks, v_ref, None)
    q2 = jnp.concatenate([q_ref[h*HD:(h+1)*HD, :] for h in range(group)], axis=1)
    st = jnp.concatenate([st_ref[...]]*group, axis=1)
    qp = jnp.concatenate([qp_ref[...]]*group, axis=1)
    m_s[...] = jnp.full_like(m_s, NEG)
    l_s[...] = jnp.zeros_like(l_s)
    acc[...] = jnp.zeros_like(acc)
    def step(masked, j, _):
        off = pl.multiple_of(j*tk, tk)
        s = dot(ks[pl.ds(off, tk), :], q2, 1, 0)
        if masked:
            kid = off + lax.broadcasted_iota(jnp.int32, s.shape, 0)
            s = jnp.where((kid >= st) & (kid <= qp), s, NEG)
        m_old = m_s[...]
        m_new = jnp.maximum(m_old, jnp.max(s, axis=0, keepdims=True))
        p = jnp.exp2((s - m_new)*scale2)
        al = jnp.exp2((m_old - m_new)*scale2)
        l_s[...] = l_s[...]*al + jnp.sum(p, axis=0, keepdims=True)
        m_s[...] = m_new
        acc[...] = acc[...]*al + dot(v_ref[:, pl.ds(off, tk)], p.astype(BF), 1, 0)
        return 0
    lo, a, b, hi = bounds[i,0], bounds[i,1], bounds[i,2], bounds[i,3]
    lax.fori_loop(lo, a, functools.partial(step, True), 0)
    lax.fori_loop(a, b, functools.partial(step, False), 0)
    lax.fori_loop(b, hi, functools.partial(step, True), 0)
    o = acc[...]/l_s[...]
    lse = m_s[...]*scale2 + jnp.log2(l_s[...])
    for h in range(group):
        oh = o[:, h*tq:(h+1)*tq]
        of_ref[h*HD:(h+1)*HD, :] = oh
        o_ref[h*HD:(h+1)*HD, :] = oh.astype(BF)
        lse_ref[0, h:h+1, :] = lse[:, h*tq:(h+1)*tq]

def kv_spec(source):
    return pl.BlockSpec((source.shape[0], 2, HD, source.shape[3]), lambda g,i,*_:(0,0,g,0))

def attn_fwd(qT, kv_sources, place, start, qpos, bounds, tq=256, tk=512):
    T = qT.shape[1]; kv = kv_sources[0].shape[2]//HD; group = qT.shape[0]//HD//kv
    N = sum(s.shape[0] for s in kv_sources)*T
    scale2 = HD**-0.5*math.log2(math.e)
    qs = pl.BlockSpec((group*HD, tq), lambda g,i,*_:(g,i))
    row = pl.BlockSpec((1, tq), lambda g,i,*_:(0,i))
    return pl.pallas_call(
        functools.partial(fwd_kernel, scale2, tq, tk, group, len(kv_sources)),
        out_shape=(jax.ShapeDtypeStruct(qT.shape, BF), jax.ShapeDtypeStruct(qT.shape, F32), jax.ShapeDtypeStruct((kv, group, T), F32)),
        grid_spec=pltpu.PrefetchScalarGridSpec(num_scalar_prefetch=2, grid=(kv, T//tq),
            in_specs=[qs] + [kv_spec(s) for s in kv_sources] + [row, row],
            out_specs=[qs, qs, pl.BlockSpec((1, group, tq), lambda g,i,*_:(g,0,i))],
            scratch_shapes=[pltpu.VMEM((N,HD),BF), pltpu.VMEM((HD,N),BF), pltpu.VMEM((1,group*tq),F32), pltpu.VMEM((1,group*tq),F32), pltpu.VMEM((HD,group*tq),F32)]),
        compiler_params=pltpu.CompilerParams(vmem_limit_bytes=48*2**20),
        cost_estimate=pl.CostEstimate(flops=24*10**9, bytes_accessed=8*10**6, transcendentals=0),
        name="attend",
    )(bounds, place, qT, *kv_sources, start, qpos)

def bwd_kernel(scale2, tq, tk, group, count, bounds, place, q_ref, *refs):
    sources, (st_ref, qp_ref, g_ref, of_ref, lse_ref, dq_ref) = refs[:count], refs[count:count+6]
    dkv_refs, (k_ref, ks, vs, dks, dvs, dqs) = refs[count+6:2*count+6], refs[2*count+6:]
    i = pl.program_id(1)
    @pl.when(i == 0)
    def _():
        load_blocks(place, sources, k_ref, ks, None, vs)
        dks[...] = jnp.zeros_like(dks)
        dvs[...] = jnp.zeros_like(dvs)
    cat = lambda f: jnp.concatenate([f(h) for h in range(group)], axis=1)
    q2 = cat(lambda h: q_ref[h*HD:(h+1)*HD, :])
    g2 = cat(lambda h: g_ref[h*HD:(h+1)*HD, :])
    lse = cat(lambda h: lse_ref[0, h:h+1, :])
    delta = cat(lambda h: jnp.sum(g_ref[h*HD:(h+1)*HD, :].astype(F32)*of_ref[h*HD:(h+1)*HD, :], axis=0, keepdims=True))
    st = cat(lambda h: st_ref[...])
    qp = cat(lambda h: qp_ref[...])
    dqs[...] = jnp.zeros_like(dqs)
    def step(masked, j, _):
        off = pl.multiple_of(j*tk, tk)
        s = dot(ks[pl.ds(off, tk), :], q2, 1, 0)
        if masked:
            kid = off + lax.broadcasted_iota(jnp.int32, s.shape, 0)
            s = jnp.where((kid >= st) & (kid <= qp), s, NEG)
        p = jnp.exp2(s*scale2 - lse)
        dp = dot(vs[pl.ds(off, tk), :], g2, 1, 0)
        ds = (p*(dp - delta)).astype(BF)
        dvs[:, pl.ds(off, tk)] += dot(g2, p.astype(BF), 1, 1)
        dks[:, pl.ds(off, tk)] += dot(q2, ds, 1, 1)
        dqs[...] += dot(k_ref[:, pl.ds(off, tk)], ds, 1, 0)
        return 0
    lo, a, b, hi = bounds[i,0], bounds[i,1], bounds[i,2], bounds[i,3]
    lax.fori_loop(lo, a, functools.partial(step, True), 0)
    lax.fori_loop(a, b, functools.partial(step, False), 0)
    lax.fori_loop(b, hi, functools.partial(step, True), 0)
    for h in range(group):
        dq_ref[h*HD:(h+1)*HD, :] = dqs[:, h*tq:(h+1)*tq]
    @pl.when(i == pl.num_programs(1)-1)
    def _():
        n = 0
        for dkv_ref in dkv_refs:
            width = dkv_ref.shape[3]
            for b in range(dkv_ref.shape[0]):
                at = pl.ds(pl.multiple_of(place[n]*width, width), width)
                n += 1
                dkv_ref[b, 0] = dks[:, at].astype(BF)
                dkv_ref[b, 1] = dvs[:, at].astype(BF)

def attn_bwd(qT, kv_sources, place, start, qpos, bounds, gT, of, lse, tq, tk, head):
    T = qT.shape[1]; kv = kv_sources[0].shape[2]//HD; group = qT.shape[0]//HD//kv
    N = sum(s.shape[0] for s in kv_sources)*T
    scale2 = HD**-0.5*math.log2(math.e)
    qs = pl.BlockSpec((group*HD, tq), lambda g,i,*_:(head,i))
    row = pl.BlockSpec((1, tq), lambda g,i,*_:(0,i))
    kv_in = [pl.BlockSpec((s.shape[0], 2, HD, T), lambda g,i,*_:(0,0,head,0)) for s in kv_sources]
    kv_out = [pl.BlockSpec((s.shape[0], 2, HD, T), lambda g,i,*_:(0,0,0,0)) for s in kv_sources]
    return pl.pallas_call(
        functools.partial(bwd_kernel, scale2, tq, tk, group, len(kv_sources)),
        out_shape=[jax.ShapeDtypeStruct((group*HD, T), F32)] + [jax.ShapeDtypeStruct((s.shape[0], 2, HD, T), BF) for s in kv_sources],
        grid_spec=pltpu.PrefetchScalarGridSpec(num_scalar_prefetch=2, grid=(1, T//tq),
            in_specs=[qs] + kv_in + [row, row, qs, qs, pl.BlockSpec((1, group, tq), lambda g,i,*_:(head,0,i))],
            out_specs=[pl.BlockSpec((group*HD, tq), lambda g,i,*_:(0,i))] + kv_out,
            scratch_shapes=[pltpu.VMEM((HD,N),BF), pltpu.VMEM((N,HD),BF), pltpu.VMEM((N,HD),BF), pltpu.VMEM((HD,N),F32), pltpu.VMEM((HD,N),F32), pltpu.VMEM((HD,group*tq),F32)]),
        compiler_params=pltpu.CompilerParams(vmem_limit_bytes=56*2**20),
        cost_estimate=pl.CostEstimate(flops=24*10**9, bytes_accessed=8*10**6, transcendentals=0),
        name="attend_back",
    )(bounds, place, qT, *kv_sources, start, qpos, gT, of, lse)

def make_bounds(start, q_first, T, tq, tk):
    s = start.reshape(-1, tq)
    first = q_first + jnp.arange(T//tq, dtype=jnp.int32)*tq
    lo = s[:,0]//tk
    hi = (first + tq - 1)//tk + 1
    a = jnp.minimum((s[:,-1] + tk - 1)//tk, hi)
    b = jnp.maximum(first//tk, a)
    return jnp.stack([lo,a,b,hi],axis=1).astype(jnp.int32)

EPSILON = 1e-05
ROPE_BASE = 100000.0
AXES = ("fsdp", "cx", "cc", "tp")


def swap(values, axis, step=1):
    size = lax.axis_size(axis)
    return lax.ppermute(values, axis, [(i, i ^ step) for i in range(size)])


def after_kernel(*refs):
    pass


def after(values, *others):
    values, tree = jax.tree.flatten(values)
    others = jax.tree.leaves(others)
    done = pl.pallas_call(
        after_kernel,
        out_shape=[jax.ShapeDtypeStruct(v.shape, v.dtype) for v in values],
        in_specs=[pl.BlockSpec(memory_space=pl.ANY)] * (len(values) + len(others)),
        out_specs=[pl.BlockSpec(memory_space=pl.ANY)] * len(values),
        input_output_aliases={i: i for i in range(len(values))},
        name="after",
    )(*values, *others)
    return jax.tree.unflatten(tree, list(done))


def ordered(parts, index):
    if len(parts) == 1:
        return list(parts)
    if len(parts) == 2:
        first = index == 0
        return [jnp.where(first, parts[0], parts[1]), jnp.where(first, parts[1], parts[0])]
    stacked = jnp.stack(parts)
    return [
        lax.dynamic_index_in_dim(stacked, jnp.bitwise_xor(index, a), 0, keepdims=False)
        for a in range(len(parts))
    ]


def everyone(values, axis):
    return [values] + [swap(values, axis, k) for k in range(1, lax.axis_size(axis))]


def place_kernel(counts, place, *refs):
    sources, outs = refs[: len(counts)], refs[len(counts) :]
    n = pl.program_id(0)
    first = 0
    for count, source in zip(counts, sources):

        @pl.when((n >= first) & (n < first + count))
        def _(source=source):
            at = 0
            for out in outs:
                out[...] = source[:, at : at + out.shape[1]]
                at += out.shape[1]

        first += count


def put_blocks(sources, place, cut=None):
    counts = [s.shape[0] for s in sources]
    shape = sources[0].shape[1:]
    cuts = [shape[0]] if cut is None else [cut, shape[0] - cut]
    specs = []
    first = 0
    for count in counts:
        specs.append(
            pl.BlockSpec(
                (1,) + shape,
                lambda n, place, first=first, count=count: (jnp.clip(n - first, 0, count - 1), 0, 0),
            )
        )
        first += count
    return pl.pallas_call(
        functools.partial(place_kernel, counts),
        out_shape=[jax.ShapeDtypeStruct((first, r, shape[1]), sources[0].dtype) for r in cuts],
        grid_spec=pltpu.PrefetchScalarGridSpec(
            num_scalar_prefetch=1,
            grid=(first,),
            in_specs=specs,
            out_specs=[
                pl.BlockSpec((1, r, shape[1]), lambda n, place: (place[n], 0, 0)) for r in cuts
            ],
        ),
        cost_estimate=pl.CostEstimate(flops=7*10**9, bytes_accessed=8*10**6, transcendentals=0),
        name="put_blocks",
    )(jnp.stack(place).astype(jnp.int32), *sources)


def gather_rows(shard, hold=None, hold_core=None, cut=None):
    rows, width = shard.shape
    nf, nx, nc = (lax.axis_size(a) for a in ("fsdp", "cx", "cc"))
    y, x, c = (lax.axis_index(a) for a in ("fsdp", "cx", "cc"))
    half = rows // 2
    if nf == 2 and nx == 2:
        from_x = swap(shard, "cx")
        from_y = swap(shard, "fsdp")
        x_parts = [shard, from_x]
        if hold is not None:
            from_x, from_y = after((from_x, from_y), hold)
        top = swap(from_y[:half], "cx")
        low = swap(from_x[half:], "fsdp")
        near = jnp.concatenate([shard, from_x, from_y, top, low], axis=0)
    else:
        x_parts = everyone(shard, "cx")
        near = jnp.concatenate(x_parts, axis=0)
        near = jnp.concatenate(everyone(near, "fsdp"), axis=0)
    parts = everyone(near, "cc")
    if hold_core is not None and nc > 1:
        parts[1:] = after(parts[1:], hold_core)
    sources = [v.reshape(nf * nx, rows, width) for v in parts]
    place = [
        ((y ^ dy) * nx + (x ^ dx)) * nc + (c ^ dc)
        for dc in range(nc)
        for dy in range(nf)
        for dx in range(nx)
    ]
    return put_blocks(sources, place, cut), near, x_parts


def scatter_rows(part):
    nf, nx, nc = (lax.axis_size(a) for a in ("fsdp", "cx", "cc"))
    y, x, c = (lax.axis_index(a) for a in ("fsdp", "cx", "cc"))
    width = part.shape[1]
    total = part.reshape(nf, nx, nc, -1, width)
    total = summed(total, 2, "cc", c)
    total = summed(total.astype(jnp.bfloat16), 0, "fsdp", y)
    total = summed(total.astype(jnp.bfloat16), 0, "cx", x)
    return total


def summed(part, dim, axis, index):
    take = lambda k: lax.dynamic_index_in_dim(part, index ^ k, dim, keepdims=False)
    total = take(0).astype(jnp.float32)
    for k in range(1, lax.axis_size(axis)):
        total = total + swap(take(k), axis, k).astype(jnp.float32)
    return total


def norm_parts(values):
    factor = lax.rsqrt(jnp.mean(values * values, axis=-1, keepdims=True) + EPSILON)
    return (factor, values * factor)


def norm_back(grad_normed_in, normed, factor, gain_vec):
    grad_normed = grad_normed_in * gain_vec
    return factor * (grad_normed - normed * jnp.mean(grad_normed * normed, axis=-1, keepdims=True))


def turned(values, cos_table, sin_table):
    half = values.shape[1] // 2
    low, high = values[:, :half], values[:, half:]
    return jnp.concatenate(
        [low * cos_table - high * sin_table, high * cos_table + low * sin_table], axis=1
    )


def whole_block(dims, ref):
    nf, nx, nc = dims
    feat = ref.shape[3] // nx
    return jnp.concatenate(
        [
            ref[0, f * nc + b, 0, a * feat : (a + 1) * feat, :]
            for f in range(nf)
            for a in range(nx)
            for b in range(nc)
        ],
        axis=0,
    )


def ffn_forward_kernel(dims, h_ref, wg_ref, wu_ref, wd_ref, slope_ref, act_ref, inner_ref, out_ref, acc):
    z = pl.program_id(0)
    hidden = h_ref[...]
    gate = dot(hidden, whole_block(dims, wg_ref), 1, 0)
    up = dot(hidden, whole_block(dims, wu_ref), 1, 0)
    sig = jax.nn.sigmoid(gate)
    act = gate * sig
    slope_ref[...] = up * (sig * (1.0 + gate * (1.0 - sig)))
    act_ref[...] = act
    inner = (act * up).astype(BF)
    inner_ref[...] = inner
    add_up(z, dot(inner, whole_block(dims, wd_ref), 1, 1), acc, out_ref)


def add_up(z, added, acc, out_ref):
    @pl.when(z == 0)
    def _():
        acc[...] = added

    @pl.when(z > 0)
    def _():
        acc[...] += added

    @pl.when(z == pl.num_programs(0) - 1)
    def _():
        out_ref[...] = acc[...].astype(out_ref.dtype)


def ffn_forward(hidden, weights, dims, kind):
    rows, width = hidden.shape
    nz, nb, _, nr, hs = weights.shape
    wspec = lambda m: pl.BlockSpec((1, nb, 1, nr, hs), lambda z: (z, 0, m, 0, 0))
    full = pl.BlockSpec((rows, width), lambda z: (0, 0))
    col = pl.BlockSpec((rows, hs), lambda z: (0, z))
    shape = jax.ShapeDtypeStruct
    return pl.pallas_call(
        functools.partial(ffn_forward_kernel, dims),
        out_shape=(
            shape((rows, nz * hs), F32),
            shape((rows, nz * hs), F32),
            shape((rows, nz * hs), BF),
            shape((rows, width), kind),
        ),
        grid=(nz,),
        in_specs=[full, wspec(0), wspec(1), wspec(2)],
        out_specs=[col, col, col, full],
        scratch_shapes=[pltpu.VMEM((rows, width), F32)],
        compiler_params=pltpu.CompilerParams(vmem_limit_bytes=56 * 2**20),
        cost_estimate=pl.CostEstimate(flops=12*10**9, bytes_accessed=8*10**6, transcendentals=0),
        name="feed_forward",
    )(hidden, weights, weights, weights)


def ffn_backward_kernel(dims, g_ref, wg_ref, wu_ref, wd_ref, slope_ref, act_ref, gg_ref, gu_ref, out_ref, acc):
    z = pl.program_id(0)
    grad_inner = dot(g_ref[...], whole_block(dims, wd_ref), 1, 0)
    gg = (grad_inner * slope_ref[...]).astype(BF)
    gu = (grad_inner * act_ref[...]).astype(BF)
    gg_ref[...] = gg
    gu_ref[...] = gu
    added = dot(gg, whole_block(dims, wg_ref), 1, 1) + dot(gu, whole_block(dims, wu_ref), 1, 1)
    add_up(z, added, acc, out_ref)


def ffn_backward(grad, weights, slope, act, dims, kind):
    rows, width = grad.shape
    nz, nb, _, nr, hs = weights.shape
    wspec = lambda m: pl.BlockSpec((1, nb, 1, nr, hs), lambda z: (z, 0, m, 0, 0))
    full = pl.BlockSpec((rows, width), lambda z: (0, 0))
    col = pl.BlockSpec((rows, hs), lambda z: (0, z))
    shape = jax.ShapeDtypeStruct
    return pl.pallas_call(
        functools.partial(ffn_backward_kernel, dims),
        out_shape=(
            shape((rows, nz * hs), BF),
            shape((rows, nz * hs), BF),
            shape((rows, width), kind),
        ),
        grid=(nz,),
        in_specs=[full, wspec(0), wspec(1), wspec(2), col, col],
        out_specs=[col, col, full],
        scratch_shapes=[pltpu.VMEM((rows, width), F32)],
        compiler_params=pltpu.CompilerParams(vmem_limit_bytes=56 * 2**20),
        cost_estimate=pl.CostEstimate(flops=12*10**9, bytes_accessed=8*10**6, transcendentals=0),
        name="feed_forward_back",
    )(grad, weights, weights, weights, slope, act)


def input_grad_kernel(dims, place, gq_ref, gkv_ref, w_ref, out_ref):
    nf, nx, nc = dims
    feat = w_ref.shape[2] // nx
    grads = jnp.concatenate([gq_ref[0], gkv_ref[0]], axis=0).astype(F32).T.astype(BF)
    weight = jnp.concatenate(
        [
            w_ref[0, f * nc + b, a * feat : (a + 1) * feat, :]
            for f in range(nf)
            for a in range(nx)
            for b in range(nc)
        ],
        axis=0,
    )
    added = dot(grads, weight, 1, 1)

    @pl.when(pl.program_id(0) == 0)
    def _():
        out_ref[...] = added

    @pl.when(pl.program_id(0) > 0)
    def _():
        out_ref[...] += added


def input_grad(gq, gkv, weights, place, dims):
    nz, q_cols, share = gq.shape
    nb, nr, cols = weights.shape[1:]
    width = nb * nr
    return pl.pallas_call(
        functools.partial(input_grad_kernel, dims),
        out_shape=jax.ShapeDtypeStruct((share, width), F32),
        grid_spec=pltpu.PrefetchScalarGridSpec(
            num_scalar_prefetch=1,
            grid=(nz,),
            in_specs=[
                pl.BlockSpec((1, q_cols, share), lambda k, place: (k, 0, 0)),
                pl.BlockSpec((1, gkv.shape[1], share), lambda k, place: (k, 0, 0)),
                pl.BlockSpec((1, nb, nr, cols), lambda k, place: (place[k], 0, 0, 0)),
            ],
            out_specs=pl.BlockSpec((share, width), lambda k, place: (0, 0)),
        ),
        compiler_params=pltpu.CompilerParams(vmem_limit_bytes=56 * 2**20),
        cost_estimate=pl.CostEstimate(flops=9*10**9, bytes_accessed=8*10**6, transcendentals=0),
        name="input_grad",
    )(place, gq, gkv, weights)


def weight_grad_kernel(dims, pieces, count, where, *refs):
    nf, nx, nc = dims
    lefts, rights = refs[:pieces], refs[pieces : pieces * (count + 1)]
    outs, (plain, flipped) = refs[pieces * (count + 1) : -2], refs[-2:]
    feat = plain.shape[0] // (nf * nx * nc)
    tokens = lefts[0].shape[0]

    @pl.when(pl.program_id(0) == 0)
    def _():
        for p, left in enumerate(lefts):
            plain[:, p * tokens : (p + 1) * tokens] = left[...].astype(F32).T.astype(BF)
        n = 0
        for dc in range(nc):
            for dy in range(nf):
                for a in range(nx):
                    row = ((where[0] ^ dy) * nx + a) * nc + (where[1] ^ dc)
                    flipped[n * feat : (n + 1) * feat, :] = plain[
                        pl.ds(pl.multiple_of(row * feat, feat), feat), :
                    ]
                    n += 1

    part = flipped.shape[0] // (nc * nf)
    for i in range(count):
        right = jnp.concatenate([rights[i * pieces + p][...] for p in range(pieces)], axis=0)
        done = dot(flipped[...], right, 1, 0).astype(BF)
        for b in range(nc):
            for f in range(nf):
                n = b * nf + f
                outs[i * nc + b][f, 0] = done[n * part : (n + 1) * part]


def weight_grad(lefts, rights, where, nz, dims):
    rows, width = lefts[0].shape
    nf, nx, nc = dims
    hs = rights[0][0].shape[1] // nz
    count, pieces = len(rights), len(lefts)
    shape = (nf, nz, width // (nf * nc), hs)
    return pl.pallas_call(
        functools.partial(weight_grad_kernel, dims, pieces, count),
        out_shape=(jax.ShapeDtypeStruct(shape, BF),) * (count * nc),
        grid_spec=pltpu.PrefetchScalarGridSpec(
            num_scalar_prefetch=1,
            grid=(nz,),
            in_specs=[pl.BlockSpec((rows, width), lambda z, w: (0, 0))] * pieces
            + [pl.BlockSpec((rows, hs), lambda z, w: (0, z))] * (count * pieces),
            out_specs=[pl.BlockSpec((nf, 1) + shape[2:], lambda z, w: (0, z, 0, 0))] * (count * nc),
            scratch_shapes=[pltpu.VMEM((width, rows * pieces), BF)] * 2,
        ),
        compiler_params=pltpu.CompilerParams(vmem_limit_bytes=56 * 2**20),
        cost_estimate=pl.CostEstimate(flops=10*10**9, bytes_accessed=8*10**6, transcendentals=0),
        name="weight_grad",
    )(where, *lefts, *[r for right in rights for r in right])


def on_device(
    tokens, teacher, segment_ids, positions, valid_mask, valid_count, gain_attn, w_query, w_key,
    w_value, w_out, gain_ffn, w_gate, w_up, w_down,
):
    nf, nx, nc, nz = (lax.axis_size(a) for a in AXES)
    y, x, c, z = (lax.axis_index(a) for a in AXES)
    place = x * nc + c
    rows, width = tokens.shape[1:]
    share = rows // nz
    feat = w_query.shape[0]
    q_cols, kv_cols = w_query.shape[1], w_key.shape[1]
    heads_k = kv_cols // HD
    hidden_dev = w_gate.shape[1]
    hs = hidden_dev // nx
    own_rows = lambda v: lax.dynamic_slice_in_dim(v, z * share, share, 0)
    att_scale = HD ** (-0.5)

    qkv_cols = q_cols + 2 * kv_cols
    gains = jnp.pad(jnp.stack([gain_attn, gain_ffn]), ((0, 14), (0, qkv_cols - feat)))
    in_shard = jnp.concatenate([jnp.concatenate([w_query, w_key, w_value], axis=1), gains], axis=0)
    rows_f = tokens[0].astype(F32)
    scale_a, normed_a = norm_parts(rows_f)
    out_shard = jnp.concatenate(everyone(w_out.T, "tp"), axis=1)
    (w_qkv, gain_rows), early, x_parts = gather_rows(in_shard, None, (scale_a, out_shard), feat)
    w_qkv = w_qkv.reshape(-1, qkv_cols)
    gain_rows = gain_rows[:, :2, :feat].astype(F32)
    gain_att, gain_mlp = (gain_rows[:, i].reshape(1, -1) for i in range(2))

    ffn_stack = after(jnp.stack([w_gate, w_up, w_down.T]), early)
    hidden_part = lambda k: lax.dynamic_slice_in_dim(ffn_stack, (x ^ k) * hs, hs, 2)
    pieces = [hidden_part(0)] + [swap(hidden_part(k), "cx", k) for k in range(1, nx)]
    swapped = pieces[1:]
    pieces[1:] = after(pieces[1:], w_qkv) if nx > 1 else []
    ffn_shard = jnp.stack(ordered(pieces, x), axis=1).reshape(3 * nx * feat, hs)
    ffn_weights = lax.all_gather(ffn_shard, ("tp", "fsdp", "cc"), axis=0, tiled=True)
    ffn_weights = ffn_weights.reshape(nz, nf * nc, 3, nx * feat, hs)

    half = HD // 2
    frequency = jnp.exp(
        jnp.arange(half).astype(F32) * (-2.0 * math.log(ROPE_BASE) / HD)
    )
    angles = frequency[:, None] * positions[0].astype(F32)[None]
    cos_table, sin_table = jnp.cos(angles)[None], jnp.sin(angles)[None]

    hidden_a = (normed_a * gain_att).astype(BF)
    kv_lin = dot(w_qkv[:, q_cols:], hidden_a, 0, 1)
    k_rot = turned(kv_lin[:kv_cols].reshape(heads_k, HD, rows), cos_table, sin_table)
    kv_own = jnp.concatenate([k_rot.reshape(kv_cols, rows), kv_lin[kv_cols:]], axis=0).astype(BF)
    q_lin = dot(w_qkv[:, :q_cols], hidden_a, 0, 1)
    q_rot = turned(q_lin.reshape(-1, HD, rows), cos_table, sin_table).reshape(q_cols, rows).astype(BF)
    kv_parts = everyone(kv_own.reshape(2, kv_cols, rows), "cx")

    seg_own = after(segment_ids[0][None], kv_own)
    seg_parts = everyone(seg_own, "cx")
    seg_near = jnp.concatenate(ordered(seg_parts, x), axis=0)
    seg_all = jnp.stack(ordered(everyone(seg_near, "cc"), c), axis=1).reshape(1, -1)
    doc_start = jnp.sum((seg_all < segment_ids[0][:, None]).astype(jnp.int32), axis=1)[None]
    query_place = place * rows + jnp.arange(rows, dtype=jnp.int32)[None]

    (out_weights,), out_near, out_parts = gather_rows(out_shard)
    out_weights = out_weights.reshape(width, -1)
    kv_parts[1:] = after(kv_parts[1:], q_rot, doc_start, out_parts) if nx > 1 else []
    q_rot = after(q_rot, out_near)
    kv_near = jnp.stack(kv_parts)
    kv_sources = everyone(kv_near, "cc")
    kv_place = jnp.stack(
        [(x ^ dx) * nc + (c ^ dc) for dc in range(nc) for dx in range(nx)]
    ).astype(jnp.int32)

    first_row = place * rows
    o_t, o_f, lse = attn_fwd(
        q_rot, kv_sources, kv_place, doc_start, query_place,
        make_bounds(doc_start, first_row, rows, FWD_TQ, FWD_TK), FWD_TQ, FWD_TK,
    )

    qkv_shard = jnp.concatenate(ordered([p[:feat] for p in x_parts], x), axis=0)
    qkv_weights = lax.all_gather(
        after(qkv_shard, o_t), ("tp", "fsdp", "cc"), axis=0, tiled=True
    ).reshape(nz, nf * nc, nx * feat, qkv_cols)

    chunk = lambda v, k: lax.dynamic_slice_in_dim(v, (z ^ k) * share, share, 1)
    att_t = jnp.concatenate(
        [chunk(o_t, 0)] + [swap(chunk(o_t, k), "tp", k) for k in range(1, nz)], axis=0
    )
    resid = own_rows(rows_f) + dot(att_t, out_weights, 0, 1)
    scale_f, normed_f = norm_parts(resid)
    hidden_own = (normed_f * gain_mlp).astype(BF)
    dims = (nf, nx, nc)
    hidden_parts = everyone(hidden_own, "cx")
    slopes, acts, inners, outs = zip(
        *(
            ffn_forward(h, ffn_weights, dims, F32 if k == 0 else BF)
            for k, h in enumerate(hidden_parts)
        )
    )

    def returned(parts, *others):
        total = parts[0]
        for k in range(1, nx):
            back = swap(parts[k], "cx", k)
            total = total + (after(back, *others) if others else back).astype(F32)
        return total

    result = resid + returned(outs)
    target = own_rows(teacher[0]).astype(F32)
    valid = own_rows(valid_mask[0].astype(F32)[:, None])
    error = result - target
    grad_out = valid * error
    loss_part = jnp.sum(grad_out * error)
    ffn_grads = everyone(grad_out.astype(BF), "cx")
    where = jnp.stack([y, c]).astype(jnp.int32)
    part_down = weight_grad(ffn_grads, [inners], where, nz, dims)
    mixed = lax.all_gather(result.astype(BF), "tp", axis=0, tiled=True)

    def to_rows(parts):
        others = [swap(parts[k], "cc", k) for k in range(1, nc)]

        def over_cores(f):
            total = parts[0][f].astype(F32)
            for other in others:
                total = total + other[f].astype(F32)
            return total

        return over_cores, [over_cores(k).astype(BF) for k in range(1, nf)]

    def scattered(over_cores, sends, hold):
        total = over_cores(0)
        for k in range(1, nf):
            total = total + after(swap(sends[k - 1], "fsdp", k), hold).astype(F32)
        total = total.astype(BF)
        return total, spread(total)

    def spread(total):
        done = lax.psum_scatter(
            total.reshape(nz * nx * feat, hs), "tp", scatter_dimension=0, tiled=True
        ).reshape(nx, feat, hs)
        piece = lambda k: lax.dynamic_index_in_dim(done, x ^ k, 0, keepdims=False)
        pieces = [piece(0)] + [swap(piece(k), "cx", k) for k in range(1, nx)]
        return jnp.concatenate(ordered(pieces, x), axis=1).astype(F32)

    down_own, down_sends = to_rows(part_down)
    grad_gates, grad_ups, ffn_backs = zip(
        *(
            ffn_backward(g, ffn_weights, slopes[k], acts[k], dims, F32 if k == 0 else BF)
            for k, g in enumerate(ffn_grads)
        )
    )
    part_gate_up = weight_grad(hidden_parts, [grad_gates, grad_ups], where, nz, dims)
    grad_hidden_f = returned(ffn_backs, part_down)
    part_gain_mlp = jnp.sum(grad_hidden_f * normed_f, axis=0)
    grad_mid = grad_out + norm_back(grad_hidden_f, normed_f, scale_f, gain_mlp)
    grad_attn = grad_mid.astype(BF)
    g_att = dot(out_weights, grad_attn, 0, 1).astype(BF).reshape(nz, q_cols, share)
    g_parts = [g_att[0]] + [swap(g_att[k], "tp", k) for k in range(1, nz)]
    grad_heads = jnp.concatenate(ordered(after(g_parts, part_gate_up, down_sends), z), axis=1)

    bounds = make_bounds(doc_start, first_row, rows, BWD_TQ, BWD_TK)
    dqs, kv_grads = [], []
    for head in range(heads_k):
        dq, *dkv = attn_bwd(
            q_rot, kv_sources, kv_place, doc_start, query_place, bounds, grad_heads, o_f, lse,
            BWD_TQ, BWD_TK, head,
        )
        dkv_others = [swap(dkv[k], "cc", k) for k in range(1, nc)]

        def kv_over_cores(k):
            total = dkv[0][k].astype(F32)
            for other in dkv_others:
                total = total + other[k].astype(F32)
            return total

        sends = [kv_over_cores(k).astype(BF) for k in range(1, nx)]
        if head == 0:
            down_total, shard_down_t = scattered(down_own, down_sends, dq)
            gate_own, gate_sends = to_rows(part_gate_up[:nc])
            up_own, up_sends = to_rows(part_gate_up[nc:])
            if heads_k > 1:
                grad_heads = after(grad_heads, sends, down_total, gate_sends, up_sends)
        kv_grad = kv_over_cores(0)
        for k in range(1, nx):
            kv_grad = kv_grad + swap(sends[k - 1], "cx", k).astype(F32)
        dqs.append(dq)
        kv_grads.append(kv_grad)
    gq = jnp.concatenate([turned(d.reshape(-1, HD, rows) * att_scale, cos_table, -sin_table) for d in dqs])
    gq = gq.reshape(q_cols, rows).astype(BF)
    to_owners = lambda v: jnp.stack(
        [chunk(v, 0)] + [swap(chunk(v, k), "tp", k) for k in range(1, nz)]
    )
    gq_all = to_owners(gq)
    kv_grad = jnp.stack(kv_grads, axis=1)
    gk = turned(kv_grad[0] * att_scale, cos_table, -sin_table)
    gkv = jnp.concatenate([gk, kv_grad[1]], axis=0).reshape(2 * kv_cols, rows).astype(BF)
    gkv_all = to_owners(gkv)
    grad_hidden_a = input_grad(
        gq_all, gkv_all, qkv_weights, jnp.stack([z ^ k for k in range(nz)]).astype(jnp.int32), dims
    )
    gate_total, shard_gate = scattered(gate_own, gate_sends, gkv)
    up_total, shard_up = scattered(up_own, up_sends, gkv)
    part_qkv = dot(hidden_a, jnp.concatenate([gq, gkv], axis=0), 0, 1).astype(BF)
    part_out = dot(after(grad_attn, gkv), att_t, 0, 1).astype(BF)
    normed_share = own_rows(normed_a)
    part_gain_att = jnp.sum(grad_hidden_a * normed_share, axis=0)
    grad_share = grad_mid + norm_back(grad_hidden_a, normed_share, own_rows(scale_a), gain_att)
    grad_tokens = lax.all_gather(grad_share.astype(BF), "tp", axis=0, tiled=True)

    small = jnp.stack([part_gain_att, part_gain_mlp, jnp.broadcast_to(loss_part, (width,))])
    for axis in AXES:
        step = 1
        while step < lax.axis_size(axis):
            small = small + swap(small, axis, step)
            step *= 2
    small_own = lax.dynamic_slice_in_dim(small[:2], ((y * nx + x) * nc + c) * feat, feat, 1)
    loss = small[2, 0] / (valid_count.astype(F32) * width)

    shard_qkv = scatter_rows(part_qkv)
    shard_out_t = scatter_rows(part_out)
    shard_out_t = summed(
        shard_out_t.astype(BF).reshape(feat, nz, q_cols), 1, "tp", 0
    )
    grad_tokens = after(
        grad_tokens, small_own, shard_qkv, shard_out_t, shard_gate, shard_up, shard_down_t
    ).astype(F32)
    return (
        mixed[None],
        loss,
        grad_tokens[None],
        small_own[0],
        shard_qkv[:, :q_cols],
        shard_qkv[:, q_cols : q_cols + kv_cols],
        shard_qkv[:, q_cols + kv_cols :],
        shard_out_t.T,
        small_own[1],
        shard_gate,
        shard_up,
        shard_down_t.T,
    )


FWD_TQ, FWD_TK = 256, 1024
BWD_TQ, BWD_TK = 256, 512


def solution(mesh):
    nf, nctx, nz = (mesh.shape[a] for a in ("fsdp", "ctx", "tp"))
    nc = 2 if nctx % 2 == 0 else 1
    fine = Mesh(mesh.devices.reshape(nf, nctx // nc, nc, nz), AXES)
    ctx = ("cx", "cc")
    rows = ("fsdp", "cx", "cc")
    return jax.shard_map(
        on_device,
        mesh=fine,
        in_specs=(
            P("fsdp", ctx, None),
            P("fsdp", ctx, None),
            P("fsdp", ctx),
            P("fsdp", ctx),
            P("fsdp", ctx),
            P(),
            P(rows),
            P(rows, "tp"),
            P(rows, "tp"),
            P(rows, "tp"),
            P("tp", rows),
            P(rows),
            P(rows, "tp"),
            P(rows, "tp"),
            P("tp", rows),
        ),
        out_specs=(
            P("fsdp", ctx, None),
            P(),
            P("fsdp", ctx, None),
            P(rows),
            P(rows, "tp"),
            P(rows, "tp"),
            P(rows, "tp"),
            P("tp", rows),
            P(rows),
            P(rows, "tp"),
            P(rows, "tp"),
            P("tp", rows),
        ),
        check_vma=False,
    )
```

time: 1110 us -> 664 us (0.60)
  Pallas kernels: 410 us -> 126 us
  waiting for transfers between devices: 286 us -> 192 us
  local copies, waits for them, and re-layouts: 113 us -> 53.6 us
  starting transfers between devices: 164 us -> 141 us
  other arithmetic: 85.6 us -> 107 us
    pallas_call x9 -> x27, Pallas kernels: 410 us -> 126 us  [the longest x2 24.7 us: ffn_forward(): pl.pallas_call(functools.partial(ffn_forward_kernel, dims), out_shape=(sh...]
    ppermute x55 -> x61, waiting for transfers between devices: 286 us -> 191 us  [swap(): return lax.ppermute(values, axis, [(i, i ^ step) for i in range(size)])]
    convert_element_type x9 -> x17, other arithmetic: 13.2 us -> 38.6 us  [the longest x3 12.3 us: scattered(): total = total.astype(BF)]
    concatenate x7 -> x0, local copies, waits for them, and re-layouts: 24.3 us -> none  [the longest x6 24.2 us: reordered(): jnp.concatenate([values[:, b * width:(b + 1) * width] for b in blocks], a...]
    ppermute x55 -> x61, starting transfers between devices: 164 us -> 140 us  [swap(): return lax.ppermute(values, axis, [(i, i ^ step) for i in range(size)])]
    slice x9 -> x1, local copies, waits for them, and re-layouts: 14.6 us -> 0.64 us  [on_device(): gain_att, gain_mlp = (gain_rows[:, i].reshape(1, -1) for i in range(2))]
    unnamed x142 -> x160, local copies, waits for them, and re-layouts: 31.6 us -> 21.1 us
    dot_general x7 -> x6, matrix products: 21.8 us -> 23.3 us  [dot(): lax.dot_general(a, b, (((ca,), (cb,)), ((), ())), preferred_element_type=...]
  transfers between devices with their start and end apart: 58 -> 68, of which waited for: 22 -> 32; matrix products, arithmetic and copies ran while one was open for 18% -> 24% of each run, Pallas kernels for 35% -> 19%
where the time goes in v2:
time: 664 us; the launch traced here: 660 us
  waiting for transfers between devices  192 us (29%)
  starting transfers between devices  141 us (21%)
  Pallas kernels  126 us (19%)
  other arithmetic  107 us (16%)
  local copies, waits for them, and re-layouts  53.6 us (8%)
  matrix products  23.3 us (4%)
  between operations  17.9 us (3%)
    ppermute x61, waiting for transfers between devices, swap(): return lax.ppermute(values, axis, [(i, i ^ step) for i in range(size)])  191 us
    ppermute x61, starting transfers between devices, swap(): return lax.ppermute(values, axis, [(i, i ^ step) for i in range(size)])  140 us
    pallas_call x2, Pallas kernels, ffn_forward(): pl.pallas_call(functools.partial(ffn_forward_kernel, dims), out_shape=(sh...  24.7 us
    pallas_call x2, Pallas kernels, ffn_backward(): pl.pallas_call(functools.partial(ffn_backward_kernel, dims), out_shape=(s...  24.6 us
    dot_general x6, matrix products, dot(): lax.dot_general(a, b, (((ca,), (cb,)), ((), ())), preferred_element_type=...  23.3 us
    unnamed x160, local copies, waits for them, and re-layouts  21.1 us
    pallas_call x2, Pallas kernels, weight_grad(): pl.pallas_call(functools.partial(weight_grad_kernel, dims, pieces, count)...  20.9 us
    pallas_call x2, Pallas kernels, attn_bwd(): pl.pallas_call(functools.partial(bwd_kernel, scale2, tq, tk, group, len(k...  19.6 us
  transfers between devices with their start and end apart: 68, of which 32 were waited for; matrix products, arithmetic and copies ran while one was open for 24% of the time, Pallas kernels for 19%

profile of v2, /device:TPU:0, one launch (start us, length us, event | category | flops | bytes accessed | tf_op | source)
XLA Modules:
  0.0 660.0 jit_solution(1882525275616582617)
XLA Ops:
  10.4 2.9 collective-permute-start
  14.8 6.2 collective-permute-done
  32.7 3.6 collective-permute-start.7
  41.7 8.0 %collective-permute-done.6 = bf16[192,384]{1,0:T(8,128)(2,1)} collective-permute-done((bf16[192,384]{1,0:T(8,128)(2,1)}, bf16[192,384]{1,0:T(8,128)(2,1)}, u32[]{:S(2)}, u32[]{:S(2)}) %collective-permute-start.6) | collective-permute-done | bytes 147488 | tf_op jit(solution)/shard_map/ppermute | solution.py:175
  54.5 6.7 %put_blocks.2 = (bf16[8,192,768]{2,1,0:T(8,128)(2,1)}, bf16[8,16,768]{2,1,0:T(8,128)(2,1)}) custom-call(s32[8]{0:T(128)} %stack.205.place, bf16[4,208,768]{2,1,0:T(8,128)(2,1)} %bitcast.9.refs_0_, bf16[4,208,768]{2,1,0:T(8,128)(2,1)} %bitcast.13.refs_1_), custom_call_target="tpu_custom_call" | custom-call | flops 7000000000 | bytes 8000000 | tf_op jit(solution)/shard_map/put_blocks/pallas_call | solution.py:243
  61.2 7.9 %collective-permute-done.20.refs_0_ = bf16[3,192,512]{2,1,0:T(8,128)(2,1)} collective-permute-done((bf16[3,192,512]{2,1,0:T(8,128)(2,1)}, bf16[3,192,512]{2,1,0:T(8,128)(2,1)}, u32[]{:S(2)}, u32[]{:S(2)}) %collective-permute-start.20) | collective-permute-done | bytes 589856 | tf_op jit(solution)/shard_map/ppermute | solution.py:175
  79.6 2.9 fusion.19
  90.5 2.8 fusion.3
  98.5 8.1 %collective-permute-done.14.refs_0_ = bf16[2,192,1024]{2,1,0:T(8,128)(2,1)} collective-permute-done((bf16[2,192,1024]{2,1,0:T(8,128)(2,1)}, bf16[2,192,1024]{2,1,0:T(8,128)(2,1)}, u32[]{:S(2)}, u32[]{:S(2)}) %collective-permute-start.14) | collective-permute-done | bytes 786464 | tf_op jit(solution)/shard_map/ppermute | solution.py:175
  121.2 7.6 %collective-permute-done.13 = bf16[96,1536]{1,0:T(8,128)(2,1)S(1)} collective-permute-done((bf16[96,1536]{1,0:T(8,128)(2,1)S(1)}, bf16[96,1536]{1,0:T(8,128)(2,1)S(1)}, u32[]{:S(2)}, u32[]{:S(2)}) %collective-permute-start.13) | collective-permute-done | bytes 294944 | tf_op jit(solution)/shard_map/ppermute | solution.py:175
  130.9 12.0 %attend.1 = (bf16[384,1024]{1,0:T(8,128)(2,1)S(1)}, f32[384,1024]{1,0:T(8,128)S(1)}, f32[2,2,1024]{2,1,0:T(2,128)S(1)}) custom-call(s32[4,4]{1,0:T(4,128)S(1)} %pad_add_fusion.2.bounds, s32[4]{0:T(128)S(1)} %pad_add_fusion.4.place, bf16[384,1024]{1,0:T(8,128)(2,1)S(1)} %copy-done, bf16[2,2,192,1024]{3,2,1,0:T(8,128)(2,1)S(1)} %pad_maximum_fusion.refs_0_, ...), custom_call_target="tpu_custom_call" | custom-call | flops 24000000000 | bytes 8000000 | tf_op jit(solution)/shard_map/attend/pallas_call | solution.py:80
  145.0 7.6 %collective-permute-start.19 = (bf16[768,1536]{1,0:T(8,128)(2,1)}, bf16[768,1536]{1,0:T(8,128)(2,1)}, u32[]{:S(2)}, u32[]{:S(2)}) collective-permute-start(bf16[768,1536]{1,0:T(8,128)(2,1)} %constant_dynamic-update-slice_fusion.6.refs_1_), channel_id=1, source_target_pairs={{0,4},{4,0},{1,5},{5,1},{2,6},{6,2},{3,7},{7,3},{8,12},{12,8},{9,1... | collective-permute-start | bytes 7077896 | tf_op jit(solution)/shard_map/ppermute | solution.py:175
  152.6 5.6 convert_element_type.320
  162.9 8.4 %put_blocks.3 = bf16[8,192,1536]{2,1,0:T(8,128)(2,1)} custom-call(s32[8]{0:T(128)} %stack.205.place, bf16[4,192,1536]{2,1,0:T(8,128)(2,1)} %bitcast.34.refs_0_, bf16[4,192,1536]{2,1,0:T(8,128)(2,1)} %bitcast.35.refs_1_), custom_call_target="tpu_custom_call" | custom-call | flops 7000000000 | bytes 8000000 | tf_op jit(solution)/shard_map/put_blocks/pallas_call | solution.py:243
  171.9 9.2 %collective-permute-done.17 = bf16[384,256]{1,0:T(8,128)(2,1)S(1)} collective-permute-done((bf16[384,256]{1,0:T(8,128)(2,1)S(1)}, bf16[384,256]{1,0:T(8,128)(2,1)S(1)}, u32[]{:S(2)}, u32[]{:S(2)}) %collective-permute-start.17) | collective-permute-done | bytes 196640 | tf_op jit(solution)/shard_map/ppermute | solution.py:175
  181.1 5.9 collective-permute-done.16
  187.0 4.4 multiply_reduce_fusion.4
  191.7 6.8 %collective-permute-start.21 = (bf16[256,1536]{1,0:T(8,128)(2,1)S(1)}, bf16[256,1536]{1,0:T(8,128)(2,1)S(1)}, u32[]{:S(2)}, u32[]{:S(2)}) collective-permute-start(bf16[256,1536]{1,0:T(8,128)(2,1)S(1)} %multiply_convert_fusion.3.h_ref.refs_0_), channel_id=1, source_target_pairs={{0,8},{8,0},{1,9},{9,1},{2,10},{10,2},{3,11},{11,3},{4,12},{12,4},... | collective-permute-start | bytes 2359304 | tf_op jit(solution)/shard_map/ppermute | solution.py:175
  200.4 15.8 %collective-permute-done.21.h_ref.refs_1_ = bf16[256,1536]{1,0:T(8,128)(2,1)S(1)} collective-permute-done((bf16[256,1536]{1,0:T(8,128)(2,1)S(1)}, bf16[256,1536]{1,0:T(8,128)(2,1)S(1)}, u32[]{:S(2)}, u32[]{:S(2)}) %collective-permute-start.21) | collective-permute-done | bytes 786464 | tf_op jit(solution)/shard_map/ppermute | solution.py:175
  217.1 12.2 %feed_forward.3 = (f32[256,2048]{1,0:T(8,128)}, f32[256,2048]{1,0:T(8,128)}, bf16[256,2048]{1,0:T(8,128)(2,1)}, bf16[256,1536]{1,0:T(8,128)(2,1)}) custom-call(bf16[256,1536]{1,0:T(8,128)(2,1)} %copy-done.37, bf16[4,4,3,384,512]{4,3,2,1,0:T(8,128)(2,1)} %bitcast.249, bf16[4,4,3,384,512]{4,3,2,1,0:T(8,128)(2,1)} %bitcast.250, ...), custom_call_target="tpu_custom_call" | custom-call | flops 12000000000 | bytes 8000000 | tf_op jit(solution)/shard_map/feed_forward/pallas_call | solution.py:376
  231.2 12.5 %feed_forward.2 = (f32[256,2048]{1,0:T(8,128)}, f32[256,2048]{1,0:T(8,128)}, bf16[256,2048]{1,0:T(8,128)(2,1)}, f32[256,1536]{1,0:T(8,128)}) custom-call(bf16[256,1536]{1,0:T(8,128)(2,1)} %copy-done.24, bf16[4,4,3,384,512]{4,3,2,1,0:T(8,128)(2,1)} %bitcast.252, bf16[4,4,3,384,512]{4,3,2,1,0:T(8,128)(2,1)} %bitcast.253, bf16[4,4,3,384,512]{4,3,2,1,0:T(8,128)(2,1)} %bitcast.254), custom_call_target="tpu_custom_call" | custom-call | flops 12000000000 | bytes 8000000 | tf_op jit(solution)/shard_map/feed_forward/pallas_call | solution.py:376
  243.6 5.1 collective-permute-done.22
  253.0 12.5 %feed_forward_back.2 = (bf16[256,2048]{1,0:T(8,128)(2,1)}, bf16[256,2048]{1,0:T(8,128)(2,1)}, f32[256,1536]{1,0:T(8,128)}) custom-call(bf16[256,1536]{1,0:T(8,128)(2,1)} %copy-done.25, bf16[4,4,3,384,512]{4,3,2,1,0:T(8,128)(2,1)} %bitcast.255, bf16[4,4,3,384,512]{4,3,2,1,0:T(8,128)(2,1)} %bitcast.256, bf16[4,4,3,384,512]{4,3,2,1,0:T(8,128)(2,1)} %bitcast.257, ...), custom_call_target="tpu_custom_call" | custom-call | flops 12000000000 | bytes 8000000 | tf_op jit(solution)/shard_map/feed_forward_back/pallas_call | solution.py:412
  265.5 4.3 collective-permute-done.23.g_ref.refs_1_
  270.7 8.5 %weight_grad.2 = (bf16[2,4,384,512]{3,2,1,0:T(8,128)(2,1)}, bf16[2,4,384,512]{3,2,1,0:T(8,128)(2,1)}) custom-call(s32[2]{0:T(128)} %pad_add_fusion.6.where, bf16[256,1536]{1,0:T(8,128)(2,1)} %copy-done.25, bf16[256,1536]{1,0:T(8,128)(2,1)} %copy-done.38, bf16[256,2048]{1,0:T(8,128)(2,1)} %get-tuple-element.58.refs_2_, ...), custom_call_target="tpu_custom_call" | custom-call | flops 10000000000 | bytes 8000000 | tf_op jit(solution)/shard_map/weight_grad/pallas_call | solution.py:513
  279.2 12.1 %feed_forward_back.3 = (bf16[256,2048]{1,0:T(8,128)(2,1)}, bf16[256,2048]{1,0:T(8,128)(2,1)}, bf16[256,1536]{1,0:T(8,128)(2,1)}) custom-call(bf16[256,1536]{1,0:T(8,128)(2,1)} %copy-done.38, bf16[4,4,3,384,512]{4,3,2,1,0:T(8,128)(2,1)} %bitcast.258, bf16[4,4,3,384,512]{4,3,2,1,0:T(8,128)(2,1)} %bitcast.259, bf16[4,4,3,384,512]{4,3,2,1,0:T(8,128)(2,1)} %bitcast.260, ...), custom_call_target="tpu_custom_call" | custom-call | flops 12000000000 | bytes 8000000 | tf_op jit(solution)/shard_map/feed_forward_back/pallas_call | solution.py:412
  292.5 12.4 %weight_grad.3 = (bf16[2,4,384,512]{3,2,1,0:T(8,128)(2,1)}, bf16[2,4,384,512]{3,2,1,0:T(8,128)(2,1)}, bf16[2,4,384,512]{3,2,1,0:T(8,128)(2,1)}, bf16[2,4,384,512]{3,2,1,0:T(8,128)(2,1)}) custom-call(s32[2]{0:T(128)} %pad_add_fusion.6.where, bf16[256,1536]{1,0:T(8,128)(2,1)} %copy-done.24, bf16[256,1536]{1,0:T(8,128)(2,1)} %copy-done.37, ...), custom_call_target="tpu_custom_call" | custom-call | flops 10000000000 | bytes 8000000 | tf_op jit(solution)/shard_map/weight_grad/pallas_call | solution.py:513
  305.5 6.1 collective-permute-done.24.refs_0_
  313.9 3.7 fusion.69
  317.7 4.1 convolution_convert_fusion.2
  322.6 3.2 collective-permute-start.26
  327.0 3.0 fusion.13.refs_8_
  330.0 9.2 %collective-permute-done.25.refs_1_ = bf16[384,256]{1,0:T(8,128)(2,1)S(1)} collective-permute-done((bf16[384,256]{1,0:T(8,128)(2,1)S(1)}, bf16[384,256]{1,0:T(8,128)(2,1)S(1)}, u32[]{:S(2)}, u32[]{:S(2)}) %collective-permute-start.25) | collective-permute-done | bytes 196640 | tf_op jit(solution)/shard_map/ppermute | solution.py:175
  339.2 10.0 %collective-permute-done.26.refs_2_ = bf16[384,256]{1,0:T(8,128)(2,1)S(1)} collective-permute-done((bf16[384,256]{1,0:T(8,128)(2,1)S(1)}, bf16[384,256]{1,0:T(8,128)(2,1)S(1)}, u32[]{:S(2)}, u32[]{:S(2)}) %collective-permute-start.26) | collective-permute-done | bytes 196640 | tf_op jit(solution)/shard_map/ppermute | solution.py:175
  352.2 9.6 %attend_back.2 = (f32[192,1024]{1,0:T(8,128)}, bf16[2,2,96,1024]{3,2,1,0:T(8,128)(2,1)}, bf16[2,2,96,1024]{3,2,1,0:T(8,128)(2,1)}) custom-call(s32[4,4]{1,0:T(4,128)} %pad_add_fusion.3.bounds, s32[4]{0:T(128)} %copy-done.6, bf16[384,1024]{1,0:T(8,128)(2,1)} %after.17.q_ref, bf16[2,2,192,1024]{3,2,1,0:T(8,128)(2,1)} %copy-done.3, ...), custom_call_target="tpu_custom_call" | custom-call | flops 24000000000 | bytes 8000000 | tf_op jit(solution)/shard_map/attend_back/pallas_call | solution.py:147
  361.9 3.2 fusion.14.refs_3_
  365.0 3.1 fusion.15.refs_4_
  370.2 3.7 fusion.7.refs_2_
  374.0 10.0 %attend_back.3 = (f32[192,1024]{1,0:T(8,128)}, bf16[2,2,96,1024]{3,2,1,0:T(8,128)(2,1)}, bf16[2,2,96,1024]{3,2,1,0:T(8,128)(2,1)}) custom-call(s32[4,4]{1,0:T(4,128)} %pad_add_fusion.3.bounds, s32[4]{0:T(128)} %copy-done.6, bf16[384,1024]{1,0:T(8,128)(2,1)} %after.17.q_ref, bf16[2,2,192,1024]{3,2,1,0:T(8,128)(2,1)} %copy-done.3, ...), custom_call_target="tpu_custom_call" | custom-call | flops 24000000000 | bytes 8000000 | tf_op jit(solution)/shard_map/attend_back/pallas_call | solution.py:147
  384.0 3.6 collective-permute-start.37
  387.6 2.8 collective-permute-start.56
  390.4 22.5 %collective-permute-start.36 = (bf16[2,96,1024]{2,1,0:T(8,128)(2,1)S(1)}, bf16[2,96,1024]{2,1,0:T(8,128)(2,1)S(1)}, u32[]{:S(2)}, u32[]{:S(2)}) collective-permute-start(bf16[2,96,1024]{2,1,0:T(8,128)(2,1)S(1)} %copy-done.34), channel_id=1, source_target_pairs={{0,8},{8,0},{1,9},{9,1},{2,10},{10,2},{3,11},{11,3},{4,12},{12,4},... | collective-permute-start | bytes 1179656 | tf_op jit(solution)/shard_map/ppermute | solution.py:175
  416.3 6.6 collective-permute-done.36
  423.2 7.6 %collective-permute-done.38 = bf16[2,96,1024]{2,1,0:T(8,128)(2,1)S(1)} collective-permute-done((bf16[2,96,1024]{2,1,0:T(8,128)(2,1)S(1)}, bf16[2,96,1024]{2,1,0:T(8,128)(2,1)S(1)}, u32[]{:S(2)}, u32[]{:S(2)}) %collective-permute-start.38) | collective-permute-done | bytes 393248 | tf_op jit(solution)/shard_map/ppermute | solution.py:175
  435.2 4.3 fusion.6
  442.1 3.2 bitcast_multiply_fusion
  451.0 13.2 %collective-permute-start.34 = (bf16[384,256]{1,0:T(8,128)(2,1)}, bf16[384,256]{1,0:T(8,128)(2,1)}, u32[]{:S(2)}, u32[]{:S(2)}) collective-permute-start(bf16[384,256]{1,0:T(8,128)(2,1)} %get-tuple-element.117), channel_id=1, source_target_pairs={{0,2},{1,3},{2,0},{3,1},{4,6},{5,7},{6,4},{7,5},{8,10},{9,11},{10,... | collective-permute-start | bytes 589832 | tf_op jit(solution)/shard_map/ppermute | solution.py:175
  468.1 7.9 %collective-permute-done.58.refs_0_ = bf16[4,384,512]{2,1,0:T(8,128)(2,1)} collective-permute-done((bf16[4,384,512]{2,1,0:T(8,128)(2,1)}, bf16[4,384,512]{2,1,0:T(8,128)(2,1)}, u32[]{:S(2)}, u32[]{:S(2)}) %collective-permute-start.58) | collective-permute-done | bytes 1572896 | tf_op jit(solution)/shard_map/ppermute | solution.py:175
  476.0 15.4 %collective-permute-start.40 = (bf16[384,256]{1,0:T(8,128)(2,1)}, bf16[384,256]{1,0:T(8,128)(2,1)}, u32[]{:S(2)}, u32[]{:S(2)}) collective-permute-start(bf16[384,256]{1,0:T(8,128)(2,1)} %get-tuple-element.113), channel_id=1, source_target_pairs={{0,2},{1,3},{2,0},{3,1},{4,6},{5,7},{6,4},{7,5},{8,10},{9,11},{10,... | collective-permute-start | bytes 589832 | tf_op jit(solution)/shard_map/ppermute | solution.py:175
  491.4 4.3 fusion.5
  495.7 4.4 convolution_convert_fusion.1
  501.4 4.7 convolution_convert_fusion
  509.1 10.1 %collective-permute-done.40 = bf16[384,256]{1,0:T(8,128)(2,1)} collective-permute-done((bf16[384,256]{1,0:T(8,128)(2,1)}, bf16[384,256]{1,0:T(8,128)(2,1)}, u32[]{:S(2)}, u32[]{:S(2)}) %collective-permute-start.40) | collective-permute-done | bytes 196640 | tf_op jit(solution)/shard_map/ppermute | solution.py:175
  521.2 9.1 %input_grad.1 = f32[256,1536]{1,0:T(8,128)} custom-call(s32[4]{0:T(128)} %pad_add_fusion.5.place, bf16[4,384,256]{2,1,0:T(8,128)(2,1)} %pad_maximum_fusion.9.gq_ref, bf16[4,384,256]{2,1,0:T(8,128)(2,1)} %pad_maximum_fusion.11.gkv_ref, bf16[4,4,384,768]{3,2,1,0:T(8,128)(2,1)} %bitcast.316), custom_call_target="tpu_custom_call" | custom-call | flops 8999999488 | bytes 8000000 | tf_op jit(solution)/shard_map/input_grad/pallas_call | solution.py:457
  530.3 3.1 multiply_reduce_fusion
  537.3 11.7 %collective-permute-start.43 = (f32[3,1536]{1,0:T(4,128)S(1)}, f32[3,1536]{1,0:T(4,128)S(1)}, u32[]{:S(2)}, u32[]{:S(2)}) collective-permute-start(f32[3,1536]{1,0:T(4,128)S(1)} %fusion.68), channel_id=1, source_target_pairs={{0,8},{8,0},{1,9},{9,1},{2,10},{10,2},{3,11},{11,3},{4,12},{12,4},... | collective-permute-start | bytes 55304 | tf_op jit(solution)/shard_map/ppermute | solution.py:175
  554.6 3.3 collective-permute-done.45
  562.5 2.8 add_convert_fusion.3
  567.9 8.3 %collective-permute-done.48 = bf16[2,192,768]{2,1,0:T(8,128)(2,1)S(1)} collective-permute-done((bf16[2,192,768]{2,1,0:T(8,128)(2,1)S(1)}, bf16[2,192,768]{2,1,0:T(8,128)(2,1)S(1)}, u32[]{:S(2)}, u32[]{:S(2)}) %collective-permute-start.48) | collective-permute-done | bytes 589856 | tf_op jit(solution)/shard_map/ppermute | solution.py:175
  578.3 3.0 fusion.1
  594.6 14.7 %collective-permute-done.51 = bf16[2,192,1536]{2,1,0:T(8,128)(2,1)} collective-permute-done((bf16[2,192,1536]{2,1,0:T(8,128)(2,1)}, bf16[2,192,1536]{2,1,0:T(8,128)(2,1)}, u32[]{:S(2)}, u32[]{:S(2)}) %collective-permute-start.51) | collective-permute-done | bytes 1179680 | tf_op jit(solution)/shard_map/ppermute | solution.py:175
  615.0 13.2 %collective-permute-done.59 = bf16[192,512]{1,0:T(8,128)(2,1)S(1)} collective-permute-done((bf16[192,512]{1,0:T(8,128)(2,1)S(1)}, bf16[192,512]{1,0:T(8,128)(2,1)S(1)}, u32[]{:S(2)}, u32[]{:S(2)}) %collective-permute-start.59) | collective-permute-done | bytes 196640 | tf_op jit(solution)/shard_map/ppermute | solution.py:175
  639.2 4.5 collective-permute-done.54
  644.5 5.6 bitcast_convert_fusion
  (410 shorter events, 171.5 us)
Async XLA Ops:
  7.2 209.1 %all-gather.5.cloned.1.call-start = ((), (), s32[]{:S(2)}) async-start(), calls=%async_computation.3 | async-start | bytes 20054016 | tf_op jit(solution)/shard_map/all_gather | solution.py:564
  10.4 10.7 %collective-permute-start = (bf16[208,768]{1,0:T(8,128)(2,1)}, bf16[208,768]{1,0:T(8,128)(2,1)S(1)}, u32[]{:S(2)}, u32[]{:S(2)}) collective-permute-start(bf16[208,768]{1,0:T(8,128)(2,1)} %pad_maximum_fusion.14), channel_id=1, source_target_pairs={{0,8},{8,0},{1,9},{9,1},{2,10},{10,2},{3,11},{11,3},{4,12},{12,4},... | collective-permute-start | bytes 958472 | tf_op jit(solution)/shard_map/ppermute | solution.py:175
  13.3 10.6 %collective-permute-start.1 = (bf16[208,768]{1,0:T(8,128)(2,1)}, bf16[208,768]{1,0:T(8,128)(2,1)}, u32[]{:S(2)}, u32[]{:S(2)}) collective-permute-start(bf16[208,768]{1,0:T(8,128)(2,1)} %pad_maximum_fusion.14), channel_id=1, source_target_pairs={{0,16},{16,0},{1,17},{17,1},{2,18},{18,2},{3,19},{19,3},{4,20},{20... | collective-permute-start | bytes 958472 | tf_op jit(solution)/shard_map/ppermute | solution.py:175
  24.8 5.9 collective-permute-start.2
  26.7 5.3 collective-permute-start.3
  32.7 21.8 %collective-permute-start.4 = (bf16[832,768]{1,0:T(8,128)(2,1)}, bf16[832,768]{1,0:T(8,128)(2,1)}, u32[]{:S(2)}, u32[]{:S(2)}) collective-permute-start(bf16[832,768]{1,0:T(8,128)(2,1)} %constant_dynamic-update-slice_fusion.refs_1_), channel_id=1, source_target_pairs={{0,4},{4,0},{1,5},{5,1},{2,6},{6,2},{3,7},{7,3},{8,12},{12,8},{9,1... | collective-permute-start | bytes 3833864 | tf_op jit(solution)/shard_map/ppermute | solution.py:175
  32.7 9.1 %collective-permute-start.7 = (bf16[192,384]{1,0:T(8,128)(2,1)}, bf16[192,384]{1,0:T(8,128)(2,1)}, u32[]{:S(2)}, u32[]{:S(2)}) collective-permute-start(bf16[192,384]{1,0:T(8,128)(2,1)} %bitcast.12), channel_id=1, source_target_pairs={{0,3},{1,2},{2,1},{3,0},{4,7},{5,6},{6,5},{7,4},{8,11},{9,10},{10,... | collective-permute-start | bytes 442376 | tf_op jit(solution)/shard_map/ppermute | solution.py:175
  36.3 13.5 %collective-permute-start.6 = (bf16[192,384]{1,0:T(8,128)(2,1)}, bf16[192,384]{1,0:T(8,128)(2,1)}, u32[]{:S(2)}, u32[]{:S(2)}) collective-permute-start(bf16[192,384]{1,0:T(8,128)(2,1)} %bitcast.12), channel_id=1, source_target_pairs={{0,2},{1,3},{2,0},{3,1},{4,6},{5,7},{6,4},{7,5},{8,10},{9,11},{10,... | collective-permute-start | bytes 442376 | tf_op jit(solution)/shard_map/ppermute | solution.py:175
  36.3 13.5 %collective-permute-start.5 = (bf16[192,384]{1,0:T(8,128)(2,1)}, bf16[192,384]{1,0:T(8,128)(2,1)}, u32[]{:S(2)}, u32[]{:S(2)}) collective-permute-start(bf16[192,384]{1,0:T(8,128)(2,1)} %bitcast.12), channel_id=1, source_target_pairs={{0,1},{1,0},{2,3},{3,2},{4,5},{5,4},{6,7},{7,6},{8,9},{9,8},{10,11... | collective-permute-start | bytes 442376 | tf_op jit(solution)/shard_map/ppermute | solution.py:175
  53.9 15.3 %collective-permute-start.20 = (bf16[3,192,512]{2,1,0:T(8,128)(2,1)}, bf16[3,192,512]{2,1,0:T(8,128)(2,1)}, u32[]{:S(2)}, u32[]{:S(2)}) collective-permute-start(bf16[3,192,512]{2,1,0:T(8,128)(2,1)} %constant_dynamic-slice_fusion.9), channel_id=1, source_target_pairs={{0,8},{8,0},{1,9},{9,1},{2,10},{10,2},{3,11},{11,3},{4,12},{12,4},... | collective-permute-start | bytes 1769480 | tf_op jit(solution)/shard_map/ppermute | solution.py:175
  71.9 449.3 %all-gather.9.cloned.1.call-start = ((), (), s32[]{:S(2)}) async-start(), calls=%async_computation.5 | async-start | bytes 10027008 | tf_op jit(solution)/shard_map/all_gather | solution.py:606
  75.3 23.2 %collective-permute-start.10 = (bf16[192,1536]{1,0:T(8,128)(2,1)}, bf16[192,1536]{1,0:T(8,128)(2,1)}, u32[]{:S(2)}, u32[]{:S(2)}) collective-permute-start(bf16[192,1536]{1,0:T(8,128)(2,1)} %get-tuple-element.145.refs_2_.refs_3_), channel_id=1, source_target_pairs={{0,8},{8,0},{1,9},{9,1},{2,10},{10,2},{3,11},{11,3},{4,12},{12,4},... | collective-permute-start | bytes 1769480 | tf_op jit(solution)/shard_map/ppermute | solution.py:175
  75.9 34.3 %collective-permute-start.11 = (bf16[192,1536]{1,0:T(8,128)(2,1)}, bf16[192,1536]{1,0:T(8,128)(2,1)}, u32[]{:S(2)}, u32[]{:S(2)}) collective-permute-start(bf16[192,1536]{1,0:T(8,128)(2,1)} %get-tuple-element.145.refs_2_.refs_3_), channel_id=1, source_target_pairs={{0,16},{16,0},{1,17},{17,1},{2,18},{18,2},{3,19},{19,3},{4,20},{20... | collective-permute-start | bytes 1769480 | tf_op jit(solution)/shard_map/ppermute | solution.py:175
  83.7 9.9 %collective-permute-start.8 = (s32[1,1024]{1,0:T(1,128)}, s32[1,1024]{1,0:T(1,128)}, u32[]{:S(2)}, u32[]{:S(2)}) collective-permute-start(s32[1,1024]{1,0:T(1,128)} %after.16), channel_id=1, source_target_pairs={{0,8},{8,0},{1,9},{9,1},{2,10},{10,2},{3,11},{11,3},{4,12},{12,4},... | collective-permute-start | bytes 12296 | tf_op jit(solution)/shard_map/ppermute | solution.py:175
  85.1 21.5 %collective-permute-start.14 = (bf16[2,192,1024]{2,1,0:T(8,128)(2,1)}, bf16[2,192,1024]{2,1,0:T(8,128)(2,1)}, u32[]{:S(2)}, u32[]{:S(2)}) collective-permute-start(bf16[2,192,1024]{2,1,0:T(8,128)(2,1)} %bitcast.271), channel_id=1, source_target_pairs={{0,8},{8,0},{1,9},{9,1},{2,10},{10,2},{3,11},{11,3},{4,12},{12,4},... | collective-permute-start | bytes 2359304 | tf_op jit(solution)/shard_map/ppermute | solution.py:175
  109.1 20.6 %collective-permute-start.15 = (bf16[2,2,192,1024]{3,2,1,0:T(8,128)(2,1)S(1)}, bf16[2,2,192,1024]{3,2,1,0:T(8,128)(2,1)}, u32[]{:S(2)}, u32[]{:S(2)}) collective-permute-start(bf16[2,2,192,1024]{3,2,1,0:T(8,128)(2,1)S(1)} %pad_maximum_fusion.refs_0_), channel_id=1, source_target_pairs={{0,4},{4,0},{1,5},{5,1},{2,6},{6,2},{3,7},{7,3},{8,12},{12,8},{9,1... | collective-permute-start | bytes 4718600 | tf_op jit(solution)/shard_map/ppermute | solution.py:175
  111.2 9.3 %collective-permute-start.12 = (bf16[96,1536]{1,0:T(8,128)(2,1)S(1)}, bf16[96,1536]{1,0:T(8,128)(2,1)S(1)}, u32[]{:S(2)}, u32[]{:S(2)}) collective-permute-start(bf16[96,1536]{1,0:T(8,128)(2,1)S(1)} %slice.252), channel_id=1, source_target_pairs={{0,8},{8,0},{1,9},{9,1},{2,10},{10,2},{3,11},{11,3},{4,12},{12,4},... | collective-permute-start | bytes 884744 | tf_op jit(solution)/shard_map/ppermute | solution.py:175
  112.9 15.9 %collective-permute-start.13 = (bf16[96,1536]{1,0:T(8,128)(2,1)S(1)}, bf16[96,1536]{1,0:T(8,128)(2,1)S(1)}, u32[]{:S(2)}, u32[]{:S(2)}) collective-permute-start(bf16[96,1536]{1,0:T(8,128)(2,1)S(1)} %slice.253), channel_id=1, source_target_pairs={{0,16},{16,0},{1,17},{17,1},{2,18},{18,2},{3,19},{19,3},{4,20},{20... | collective-permute-start | bytes 884744 | tf_op jit(solution)/shard_map/ppermute | solution.py:175
  145.0 408.0 %all-gather.7.cloned.1.call-start = ((), (), s32[]{:S(2)}) async-start(), calls=%async_computation.4 | async-start | bytes 3932160 | tf_op jit(solution)/shard_map/all_gather | solution.py:642
  145.0 17.9 %collective-permute-start.19 = (bf16[768,1536]{1,0:T(8,128)(2,1)}, bf16[768,1536]{1,0:T(8,128)(2,1)}, u32[]{:S(2)}, u32[]{:S(2)}) collective-permute-start(bf16[768,1536]{1,0:T(8,128)(2,1)} %constant_dynamic-update-slice_fusion.6.refs_1_), channel_id=1, source_target_pairs={{0,4},{4,0},{1,5},{5,1},{2,6},{6,2},{3,7},{7,3},{8,12},{12,8},{9,1... | collective-permute-start | bytes 7077896 | tf_op jit(solution)/shard_map/ppermute | solution.py:175
  158.4 13.4 %collective-permute-start.18 = (bf16[384,256]{1,0:T(8,128)(2,1)S(1)}, bf16[384,256]{1,0:T(8,128)(2,1)S(1)}, u32[]{:S(2)}, u32[]{:S(2)}) collective-permute-start(bf16[384,256]{1,0:T(8,128)(2,1)S(1)} %get-tuple-element.128), channel_id=1, source_target_pairs={{0,3},{1,2},{2,1},{3,0},{4,7},{5,6},{6,5},{7,4},{8,11},{9,10},{10,... | collective-permute-start | bytes 589832 | tf_op jit(solution)/shard_map/ppermute | solution.py:175
  161.0 20.1 %collective-permute-start.17 = (bf16[384,256]{1,0:T(8,128)(2,1)S(1)}, bf16[384,256]{1,0:T(8,128)(2,1)S(1)}, u32[]{:S(2)}, u32[]{:S(2)}) collective-permute-start(bf16[384,256]{1,0:T(8,128)(2,1)S(1)} %get-tuple-element.129), channel_id=1, source_target_pairs={{0,2},{1,3},{2,0},{3,1},{4,6},{5,7},{6,4},{7,5},{8,10},{9,11},{10,... | collective-permute-start | bytes 589832 | tf_op jit(solution)/shard_map/ppermute | solution.py:175
  161.0 26.0 %collective-permute-start.16 = (bf16[384,256]{1,0:T(8,128)(2,1)S(1)}, bf16[384,256]{1,0:T(8,128)(2,1)S(1)}, u32[]{:S(2)}, u32[]{:S(2)}) collective-permute-start(bf16[384,256]{1,0:T(8,128)(2,1)S(1)} %get-tuple-element.130), channel_id=1, source_target_pairs={{0,1},{1,0},{2,3},{3,2},{4,5},{5,4},{6,7},{7,6},{8,9},{9,8},{10,11... | collective-permute-start | bytes 589832 | tf_op jit(solution)/shard_map/ppermute | solution.py:175
  191.7 24.6 %collective-permute-start.21 = (bf16[256,1536]{1,0:T(8,128)(2,1)S(1)}, bf16[256,1536]{1,0:T(8,128)(2,1)S(1)}, u32[]{:S(2)}, u32[]{:S(2)}) collective-permute-start(bf16[256,1536]{1,0:T(8,128)(2,1)S(1)} %multiply_convert_fusion.3.h_ref.refs_0_), channel_id=1, source_target_pairs={{0,8},{8,0},{1,9},{9,1},{2,10},{10,2},{3,11},{11,3},{4,12},{12,4},... | collective-permute-start | bytes 2359304 | tf_op jit(solution)/shard_map/ppermute | solution.py:175
  229.4 19.3 %collective-permute-start.22 = (bf16[256,1536]{1,0:T(8,128)(2,1)}, bf16[256,1536]{1,0:T(8,128)(2,1)S(1)}, u32[]{:S(2)}, u32[]{:S(2)}) collective-permute-start(bf16[256,1536]{1,0:T(8,128)(2,1)} %get-tuple-element.51), channel_id=1, source_target_pairs={{0,8},{8,0},{1,9},{9,1},{2,10},{10,2},{3,11},{11,3},{4,12},{12,4},... | collective-permute-start | bytes 2359304 | tf_op jit(solution)/shard_map/ppermute | solution.py:175
  251.5 18.3 %collective-permute-start.23 = (bf16[256,1536]{1,0:T(8,128)(2,1)S(1)}, bf16[256,1536]{1,0:T(8,128)(2,1)S(1)}, u32[]{:S(2)}, u32[]{:S(2)}) collective-permute-start(bf16[256,1536]{1,0:T(8,128)(2,1)S(1)} %multiply_convert_fusion.2.g_ref.refs_0_), channel_id=1, source_target_pairs={{0,8},{8,0},{1,9},{9,1},{2,10},{10,2},{3,11},{11,3},{4,12},{12,4},... | collective-permute-start | bytes 2359304 | tf_op jit(solution)/shard_map/ppermute | solution.py:175
  279.2 46.6 %collective-permute-start.28 = (bf16[2,4,384,512]{3,2,1,0:T(8,128)(2,1)}, bf16[2,4,384,512]{3,2,1,0:T(8,128)(2,1)}, u32[]{:S(2)}, u32[]{:S(2)}) collective-permute-start(bf16[2,4,384,512]{3,2,1,0:T(8,128)(2,1)} %get-tuple-element.61.refs_2_), channel_id=1, source_target_pairs={{0,4},{4,0},{1,5},{5,1},{2,6},{6,2},{3,7},{7,3},{8,12},{12,8},{9,1... | collective-permute-start | bytes 9437192 | tf_op jit(solution)/shard_map/ppermute | solution.py:175
  291.4 20.3 %collective-permute-start.24 = (bf16[256,1536]{1,0:T(8,128)(2,1)}, bf16[256,1536]{1,0:T(8,128)(2,1)}, u32[]{:S(2)}, u32[]{:S(2)}) collective-permute-start(bf16[256,1536]{1,0:T(8,128)(2,1)} %get-tuple-element.57), channel_id=1, source_target_pairs={{0,8},{8,0},{1,9},{9,1},{2,10},{10,2},{3,11},{11,3},{4,12},{12,4},... | collective-permute-start | bytes 2359304 | tf_op jit(solution)/shard_map/ppermute | solution.py:175
  304.9 56.9 %collective-permute-start.31 = (bf16[2,4,384,512]{3,2,1,0:T(8,128)(2,1)}, bf16[2,4,384,512]{3,2,1,0:T(8,128)(2,1)}, u32[]{:S(2)}, u32[]{:S(2)}) collective-permute-start(bf16[2,4,384,512]{3,2,1,0:T(8,128)(2,1)} %get-tuple-element.67.refs_5_), channel_id=1, source_target_pairs={{0,4},{4,0},{1,5},{5,1},{2,6},{6,2},{3,7},{7,3},{8,12},{12,8},{9,1... | collective-permute-start | bytes 9437192 | tf_op jit(solution)/shard_map/ppermute | solution.py:175
  305.2 59.8 %collective-permute-start.32 = (bf16[2,4,384,512]{3,2,1,0:T(8,128)(2,1)}, bf16[2,4,384,512]{3,2,1,0:T(8,128)(2,1)}, u32[]{:S(2)}, u32[]{:S(2)}) collective-permute-start(bf16[2,4,384,512]{3,2,1,0:T(8,128)(2,1)} %get-tuple-element.69.refs_7_), channel_id=1, source_target_pairs={{0,4},{4,0},{1,5},{5,1},{2,6},{6,2},{3,7},{7,3},{8,12},{12,8},{9,1... | collective-permute-start | bytes 9437192 | tf_op jit(solution)/shard_map/ppermute | solution.py:175
  317.7 266.9 %reduce-scatter.8.cloned.1.call-start = ((), (), s32[]{:S(2)}) async-start(), calls=%async_computation.9 | async-start | bytes 1966080 | tf_op jit(solution)/shard_map/reduce_scatter | solution.py:663
  322.6 16.5 %collective-permute-start.25 = (bf16[384,256]{1,0:T(8,128)(2,1)S(1)}, bf16[384,256]{1,0:T(8,128)(2,1)S(1)}, u32[]{:S(2)}, u32[]{:S(2)}) collective-permute-start(bf16[384,256]{1,0:T(8,128)(2,1)S(1)} %get-tuple-element.125), channel_id=1, source_target_pairs={{0,1},{1,0},{2,3},{3,2},{4,5},{5,4},{6,7},{7,6},{8,9},{9,8},{10,11... | collective-permute-start | bytes 589832 | tf_op jit(solution)/shard_map/ppermute | solution.py:175
  322.6 26.5 %collective-permute-start.26 = (bf16[384,256]{1,0:T(8,128)(2,1)S(1)}, bf16[384,256]{1,0:T(8,128)(2,1)S(1)}, u32[]{:S(2)}, u32[]{:S(2)}) collective-permute-start(bf16[384,256]{1,0:T(8,128)(2,1)S(1)} %get-tuple-element.124), channel_id=1, source_target_pairs={{0,2},{1,3},{2,0},{3,1},{4,6},{5,7},{6,4},{7,5},{8,10},{9,11},{10,... | collective-permute-start | bytes 589832 | tf_op jit(solution)/shard_map/ppermute | solution.py:175
  325.8 23.3 %collective-permute-start.27 = (bf16[384,256]{1,0:T(8,128)(2,1)S(1)}, bf16[384,256]{1,0:T(8,128)(2,1)}, u32[]{:S(2)}, u32[]{:S(2)}) collective-permute-start(bf16[384,256]{1,0:T(8,128)(2,1)S(1)} %get-tuple-element.123), channel_id=1, source_target_pairs={{0,3},{1,2},{2,1},{3,0},{4,7},{5,6},{6,5},{7,4},{8,11},{9,10},{10,... | collective-permute-start | bytes 589832 | tf_op jit(solution)/shard_map/ppermute | solution.py:175
  339.2 31.0 %collective-permute-start.30 = (bf16[4,384,512]{2,1,0:T(8,128)(2,1)}, bf16[4,384,512]{2,1,0:T(8,128)(2,1)}, u32[]{:S(2)}, u32[]{:S(2)}) collective-permute-start(bf16[4,384,512]{2,1,0:T(8,128)(2,1)} %fusion.13.refs_8_), channel_id=1, source_target_pairs={{0,16},{16,0},{1,17},{17,1},{2,18},{18,2},{3,19},{19,3},{4,20},{20... | collective-permute-start | bytes 4718600 | tf_op jit(solution)/shard_map/ppermute | solution.py:175
  361.8 6.4 collective-permute-start.29
  373.9 218.7 %reduce-scatter.4.cloned.1.call-start = ((), (), s32[]{:S(2)}) async-start(), calls=%async_computation.7 | async-start | bytes 1966080 | tf_op jit(solution)/shard_map/reduce_scatter | solution.py:663
  384.0 29.0 %collective-permute-start.37 = (bf16[2,2,96,1024]{3,2,1,0:T(8,128)(2,1)}, bf16[2,2,96,1024]{3,2,1,0:T(8,128)(2,1)S(1)}, u32[]{:S(2)}, u32[]{:S(2)}) collective-permute-start(bf16[2,2,96,1024]{3,2,1,0:T(8,128)(2,1)} %get-tuple-element.81), channel_id=1, source_target_pairs={{0,4},{4,0},{1,5},{5,1},{2,6},{6,2},{3,7},{7,3},{8,12},{12,8},{9,1... | collective-permute-start | bytes 2359304 | tf_op jit(solution)/shard_map/ppermute | solution.py:175
  387.6 46.5 %collective-permute-start.56 = (bf16[4,384,512]{2,1,0:T(8,128)(2,1)S(1)}, bf16[4,384,512]{2,1,0:T(8,128)(2,1)S(1)}, u32[]{:S(2)}, u32[]{:S(2)}) collective-permute-start(bf16[4,384,512]{2,1,0:T(8,128)(2,1)S(1)} %copy-done.21), channel_id=1, source_target_pairs={{0,16},{16,0},{1,17},{17,1},{2,18},{18,2},{3,19},{19,3},{4,20},{20... | collective-permute-start | bytes 4718600 | tf_op jit(solution)/shard_map/ppermute | solution.py:175
  390.4 32.4 %collective-permute-start.36 = (bf16[2,96,1024]{2,1,0:T(8,128)(2,1)S(1)}, bf16[2,96,1024]{2,1,0:T(8,128)(2,1)S(1)}, u32[]{:S(2)}, u32[]{:S(2)}) collective-permute-start(bf16[2,96,1024]{2,1,0:T(8,128)(2,1)S(1)} %copy-done.34), channel_id=1, source_target_pairs={{0,8},{8,0},{1,9},{9,1},{2,10},{10,2},{3,11},{11,3},{4,12},{12,4},... | collective-permute-start | bytes 1179656 | tf_op jit(solution)/shard_map/ppermute | solution.py:175
  414.3 16.5 %collective-permute-start.38 = (bf16[2,96,1024]{2,1,0:T(8,128)(2,1)S(1)}, bf16[2,96,1024]{2,1,0:T(8,128)(2,1)S(1)}, u32[]{:S(2)}, u32[]{:S(2)}) collective-permute-start(bf16[2,96,1024]{2,1,0:T(8,128)(2,1)S(1)} %fusion.31), channel_id=1, source_target_pairs={{0,8},{8,0},{1,9},{9,1},{2,10},{10,2},{3,11},{11,3},{4,12},{12,4},... | collective-permute-start | bytes 1179656 | tf_op jit(solution)/shard_map/ppermute | solution.py:175
  439.6 171.7 %reduce-scatter.6.cloned.1.call-start = ((), (), s32[]{:S(2)}) async-start(), calls=%async_computation.8 | async-start | bytes 1966080 | tf_op jit(solution)/shard_map/reduce_scatter | solution.py:663
  439.7 36.4 %collective-permute-start.58 = (bf16[4,384,512]{2,1,0:T(8,128)(2,1)}, bf16[4,384,512]{2,1,0:T(8,128)(2,1)}, u32[]{:S(2)}, u32[]{:S(2)}) collective-permute-start(bf16[4,384,512]{2,1,0:T(8,128)(2,1)} %fusion.15.refs_4_), channel_id=1, source_target_pairs={{0,16},{16,0},{1,17},{17,1},{2,18},{18,2},{3,19},{19,3},{4,20},{20... | collective-permute-start | bytes 4718600 | tf_op jit(solution)/shard_map/ppermute | solution.py:175
  448.7 57.3 %collective-permute-start.35 = (bf16[384,256]{1,0:T(8,128)(2,1)}, bf16[384,256]{1,0:T(8,128)(2,1)}, u32[]{:S(2)}, u32[]{:S(2)}) collective-permute-start(bf16[384,256]{1,0:T(8,128)(2,1)} %get-tuple-element.116), channel_id=1, source_target_pairs={{0,3},{1,2},{2,1},{3,0},{4,7},{5,6},{6,5},{7,4},{8,11},{9,10},{10,... | collective-permute-start | bytes 589832 | tf_op jit(solution)/shard_map/ppermute | solution.py:175
  451.0 55.3 %collective-permute-start.34 = (bf16[384,256]{1,0:T(8,128)(2,1)}, bf16[384,256]{1,0:T(8,128)(2,1)}, u32[]{:S(2)}, u32[]{:S(2)}) collective-permute-start(bf16[384,256]{1,0:T(8,128)(2,1)} %get-tuple-element.117), channel_id=1, source_target_pairs={{0,2},{1,3},{2,0},{3,1},{4,6},{5,7},{6,4},{7,5},{8,10},{9,11},{10,... | collective-permute-start | bytes 589832 | tf_op jit(solution)/shard_map/ppermute | solution.py:175
  464.2 42.1 %collective-permute-start.33 = (bf16[384,256]{1,0:T(8,128)(2,1)}, bf16[384,256]{1,0:T(8,128)(2,1)}, u32[]{:S(2)}, u32[]{:S(2)}) collective-permute-start(bf16[384,256]{1,0:T(8,128)(2,1)} %get-tuple-element.118), channel_id=1, source_target_pairs={{0,1},{1,0},{2,3},{3,2},{4,5},{5,4},{6,7},{7,6},{8,9},{9,8},{10,11... | collective-permute-start | bytes 589832 | tf_op jit(solution)/shard_map/ppermute | solution.py:175
  465.7 43.4 %collective-permute-start.41 = (bf16[384,256]{1,0:T(8,128)(2,1)}, bf16[384,256]{1,0:T(8,128)(2,1)}, u32[]{:S(2)}, u32[]{:S(2)}) collective-permute-start(bf16[384,256]{1,0:T(8,128)(2,1)} %get-tuple-element.112), channel_id=1, source_target_pairs={{0,3},{1,2},{2,1},{3,0},{4,7},{5,6},{6,5},{7,4},{8,11},{9,10},{10,... | collective-permute-start | bytes 589832 | tf_op jit(solution)/shard_map/ppermute | solution.py:175
  476.0 43.1 %collective-permute-start.40 = (bf16[384,256]{1,0:T(8,128)(2,1)}, bf16[384,256]{1,0:T(8,128)(2,1)}, u32[]{:S(2)}, u32[]{:S(2)}) collective-permute-start(bf16[384,256]{1,0:T(8,128)(2,1)} %get-tuple-element.113), channel_id=1, source_target_pairs={{0,2},{1,3},{2,0},{3,1},{4,6},{5,7},{6,4},{7,5},{8,10},{9,11},{10,... | collective-permute-start | bytes 589832 | tf_op jit(solution)/shard_map/ppermute | solution.py:175
  500.2 144.4 %all-gather.11.cloned.1.call-start = ((), (), s32[]{:S(2)}) async-start(), calls=%async_computation.6 | async-start | bytes 3932160 | tf_op jit(solution)/shard_map/all_gather | solution.py:733
  506.1 13.1 %collective-permute-start.39 = (bf16[384,256]{1,0:T(8,128)(2,1)S(1)}, bf16[384,256]{1,0:T(8,128)(2,1)S(1)}, u32[]{:S(2)}, u32[]{:S(2)}) collective-permute-start(bf16[384,256]{1,0:T(8,128)(2,1)S(1)} %copy-done.59), channel_id=1, source_target_pairs={{0,1},{1,0},{2,3},{3,2},{4,5},{5,4},{6,7},{7,6},{8,9},{9,8},{10,11... | collective-permute-start | bytes 589832 | tf_op jit(solution)/shard_map/ppermute | solution.py:175
  506.3 53.0 %collective-permute-start.47 = (bf16[2,2,192,768]{3,2,1,0:T(8,128)(2,1)S(1)}, bf16[2,2,192,768]{3,2,1,0:T(8,128)(2,1)}, u32[]{:S(2)}, u32[]{:S(2)}) collective-permute-start(bf16[2,2,192,768]{3,2,1,0:T(8,128)(2,1)S(1)} %dynamic-slice_bitcast_fusion.2), channel_id=1, source_target_pairs={{0,4},{4,0},{1,5},{5,1},{2,6},{6,2},{3,7},{7,3},{8,12},{12,8},{9,1... | collective-permute-start | bytes 3538952 | tf_op jit(solution)/shard_map/ppermute | solution.py:175
  535.9 42.4 %collective-permute-start.50 = (bf16[2,2,192,1536]{3,2,1,0:T(8,128)(2,1)}, bf16[2,2,192,1536]{3,2,1,0:T(8,128)(2,1)}, u32[]{:S(2)}, u32[]{:S(2)}) collective-permute-start(bf16[2,2,192,1536]{3,2,1,0:T(8,128)(2,1)} %dynamic-slice_bitcast_fusion), channel_id=1, source_target_pairs={{0,4},{4,0},{1,5},{5,1},{2,6},{6,2},{3,7},{7,3},{8,12},{12,8},{9,1... | collective-permute-start | bytes 7077896 | tf_op jit(solution)/shard_map/ppermute | solution.py:175
  537.3 13.5 %collective-permute-start.43 = (f32[3,1536]{1,0:T(4,128)S(1)}, f32[3,1536]{1,0:T(4,128)S(1)}, u32[]{:S(2)}, u32[]{:S(2)}) collective-permute-start(f32[3,1536]{1,0:T(4,128)S(1)} %fusion.68), channel_id=1, source_target_pairs={{0,8},{8,0},{1,9},{9,1},{2,10},{10,2},{3,11},{11,3},{4,12},{12,4},... | collective-permute-start | bytes 55304 | tf_op jit(solution)/shard_map/ppermute | solution.py:175
  558.4 6.9 %collective-permute-start.46 = (f32[3,1536]{1,0:T(4,128)}, f32[3,1536]{1,0:T(4,128)}, u32[]{:S(2)}, u32[]{:S(2)}) collective-permute-start(f32[3,1536]{1,0:T(4,128)} %add.545), channel_id=1, source_target_pairs={{0,2},{1,3},{2,0},{3,1},{4,6},{5,7},{6,4},{7,5},{8,10},{9,11},{10,... | collective-permute-start | bytes 55304 | tf_op jit(solution)/shard_map/ppermute | solution.py:175
  561.0 15.2 %collective-permute-start.48 = (bf16[2,192,768]{2,1,0:T(8,128)(2,1)S(1)}, bf16[2,192,768]{2,1,0:T(8,128)(2,1)S(1)}, u32[]{:S(2)}, u32[]{:S(2)}) collective-permute-start(bf16[2,192,768]{2,1,0:T(8,128)(2,1)S(1)} %dynamic-slice_bitcast_fusion.4), channel_id=1, source_target_pairs={{0,16},{16,0},{1,17},{17,1},{2,18},{18,2},{3,19},{19,3},{4,20},{20... | collective-permute-start | bytes 1769480 | tf_op jit(solution)/shard_map/ppermute | solution.py:175
  576.4 9.5 %collective-permute-start.49 = (bf16[192,768]{1,0:T(8,128)(2,1)S(1)}, bf16[192,768]{1,0:T(8,128)(2,1)}, u32[]{:S(2)}, u32[]{:S(2)}) collective-permute-start(bf16[192,768]{1,0:T(8,128)(2,1)S(1)} %dynamic-slice_bitcast_fusion.5), channel_id=1, source_target_pairs={{0,8},{8,0},{1,9},{9,1},{2,10},{10,2},{3,11},{11,3},{4,12},{12,4},... | collective-permute-start | bytes 884744 | tf_op jit(solution)/shard_map/ppermute | solution.py:175
  582.4 26.8 %collective-permute-start.51 = (bf16[2,192,1536]{2,1,0:T(8,128)(2,1)}, bf16[2,192,1536]{2,1,0:T(8,128)(2,1)}, u32[]{:S(2)}, u32[]{:S(2)}) collective-permute-start(bf16[2,192,1536]{2,1,0:T(8,128)(2,1)} %dynamic-slice_bitcast_fusion.1), channel_id=1, source_target_pairs={{0,16},{16,0},{1,17},{17,1},{2,18},{18,2},{3,19},{19,3},{4,20},{20... | collective-permute-start | bytes 3538952 | tf_op jit(solution)/shard_map/ppermute | solution.py:175
  585.6 5.7 collective-permute-start.60
  594.3 19.7 %collective-permute-start.57 = (bf16[192,512]{1,0:T(8,128)(2,1)}, bf16[192,512]{1,0:T(8,128)(2,1)}, u32[]{:S(2)}, u32[]{:S(2)}) collective-permute-start(bf16[192,512]{1,0:T(8,128)(2,1)} %dynamic-slice_bitcast_fusion.8), channel_id=1, source_target_pairs={{0,8},{8,0},{1,9},{9,1},{2,10},{10,2},{3,11},{11,3},{4,12},{12,4},... | collective-permute-start | bytes 589832 | tf_op jit(solution)/shard_map/ppermute | solution.py:175
  610.9 18.2 %collective-permute-start.52 = (bf16[192,1536]{1,0:T(8,128)(2,1)S(1)}, bf16[192,1536]{1,0:T(8,128)(2,1)}, u32[]{:S(2)}, u32[]{:S(2)}) collective-permute-start(bf16[192,1536]{1,0:T(8,128)(2,1)S(1)} %dynamic-slice_bitcast_fusion.3), channel_id=1, source_target_pairs={{0,8},{8,0},{1,9},{9,1},{2,10},{10,2},{3,11},{11,3},{4,12},{12,4},... | collective-permute-start | bytes 1769480 | tf_op jit(solution)/shard_map/ppermute | solution.py:175
  612.3 15.8 %collective-permute-start.59 = (bf16[192,512]{1,0:T(8,128)(2,1)S(1)}, bf16[192,512]{1,0:T(8,128)(2,1)S(1)}, u32[]{:S(2)}, u32[]{:S(2)}) collective-permute-start(bf16[192,512]{1,0:T(8,128)(2,1)S(1)} %dynamic-slice_bitcast_fusion.7), channel_id=1, source_target_pairs={{0,8},{8,0},{1,9},{9,1},{2,10},{10,2},{3,11},{11,3},{4,12},{12,4},... | collective-permute-start | bytes 589832 | tf_op jit(solution)/shard_map/ppermute | solution.py:175
  631.3 7.9 %collective-permute-start.55 = (bf16[192,384]{1,0:T(8,128)(2,1)S(1)}, bf16[192,384]{1,0:T(8,128)(2,1)S(1)}, u32[]{:S(2)}, u32[]{:S(2)}) collective-permute-start(bf16[192,384]{1,0:T(8,128)(2,1)S(1)} %bitcast.303), channel_id=1, source_target_pairs={{0,3},{1,2},{2,1},{3,0},{4,7},{5,6},{6,5},{7,4},{8,11},{9,10},{10,... | collective-permute-start | bytes 442376 | tf_op jit(solution)/shard_map/ppermute | solution.py:175
  633.6 10.2 %collective-permute-start.54 = (bf16[192,384]{1,0:T(8,128)(2,1)S(1)}, bf16[192,384]{1,0:T(8,128)(2,1)S(1)}, u32[]{:S(2)}, u32[]{:S(2)}) collective-permute-start(bf16[192,384]{1,0:T(8,128)(2,1)S(1)} %bitcast.304), channel_id=1, source_target_pairs={{0,2},{1,3},{2,0},{3,1},{4,6},{5,7},{6,4},{7,5},{8,10},{9,11},{10,... | collective-permute-start | bytes 442376 | tf_op jit(solution)/shard_map/ppermute | solution.py:175
  633.8 9.9 %collective-permute-start.53 = (bf16[192,384]{1,0:T(8,128)(2,1)S(1)}, bf16[192,384]{1,0:T(8,128)(2,1)S(1)}, u32[]{:S(2)}, u32[]{:S(2)}) collective-permute-start(bf16[192,384]{1,0:T(8,128)(2,1)S(1)} %bitcast.305), channel_id=1, source_target_pairs={{0,1},{1,0},{2,3},{3,2},{4,5},{5,4},{6,7},{7,6},{8,9},{9,8},{10,11... | collective-permute-start | bytes 442376 | tf_op jit(solution)/shard_map/ppermute | solution.py:175
  (78 other events, 762.2 us)
Sparse Core Ops, SparseCore 0:
  72.0 116.8 all-gather.4
  191.2 83.2 all-gather.8
  317.8 76.1 all-gather.6
  396.2 35.6 reduce-scatter.7
  439.7 79.2 reduce-scatter.3
  521.2 39.6 reduce-scatter.5
  565.4 63.2 all-gather.10

commit v3 on v2

--- a/solution.py
+++ b/solution.py
@@ -10,6 +10,11 @@
 from jax.sharding import PartitionSpec as P
 
 HD=96
+NO_COST = pl.CostEstimate(flops=0, bytes_accessed=0, transcendentals=0)
+
+
+def about(us):
+    return pl.CostEstimate(flops=us*10**9, bytes_accessed=10**6, transcendentals=0)
 NEG=-1e30
 F32=jnp.float32; BF=jnp.bfloat16
 def dot(a,b,ca,cb):
@@ -85,7 +90,7 @@
             out_specs=[qs, qs, pl.BlockSpec((1, group, tq), lambda g,i,*_:(g,0,i))],
             scratch_shapes=[pltpu.VMEM((N,HD),BF), pltpu.VMEM((HD,N),BF), pltpu.VMEM((1,group*tq),F32), pltpu.VMEM((1,group*tq),F32), pltpu.VMEM((HD,group*tq),F32)]),
         compiler_params=pltpu.CompilerParams(vmem_limit_bytes=48*2**20),
-        cost_estimate=pl.CostEstimate(flops=24*10**9, bytes_accessed=8*10**6, transcendentals=0),
+        cost_estimate=about(12),
         name="attend",
     )(bounds, place, qT, *kv_sources, start, qpos)
 
@@ -152,7 +157,7 @@
             out_specs=[pl.BlockSpec((group*HD, tq), lambda g,i,*_:(0,i))] + kv_out,
             scratch_shapes=[pltpu.VMEM((HD,N),BF), pltpu.VMEM((N,HD),BF), pltpu.VMEM((N,HD),BF), pltpu.VMEM((HD,N),F32), pltpu.VMEM((HD,N),F32), pltpu.VMEM((HD,group*tq),F32)]),
         compiler_params=pltpu.CompilerParams(vmem_limit_bytes=56*2**20),
-        cost_estimate=pl.CostEstimate(flops=24*10**9, bytes_accessed=8*10**6, transcendentals=0),
+        cost_estimate=about(12),
         name="attend_back",
     )(bounds, place, qT, *kv_sources, start, qpos, gT, of, lse)
 
@@ -188,6 +193,7 @@
         in_specs=[pl.BlockSpec(memory_space=pl.ANY)] * (len(values) + len(others)),
         out_specs=[pl.BlockSpec(memory_space=pl.ANY)] * len(values),
         input_output_aliases={i: i for i in range(len(values))},
+        cost_estimate=NO_COST,
         name="after",
     )(*values, *others)
     return jax.tree.unflatten(tree, list(done))
@@ -210,81 +216,93 @@
     return [values] + [swap(values, axis, k) for k in range(1, lax.axis_size(axis))]
 
 
-def place_kernel(counts, place, *refs):
-    sources, outs = refs[: len(counts)], refs[len(counts) :]
-    n = pl.program_id(0)
-    first = 0
-    for count, source in zip(counts, sources):
-
-        @pl.when((n >= first) & (n < first + count))
-        def _(source=source):
-            at = 0
-            for out in outs:
-                out[...] = source[:, at : at + out.shape[1]]
-                at += out.shape[1]
-
-        first += count
-
-
-def put_blocks(sources, place, cut=None):
-    counts = [s.shape[0] for s in sources]
-    shape = sources[0].shape[1:]
-    cuts = [shape[0]] if cut is None else [cut, shape[0] - cut]
-    specs = []
-    first = 0
-    for count in counts:
-        specs.append(
-            pl.BlockSpec(
-                (1,) + shape,
-                lambda n, place, first=first, count=count: (jnp.clip(n - first, 0, count - 1), 0, 0),
-            )
+def place_kernel(plan, count, place, *refs):
+    sources, outs, sems = refs[:count], refs[count:-1], refs[-1]
+    copies = [
+        pltpu.make_async_copy(
+            sources[source].at[pl.ds(first, n)], outs[out].at[place[spot], pl.ds(row, n)], sems.at[i]
         )
-        first += count
+        for i, (source, first, n, out, spot, row) in enumerate(plan)
+    ]
+    for copy in copies:
+        copy.start()
+    for copy in copies:
+        copy.wait()
+
+
+def put_blocks(pieces, place, rows, cut=None):
+    width, kind = pieces[0][0].shape[1], pieces[0][0].dtype
+    cuts = [0, rows] if cut is None else [0, cut, rows]
+    sources, plan = [], []
+    for array, first, n, spot, row in pieces:
+        known = [i for i, s in enumerate(sources) if s is array]
+        if not known:
+            known = [len(sources)]
+            sources.append(array)
+        for out, (low, high) in enumerate(zip(cuts[:-1], cuts[1:])):
+            a, b = max(row, low), min(row + n, high)
+            if a < b:
+                plan.append((known[0], first + a - row, b - a, out, spot, a - low))
     return pl.pallas_call(
-        functools.partial(place_kernel, counts),
-        out_shape=[jax.ShapeDtypeStruct((first, r, shape[1]), sources[0].dtype) for r in cuts],
-        grid_spec=pltpu.PrefetchScalarGridSpec(
-            num_scalar_prefetch=1,
-            grid=(first,),
-            in_specs=specs,
-            out_specs=[
-                pl.BlockSpec((1, r, shape[1]), lambda n, place: (place[n], 0, 0)) for r in cuts
-            ],
-        ),
-        cost_estimate=pl.CostEstimate(flops=7*10**9, bytes_accessed=8*10**6, transcendentals=0),
+        functools.partial(place_kernel, plan, len(sources)),
+        out_shape=[
+            jax.ShapeDtypeStruct((len(place), b - a, width), kind) for a, b in zip(cuts[:-1], cuts[1:])
+        ],
+        in_specs=[pl.BlockSpec(memory_space=pltpu.SMEM)]
+        + [pl.BlockSpec(memory_space=pltpu.VMEM)] * len(sources),
+        out_specs=[pl.BlockSpec(memory_space=pl.ANY)] * (len(cuts) - 1),
+        scratch_shapes=[pltpu.SemaphoreType.DMA((len(plan),))],
+        compiler_params=pltpu.CompilerParams(vmem_limit_bytes=32 * 2**20),
+        cost_estimate=about(2),
         name="put_blocks",
     )(jnp.stack(place).astype(jnp.int32), *sources)
 
 
-def gather_rows(shard, hold=None, hold_core=None, cut=None):
+def gather_rows(shard, hold_near=None, hold_core=None, cut=None, from_y=None, hold_x=None):
     rows, width = shard.shape
     nf, nx, nc = (lax.axis_size(a) for a in ("fsdp", "cx", "cc"))
     y, x, c = (lax.axis_index(a) for a in ("fsdp", "cx", "cc"))
-    half = rows // 2
     if nf == 2 and nx == 2:
-        from_x = swap(shard, "cx")
-        from_y = swap(shard, "fsdp")
-        x_parts = [shard, from_x]
-        if hold is not None:
-            from_x, from_y = after((from_x, from_y), hold)
+        half = rows // 2 // 16 * 16
+        from_x = swap(shard if hold_x is None else after(shard, hold_x), "cx")
+        if from_y is None:
+            from_y = swap(shard, "fsdp")
         top = swap(from_y[:half], "cx")
         low = swap(from_x[half:], "fsdp")
-        near = jnp.concatenate([shard, from_x, from_y, top, low], axis=0)
+        x_parts = [shard, from_x]
+        came = [from_x, from_y, top, low]
+        if hold_near is not None:
+            top, low = after((top, low), hold_near)
+        own = [
+            (shard, 0, rows, 0, 0),
+            (from_x, 0, rows, 1, 0),
+            (from_y, 0, rows, 2, 0),
+            (top, 0, half, 3, 0),
+            (low, 0, rows - half, 3, half),
+        ]
     else:
         x_parts = everyone(shard, "cx")
         near = jnp.concatenate(x_parts, axis=0)
         near = jnp.concatenate(everyone(near, "fsdp"), axis=0)
-    parts = everyone(near, "cc")
-    if hold_core is not None and nc > 1:
-        parts[1:] = after(parts[1:], hold_core)
-    sources = [v.reshape(nf * nx, rows, width) for v in parts]
+        came = [near]
+        own = [(near, i * rows, rows, i, 0) for i in range(nf * nx)]
+    pieces = list(own)
+    for k in range(1, nc):
+        given = {}
+        for array, first, n, spot, row in own:
+            if id(array) not in given:
+                given[id(array)] = swap(array, "cc", k)
+                last = id(array)
+        if hold_core is not None:
+            given[last] = after(given[last], hold_core)
+        pieces += [(given[id(a)], first, n, spot + k * nf * nx, row) for a, first, n, spot, row in own]
     place = [
         ((y ^ dy) * nx + (x ^ dx)) * nc + (c ^ dc)
         for dc in range(nc)
         for dy in range(nf)
         for dx in range(nx)
     ]
-    return put_blocks(sources, place, cut), near, x_parts
+    return put_blocks(pieces, place, rows, cut), x_parts, came
 
 
 def scatter_rows(part):
@@ -292,10 +310,10 @@
     y, x, c = (lax.axis_index(a) for a in ("fsdp", "cx", "cc"))
     width = part.shape[1]
     total = part.reshape(nf, nx, nc, -1, width)
-    total = summed(total, 2, "cc", c)
-    total = summed(total.astype(jnp.bfloat16), 0, "fsdp", y)
-    total = summed(total.astype(jnp.bfloat16), 0, "cx", x)
-    return total
+    on_chip = summed(total, 2, "cc", c).astype(jnp.bfloat16)
+    on_y = summed(on_chip, 0, "fsdp", y).astype(jnp.bfloat16)
+    total = summed(on_y, 0, "cx", x)
+    return total, on_y
 
 
 def summed(part, dim, axis, index):
@@ -386,7 +404,7 @@
         out_specs=[col, col, col, full],
         scratch_shapes=[pltpu.VMEM((rows, width), F32)],
         compiler_params=pltpu.CompilerParams(vmem_limit_bytes=56 * 2**20),
-        cost_estimate=pl.CostEstimate(flops=12*10**9, bytes_accessed=8*10**6, transcendentals=0),
+        cost_estimate=about(6),
         name="feed_forward",
     )(hidden, weights, weights, weights)
 
@@ -421,56 +439,9 @@
         out_specs=[col, col, full],
         scratch_shapes=[pltpu.VMEM((rows, width), F32)],
         compiler_params=pltpu.CompilerParams(vmem_limit_bytes=56 * 2**20),
-        cost_estimate=pl.CostEstimate(flops=12*10**9, bytes_accessed=8*10**6, transcendentals=0),
+        cost_estimate=about(6),
         name="feed_forward_back",
     )(grad, weights, weights, weights, slope, act)
-
-
-def input_grad_kernel(dims, place, gq_ref, gkv_ref, w_ref, out_ref):
-    nf, nx, nc = dims
-    feat = w_ref.shape[2] // nx
-    grads = jnp.concatenate([gq_ref[0], gkv_ref[0]], axis=0).astype(F32).T.astype(BF)
-    weight = jnp.concatenate(
-        [
-            w_ref[0, f * nc + b, a * feat : (a + 1) * feat, :]
-            for f in range(nf)
-            for a in range(nx)
-            for b in range(nc)
-        ],
-        axis=0,
-    )
-    added = dot(grads, weight, 1, 1)
-
-    @pl.when(pl.program_id(0) == 0)
-    def _():
-        out_ref[...] = added
-
-    @pl.when(pl.program_id(0) > 0)
-    def _():
-        out_ref[...] += added
-
-
-def input_grad(gq, gkv, weights, place, dims):
-    nz, q_cols, share = gq.shape
-    nb, nr, cols = weights.shape[1:]
-    width = nb * nr
-    return pl.pallas_call(
-        functools.partial(input_grad_kernel, dims),
-        out_shape=jax.ShapeDtypeStruct((share, width), F32),
-        grid_spec=pltpu.PrefetchScalarGridSpec(
-            num_scalar_prefetch=1,
-            grid=(nz,),
-            in_specs=[
-                pl.BlockSpec((1, q_cols, share), lambda k, place: (k, 0, 0)),
-                pl.BlockSpec((1, gkv.shape[1], share), lambda k, place: (k, 0, 0)),
-                pl.BlockSpec((1, nb, nr, cols), lambda k, place: (place[k], 0, 0, 0)),
-            ],
-            out_specs=pl.BlockSpec((share, width), lambda k, place: (0, 0)),
-        ),
-        compiler_params=pltpu.CompilerParams(vmem_limit_bytes=56 * 2**20),
-        cost_estimate=pl.CostEstimate(flops=9*10**9, bytes_accessed=8*10**6, transcendentals=0),
-        name="input_grad",
-    )(place, gq, gkv, weights)
 
 
 def weight_grad_kernel(dims, pieces, count, where, *refs):
@@ -522,7 +493,7 @@
             scratch_shapes=[pltpu.VMEM((width, rows * pieces), BF)] * 2,
         ),
         compiler_params=pltpu.CompilerParams(vmem_limit_bytes=56 * 2**20),
-        cost_estimate=pl.CostEstimate(flops=10*10**9, bytes_accessed=8*10**6, transcendentals=0),
+        cost_estimate=about(5),
         name="weight_grad",
     )(where, *lefts, *[r for right in rights for r in right])
 
@@ -547,15 +518,16 @@
     qkv_cols = q_cols + 2 * kv_cols
     gains = jnp.pad(jnp.stack([gain_attn, gain_ffn]), ((0, 14), (0, qkv_cols - feat)))
     in_shard = jnp.concatenate([jnp.concatenate([w_query, w_key, w_value], axis=1), gains], axis=0)
-    rows_f = tokens[0].astype(F32)
-    scale_a, normed_a = norm_parts(rows_f)
-    out_shard = jnp.concatenate(everyone(w_out.T, "tp"), axis=1)
-    (w_qkv, gain_rows), early, x_parts = gather_rows(in_shard, None, (scale_a, out_shard), feat)
+    scale_a, normed_a = norm_parts(tokens[0].astype(F32))
+    out_parts = everyone(w_out.T, "tp")
+    out_shard = jnp.concatenate(out_parts, axis=1)
+    out_y = swap(out_shard, "fsdp") if nf == 2 else out_shard
+    (w_qkv, gain_rows), x_parts, came = gather_rows(in_shard, out_parts[1:] or None, (scale_a, out_y), feat)
     w_qkv = w_qkv.reshape(-1, qkv_cols)
     gain_rows = gain_rows[:, :2, :feat].astype(F32)
     gain_att, gain_mlp = (gain_rows[:, i].reshape(1, -1) for i in range(2))
 
-    ffn_stack = after(jnp.stack([w_gate, w_up, w_down.T]), early)
+    ffn_stack = after(jnp.stack([w_gate, w_up, w_down.T]), came[:2])
     hidden_part = lambda k: lax.dynamic_slice_in_dim(ffn_stack, (x ^ k) * hs, hs, 2)
     pieces = [hidden_part(0)] + [swap(hidden_part(k), "cx", k) for k in range(1, nx)]
     swapped = pieces[1:]
@@ -577,6 +549,8 @@
     kv_own = jnp.concatenate([k_rot.reshape(kv_cols, rows), kv_lin[kv_cols:]], axis=0).astype(BF)
     q_lin = dot(w_qkv[:, :q_cols], hidden_a, 0, 1)
     q_rot = turned(q_lin.reshape(-1, HD, rows), cos_table, sin_table).reshape(q_cols, rows).astype(BF)
+    (out_weights,), out_x, out_came = gather_rows(out_shard, from_y=out_y, hold_x=came)
+    out_weights = out_weights.reshape(width, -1)
     kv_parts = everyone(kv_own.reshape(2, kv_cols, rows), "cx")
 
     seg_own = after(segment_ids[0][None], kv_own)
@@ -586,10 +560,9 @@
     doc_start = jnp.sum((seg_all < segment_ids[0][:, None]).astype(jnp.int32), axis=1)[None]
     query_place = place * rows + jnp.arange(rows, dtype=jnp.int32)[None]
 
-    (out_weights,), out_near, out_parts = gather_rows(out_shard)
-    out_weights = out_weights.reshape(width, -1)
-    kv_parts[1:] = after(kv_parts[1:], q_rot, doc_start, out_parts) if nx > 1 else []
-    q_rot = after(q_rot, out_near)
+    q_rot = after(q_rot, out_weights)
+    if nx > 1:
+        kv_parts[1:] = after(kv_parts[1:], q_rot, doc_start)
     kv_near = jnp.stack(kv_parts)
     kv_sources = everyone(kv_near, "cc")
     kv_place = jnp.stack(
@@ -602,26 +575,21 @@
         make_bounds(doc_start, first_row, rows, FWD_TQ, FWD_TK), FWD_TQ, FWD_TK,
     )
 
-    qkv_shard = jnp.concatenate(ordered([p[:feat] for p in x_parts], x), axis=0)
-    qkv_weights = lax.all_gather(
-        after(qkv_shard, o_t), ("tp", "fsdp", "cc"), axis=0, tiled=True
-    ).reshape(nz, nf * nc, nx * feat, qkv_cols)
-
     chunk = lambda v, k: lax.dynamic_slice_in_dim(v, (z ^ k) * share, share, 1)
     att_t = jnp.concatenate(
         [chunk(o_t, 0)] + [swap(chunk(o_t, k), "tp", k) for k in range(1, nz)], axis=0
     )
-    resid = own_rows(rows_f) + dot(att_t, out_weights, 0, 1)
+    rows_own = own_rows(tokens[0]).astype(F32)
+    resid = rows_own + dot(att_t, out_weights, 0, 1)
     scale_f, normed_f = norm_parts(resid)
     hidden_own = (normed_f * gain_mlp).astype(BF)
     dims = (nf, nx, nc)
     hidden_parts = everyone(hidden_own, "cx")
-    slopes, acts, inners, outs = zip(
-        *(
-            ffn_forward(h, ffn_weights, dims, F32 if k == 0 else BF)
-            for k, h in enumerate(hidden_parts)
-        )
-    )
+    done = []
+    for k, h in enumerate(hidden_parts):
+        hidden_parts[k] = after(h, done[-1]) if k else h
+        done.append(ffn_forward(hidden_parts[k], ffn_weights, dims, BF if k else F32))
+    slopes, acts, inners, outs = zip(*done)
 
     def returned(parts, *others):
         total = parts[0]
@@ -636,10 +604,10 @@
     error = result - target
     grad_out = valid * error
     loss_part = jnp.sum(grad_out * error)
-    ffn_grads = everyone(grad_out.astype(BF), "cx")
+    grad_out_low, result_low = after((grad_out.astype(BF), result.astype(BF)), loss_part[None])
+    ffn_grads = everyone(grad_out_low, "cx")
     where = jnp.stack([y, c]).astype(jnp.int32)
-    part_down = weight_grad(ffn_grads, [inners], where, nz, dims)
-    mixed = lax.all_gather(result.astype(BF), "tp", axis=0, tiled=True)
+    mixed = lax.all_gather(result_low, "tp", axis=0, tiled=True)
 
     def to_rows(parts):
         others = [swap(parts[k], "cc", k) for k in range(1, nc)]
@@ -650,14 +618,15 @@
                 total = total + other[f].astype(F32)
             return total
 
-        return over_cores, [over_cores(k).astype(BF) for k in range(1, nf)]
-
-    def scattered(over_cores, sends, hold):
+        sends = [over_cores(k).astype(BF) for k in range(1, nf)]
+        return over_cores, sends, [swap(sends[k - 1], "fsdp", k) for k in range(1, nf)]
+
+    def scattered(over_cores, given, hold):
         total = over_cores(0)
         for k in range(1, nf):
-            total = total + after(swap(sends[k - 1], "fsdp", k), hold).astype(F32)
+            total = total + after(given[k - 1], hold).astype(F32)
         total = total.astype(BF)
-        return total, spread(total)
+        return (total,) + spread(total)
 
     def spread(total):
         done = lax.psum_scatter(
@@ -665,31 +634,38 @@
         ).reshape(nx, feat, hs)
         piece = lambda k: lax.dynamic_index_in_dim(done, x ^ k, 0, keepdims=False)
         pieces = [piece(0)] + [swap(piece(k), "cx", k) for k in range(1, nx)]
-        return jnp.concatenate(ordered(pieces, x), axis=1).astype(F32)
-
-    down_own, down_sends = to_rows(part_down)
-    grad_gates, grad_ups, ffn_backs = zip(
-        *(
-            ffn_backward(g, ffn_weights, slopes[k], acts[k], dims, F32 if k == 0 else BF)
-            for k, g in enumerate(ffn_grads)
-        )
-    )
+        return done, jnp.concatenate(ordered(pieces, x), axis=1).astype(F32)
+
+    done = []
+    for k, g in enumerate(ffn_grads):
+        ffn_grads[k] = after(g, done[-1]) if k else g
+        done.append(ffn_backward(ffn_grads[k], ffn_weights, slopes[k], acts[k], dims, BF if k else F32))
+    grad_gates, grad_ups, ffn_backs = zip(*done)
+    inners = (after(inners[0], ffn_backs[-1]),) + inners[1:]
+    part_down = weight_grad(ffn_grads, [inners], where, nz, dims)
+    grad_gates = (after(grad_gates[0], part_down),) + grad_gates[1:]
     part_gate_up = weight_grad(hidden_parts, [grad_gates, grad_ups], where, nz, dims)
-    grad_hidden_f = returned(ffn_backs, part_down)
+    down_own, down_sends, down_given = to_rows(part_down)
+    grad_hidden_f = returned(ffn_backs, down_sends, part_gate_up)
     part_gain_mlp = jnp.sum(grad_hidden_f * normed_f, axis=0)
     grad_mid = grad_out + norm_back(grad_hidden_f, normed_f, scale_f, gain_mlp)
-    grad_attn = grad_mid.astype(BF)
+    grad_attn = after(grad_mid.astype(BF), mixed)
     g_att = dot(out_weights, grad_attn, 0, 1).astype(BF).reshape(nz, q_cols, share)
     g_parts = [g_att[0]] + [swap(g_att[k], "tp", k) for k in range(1, nz)]
-    grad_heads = jnp.concatenate(ordered(after(g_parts, part_gate_up, down_sends), z), axis=1)
+    down_total, down_done, shard_down_t = scattered(down_own, down_given, g_parts[1:])
+    gate_own, gate_sends, gate_given = to_rows(part_gate_up[:nc])
+    up_own, up_sends, up_given = to_rows(part_gate_up[nc:])
+    grad_heads = jnp.concatenate(ordered(after(g_parts, down_total, gate_sends), z), axis=1)
 
     bounds = make_bounds(doc_start, first_row, rows, BWD_TQ, BWD_TK)
-    dqs, kv_grads = [], []
+    dqs, kv_sends, kv_grads = [], [], []
     for head in range(heads_k):
         dq, *dkv = attn_bwd(
             q_rot, kv_sources, kv_place, doc_start, query_place, bounds, grad_heads, o_f, lse,
             BWD_TQ, BWD_TK, head,
         )
+        if head == heads_k - 1 and head:
+            dkv[-1] = after(dkv[-1], gate_done)
         dkv_others = [swap(dkv[k], "cc", k) for k in range(1, nc)]
 
         def kv_over_cores(k):
@@ -699,40 +675,46 @@
             return total
 
         sends = [kv_over_cores(k).astype(BF) for k in range(1, nx)]
-        if head == 0:
-            down_total, shard_down_t = scattered(down_own, down_sends, dq)
-            gate_own, gate_sends = to_rows(part_gate_up[:nc])
-            up_own, up_sends = to_rows(part_gate_up[nc:])
-            if heads_k > 1:
-                grad_heads = after(grad_heads, sends, down_total, gate_sends, up_sends)
-        kv_grad = kv_over_cores(0)
-        for k in range(1, nx):
-            kv_grad = kv_grad + swap(sends[k - 1], "cx", k).astype(F32)
+        if head == 0 and heads_k > 1:
+            gate_total, gate_done, shard_gate = scattered(gate_own, gate_given, sends)
+            grad_heads = after(grad_heads, sends, gate_total, up_sends, down_done)
+        if head == heads_k - 1 and sends:
+            sends = after(sends, up_given)
         dqs.append(dq)
-        kv_grads.append(kv_grad)
+        kv_sends.append((kv_over_cores(0), [swap(sends[k - 1], "cx", k) for k in range(1, nx)]))
+    if heads_k == 1:
+        gate_total, gate_done, shard_gate = scattered(gate_own, gate_given, sends)
     gq = jnp.concatenate([turned(d.reshape(-1, HD, rows) * att_scale, cos_table, -sin_table) for d in dqs])
     gq = gq.reshape(q_cols, rows).astype(BF)
-    to_owners = lambda v: jnp.stack(
-        [chunk(v, 0)] + [swap(chunk(v, k), "tp", k) for k in range(1, nz)]
-    )
-    gq_all = to_owners(gq)
+    up_total, up_done, shard_up = scattered(up_own, up_given, sends)
+    for kv_grad, others in kv_sends:
+        for other in others:
+            kv_grad = kv_grad + after(other, up_total).astype(F32)
+        kv_grads.append(kv_grad)
     kv_grad = jnp.stack(kv_grads, axis=1)
     gk = turned(kv_grad[0] * att_scale, cos_table, -sin_table)
     gkv = jnp.concatenate([gk, kv_grad[1]], axis=0).reshape(2 * kv_cols, rows).astype(BF)
-    gkv_all = to_owners(gkv)
-    grad_hidden_a = input_grad(
-        gq_all, gkv_all, qkv_weights, jnp.stack([z ^ k for k in range(nz)]).astype(jnp.int32), dims
+    grad_qkv = jnp.concatenate([gq, gkv], axis=0)
+    part_h1 = dot(grad_qkv, w_qkv, 0, 1).astype(BF)
+    part_h1 = after(part_h1, up_done)
+    grad_hidden_a = lax.psum_scatter(part_h1, "tp", scatter_dimension=0, tiled=True)
+    part_out = dot(after(grad_attn, sends), att_t, 0, 1).astype(BF)
+    part_qkv = dot(after(hidden_a, part_h1), grad_qkv, 0, 1).astype(BF)
+    shard_out_t, out_y = scatter_rows(part_out)
+    shard_qkv, qkv_y = scatter_rows(part_qkv)
+    shard_out_t = summed(
+        shard_out_t.astype(BF).reshape(feat, nz, q_cols), 1, "tp", 0
     )
-    gate_total, shard_gate = scattered(gate_own, gate_sends, gkv)
-    up_total, shard_up = scattered(up_own, up_sends, gkv)
-    part_qkv = dot(hidden_a, jnp.concatenate([gq, gkv], axis=0), 0, 1).astype(BF)
-    part_out = dot(after(grad_attn, gkv), att_t, 0, 1).astype(BF)
-    normed_share = own_rows(normed_a)
+    grad_hidden_a = after(grad_hidden_a, out_y, qkv_y).astype(F32)
+    scale_share = own_rows(scale_a)
+    normed_share = rows_own * scale_share
     part_gain_att = jnp.sum(grad_hidden_a * normed_share, axis=0)
-    grad_share = grad_mid + norm_back(grad_hidden_a, normed_share, own_rows(scale_a), gain_att)
-    grad_tokens = lax.all_gather(grad_share.astype(BF), "tp", axis=0, tiled=True)
+    grad_share = grad_mid + norm_back(grad_hidden_a, normed_share, scale_share, gain_att)
+    grad_share = grad_share.astype(BF)
+    grad_tokens = lax.all_gather(grad_share, "tp", axis=0, tiled=True)
 
     small = jnp.stack([part_gain_att, part_gain_mlp, jnp.broadcast_to(loss_part, (width,))])
+    small = after(small, grad_share)
     for axis in AXES:
         step = 1
         while step < lax.axis_size(axis):
@@ -741,11 +723,6 @@
     small_own = lax.dynamic_slice_in_dim(small[:2], ((y * nx + x) * nc + c) * feat, feat, 1)
     loss = small[2, 0] / (valid_count.astype(F32) * width)
 
-    shard_qkv = scatter_rows(part_qkv)
-    shard_out_t = scatter_rows(part_out)
-    shard_out_t = summed(
-        shard_out_t.astype(BF).reshape(feat, nz, q_cols), 1, "tp", 0
-    )
     grad_tokens = after(
         grad_tokens, small_own, shard_qkv, shard_out_t, shard_gate, shard_up, shard_down_t
     ).astype(F32)

time: 664 us -> 619 us (0.932)
  starting transfers between devices: 141 us -> 105 us
  waiting for transfers between devices: 192 us -> 218 us
  other arithmetic: 107 us -> 85.7 us
  Pallas kernels: 126 us -> 108 us
    ppermute x61 -> x63, starting transfers between devices: 140 us -> 105 us  [swap(): return lax.ppermute(values, axis, [(i, i ^ step) for i in range(size)])]
    reduce_scatter x3, waiting for transfers between devices: 0.01 us -> 23 us  [spread(): lax.psum_scatter(total.reshape(nz * nx * feat, hs), 'tp', scatter_dimensi...]
    pallas_call x3 -> x2, Pallas kernels: 24.2 us -> 4.29 us  [put_blocks(): pl.pallas_call(functools.partial(place_kernel, plan, len(sources)), out_s...]
    unnamed x160 -> x197, local copies, waits for them, and re-layouts: 21.1 us -> 32 us
    dot_general x6 -> x7, matrix products: 23.3 us -> 25.9 us  [dot(): lax.dot_general(a, b, (((ca,), (cb,)), ((), ())), preferred_element_type=...]
    ppermute x61 -> x63, waiting for transfers between devices: 191 us -> 191 us  [swap(): return lax.ppermute(values, axis, [(i, i ^ step) for i in range(size)])]
  transfers between devices with their start and end apart: 68 -> 70, of which waited for: 32 -> 38; matrix products, arithmetic and copies ran while one was open for 24% -> 18% of each run, Pallas kernels for 19% -> 16%
where the time goes in v3:
time: 619 us; the launch traced here: 610 us
  waiting for transfers between devices  218 us (35%)
  Pallas kernels  108 us (17%)
  starting transfers between devices  105 us (17%)
  other arithmetic  85.7 us (14%)
  local copies, waits for them, and re-layouts  49.4 us (8%)
  matrix products  25.9 us (4%)
  between operations  18.1 us (3%)
    ppermute x63, waiting for transfers between devices, swap(): return lax.ppermute(values, axis, [(i, i ^ step) for i in range(size)])  191 us
    ppermute x63, starting transfers between devices, swap(): return lax.ppermute(values, axis, [(i, i ^ step) for i in range(size)])  105 us
    unnamed x197, local copies, waits for them, and re-layouts  32 us
    dot_general x7, matrix products, dot(): lax.dot_general(a, b, (((ca,), (cb,)), ((), ())), preferred_element_type=...  25.9 us
    pallas_call x2, Pallas kernels, ffn_forward(): pl.pallas_call(functools.partial(ffn_forward_kernel, dims), out_shape=(sh...  25 us
    pallas_call x2, Pallas kernels, ffn_backward(): pl.pallas_call(functools.partial(ffn_backward_kernel, dims), out_shape=(s...  24.9 us
    reduce_scatter x3, waiting for transfers between devices, spread(): lax.psum_scatter(total.reshape(nz * nx * feat, hs), 'tp', scatter_dimensi...  23 us
    pallas_call x2, Pallas kernels, weight_grad(): pl.pallas_call(functools.partial(weight_grad_kernel, dims, pieces, count)...  21 us
  transfers between devices with their start and end apart: 70, of which 38 were waited for; matrix products, arithmetic and copies ran while one was open for 18% of the time, Pallas kernels for 16%

profile of v3, /device:TPU:0, one launch (start us, length us, event | category | flops | bytes accessed | tf_op | source)
XLA Modules:
  0.0 610.5 jit_solution(15728187439854502109)
XLA Ops:
  9.7 3.0 collective-permute-start
  15.8 2.6 collective-permute-start.5
  23.6 5.9 collective-permute-done.5.refs_3_
  34.0 2.4 pad_maximum_fusion.2.refs_0_
  39.5 2.6 fusion.2
  44.5 2.7 put_blocks.2
  48.5 5.4 collective-permute-done.28.refs_0_
  60.7 2.8 fusion.4.refs_0_
  72.6 3.9 fusion.9
  83.0 4.7 collective-permute-done.16.refs_3_
  87.7 9.6 %collective-permute-done.17.refs_4_ = bf16[96,1536]{1,0:T(8,128)(2,1)S(1)} collective-permute-done((bf16[96,1536]{1,0:T(8,128)(2,1)S(1)}, bf16[96,1536]{1,0:T(8,128)(2,1)S(1)}, u32[]{:S(2)}, u32[]{:S(2)}) %collective-permute-start.17) | collective-permute-done | bytes 294944 | tf_op jit(solution)/shard_map/ppermute | solution.py:180
  97.3 2.5 convert_reduce_fusion
  108.8 12.0 %attend.1 = (bf16[384,1024]{1,0:T(8,128)(2,1)S(1)}, f32[384,1024]{1,0:T(8,128)S(1)}, f32[2,2,1024]{2,1,0:T(2,128)S(1)}) custom-call(s32[4,4]{1,0:T(4,128)S(1)} %pad_add_fusion.2.bounds, s32[4]{0:T(128)S(1)} %pad_add_fusion.4.place, bf16[384,1024]{1,0:T(8,128)(2,1)S(1)} %copy-done.1, bf16[2,2,192,1024]{3,2,1,0:T(8,128)(2,1)S(1)} %pad_maximum_fusion.refs_0_, ...), custom_call_target="tpu_custom_call" | custom-call | flops 12000000000 | bytes 1000000 | tf_op jit(solution)/shard_map/attend/pallas_call | solution.py:85
  127.1 7.5 %collective-permute-done.25 = bf16[384,256]{1,0:T(8,128)(2,1)S(1)} collective-permute-done((bf16[384,256]{1,0:T(8,128)(2,1)S(1)}, bf16[384,256]{1,0:T(8,128)(2,1)S(1)}, u32[]{:S(2)}, u32[]{:S(2)}) %collective-permute-start.25) | collective-permute-done | bytes 196640 | tf_op jit(solution)/shard_map/ppermute | solution.py:180
  134.5 4.7 collective-permute-done.26
  139.2 11.8 %collective-permute-done.27 = bf16[384,256]{1,0:T(8,128)(2,1)S(1)} collective-permute-done((bf16[384,256]{1,0:T(8,128)(2,1)S(1)}, bf16[384,256]{1,0:T(8,128)(2,1)S(1)}, u32[]{:S(2)}, u32[]{:S(2)}) %collective-permute-start.27) | collective-permute-done | bytes 196640 | tf_op jit(solution)/shard_map/ppermute | solution.py:180
  151.0 4.2 multiply_reduce_fusion.2
  155.4 15.8 %collective-permute-start.29 = (bf16[256,1536]{1,0:T(8,128)(2,1)S(1)}, bf16[256,1536]{1,0:T(8,128)(2,1)S(1)}, u32[]{:S(2)}, u32[]{:S(2)}) collective-permute-start(bf16[256,1536]{1,0:T(8,128)(2,1)S(1)} %multiply_convert_fusion.1.h_ref.refs_0_), channel_id=1, source_target_pairs={{0,8},{8,0},{1,9},{9,1},{2,10},{10,2},{3,11},{11,3},{4,12},{12,4},... | collective-permute-start | bytes 2359304 | tf_op jit(solution)/shard_map/ppermute | solution.py:180
  171.3 12.5 %feed_forward.2 = (f32[256,2048]{1,0:T(8,128)}, f32[256,2048]{1,0:T(8,128)}, bf16[256,2048]{1,0:T(8,128)(2,1)}, f32[256,1536]{1,0:T(8,128)}) custom-call(bf16[256,1536]{1,0:T(8,128)(2,1)} %copy-done.51, bf16[4,4,3,384,512]{4,3,2,1,0:T(8,128)(2,1)} %bitcast.245, bf16[4,4,3,384,512]{4,3,2,1,0:T(8,128)(2,1)} %bitcast.246, bf16[4,4,3,384,512]{4,3,2,1,0:T(8,128)(2,1)} %bitcast.247), custom_call_target="tpu_custom_call" | custom-call | flops 6000000000 | bytes 1000000 | tf_op jit(solution)/shard_map/feed_forward/pallas_call | solution.py:394
  184.7 12.5 %feed_forward.3 = (f32[256,2048]{1,0:T(8,128)}, f32[256,2048]{1,0:T(8,128)}, bf16[256,2048]{1,0:T(8,128)(2,1)}, bf16[256,1536]{1,0:T(8,128)(2,1)}) custom-call(bf16[256,1536]{1,0:T(8,128)(2,1)} %after.38.h_ref.refs_1_, bf16[4,4,3,384,512]{4,3,2,1,0:T(8,128)(2,1)} %bitcast.248, bf16[4,4,3,384,512]{4,3,2,1,0:T(8,128)(2,1)} %bitcast.249, ...), custom_call_target="tpu_custom_call" | custom-call | flops 6000000000 | bytes 1000000 | tf_op jit(solution)/shard_map/feed_forward/pallas_call | solution.py:394
  198.7 16.5 %collective-permute-done.30 = bf16[256,1536]{1,0:T(8,128)(2,1)S(1)} collective-permute-done((bf16[256,1536]{1,0:T(8,128)(2,1)}, bf16[256,1536]{1,0:T(8,128)(2,1)S(1)}, u32[]{:S(2)}, u32[]{:S(2)}) %collective-permute-start.30) | collective-permute-done | bytes 786464 | tf_op jit(solution)/shard_map/ppermute | solution.py:180
  221.0 12.8 %feed_forward_back.2 = (bf16[256,2048]{1,0:T(8,128)(2,1)}, bf16[256,2048]{1,0:T(8,128)(2,1)}, f32[256,1536]{1,0:T(8,128)}) custom-call(bf16[256,1536]{1,0:T(8,128)(2,1)} %get-tuple-element.62.g_ref.refs_0_, bf16[4,4,3,384,512]{4,3,2,1,0:T(8,128)(2,1)} %bitcast.251, bf16[4,4,3,384,512]{4,3,2,1,0:T(8,128)(2,1)} %bitcast.252, ...), custom_call_target="tpu_custom_call" | custom-call | flops 6000000000 | bytes 1000000 | tf_op jit(solution)/shard_map/feed_forward_back/pallas_call | solution.py:430
  233.8 2.5 collective-permute-done.31.refs_0_
  237.2 12.2 %feed_forward_back.3 = (bf16[256,2048]{1,0:T(8,128)(2,1)}, bf16[256,2048]{1,0:T(8,128)(2,1)}, bf16[256,1536]{1,0:T(8,128)(2,1)}) custom-call(bf16[256,1536]{1,0:T(8,128)(2,1)} %after.40.g_ref.refs_1_, bf16[4,4,3,384,512]{4,3,2,1,0:T(8,128)(2,1)} %bitcast.254, bf16[4,4,3,384,512]{4,3,2,1,0:T(8,128)(2,1)} %bitcast.255, bf16[4,4,3,384,512]{4,3,2,1,0:T(8,128)(2,1)} %bitcast.256, ...), custom_call_target="tpu_custom_call" | custom-call | flops 6000000000 | bytes 1000000 | tf_op jit(solution)/shard_map/feed_forward_back/pallas_call | solution.py:430
  249.4 8.7 %weight_grad.2 = (bf16[2,4,384,512]{3,2,1,0:T(8,128)(2,1)}, bf16[2,4,384,512]{3,2,1,0:T(8,128)(2,1)}) custom-call(s32[2]{0:T(128)} %pad_add_fusion.5.where, bf16[256,1536]{1,0:T(8,128)(2,1)} %get-tuple-element.62.g_ref.refs_0_, bf16[256,1536]{1,0:T(8,128)(2,1)} %after.40.g_ref.refs_1_, bf16[256,2048]{1,0:T(8,128)(2,1)} %after.41.refs_2_, ...), custom_call_target="tpu_custom_call" | custom-call | flops 5000000000 | bytes 1000000 | tf_op jit(solution)/shard_map/weight_grad/pallas_call | solution.py:484
  260.0 12.3 %weight_grad.3 = (bf16[2,4,384,512]{3,2,1,0:T(8,128)(2,1)}, bf16[2,4,384,512]{3,2,1,0:T(8,128)(2,1)}, bf16[2,4,384,512]{3,2,1,0:T(8,128)(2,1)}, bf16[2,4,384,512]{3,2,1,0:T(8,128)(2,1)}) custom-call(s32[2]{0:T(128)} %pad_add_fusion.5.where, bf16[256,1536]{1,0:T(8,128)(2,1)} %copy-done.51, bf16[256,1536]{1,0:T(8,128)(2,1)} %after.38.h_ref.refs_1_, ...), custom_call_target="tpu_custom_call" | custom-call | flops 5000000000 | bytes 1000000 | tf_op jit(solution)/shard_map/weight_grad/pallas_call | solution.py:484
  272.4 3.5 fusion.28.refs_1_
  275.9 11.8 %collective-permute-start.37 = (bf16[4,384,512]{2,1,0:T(8,128)(2,1)}, bf16[4,384,512]{2,1,0:T(8,128)(2,1)}, u32[]{:S(2)}, u32[]{:S(2)}) collective-permute-start(bf16[4,384,512]{2,1,0:T(8,128)(2,1)} %fusion.28.refs_1_), channel_id=1, source_target_pairs={{0,16},{16,0},{1,17},{17,1},{2,18},{18,2},{3,19},{19,3},{4,20},{20... | collective-permute-start | bytes 4718600 | tf_op jit(solution)/shard_map/ppermute | solution.py:180
  291.9 3.2 fusion.81
  295.0 4.0 convolution_convert_fusion.3
  304.9 4.9 collective-permute-done.34.refs_1_
  309.7 7.2 %collective-permute-done.35.refs_2_ = bf16[384,256]{1,0:T(8,128)(2,1)S(1)} collective-permute-done((bf16[384,256]{1,0:T(8,128)(2,1)S(1)}, bf16[384,256]{1,0:T(8,128)(2,1)S(1)}, u32[]{:S(2)}, u32[]{:S(2)}) %collective-permute-start.35) | collective-permute-done | bytes 196640 | tf_op jit(solution)/shard_map/ppermute | solution.py:180
  316.9 6.0 collective-permute-done.37.refs_0_
  322.9 3.7 fusion.13.refs_4_
  333.3 10.4 %attend_back.2 = (f32[192,1024]{1,0:T(8,128)}, bf16[2,2,96,1024]{3,2,1,0:T(8,128)(2,1)}, bf16[2,2,96,1024]{3,2,1,0:T(8,128)(2,1)}) custom-call(s32[4,4]{1,0:T(4,128)} %pad_add_fusion.3.bounds, s32[4]{0:T(128)} %copy-done.20, bf16[384,1024]{1,0:T(8,128)(2,1)} %after.34.refs_1_.q_ref, bf16[2,2,192,1024]{3,2,1,0:T(8,128)(2,1)} %copy-done.11, ...), custom_call_target="tpu_custom_call" | custom-call | flops 12000000000 | bytes 1000000 | tf_op jit(solution)/shard_map/attend_back/pallas_call | solution.py:152
  343.7 5.6 collective-permute-start.39
  354.1 11.1 %collective-permute-done.40.refs_0_ = bf16[4,384,512]{2,1,0:T(8,128)(2,1)S(1)} collective-permute-done((bf16[4,384,512]{2,1,0:T(8,128)(2,1)S(1)}, bf16[4,384,512]{2,1,0:T(8,128)(2,1)S(1)}, u32[]{:S(2)}, u32[]{:S(2)}) %collective-permute-start.40) | collective-permute-done | bytes 1572896 | tf_op jit(solution)/shard_map/ppermute | solution.py:180
  366.4 4.3 fusion.12.refs_2_
  370.8 3.0 fusion.30.refs_3_
  375.3 10.2 %attend_back.3 = (f32[192,1024]{1,0:T(8,128)}, bf16[2,2,96,1024]{3,2,1,0:T(8,128)(2,1)}, bf16[2,2,96,1024]{3,2,1,0:T(8,128)(2,1)}) custom-call(s32[4,4]{1,0:T(4,128)} %pad_add_fusion.3.bounds, s32[4]{0:T(128)} %copy-done.20, bf16[384,1024]{1,0:T(8,128)(2,1)} %after.34.refs_1_.q_ref, bf16[2,2,192,1024]{3,2,1,0:T(8,128)(2,1)} %copy-done.11, ...), custom_call_target="tpu_custom_call" | custom-call | flops 12000000000 | bytes 1000000 | tf_op jit(solution)/shard_map/attend_back/pallas_call | solution.py:152
  385.5 18.8 %reduce-scatter.7.cloned.1.call-done = bf16[384,512]{1,0:T(8,128)(2,1)} async-done(((bf16[1536,512]{1,0:T(8,128)(2,1)}), bf16[384,512]{1,0:T(8,128)(2,1)}) %reduce-scatter.7.cloned.1.call-update) | async-done | bytes 393232 | tf_op jit(solution)/shard_map/reduce_scatter | solution.py:632
  404.3 2.5 collective-permute-done.44
  412.2 3.7 fusion.11.refs_1_
  420.5 8.5 %collective-permute-done.42.refs_0_ = bf16[2,96,1024]{2,1,0:T(8,128)(2,1)S(1)} collective-permute-done((bf16[2,96,1024]{2,1,0:T(8,128)(2,1)S(1)}, bf16[2,96,1024]{2,1,0:T(8,128)(2,1)S(1)}, u32[]{:S(2)}, u32[]{:S(2)}) %collective-permute-start.42) | collective-permute-done | bytes 393248 | tf_op jit(solution)/shard_map/ppermute | solution.py:180
  431.1 4.0 collective-permute-done.45.refs_0_
  441.0 4.1 convolution_convert_fusion.1.refs_0_
  445.1 4.1 reduce-scatter.9.cloned.1.call-done
  450.5 2.6 convolution_convert_fusion
  455.2 5.7 convolution_convert_fusion.2
  469.3 24.9 %collective-permute-done.47 = bf16[2,192,1536]{2,1,0:T(8,128)(2,1)} collective-permute-done((bf16[2,192,1536]{2,1,0:T(8,128)(2,1)}, bf16[2,192,1536]{2,1,0:T(8,128)(2,1)}, u32[]{:S(2)}, u32[]{:S(2)}) %collective-permute-start.47) | collective-permute-done | bytes 1179680 | tf_op jit(solution)/shard_map/ppermute | solution.py:180
  494.2 2.6 fusion.17.refs_1_
  496.7 9.2 %collective-permute-done.49 = bf16[2,192,768]{2,1,0:T(8,128)(2,1)} collective-permute-done((bf16[2,192,768]{2,1,0:T(8,128)(2,1)S(1)}, bf16[2,192,768]{2,1,0:T(8,128)(2,1)}, u32[]{:S(2)}, u32[]{:S(2)}) %collective-permute-start.49) | collective-permute-done | bytes 589856 | tf_op jit(solution)/shard_map/ppermute | solution.py:180
  507.9 3.3 reduce-scatter.11.cloned.1.call-done.refs_0_
  511.2 2.5 fusion.26
  513.7 2.8 fusion.24.refs_1_
  519.5 3.6 collective-permute-done.62
  528.3 4.1 collective-permute-done.60
  533.4 3.2 collective-permute-done.61
  536.7 10.3 %collective-permute-done.56 = bf16[192,1536]{1,0:T(8,128)(2,1)S(1)} collective-permute-done((bf16[192,1536]{1,0:T(8,128)(2,1)S(1)}, bf16[192,1536]{1,0:T(8,128)(2,1)S(1)}, u32[]{:S(2)}, u32[]{:S(2)}) %collective-permute-start.56) | collective-permute-done | bytes 589856 | tf_op jit(solution)/shard_map/ppermute | solution.py:180
  564.6 6.0 collective-permute-done.58
  573.0 10.6 %collective-permute-start.53 = (f32[3,1536]{1,0:T(4,128)S(1)}, f32[3,1536]{1,0:T(4,128)S(1)}, u32[]{:S(2)}, u32[]{:S(2)}) collective-permute-start(f32[3,1536]{1,0:T(4,128)S(1)} %add.552), channel_id=1, source_target_pairs={{0,1},{1,0},{2,3},{3,2},{4,5},{5,4},{6,7},{7,6},{8,9},{9,8},{10,11... | collective-permute-start | bytes 55304 | tf_op jit(solution)/shard_map/ppermute | solution.py:180
  583.7 2.4 collective-permute-done.53
  586.0 3.8 collective-permute-start.54
  595.0 5.6 bitcast_convert_fusion
  (454 shorter events, 160.9 us)
Async XLA Ops:
  7.2 164.1 %all-gather.4.cloned.1.call-start = ((), (), s32[]{:S(2)}) async-start(), calls=%async_computation.4 | async-start | bytes 20054016 | tf_op jit(solution)/shard_map/all_gather | solution.py:536
  9.7 10.5 %collective-permute-start = (bf16[208,768]{1,0:T(8,128)(2,1)S(1)}, bf16[208,768]{1,0:T(8,128)(2,1)S(1)}, u32[]{:S(2)}, u32[]{:S(2)}) collective-permute-start(bf16[208,768]{1,0:T(8,128)(2,1)S(1)} %pad_maximum_fusion.14.refs_0_), channel_id=1, source_target_pairs={{0,8},{8,0},{1,9},{9,1},{2,10},{10,2},{3,11},{11,3},{4,12},{12,4},... | collective-permute-start | bytes 958472 | tf_op jit(solution)/shard_map/ppermute | solution.py:180
  12.7 9.4 %collective-permute-start.1 = (bf16[208,768]{1,0:T(8,128)(2,1)S(1)}, bf16[208,768]{1,0:T(8,128)(2,1)S(1)}, u32[]{:S(2)}, u32[]{:S(2)}) collective-permute-start(bf16[208,768]{1,0:T(8,128)(2,1)S(1)} %pad_maximum_fusion.14.refs_0_), channel_id=1, source_target_pairs={{0,16},{16,0},{1,17},{17,1},{2,18},{18,2},{3,19},{19,3},{4,20},{20... | collective-permute-start | bytes 958472 | tf_op jit(solution)/shard_map/ppermute | solution.py:180
  14.2 9.4 %collective-permute-start.4 = (bf16[192,384]{1,0:T(8,128)(2,1)}, bf16[192,384]{1,0:T(8,128)(2,1)S(1)}, u32[]{:S(2)}, u32[]{:S(2)}) collective-permute-start(bf16[192,384]{1,0:T(8,128)(2,1)} %bitcast.295), channel_id=1, source_target_pairs={{0,1},{1,0},{2,3},{3,2},{4,5},{5,4},{6,7},{7,6},{8,9},{9,8},{10,11... | collective-permute-start | bytes 442376 | tf_op jit(solution)/shard_map/ppermute | solution.py:180
  15.8 13.8 %collective-permute-start.5 = (bf16[192,384]{1,0:T(8,128)(2,1)}, bf16[192,384]{1,0:T(8,128)(2,1)S(1)}, u32[]{:S(2)}, u32[]{:S(2)}) collective-permute-start(bf16[192,384]{1,0:T(8,128)(2,1)} %bitcast.296), channel_id=1, source_target_pairs={{0,2},{1,3},{2,0},{3,1},{4,6},{5,7},{6,4},{7,5},{8,10},{9,11},{10,... | collective-permute-start | bytes 442376 | tf_op jit(solution)/shard_map/ppermute | solution.py:180
  18.4 11.2 %collective-permute-start.6 = (bf16[192,384]{1,0:T(8,128)(2,1)}, bf16[192,384]{1,0:T(8,128)(2,1)S(1)}, u32[]{:S(2)}, u32[]{:S(2)}) collective-permute-start(bf16[192,384]{1,0:T(8,128)(2,1)} %bitcast.297), channel_id=1, source_target_pairs={{0,3},{1,2},{2,1},{3,0},{4,7},{5,6},{6,5},{7,4},{8,11},{9,10},{10,... | collective-permute-start | bytes 442376 | tf_op jit(solution)/shard_map/ppermute | solution.py:180
  20.2 11.8 %collective-permute-start.3 = (bf16[112,768]{1,0:T(8,128)(2,1)S(1)}, bf16[112,768]{1,0:T(8,128)(2,1)S(1)}, u32[]{:S(2)}, u32[]{:S(2)}) collective-permute-start(bf16[112,768]{1,0:T(8,128)(2,1)S(1)} %slice.236), channel_id=1, source_target_pairs={{0,16},{16,0},{1,17},{17,1},{2,18},{18,2},{3,19},{19,3},{4,20},{20... | collective-permute-start | bytes 516104 | tf_op jit(solution)/shard_map/ppermute | solution.py:180
  22.1 10.0 %collective-permute-start.2 = (bf16[96,768]{1,0:T(8,128)(2,1)S(1)}, bf16[96,768]{1,0:T(8,128)(2,1)S(1)}, u32[]{:S(2)}, u32[]{:S(2)}) collective-permute-start(bf16[96,768]{1,0:T(8,128)(2,1)S(1)} %slice.235), channel_id=1, source_target_pairs={{0,8},{8,0},{1,9},{9,1},{2,10},{10,2},{3,11},{11,3},{4,12},{12,4},... | collective-permute-start | bytes 442376 | tf_op jit(solution)/shard_map/ppermute | solution.py:180
  30.7 11.5 %collective-permute-start.12 = (bf16[192,1536]{1,0:T(8,128)(2,1)S(1)}, bf16[192,1536]{1,0:T(8,128)(2,1)S(1)}, u32[]{:S(2)}, u32[]{:S(2)}) collective-permute-start(bf16[192,1536]{1,0:T(8,128)(2,1)S(1)} %pad_maximum_fusion.13.refs_0_), channel_id=1, source_target_pairs={{0,16},{16,0},{1,17},{17,1},{2,18},{18,2},{3,19},{19,3},{4,20},{20... | collective-permute-start | bytes 1769480 | tf_op jit(solution)/shard_map/ppermute | solution.py:180
  31.2 12.1 %collective-permute-start.7 = (bf16[208,768]{1,0:T(8,128)(2,1)S(1)}, bf16[208,768]{1,0:T(8,128)(2,1)S(1)}, u32[]{:S(2)}, u32[]{:S(2)}) collective-permute-start(bf16[208,768]{1,0:T(8,128)(2,1)S(1)} %pad_maximum_fusion.14.refs_0_), channel_id=1, source_target_pairs={{0,4},{4,0},{1,5},{5,1},{2,6},{6,2},{3,7},{7,3},{8,12},{12,8},{9,1... | collective-permute-start | bytes 958472 | tf_op jit(solution)/shard_map/ppermute | solution.py:180
  33.4 5.5 collective-permute-start.11
  38.3 15.6 %collective-permute-start.28 = (bf16[3,192,512]{2,1,0:T(8,128)(2,1)}, bf16[3,192,512]{2,1,0:T(8,128)(2,1)}, u32[]{:S(2)}, u32[]{:S(2)}) collective-permute-start(bf16[3,192,512]{2,1,0:T(8,128)(2,1)} %constant_dynamic-slice_fusion.2), channel_id=1, source_target_pairs={{0,8},{8,0},{1,9},{9,1},{2,10},{10,2},{3,11},{11,3},{4,12},{12,4},... | collective-permute-start | bytes 1769480 | tf_op jit(solution)/shard_map/ppermute | solution.py:180
  38.9 4.5 collective-permute-start.8
  38.9 4.5 collective-permute-start.9
  57.8 237.3 %all-gather.6.cloned.1.call-start = ((), (), s32[]{:S(2)}) async-start(), calls=%async_computation.5 | async-start | bytes 3932160 | tf_op jit(solution)/shard_map/all_gather | solution.py:610
  60.0 21.4 %collective-permute-start.18 = (bf16[192,1536]{1,0:T(8,128)(2,1)S(1)}, bf16[192,1536]{1,0:T(8,128)(2,1)S(1)}, u32[]{:S(2)}, u32[]{:S(2)}) collective-permute-start(bf16[192,1536]{1,0:T(8,128)(2,1)S(1)} %pad_maximum_fusion.13.refs_0_), channel_id=1, source_target_pairs={{0,4},{4,0},{1,5},{5,1},{2,6},{6,2},{3,7},{7,3},{8,12},{12,8},{9,1... | collective-permute-start | bytes 1769480 | tf_op jit(solution)/shard_map/ppermute | solution.py:180
  60.0 20.9 %collective-permute-start.15 = (bf16[192,1536]{1,0:T(8,128)(2,1)}, bf16[192,1536]{1,0:T(8,128)(2,1)S(1)}, u32[]{:S(2)}, u32[]{:S(2)}) collective-permute-start(bf16[192,1536]{1,0:T(8,128)(2,1)} %after.33), channel_id=1, source_target_pairs={{0,8},{8,0},{1,9},{9,1},{2,10},{10,2},{3,11},{11,3},{4,12},{12,4},... | collective-permute-start | bytes 1769480 | tf_op jit(solution)/shard_map/ppermute | solution.py:180
  71.0 8.8 %collective-permute-start.13 = (s32[1,1024]{1,0:T(1,128)}, s32[1,1024]{1,0:T(1,128)S(1)}, u32[]{:S(2)}, u32[]{:S(2)}) collective-permute-start(s32[1,1024]{1,0:T(1,128)} %after.32), channel_id=1, source_target_pairs={{0,8},{8,0},{1,9},{9,1},{2,10},{10,2},{3,11},{11,3},{4,12},{12,4},... | collective-permute-start | bytes 12296 | tf_op jit(solution)/shard_map/ppermute | solution.py:180
  77.7 10.0 %collective-permute-start.16 = (bf16[96,1536]{1,0:T(8,128)(2,1)S(1)}, bf16[96,1536]{1,0:T(8,128)(2,1)S(1)}, u32[]{:S(2)}, u32[]{:S(2)}) collective-permute-start(bf16[96,1536]{1,0:T(8,128)(2,1)S(1)} %slice.248), channel_id=1, source_target_pairs={{0,8},{8,0},{1,9},{9,1},{2,10},{10,2},{3,11},{11,3},{4,12},{12,4},... | collective-permute-start | bytes 884744 | tf_op jit(solution)/shard_map/ppermute | solution.py:180
  78.0 25.7 %collective-permute-start.23 = (bf16[2,192,1024]{2,1,0:T(8,128)(2,1)S(1)}, bf16[2,192,1024]{2,1,0:T(8,128)(2,1)}, u32[]{:S(2)}, u32[]{:S(2)}) collective-permute-start(bf16[2,192,1024]{2,1,0:T(8,128)(2,1)S(1)} %bitcast.265), channel_id=1, source_target_pairs={{0,8},{8,0},{1,9},{9,1},{2,10},{10,2},{3,11},{11,3},{4,12},{12,4},... | collective-permute-start | bytes 2359304 | tf_op jit(solution)/shard_map/ppermute | solution.py:180
  80.8 18.9 %collective-permute-start.20 = (bf16[192,1536]{1,0:T(8,128)(2,1)S(1)}, bf16[192,1536]{1,0:T(8,128)(2,1)S(1)}, u32[]{:S(2)}, u32[]{:S(2)}) collective-permute-start(bf16[192,1536]{1,0:T(8,128)(2,1)S(1)} %copy-done.6), channel_id=1, source_target_pairs={{0,4},{4,0},{1,5},{5,1},{2,6},{6,2},{3,7},{7,3},{8,12},{12,8},{9,1... | collective-permute-start | bytes 1769480 | tf_op jit(solution)/shard_map/ppermute | solution.py:180
  81.4 15.9 %collective-permute-start.17 = (bf16[96,1536]{1,0:T(8,128)(2,1)S(1)}, bf16[96,1536]{1,0:T(8,128)(2,1)S(1)}, u32[]{:S(2)}, u32[]{:S(2)}) collective-permute-start(bf16[96,1536]{1,0:T(8,128)(2,1)S(1)} %slice.249), channel_id=1, source_target_pairs={{0,16},{16,0},{1,17},{17,1},{2,18},{18,2},{3,19},{19,3},{4,20},{20... | collective-permute-start | bytes 884744 | tf_op jit(solution)/shard_map/ppermute | solution.py:180
  82.9 16.9 %collective-permute-start.19 = (bf16[192,1536]{1,0:T(8,128)(2,1)S(1)}, bf16[192,1536]{1,0:T(8,128)(2,1)S(1)}, u32[]{:S(2)}, u32[]{:S(2)}) collective-permute-start(bf16[192,1536]{1,0:T(8,128)(2,1)S(1)} %collective-permute-done.15.refs_1_), channel_id=1, source_target_pairs={{0,4},{4,0},{1,5},{5,1},{2,6},{6,2},{3,7},{7,3},{8,12},{12,8},{9,1... | collective-permute-start | bytes 1769480 | tf_op jit(solution)/shard_map/ppermute | solution.py:180
  87.7 12.1 %collective-permute-start.21 = (bf16[96,1536]{1,0:T(8,128)(2,1)S(1)}, bf16[96,1536]{1,0:T(8,128)(2,1)S(1)}, u32[]{:S(2)}, u32[]{:S(2)}) collective-permute-start(bf16[96,1536]{1,0:T(8,128)(2,1)S(1)} %collective-permute-done.16.refs_3_), channel_id=1, source_target_pairs={{0,4},{4,0},{1,5},{5,1},{2,6},{6,2},{3,7},{7,3},{8,12},{12,8},{9,1... | collective-permute-start | bytes 884744 | tf_op jit(solution)/shard_map/ppermute | solution.py:180
  122.6 11.9 %collective-permute-start.25 = (bf16[384,256]{1,0:T(8,128)(2,1)S(1)}, bf16[384,256]{1,0:T(8,128)(2,1)S(1)}, u32[]{:S(2)}, u32[]{:S(2)}) collective-permute-start(bf16[384,256]{1,0:T(8,128)(2,1)S(1)} %get-tuple-element.131), channel_id=1, source_target_pairs={{0,1},{1,0},{2,3},{3,2},{4,5},{5,4},{6,7},{7,6},{8,9},{9,8},{10,11... | collective-permute-start | bytes 589832 | tf_op jit(solution)/shard_map/ppermute | solution.py:180
  124.2 15.0 %collective-permute-start.26 = (bf16[384,256]{1,0:T(8,128)(2,1)S(1)}, bf16[384,256]{1,0:T(8,128)(2,1)S(1)}, u32[]{:S(2)}, u32[]{:S(2)}) collective-permute-start(bf16[384,256]{1,0:T(8,128)(2,1)S(1)} %get-tuple-element.130), channel_id=1, source_target_pairs={{0,2},{1,3},{2,0},{3,1},{4,6},{5,7},{6,4},{7,5},{8,10},{9,11},{10,... | collective-permute-start | bytes 589832 | tf_op jit(solution)/shard_map/ppermute | solution.py:180
  125.4 25.6 %collective-permute-start.27 = (bf16[384,256]{1,0:T(8,128)(2,1)S(1)}, bf16[384,256]{1,0:T(8,128)(2,1)S(1)}, u32[]{:S(2)}, u32[]{:S(2)}) collective-permute-start(bf16[384,256]{1,0:T(8,128)(2,1)S(1)} %get-tuple-element.129), channel_id=1, source_target_pairs={{0,3},{1,2},{2,1},{3,0},{4,7},{5,6},{6,5},{7,4},{8,11},{9,10},{10,... | collective-permute-start | bytes 589832 | tf_op jit(solution)/shard_map/ppermute | solution.py:180
  155.4 28.3 %collective-permute-start.29 = (bf16[256,1536]{1,0:T(8,128)(2,1)S(1)}, bf16[256,1536]{1,0:T(8,128)(2,1)S(1)}, u32[]{:S(2)}, u32[]{:S(2)}) collective-permute-start(bf16[256,1536]{1,0:T(8,128)(2,1)S(1)} %multiply_convert_fusion.1.h_ref.refs_0_), channel_id=1, source_target_pairs={{0,8},{8,0},{1,9},{9,1},{2,10},{10,2},{3,11},{11,3},{4,12},{12,4},... | collective-permute-start | bytes 2359304 | tf_op jit(solution)/shard_map/ppermute | solution.py:180
  197.1 18.0 %collective-permute-start.30 = (bf16[256,1536]{1,0:T(8,128)(2,1)}, bf16[256,1536]{1,0:T(8,128)(2,1)S(1)}, u32[]{:S(2)}, u32[]{:S(2)}) collective-permute-start(bf16[256,1536]{1,0:T(8,128)(2,1)} %get-tuple-element.60), channel_id=1, source_target_pairs={{0,8},{8,0},{1,9},{9,1},{2,10},{10,2},{3,11},{11,3},{4,12},{12,4},... | collective-permute-start | bytes 2359304 | tf_op jit(solution)/shard_map/ppermute | solution.py:180
  218.9 17.5 %collective-permute-start.31 = (bf16[256,1536]{1,0:T(8,128)(2,1)}, bf16[256,1536]{1,0:T(8,128)(2,1)S(1)}, u32[]{:S(2)}, u32[]{:S(2)}) collective-permute-start(bf16[256,1536]{1,0:T(8,128)(2,1)} %get-tuple-element.62.g_ref.refs_0_), channel_id=1, source_target_pairs={{0,8},{8,0},{1,9},{9,1},{2,10},{10,2},{3,11},{11,3},{4,12},{12,4},... | collective-permute-start | bytes 2359304 | tf_op jit(solution)/shard_map/ppermute | solution.py:180
  221.0 154.3 %reduce-scatter.5.cloned.1.call-start = ((), (), s32[]{:S(2)}) async-start(), calls=%async_computation.6 | async-start | bytes 1966080 | tf_op jit(solution)/shard_map/reduce_scatter | solution.py:632
  258.2 14.2 %collective-permute-start.33 = (bf16[2,4,384,512]{3,2,1,0:T(8,128)(2,1)}, bf16[2,4,384,512]{3,2,1,0:T(8,128)(2,1)}, u32[]{:S(2)}, u32[]{:S(2)}) collective-permute-start(bf16[2,4,384,512]{3,2,1,0:T(8,128)(2,1)} %get-tuple-element.71.refs_2_), channel_id=1, source_target_pairs={{0,4},{4,0},{1,5},{5,1},{2,6},{6,2},{3,7},{7,3},{8,12},{12,8},{9,1... | collective-permute-start | bytes 9437192 | tf_op jit(solution)/shard_map/ppermute | solution.py:180
  258.2 29.5 %collective-permute-start.32 = (bf16[256,1536]{1,0:T(8,128)(2,1)S(1)}, bf16[256,1536]{1,0:T(8,128)(2,1)S(1)}, u32[]{:S(2)}, u32[]{:S(2)}) collective-permute-start(bf16[256,1536]{1,0:T(8,128)(2,1)S(1)} %copy-done.68), channel_id=1, source_target_pairs={{0,8},{8,0},{1,9},{9,1},{2,10},{10,2},{3,11},{11,3},{4,12},{12,4},... | collective-permute-start | bytes 2359304 | tf_op jit(solution)/shard_map/ppermute | solution.py:180
  272.3 54.4 %collective-permute-start.38 = (bf16[2,4,384,512]{3,2,1,0:T(8,128)(2,1)}, bf16[2,4,384,512]{3,2,1,0:T(8,128)(2,1)}, u32[]{:S(2)}, u32[]{:S(2)}) collective-permute-start(bf16[2,4,384,512]{3,2,1,0:T(8,128)(2,1)} %get-tuple-element.75.refs_3_), channel_id=1, source_target_pairs={{0,4},{4,0},{1,5},{5,1},{2,6},{6,2},{3,7},{7,3},{8,12},{12,8},{9,1... | collective-permute-start | bytes 9437192 | tf_op jit(solution)/shard_map/ppermute | solution.py:180
  275.9 47.0 %collective-permute-start.37 = (bf16[4,384,512]{2,1,0:T(8,128)(2,1)}, bf16[4,384,512]{2,1,0:T(8,128)(2,1)}, u32[]{:S(2)}, u32[]{:S(2)}) collective-permute-start(bf16[4,384,512]{2,1,0:T(8,128)(2,1)} %fusion.28.refs_1_), channel_id=1, source_target_pairs={{0,16},{16,0},{1,17},{17,1},{2,18},{18,2},{3,19},{19,3},{4,20},{20... | collective-permute-start | bytes 4718600 | tf_op jit(solution)/shard_map/ppermute | solution.py:180
  299.8 10.0 %collective-permute-start.34 = (bf16[384,256]{1,0:T(8,128)(2,1)S(1)}, bf16[384,256]{1,0:T(8,128)(2,1)S(1)}, u32[]{:S(2)}, u32[]{:S(2)}) collective-permute-start(bf16[384,256]{1,0:T(8,128)(2,1)S(1)} %get-tuple-element.126), channel_id=1, source_target_pairs={{0,1},{1,0},{2,3},{3,2},{4,5},{5,4},{6,7},{7,6},{8,9},{9,8},{10,11... | collective-permute-start | bytes 589832 | tf_op jit(solution)/shard_map/ppermute | solution.py:180
  299.8 17.1 %collective-permute-start.35 = (bf16[384,256]{1,0:T(8,128)(2,1)S(1)}, bf16[384,256]{1,0:T(8,128)(2,1)S(1)}, u32[]{:S(2)}, u32[]{:S(2)}) collective-permute-start(bf16[384,256]{1,0:T(8,128)(2,1)S(1)} %get-tuple-element.125), channel_id=1, source_target_pairs={{0,2},{1,3},{2,0},{3,1},{4,6},{5,7},{6,4},{7,5},{8,10},{9,11},{10,... | collective-permute-start | bytes 589832 | tf_op jit(solution)/shard_map/ppermute | solution.py:180
  301.8 15.1 %collective-permute-start.36 = (bf16[384,256]{1,0:T(8,128)(2,1)S(1)}, bf16[384,256]{1,0:T(8,128)(2,1)}, u32[]{:S(2)}, u32[]{:S(2)}) collective-permute-start(bf16[384,256]{1,0:T(8,128)(2,1)S(1)} %get-tuple-element.124), channel_id=1, source_target_pairs={{0,3},{1,2},{2,1},{3,0},{4,7},{5,6},{6,5},{7,4},{8,11},{9,10},{10,... | collective-permute-start | bytes 589832 | tf_op jit(solution)/shard_map/ppermute | solution.py:180
  309.7 61.0 %collective-permute-start.41 = (bf16[2,4,384,512]{3,2,1,0:T(8,128)(2,1)}, bf16[2,4,384,512]{3,2,1,0:T(8,128)(2,1)}, u32[]{:S(2)}, u32[]{:S(2)}) collective-permute-start(bf16[2,4,384,512]{3,2,1,0:T(8,128)(2,1)} %get-tuple-element.77.refs_5_), channel_id=1, source_target_pairs={{0,4},{4,0},{1,5},{5,1},{2,6},{6,2},{3,7},{7,3},{8,12},{12,8},{9,1... | collective-permute-start | bytes 9437192 | tf_op jit(solution)/shard_map/ppermute | solution.py:180
  326.6 77.7 %reduce-scatter.7.cloned.1.call-start = ((), (), s32[]{:S(2)}) async-start(), calls=%async_computation.7 | async-start | bytes 1966080 | tf_op jit(solution)/shard_map/reduce_scatter | solution.py:632
  329.1 36.2 %collective-permute-start.40 = (bf16[4,384,512]{2,1,0:T(8,128)(2,1)S(1)}, bf16[4,384,512]{2,1,0:T(8,128)(2,1)S(1)}, u32[]{:S(2)}, u32[]{:S(2)}) collective-permute-start(bf16[4,384,512]{2,1,0:T(8,128)(2,1)S(1)} %fusion.29.refs_5_), channel_id=1, source_target_pairs={{0,16},{16,0},{1,17},{17,1},{2,18},{18,2},{3,19},{19,3},{4,20},{20... | collective-permute-start | bytes 4718600 | tf_op jit(solution)/shard_map/ppermute | solution.py:180
  343.7 7.7 %collective-permute-start.39 = (bf16[2,2,96,1024]{3,2,1,0:T(8,128)(2,1)}, bf16[2,2,96,1024]{3,2,1,0:T(8,128)(2,1)S(1)}, u32[]{:S(2)}, u32[]{:S(2)}) collective-permute-start(bf16[2,2,96,1024]{3,2,1,0:T(8,128)(2,1)} %get-tuple-element.86), channel_id=1, source_target_pairs={{0,4},{4,0},{1,5},{5,1},{2,6},{6,2},{3,7},{7,3},{8,12},{12,8},{9,1... | collective-permute-start | bytes 2359304 | tf_op jit(solution)/shard_map/ppermute | solution.py:180
  370.7 78.5 %reduce-scatter.9.cloned.1.call-start = ((), (), s32[]{:S(2)}) async-start(), calls=%async_computation.8 | async-start | bytes 1966080 | tf_op jit(solution)/shard_map/reduce_scatter | solution.py:632
  373.8 35.4 %collective-permute-start.43 = (bf16[4,384,512]{2,1,0:T(8,128)(2,1)}, bf16[4,384,512]{2,1,0:T(8,128)(2,1)S(1)}, u32[]{:S(2)}, u32[]{:S(2)}) collective-permute-start(bf16[4,384,512]{2,1,0:T(8,128)(2,1)} %fusion.30.refs_3_), channel_id=1, source_target_pairs={{0,16},{16,0},{1,17},{17,1},{2,18},{18,2},{3,19},{19,3},{4,20},{20... | collective-permute-start | bytes 4718600 | tf_op jit(solution)/shard_map/ppermute | solution.py:180
  415.9 95.3 %reduce-scatter.11.cloned.1.call-start = ((), (), s32[]{:S(2)}) async-start(), calls=%async_computation.9 | async-start | bytes 3932160 | tf_op jit(solution)/shard_map/reduce_scatter | solution.py:700
  416.9 12.1 %collective-permute-start.42 = (bf16[2,96,1024]{2,1,0:T(8,128)(2,1)S(1)}, bf16[2,96,1024]{2,1,0:T(8,128)(2,1)S(1)}, u32[]{:S(2)}, u32[]{:S(2)}) collective-permute-start(bf16[2,96,1024]{2,1,0:T(8,128)(2,1)S(1)} %copy-done.48), channel_id=1, source_target_pairs={{0,8},{8,0},{1,9},{9,1},{2,10},{10,2},{3,11},{11,3},{4,12},{12,4},... | collective-permute-start | bytes 1179656 | tf_op jit(solution)/shard_map/ppermute | solution.py:180
  417.3 17.9 %collective-permute-start.45 = (bf16[2,96,1024]{2,1,0:T(8,128)(2,1)S(1)}, bf16[2,96,1024]{2,1,0:T(8,128)(2,1)S(1)}, u32[]{:S(2)}, u32[]{:S(2)}) collective-permute-start(bf16[2,96,1024]{2,1,0:T(8,128)(2,1)S(1)} %copy-done.42), channel_id=1, source_target_pairs={{0,8},{8,0},{1,9},{9,1},{2,10},{10,2},{3,11},{11,3},{4,12},{12,4},... | collective-permute-start | bytes 1179656 | tf_op jit(solution)/shard_map/ppermute | solution.py:180
  449.3 145.7 %all-gather.8.cloned.1.call-start = ((), (), s32[]{:S(2)}) async-start(), calls=%async_computation.10 | async-start | bytes 3932160 | tf_op jit(solution)/shard_map/all_gather | solution.py:714
  455.2 6.4 %collective-permute-start.46 = (bf16[2,2,192,1536]{3,2,1,0:T(8,128)(2,1)S(1)}, bf16[2,2,192,1536]{3,2,1,0:T(8,128)(2,1)}, u32[]{:S(2)}, u32[]{:S(2)}) collective-permute-start(bf16[2,2,192,1536]{3,2,1,0:T(8,128)(2,1)S(1)} %dynamic-slice_bitcast_fusion), channel_id=1, source_target_pairs={{0,4},{4,0},{1,5},{5,1},{2,6},{6,2},{3,7},{7,3},{8,12},{12,8},{9,1... | collective-permute-start | bytes 7077896 | tf_op jit(solution)/shard_map/ppermute | solution.py:180
  461.1 5.4 collective-permute-start.48
  465.0 29.1 %collective-permute-start.47 = (bf16[2,192,1536]{2,1,0:T(8,128)(2,1)}, bf16[2,192,1536]{2,1,0:T(8,128)(2,1)}, u32[]{:S(2)}, u32[]{:S(2)}) collective-permute-start(bf16[2,192,1536]{2,1,0:T(8,128)(2,1)} %dynamic-slice_bitcast_fusion.2), channel_id=1, source_target_pairs={{0,16},{16,0},{1,17},{17,1},{2,18},{18,2},{3,19},{19,3},{4,20},{20... | collective-permute-start | bytes 3538952 | tf_op jit(solution)/shard_map/ppermute | solution.py:180
  467.9 38.0 %collective-permute-start.49 = (bf16[2,192,768]{2,1,0:T(8,128)(2,1)S(1)}, bf16[2,192,768]{2,1,0:T(8,128)(2,1)}, u32[]{:S(2)}, u32[]{:S(2)}) collective-permute-start(bf16[2,192,768]{2,1,0:T(8,128)(2,1)S(1)} %dynamic-slice_bitcast_fusion.4), channel_id=1, source_target_pairs={{0,16},{16,0},{1,17},{17,1},{2,18},{18,2},{3,19},{19,3},{4,20},{20... | collective-permute-start | bytes 1769480 | tf_op jit(solution)/shard_map/ppermute | solution.py:180
  516.6 6.5 %collective-permute-start.62 = (bf16[192,512]{1,0:T(8,128)(2,1)S(1)}, bf16[192,512]{1,0:T(8,128)(2,1)S(1)}, u32[]{:S(2)}, u32[]{:S(2)}) collective-permute-start(bf16[192,512]{1,0:T(8,128)(2,1)S(1)} %dynamic-slice_bitcast_fusion.6), channel_id=1, source_target_pairs={{0,8},{8,0},{1,9},{9,1},{2,10},{10,2},{3,11},{11,3},{4,12},{12,4},... | collective-permute-start | bytes 589832 | tf_op jit(solution)/shard_map/ppermute | solution.py:180
  524.5 7.9 %collective-permute-start.60 = (bf16[192,512]{1,0:T(8,128)(2,1)S(1)}, bf16[192,512]{1,0:T(8,128)(2,1)S(1)}, u32[]{:S(2)}, u32[]{:S(2)}) collective-permute-start(bf16[192,512]{1,0:T(8,128)(2,1)S(1)} %dynamic-slice_bitcast_fusion.8), channel_id=1, source_target_pairs={{0,8},{8,0},{1,9},{9,1},{2,10},{10,2},{3,11},{11,3},{4,12},{12,4},... | collective-permute-start | bytes 589832 | tf_op jit(solution)/shard_map/ppermute | solution.py:180
  526.1 10.5 %collective-permute-start.61 = (bf16[192,512]{1,0:T(8,128)(2,1)S(1)}, bf16[192,512]{1,0:T(8,128)(2,1)S(1)}, u32[]{:S(2)}, u32[]{:S(2)}) collective-permute-start(bf16[192,512]{1,0:T(8,128)(2,1)S(1)} %dynamic-slice_bitcast_fusion.7), channel_id=1, source_target_pairs={{0,8},{8,0},{1,9},{9,1},{2,10},{10,2},{3,11},{11,3},{4,12},{12,4},... | collective-permute-start | bytes 589832 | tf_op jit(solution)/shard_map/ppermute | solution.py:180
  526.8 20.3 %collective-permute-start.56 = (bf16[192,1536]{1,0:T(8,128)(2,1)S(1)}, bf16[192,1536]{1,0:T(8,128)(2,1)S(1)}, u32[]{:S(2)}, u32[]{:S(2)}) collective-permute-start(bf16[192,1536]{1,0:T(8,128)(2,1)S(1)} %dynamic-slice_bitcast_fusion.3), channel_id=1, source_target_pairs={{0,8},{8,0},{1,9},{9,1},{2,10},{10,2},{3,11},{11,3},{4,12},{12,4},... | collective-permute-start | bytes 1769480 | tf_op jit(solution)/shard_map/ppermute | solution.py:180
  548.2 16.3 %collective-permute-start.57 = (bf16[192,384]{1,0:T(8,128)(2,1)S(1)}, bf16[192,384]{1,0:T(8,128)(2,1)S(1)}, u32[]{:S(2)}, u32[]{:S(2)}) collective-permute-start(bf16[192,384]{1,0:T(8,128)(2,1)S(1)} %bitcast.299), channel_id=1, source_target_pairs={{0,1},{1,0},{2,3},{3,2},{4,5},{5,4},{6,7},{7,6},{8,9},{9,8},{10,11... | collective-permute-start | bytes 442376 | tf_op jit(solution)/shard_map/ppermute | solution.py:180
  549.8 20.8 %collective-permute-start.58 = (bf16[192,384]{1,0:T(8,128)(2,1)S(1)}, bf16[192,384]{1,0:T(8,128)(2,1)S(1)}, u32[]{:S(2)}, u32[]{:S(2)}) collective-permute-start(bf16[192,384]{1,0:T(8,128)(2,1)S(1)} %bitcast.300), channel_id=1, source_target_pairs={{0,2},{1,3},{2,0},{3,1},{4,6},{5,7},{6,4},{7,5},{8,10},{9,11},{10,... | collective-permute-start | bytes 442376 | tf_op jit(solution)/shard_map/ppermute | solution.py:180
  551.9 20.3 %collective-permute-start.59 = (bf16[192,384]{1,0:T(8,128)(2,1)S(1)}, bf16[192,384]{1,0:T(8,128)(2,1)S(1)}, u32[]{:S(2)}, u32[]{:S(2)}) collective-permute-start(bf16[192,384]{1,0:T(8,128)(2,1)S(1)} %bitcast.301), channel_id=1, source_target_pairs={{0,3},{1,2},{2,1},{3,0},{4,7},{5,6},{6,5},{7,4},{8,11},{9,10},{10,... | collective-permute-start | bytes 442376 | tf_op jit(solution)/shard_map/ppermute | solution.py:180
  553.6 4.0 collective-permute-start.50
  555.1 28.5 %collective-permute-start.55 = (bf16[192,768]{1,0:T(8,128)(2,1)S(1)}, bf16[192,768]{1,0:T(8,128)(2,1)S(1)}, u32[]{:S(2)}, u32[]{:S(2)}) collective-permute-start(bf16[192,768]{1,0:T(8,128)(2,1)S(1)} %dynamic-slice_bitcast_fusion.5), channel_id=1, source_target_pairs={{0,8},{8,0},{1,9},{9,1},{2,10},{10,2},{3,11},{11,3},{4,12},{12,4},... | collective-permute-start | bytes 884744 | tf_op jit(solution)/shard_map/ppermute | solution.py:180
  562.2 10.8 %collective-permute-start.52 = (f32[3,1536]{1,0:T(4,128)S(1)}, f32[3,1536]{1,0:T(4,128)S(1)}, u32[]{:S(2)}, u32[]{:S(2)}) collective-permute-start(f32[3,1536]{1,0:T(4,128)S(1)} %add.551), channel_id=1, source_target_pairs={{0,4},{4,0},{1,5},{5,1},{2,6},{6,2},{3,7},{7,3},{8,12},{12,8},{9,1... | collective-permute-start | bytes 55304 | tf_op jit(solution)/shard_map/ppermute | solution.py:180
  573.0 13.0 %collective-permute-start.53 = (f32[3,1536]{1,0:T(4,128)S(1)}, f32[3,1536]{1,0:T(4,128)S(1)}, u32[]{:S(2)}, u32[]{:S(2)}) collective-permute-start(f32[3,1536]{1,0:T(4,128)S(1)} %add.552), channel_id=1, source_target_pairs={{0,1},{1,0},{2,3},{3,2},{4,5},{5,4},{6,7},{7,6},{8,9},{9,8},{10,11... | collective-permute-start | bytes 55304 | tf_op jit(solution)/shard_map/ppermute | solution.py:180
  586.0 6.4 %collective-permute-start.54 = (f32[3,1536]{1,0:T(4,128)S(1)}, f32[3,1536]{1,0:T(4,128)S(1)}, u32[]{:S(2)}, u32[]{:S(2)}) collective-permute-start(f32[3,1536]{1,0:T(4,128)S(1)} %add.553), channel_id=1, source_target_pairs={{0,2},{1,3},{2,0},{3,1},{4,6},{5,7},{6,4},{7,5},{8,10},{9,11},{10,... | collective-permute-start | bytes 55304 | tf_op jit(solution)/shard_map/ppermute | solution.py:180
  (101 other events, 625.7 us)
Sparse Core Ops, SparseCore 0:
  57.9 111.3 all-gather.3
  221.1 69.8 all-gather.5
  326.8 33.6 reduce-scatter.4
  370.8 33.4 reduce-scatter.6
  416.0 33.1 reduce-scatter.8
  451.9 59.2 reduce-scatter.10
  516.7 76.8 all-gather.7

commit v4 on v3

--- a/solution.py
+++ b/solution.py
@@ -456,23 +456,19 @@
         for p, left in enumerate(lefts):
             plain[:, p * tokens : (p + 1) * tokens] = left[...].astype(F32).T.astype(BF)
         n = 0
-        for dc in range(nc):
-            for dy in range(nf):
-                for a in range(nx):
-                    row = ((where[0] ^ dy) * nx + a) * nc + (where[1] ^ dc)
-                    flipped[n * feat : (n + 1) * feat, :] = plain[
-                        pl.ds(pl.multiple_of(row * feat, feat), feat), :
-                    ]
-                    n += 1
-
-    part = flipped.shape[0] // (nc * nf)
+        for dy in range(nf):
+            for a in range(nx):
+                row = ((where[0] ^ dy) * nx + a) * nc + where[1]
+                flipped[n * feat : (n + 1) * feat, :] = plain[
+                    pl.ds(pl.multiple_of(row * feat, feat), feat), :
+                ]
+                n += 1
+
     for i in range(count):
         right = jnp.concatenate([rights[i * pieces + p][...] for p in range(pieces)], axis=0)
         done = dot(flipped[...], right, 1, 0).astype(BF)
-        for b in range(nc):
-            for f in range(nf):
-                n = b * nf + f
-                outs[i * nc + b][f, 0] = done[n * part : (n + 1) * part]
+        for f in range(nf):
+            outs[i * nf + f][0] = done[f * nx * feat : (f + 1) * nx * feat]
 
 
 def weight_grad(lefts, rights, where, nz, dims):
@@ -480,17 +476,20 @@
     nf, nx, nc = dims
     hs = rights[0][0].shape[1] // nz
     count, pieces = len(rights), len(lefts)
-    shape = (nf, nz, width // (nf * nc), hs)
+    shape = (nz, width // (nf * nc), hs)
     return pl.pallas_call(
         functools.partial(weight_grad_kernel, dims, pieces, count),
-        out_shape=(jax.ShapeDtypeStruct(shape, BF),) * (count * nc),
+        out_shape=(jax.ShapeDtypeStruct(shape, BF),) * (count * nf),
         grid_spec=pltpu.PrefetchScalarGridSpec(
             num_scalar_prefetch=1,
             grid=(nz,),
             in_specs=[pl.BlockSpec((rows, width), lambda z, w: (0, 0))] * pieces
             + [pl.BlockSpec((rows, hs), lambda z, w: (0, z))] * (count * pieces),
-            out_specs=[pl.BlockSpec((nf, 1) + shape[2:], lambda z, w: (0, z, 0, 0))] * (count * nc),
-            scratch_shapes=[pltpu.VMEM((width, rows * pieces), BF)] * 2,
+            out_specs=[pl.BlockSpec((1,) + shape[1:], lambda z, w: (z, 0, 0))] * (count * nf),
+            scratch_shapes=[
+                pltpu.VMEM((width, rows * pieces), BF),
+                pltpu.VMEM((width // nc, rows * pieces), BF),
+            ],
         ),
         compiler_params=pltpu.CompilerParams(vmem_limit_bytes=56 * 2**20),
         cost_estimate=about(5),
@@ -609,20 +608,14 @@
     where = jnp.stack([y, c]).astype(jnp.int32)
     mixed = lax.all_gather(result_low, "tp", axis=0, tiled=True)
 
+    def both_cores(parts):
+        return [v for part in parts for v in everyone(part, "cc")]
+
     def to_rows(parts):
-        others = [swap(parts[k], "cc", k) for k in range(1, nc)]
-
-        def over_cores(f):
-            total = parts[0][f].astype(F32)
-            for other in others:
-                total = total + other[f].astype(F32)
-            return total
-
-        sends = [over_cores(k).astype(BF) for k in range(1, nf)]
-        return over_cores, sends, [swap(sends[k - 1], "fsdp", k) for k in range(1, nf)]
-
-    def scattered(over_cores, given, hold):
-        total = over_cores(0)
+        return parts[0], parts[1:], [swap(parts[k], "fsdp", k) for k in range(1, nf)]
+
+    def scattered(own, given, hold):
+        total = own.astype(F32)
         for k in range(1, nf):
             total = total + after(given[k - 1], hold).astype(F32)
         total = total.astype(BF)
@@ -641,10 +634,12 @@
         ffn_grads[k] = after(g, done[-1]) if k else g
         done.append(ffn_backward(ffn_grads[k], ffn_weights, slopes[k], acts[k], dims, BF if k else F32))
     grad_gates, grad_ups, ffn_backs = zip(*done)
-    inners = (after(inners[0], ffn_backs[-1]),) + inners[1:]
-    part_down = weight_grad(ffn_grads, [inners], where, nz, dims)
-    grad_gates = (after(grad_gates[0], part_down),) + grad_gates[1:]
-    part_gate_up = weight_grad(hidden_parts, [grad_gates, grad_ups], where, nz, dims)
+    inners = both_cores(inners)
+    inners[0] = after(inners[0], ffn_backs[-1])
+    part_down = weight_grad(both_cores(ffn_grads), [inners], where, nz, dims)
+    grad_gates, grad_ups = both_cores(grad_gates), both_cores(grad_ups)
+    grad_gates[0] = after(grad_gates[0], part_down)
+    part_gate_up = weight_grad(both_cores(hidden_parts), [grad_gates, grad_ups], where, nz, dims)
     down_own, down_sends, down_given = to_rows(part_down)
     grad_hidden_f = returned(ffn_backs, down_sends, part_gate_up)
     part_gain_mlp = jnp.sum(grad_hidden_f * normed_f, axis=0)
@@ -653,8 +648,8 @@
     g_att = dot(out_weights, grad_attn, 0, 1).astype(BF).reshape(nz, q_cols, share)
     g_parts = [g_att[0]] + [swap(g_att[k], "tp", k) for k in range(1, nz)]
     down_total, down_done, shard_down_t = scattered(down_own, down_given, g_parts[1:])
-    gate_own, gate_sends, gate_given = to_rows(part_gate_up[:nc])
-    up_own, up_sends, up_given = to_rows(part_gate_up[nc:])
+    gate_own, gate_sends, gate_given = to_rows(part_gate_up[:nf])
+    up_own, up_sends, up_given = to_rows(part_gate_up[nf:])
     grad_heads = jnp.concatenate(ordered(after(g_parts, down_total, gate_sends), z), axis=1)
 
     bounds = make_bounds(doc_start, first_row, rows, BWD_TQ, BWD_TK)
@@ -665,7 +660,7 @@
             BWD_TQ, BWD_TK, head,
         )
         if head == heads_k - 1 and head:
-            dkv[-1] = after(dkv[-1], gate_done)
+            dkv[-1] = after(dkv[-1], gate_done, [o for _, o in kv_sends])
         dkv_others = [swap(dkv[k], "cc", k) for k in range(1, nc)]
 
         def kv_over_cores(k):
@@ -678,15 +673,13 @@
         if head == 0 and heads_k > 1:
             gate_total, gate_done, shard_gate = scattered(gate_own, gate_given, sends)
             grad_heads = after(grad_heads, sends, gate_total, up_sends, down_done)
-        if head == heads_k - 1 and sends:
-            sends = after(sends, up_given)
         dqs.append(dq)
         kv_sends.append((kv_over_cores(0), [swap(sends[k - 1], "cx", k) for k in range(1, nx)]))
     if heads_k == 1:
         gate_total, gate_done, shard_gate = scattered(gate_own, gate_given, sends)
     gq = jnp.concatenate([turned(d.reshape(-1, HD, rows) * att_scale, cos_table, -sin_table) for d in dqs])
     gq = gq.reshape(q_cols, rows).astype(BF)
-    up_total, up_done, shard_up = scattered(up_own, up_given, sends)
+    up_total, up_done, shard_up = scattered(up_own, up_given, [kv_sends[0][1], dq])
     for kv_grad, others in kv_sends:
         for other in others:
             kv_grad = kv_grad + after(other, up_total).astype(F32)

time: 619 us -> 609 us (0.984)
  starting transfers between devices: 105 us -> 81.9 us
  waiting for transfers between devices: 218 us -> 234 us
  other arithmetic: 85.7 us -> 76.9 us
    ppermute x63 -> x70, waiting for transfers between devices: 191 us -> 220 us  [swap(): return lax.ppermute(values, axis, [(i, i ^ step) for i in range(size)])]
    ppermute x63 -> x70, starting transfers between devices: 105 us -> 81.4 us  [swap(): return lax.ppermute(values, axis, [(i, i ^ step) for i in range(size)])]
    reduce_scatter x3, waiting for transfers between devices: 23 us -> 13.6 us  [spread(): lax.psum_scatter(total.reshape(nz * nx * feat, hs), 'tp', scatter_dimensi...]
    convert_element_type x3 -> x0, other arithmetic: 8.84 us -> none  [to_rows(): sends = [over_cores(k).astype(BF) for k in range(1, nf)]]
  transfers between devices with their start and end apart: 70 -> 77, of which waited for: 38 -> 32; matrix products, arithmetic and copies ran while one was open for 18% -> 17% of each run, Pallas kernels for 16% -> 16%
where the time goes in v4:
time: 609 us; the launch traced here: 601 us
  waiting for transfers between devices  234 us (38%)
  Pallas kernels  110 us (18%)
  starting transfers between devices  81.9 us (13%)
  other arithmetic  76.9 us (13%)
  local copies, waits for them, and re-layouts  54.7 us (9%)
  matrix products  25.4 us (4%)
  between operations  18.2 us (3%)
    ppermute x70, waiting for transfers between devices, swap(): return lax.ppermute(values, axis, [(i, i ^ step) for i in range(size)])  220 us
    ppermute x70, starting transfers between devices, swap(): return lax.ppermute(values, axis, [(i, i ^ step) for i in range(size)])  81.4 us
    unnamed x197, local copies, waits for them, and re-layouts  36 us
    pallas_call x2, Pallas kernels, ffn_backward(): pl.pallas_call(functools.partial(ffn_backward_kernel, dims), out_shape=(s...  26.5 us
    dot_general x7, matrix products, dot(): lax.dot_general(a, b, (((ca,), (cb,)), ((), ())), preferred_element_type=...  25.4 us
    pallas_call x2, Pallas kernels, ffn_forward(): pl.pallas_call(functools.partial(ffn_forward_kernel, dims), out_shape=(sh...  24.9 us
    pallas_call x2, Pallas kernels, weight_grad(): pl.pallas_call(functools.partial(weight_grad_kernel, dims, pieces, count)...  22 us
    pallas_call x2, Pallas kernels, attn_bwd(): pl.pallas_call(functools.partial(bwd_kernel, scale2, tq, tk, group, len(k...  19.3 us
  transfers between devices with their start and end apart: 77, of which 32 were waited for; matrix products, arithmetic and copies ran while one was open for 17% of the time, Pallas kernels for 16%

profile of v4, /device:TPU:0, one launch (start us, length us, event | category | flops | bytes accessed | tf_op | source)
XLA Modules:
  0.0 600.8 jit_solution(3461781895718852269)
XLA Ops:
  9.7 3.0 collective-permute-start
  15.8 2.6 collective-permute-start.5
  23.6 5.9 collective-permute-done.5.refs_3_
  34.0 2.4 pad_maximum_fusion.2.refs_0_
  36.4 2.0 constant_dynamic-slice_fusion.2
  39.5 2.6 fusion.2
  44.5 2.7 put_blocks.2
  48.5 5.4 collective-permute-done.28.refs_0_
  60.6 2.8 fusion.4.refs_0_
  72.6 3.9 fusion.9
  83.0 4.7 collective-permute-done.16.refs_3_
  87.6 9.6 %collective-permute-done.17.refs_4_ = bf16[96,1536]{1,0:T(8,128)(2,1)S(1)} collective-permute-done((bf16[96,1536]{1,0:T(8,128)(2,1)S(1)}, bf16[96,1536]{1,0:T(8,128)(2,1)S(1)}, u32[]{:S(2)}, u32[]{:S(2)}) %collective-permute-start.17) | collective-permute-done | bytes 294944 | tf_op jit(solution)/shard_map/ppermute | solution.py:180
  97.3 2.5 convert_reduce_fusion
  101.5 2.2 copy-done
  106.4 2.4 collective-permute-done.24.refs_1_
  108.8 12.0 %attend.1 = (bf16[384,1024]{1,0:T(8,128)(2,1)S(1)}, f32[384,1024]{1,0:T(8,128)S(1)}, f32[2,2,1024]{2,1,0:T(2,128)S(1)}) custom-call(s32[4,4]{1,0:T(4,128)S(1)} %pad_add_fusion.2.bounds, s32[4]{0:T(128)S(1)} %pad_add_fusion.4.place, bf16[384,1024]{1,0:T(8,128)(2,1)S(1)} %copy-done.1, bf16[2,2,192,1024]{3,2,1,0:T(8,128)(2,1)S(1)} %pad_maximum_fusion.refs_0_, ...), custom_call_target="tpu_custom_call" | custom-call | flops 12000000000 | bytes 1000000 | tf_op jit(solution)/shard_map/attend/pallas_call | solution.py:85
  127.0 7.4 %collective-permute-done.25 = bf16[384,256]{1,0:T(8,128)(2,1)S(1)} collective-permute-done((bf16[384,256]{1,0:T(8,128)(2,1)S(1)}, bf16[384,256]{1,0:T(8,128)(2,1)S(1)}, u32[]{:S(2)}, u32[]{:S(2)}) %collective-permute-start.25) | collective-permute-done | bytes 196640 | tf_op jit(solution)/shard_map/ppermute | solution.py:180
  134.4 4.9 collective-permute-done.26
  139.2 11.8 %collective-permute-done.27 = bf16[384,256]{1,0:T(8,128)(2,1)S(1)} collective-permute-done((bf16[384,256]{1,0:T(8,128)(2,1)S(1)}, bf16[384,256]{1,0:T(8,128)(2,1)S(1)}, u32[]{:S(2)}, u32[]{:S(2)}) %collective-permute-start.27) | collective-permute-done | bytes 196640 | tf_op jit(solution)/shard_map/ppermute | solution.py:180
  151.0 4.2 multiply_reduce_fusion.2
  156.3 18.9 %collective-permute-start.29 = (bf16[256,1536]{1,0:T(8,128)(2,1)}, bf16[256,1536]{1,0:T(8,128)(2,1)}, u32[]{:S(2)}, u32[]{:S(2)}) collective-permute-start(bf16[256,1536]{1,0:T(8,128)(2,1)} %multiply_convert_fusion.1.h_ref.refs_0_), channel_id=1, source_target_pairs={{0,8},{8,0},{1,9},{9,1},{2,10},{10,2},{3,11},{11,3},{4,12},{12,4},... | collective-permute-start | bytes 2359304 | tf_op jit(solution)/shard_map/ppermute | solution.py:180
  175.2 12.5 %feed_forward.2 = (f32[256,2048]{1,0:T(8,128)}, f32[256,2048]{1,0:T(8,128)}, bf16[256,2048]{1,0:T(8,128)(2,1)}, f32[256,1536]{1,0:T(8,128)}) custom-call(bf16[256,1536]{1,0:T(8,128)(2,1)} %multiply_convert_fusion.1.h_ref.refs_0_, bf16[4,4,3,384,512]{4,3,2,1,0:T(8,128)(2,1)} %bitcast.227, bf16[4,4,3,384,512]{4,3,2,1,0:T(8,128)(2,1)} %bitcast.228, ...), custom_call_target="tpu_custom_call" | custom-call | flops 6000000000 | bytes 1000000 | tf_op jit(solution)/shard_map/feed_forward/pallas_call | solution.py:394
  187.7 6.1 %collective-permute-done.29.refs_0_ = bf16[256,1536]{1,0:T(8,128)(2,1)} collective-permute-done((bf16[256,1536]{1,0:T(8,128)(2,1)}, bf16[256,1536]{1,0:T(8,128)(2,1)}, u32[]{:S(2)}, u32[]{:S(2)}) %collective-permute-start.29) | collective-permute-done | bytes 786464 | tf_op jit(solution)/shard_map/ppermute | solution.py:180
  193.8 12.4 %feed_forward.3 = (f32[256,2048]{1,0:T(8,128)}, f32[256,2048]{1,0:T(8,128)}, bf16[256,2048]{1,0:T(8,128)(2,1)}, bf16[256,1536]{1,0:T(8,128)(2,1)}) custom-call(bf16[256,1536]{1,0:T(8,128)(2,1)} %after.37.h_ref.refs_2_, bf16[4,4,3,384,512]{4,3,2,1,0:T(8,128)(2,1)} %bitcast.230, bf16[4,4,3,384,512]{4,3,2,1,0:T(8,128)(2,1)} %bitcast.231, ...), custom_call_target="tpu_custom_call" | custom-call | flops 6000000000 | bytes 1000000 | tf_op jit(solution)/shard_map/feed_forward/pallas_call | solution.py:394
  208.7 17.3 %collective-permute-done.30 = bf16[256,1536]{1,0:T(8,128)(2,1)S(1)} collective-permute-done((bf16[256,1536]{1,0:T(8,128)(2,1)}, bf16[256,1536]{1,0:T(8,128)(2,1)S(1)}, u32[]{:S(2)}, u32[]{:S(2)}) %collective-permute-start.30) | collective-permute-done | bytes 786464 | tf_op jit(solution)/shard_map/ppermute | solution.py:180
  231.9 14.3 %feed_forward_back.2 = (bf16[256,2048]{1,0:T(8,128)(2,1)}, bf16[256,2048]{1,0:T(8,128)(2,1)}, f32[256,1536]{1,0:T(8,128)}) custom-call(bf16[256,1536]{1,0:T(8,128)(2,1)} %get-tuple-element.62.g_ref.refs_0_, bf16[4,4,3,384,512]{4,3,2,1,0:T(8,128)(2,1)} %bitcast.233, bf16[4,4,3,384,512]{4,3,2,1,0:T(8,128)(2,1)} %bitcast.234, ...), custom_call_target="tpu_custom_call" | custom-call | flops 6000000000 | bytes 1000000 | tf_op jit(solution)/shard_map/feed_forward_back/pallas_call | solution.py:430
  249.5 12.2 %feed_forward_back.3 = (bf16[256,2048]{1,0:T(8,128)(2,1)}, bf16[256,2048]{1,0:T(8,128)(2,1)}, bf16[256,1536]{1,0:T(8,128)(2,1)}) custom-call(bf16[256,1536]{1,0:T(8,128)(2,1)} %after.39.g_ref.refs_2_, bf16[4,4,3,384,512]{4,3,2,1,0:T(8,128)(2,1)} %bitcast.236, bf16[4,4,3,384,512]{4,3,2,1,0:T(8,128)(2,1)} %bitcast.237, bf16[4,4,3,384,512]{4,3,2,1,0:T(8,128)(2,1)} %bitcast.238, ...), custom_call_target="tpu_custom_call" | custom-call | flops 6000000000 | bytes 1000000 | tf_op jit(solution)/shard_map/feed_forward_back/pallas_call | solution.py:430
  264.8 9.3 %weight_grad.2 = (bf16[4,384,512]{2,1,0:T(8,128)(2,1)}, bf16[4,384,512]{2,1,0:T(8,128)(2,1)}) custom-call(s32[2]{0:T(128)} %pad_add_fusion.5.where, bf16[256,1536]{1,0:T(8,128)(2,1)} %get-tuple-element.62.g_ref.refs_0_, bf16[256,1536]{1,0:T(8,128)(2,1)} %collective-permute-done.33.refs_1_, bf16[256,1536]{1,0:T(8,128)(2,1)} %after.39.g_ref.refs_2_, ...), custom_call_target="tpu_custom_call" | custom-call | flops 5000000000 | bytes 1000000 | tf_op jit(solution)/shard_map/weight_grad/pallas_call | solution.py:480
  274.2 12.7 %weight_grad.3 = (bf16[4,384,512]{2,1,0:T(8,128)(2,1)}, bf16[4,384,512]{2,1,0:T(8,128)(2,1)}, bf16[4,384,512]{2,1,0:T(8,128)(2,1)}, bf16[4,384,512]{2,1,0:T(8,128)(2,1)}) custom-call(s32[2]{0:T(128)} %pad_add_fusion.5.where, bf16[256,1536]{1,0:T(8,128)(2,1)} %multiply_convert_fusion.1.h_ref.refs_0_, bf16[256,1536]{1,0:T(8,128)(2,1)} %collective-permute-done.37.refs_1_, ...), custom_call_target="tpu_custom_call" | custom-call | flops 5000000000 | bytes 1000000 | tf_op jit(solution)/shard_map/weight_grad/pallas_call | solution.py:480
  291.1 3.2 fusion.75
  294.3 4.0 convolution_convert_fusion.3
  299.0 1.9 collective-permute-start.43
  303.4 7.6 %collective-permute-done.46.refs_0_ = bf16[4,384,512]{2,1,0:T(8,128)(2,1)} collective-permute-done((bf16[4,384,512]{2,1,0:T(8,128)(2,1)}, bf16[4,384,512]{2,1,0:T(8,128)(2,1)}, u32[]{:S(2)}, u32[]{:S(2)}) %collective-permute-start.46) | collective-permute-done | bytes 1572896 | tf_op jit(solution)/shard_map/ppermute | solution.py:180
  311.0 7.1 %collective-permute-done.44.refs_2_ = bf16[384,256]{1,0:T(8,128)(2,1)S(1)} collective-permute-done((bf16[384,256]{1,0:T(8,128)(2,1)S(1)}, bf16[384,256]{1,0:T(8,128)(2,1)S(1)}, u32[]{:S(2)}, u32[]{:S(2)}) %collective-permute-start.44) | collective-permute-done | bytes 196640 | tf_op jit(solution)/shard_map/ppermute | solution.py:180
  319.4 3.0 add_convert_fusion.2.refs_4_
  323.8 2.0 collective-permute-start.48
  328.2 9.7 %attend_back.2 = (f32[192,1024]{1,0:T(8,128)}, bf16[2,2,96,1024]{3,2,1,0:T(8,128)(2,1)}, bf16[2,2,96,1024]{3,2,1,0:T(8,128)(2,1)}) custom-call(s32[4,4]{1,0:T(4,128)} %pad_add_fusion.3.bounds, s32[4]{0:T(128)} %copy-done.20, bf16[384,1024]{1,0:T(8,128)(2,1)} %after.33.refs_1_.q_ref, bf16[2,2,192,1024]{3,2,1,0:T(8,128)(2,1)} %copy-done.11, ...), custom_call_target="tpu_custom_call" | custom-call | flops 12000000000 | bytes 1000000 | tf_op jit(solution)/shard_map/attend_back/pallas_call | solution.py:152
  338.3 2.1 collective-permute-done.47
  343.2 14.3 %collective-permute-done.48.refs_0_ = bf16[4,384,512]{2,1,0:T(8,128)(2,1)} collective-permute-done((bf16[4,384,512]{2,1,0:T(8,128)(2,1)S(1)}, bf16[4,384,512]{2,1,0:T(8,128)(2,1)}, u32[]{:S(2)}, u32[]{:S(2)}) %collective-permute-start.48) | collective-permute-done | bytes 1572896 | tf_op jit(solution)/shard_map/ppermute | solution.py:180
  357.6 3.0 add_convert_fusion.1.refs_2_
  364.0 9.6 %attend_back.3 = (f32[192,1024]{1,0:T(8,128)}, bf16[2,2,96,1024]{3,2,1,0:T(8,128)(2,1)}, bf16[2,2,96,1024]{3,2,1,0:T(8,128)(2,1)}) custom-call(s32[4,4]{1,0:T(4,128)} %pad_add_fusion.3.bounds, s32[4]{0:T(128)} %copy-done.20, bf16[384,1024]{1,0:T(8,128)(2,1)} %after.33.refs_1_.q_ref, bf16[2,2,192,1024]{3,2,1,0:T(8,128)(2,1)} %copy-done.11, ...), custom_call_target="tpu_custom_call" | custom-call | flops 12000000000 | bytes 1000000 | tf_op jit(solution)/shard_map/attend_back/pallas_call | solution.py:152
  373.6 21.2 %collective-permute-done.50.refs_0_ = bf16[4,384,512]{2,1,0:T(8,128)(2,1)S(1)} collective-permute-done((bf16[4,384,512]{2,1,0:T(8,128)(2,1)S(1)}, bf16[4,384,512]{2,1,0:T(8,128)(2,1)S(1)}, u32[]{:S(2)}, u32[]{:S(2)}) %collective-permute-start.50) | collective-permute-done | bytes 1572896 | tf_op jit(solution)/shard_map/ppermute | solution.py:180
  397.4 3.0 add_convert_fusion.refs_1_
  407.0 8.1 %collective-permute-done.52.refs_0_ = bf16[2,96,1024]{2,1,0:T(8,128)(2,1)S(1)} collective-permute-done((bf16[2,96,1024]{2,1,0:T(8,128)(2,1)S(1)}, bf16[2,96,1024]{2,1,0:T(8,128)(2,1)S(1)}, u32[]{:S(2)}, u32[]{:S(2)}) %collective-permute-start.52) | collective-permute-done | bytes 393248 | tf_op jit(solution)/shard_map/ppermute | solution.py:180
  421.8 4.1 convolution_convert_fusion.1.refs_0_
  425.9 13.6 %reduce-scatter.9.cloned.1.call-done = bf16[384,512]{1,0:T(8,128)(2,1)} async-done(((bf16[1536,512]{1,0:T(8,128)(2,1)}), bf16[384,512]{1,0:T(8,128)(2,1)}) %reduce-scatter.9.cloned.1.call-update) | async-done | bytes 393232 | tf_op jit(solution)/shard_map/reduce_scatter | solution.py:625
  440.8 2.6 convolution_convert_fusion
  443.5 2.0 copy-done.23
  445.6 5.2 convolution_convert_fusion.2
  453.0 3.0 fusion.7
  463.1 34.9 %collective-permute-done.56 = bf16[2,192,768]{2,1,0:T(8,128)(2,1)} collective-permute-done((bf16[2,192,768]{2,1,0:T(8,128)(2,1)}, bf16[2,192,768]{2,1,0:T(8,128)(2,1)}, u32[]{:S(2)}, u32[]{:S(2)}) %collective-permute-start.56) | collective-permute-done | bytes 589856 | tf_op jit(solution)/shard_map/ppermute | solution.py:180
  498.0 2.0 fusion.28.refs_2_
  500.1 2.6 fusion.14.refs_1_
  504.5 2.5 fusion.23
  507.0 2.8 fusion.21.refs_1_
  512.6 3.4 collective-permute-done.69
  519.6 4.2 collective-permute-done.67
  531.3 5.7 collective-permute-done.62
  540.4 6.3 %collective-permute-done.63 = bf16[192,1536]{1,0:T(8,128)(2,1)S(1)} collective-permute-done((bf16[192,1536]{1,0:T(8,128)(2,1)S(1)}, bf16[192,1536]{1,0:T(8,128)(2,1)S(1)}, u32[]{:S(2)}, u32[]{:S(2)}) %collective-permute-start.63) | collective-permute-done | bytes 589856 | tf_op jit(solution)/shard_map/ppermute | solution.py:180
  550.5 2.9 collective-permute-start.66
  555.1 14.8 %collective-permute-done.60 = f32[3,1536]{1,0:T(4,128)S(1)} collective-permute-done((f32[3,1536]{1,0:T(4,128)S(1)}, f32[3,1536]{1,0:T(4,128)S(1)}, u32[]{:S(2)}, u32[]{:S(2)}) %collective-permute-start.60) | collective-permute-done | bytes 18464 | tf_op jit(solution)/shard_map/ppermute | solution.py:180
  569.9 3.4 collective-permute-start.61
  574.0 8.3 %collective-permute-done.61 = f32[3,1536]{1,0:T(4,128)S(1)} collective-permute-done((f32[3,1536]{1,0:T(4,128)S(1)}, f32[3,1536]{1,0:T(4,128)S(1)}, u32[]{:S(2)}, u32[]{:S(2)}) %collective-permute-start.61) | collective-permute-done | bytes 18464 | tf_op jit(solution)/shard_map/ppermute | solution.py:180
  585.4 5.6 bitcast_convert_fusion
  (463 shorter events, 142.6 us)
Async XLA Ops:
  7.2 168.0 %all-gather.4.cloned.1.call-start = ((), (), s32[]{:S(2)}) async-start(), calls=%async_computation.4 | async-start | bytes 20054016 | tf_op jit(solution)/shard_map/all_gather | solution.py:535
  9.7 10.5 %collective-permute-start = (bf16[208,768]{1,0:T(8,128)(2,1)S(1)}, bf16[208,768]{1,0:T(8,128)(2,1)S(1)}, u32[]{:S(2)}, u32[]{:S(2)}) collective-permute-start(bf16[208,768]{1,0:T(8,128)(2,1)S(1)} %pad_maximum_fusion.14.refs_0_), channel_id=1, source_target_pairs={{0,8},{8,0},{1,9},{9,1},{2,10},{10,2},{3,11},{11,3},{4,12},{12,4},... | collective-permute-start | bytes 958472 | tf_op jit(solution)/shard_map/ppermute | solution.py:180
  12.7 9.4 %collective-permute-start.1 = (bf16[208,768]{1,0:T(8,128)(2,1)S(1)}, bf16[208,768]{1,0:T(8,128)(2,1)S(1)}, u32[]{:S(2)}, u32[]{:S(2)}) collective-permute-start(bf16[208,768]{1,0:T(8,128)(2,1)S(1)} %pad_maximum_fusion.14.refs_0_), channel_id=1, source_target_pairs={{0,16},{16,0},{1,17},{17,1},{2,18},{18,2},{3,19},{19,3},{4,20},{20... | collective-permute-start | bytes 958472 | tf_op jit(solution)/shard_map/ppermute | solution.py:180
  14.2 9.4 %collective-permute-start.4 = (bf16[192,384]{1,0:T(8,128)(2,1)}, bf16[192,384]{1,0:T(8,128)(2,1)S(1)}, u32[]{:S(2)}, u32[]{:S(2)}) collective-permute-start(bf16[192,384]{1,0:T(8,128)(2,1)} %bitcast.276), channel_id=1, source_target_pairs={{0,1},{1,0},{2,3},{3,2},{4,5},{5,4},{6,7},{7,6},{8,9},{9,8},{10,11... | collective-permute-start | bytes 442376 | tf_op jit(solution)/shard_map/ppermute | solution.py:180
  15.8 13.8 %collective-permute-start.5 = (bf16[192,384]{1,0:T(8,128)(2,1)}, bf16[192,384]{1,0:T(8,128)(2,1)S(1)}, u32[]{:S(2)}, u32[]{:S(2)}) collective-permute-start(bf16[192,384]{1,0:T(8,128)(2,1)} %bitcast.277), channel_id=1, source_target_pairs={{0,2},{1,3},{2,0},{3,1},{4,6},{5,7},{6,4},{7,5},{8,10},{9,11},{10,... | collective-permute-start | bytes 442376 | tf_op jit(solution)/shard_map/ppermute | solution.py:180
  18.4 11.2 %collective-permute-start.6 = (bf16[192,384]{1,0:T(8,128)(2,1)}, bf16[192,384]{1,0:T(8,128)(2,1)S(1)}, u32[]{:S(2)}, u32[]{:S(2)}) collective-permute-start(bf16[192,384]{1,0:T(8,128)(2,1)} %bitcast.278), channel_id=1, source_target_pairs={{0,3},{1,2},{2,1},{3,0},{4,7},{5,6},{6,5},{7,4},{8,11},{9,10},{10,... | collective-permute-start | bytes 442376 | tf_op jit(solution)/shard_map/ppermute | solution.py:180
  20.2 11.8 %collective-permute-start.3 = (bf16[112,768]{1,0:T(8,128)(2,1)S(1)}, bf16[112,768]{1,0:T(8,128)(2,1)S(1)}, u32[]{:S(2)}, u32[]{:S(2)}) collective-permute-start(bf16[112,768]{1,0:T(8,128)(2,1)S(1)} %slice.188), channel_id=1, source_target_pairs={{0,16},{16,0},{1,17},{17,1},{2,18},{18,2},{3,19},{19,3},{4,20},{20... | collective-permute-start | bytes 516104 | tf_op jit(solution)/shard_map/ppermute | solution.py:180
  22.1 10.0 %collective-permute-start.2 = (bf16[96,768]{1,0:T(8,128)(2,1)S(1)}, bf16[96,768]{1,0:T(8,128)(2,1)S(1)}, u32[]{:S(2)}, u32[]{:S(2)}) collective-permute-start(bf16[96,768]{1,0:T(8,128)(2,1)S(1)} %slice.187), channel_id=1, source_target_pairs={{0,8},{8,0},{1,9},{9,1},{2,10},{10,2},{3,11},{11,3},{4,12},{12,4},... | collective-permute-start | bytes 442376 | tf_op jit(solution)/shard_map/ppermute | solution.py:180
  30.7 11.5 %collective-permute-start.12 = (bf16[192,1536]{1,0:T(8,128)(2,1)S(1)}, bf16[192,1536]{1,0:T(8,128)(2,1)S(1)}, u32[]{:S(2)}, u32[]{:S(2)}) collective-permute-start(bf16[192,1536]{1,0:T(8,128)(2,1)S(1)} %pad_maximum_fusion.13.refs_0_), channel_id=1, source_target_pairs={{0,16},{16,0},{1,17},{17,1},{2,18},{18,2},{3,19},{19,3},{4,20},{20... | collective-permute-start | bytes 1769480 | tf_op jit(solution)/shard_map/ppermute | solution.py:180
  31.2 12.1 %collective-permute-start.7 = (bf16[208,768]{1,0:T(8,128)(2,1)S(1)}, bf16[208,768]{1,0:T(8,128)(2,1)S(1)}, u32[]{:S(2)}, u32[]{:S(2)}) collective-permute-start(bf16[208,768]{1,0:T(8,128)(2,1)S(1)} %pad_maximum_fusion.14.refs_0_), channel_id=1, source_target_pairs={{0,4},{4,0},{1,5},{5,1},{2,6},{6,2},{3,7},{7,3},{8,12},{12,8},{9,1... | collective-permute-start | bytes 958472 | tf_op jit(solution)/shard_map/ppermute | solution.py:180
  38.3 15.6 %collective-permute-start.28 = (bf16[3,192,512]{2,1,0:T(8,128)(2,1)}, bf16[3,192,512]{2,1,0:T(8,128)(2,1)}, u32[]{:S(2)}, u32[]{:S(2)}) collective-permute-start(bf16[3,192,512]{2,1,0:T(8,128)(2,1)} %constant_dynamic-slice_fusion.2), channel_id=1, source_target_pairs={{0,8},{8,0},{1,9},{9,1},{2,10},{10,2},{3,11},{11,3},{4,12},{12,4},... | collective-permute-start | bytes 1769480 | tf_op jit(solution)/shard_map/ppermute | solution.py:180
  57.8 236.5 %all-gather.6.cloned.1.call-start = ((), (), s32[]{:S(2)}) async-start(), calls=%async_computation.5 | async-start | bytes 3932160 | tf_op jit(solution)/shard_map/all_gather | solution.py:609
  60.0 21.4 %collective-permute-start.18 = (bf16[192,1536]{1,0:T(8,128)(2,1)S(1)}, bf16[192,1536]{1,0:T(8,128)(2,1)S(1)}, u32[]{:S(2)}, u32[]{:S(2)}) collective-permute-start(bf16[192,1536]{1,0:T(8,128)(2,1)S(1)} %pad_maximum_fusion.13.refs_0_), channel_id=1, source_target_pairs={{0,4},{4,0},{1,5},{5,1},{2,6},{6,2},{3,7},{7,3},{8,12},{12,8},{9,1... | collective-permute-start | bytes 1769480 | tf_op jit(solution)/shard_map/ppermute | solution.py:180
  60.0 20.9 %collective-permute-start.15 = (bf16[192,1536]{1,0:T(8,128)(2,1)}, bf16[192,1536]{1,0:T(8,128)(2,1)S(1)}, u32[]{:S(2)}, u32[]{:S(2)}) collective-permute-start(bf16[192,1536]{1,0:T(8,128)(2,1)} %after.32), channel_id=1, source_target_pairs={{0,8},{8,0},{1,9},{9,1},{2,10},{10,2},{3,11},{11,3},{4,12},{12,4},... | collective-permute-start | bytes 1769480 | tf_op jit(solution)/shard_map/ppermute | solution.py:180
  71.0 8.8 %collective-permute-start.13 = (s32[1,1024]{1,0:T(1,128)}, s32[1,1024]{1,0:T(1,128)S(1)}, u32[]{:S(2)}, u32[]{:S(2)}) collective-permute-start(s32[1,1024]{1,0:T(1,128)} %after.31), channel_id=1, source_target_pairs={{0,8},{8,0},{1,9},{9,1},{2,10},{10,2},{3,11},{11,3},{4,12},{12,4},... | collective-permute-start | bytes 12296 | tf_op jit(solution)/shard_map/ppermute | solution.py:180
  77.7 9.9 %collective-permute-start.16 = (bf16[96,1536]{1,0:T(8,128)(2,1)S(1)}, bf16[96,1536]{1,0:T(8,128)(2,1)S(1)}, u32[]{:S(2)}, u32[]{:S(2)}) collective-permute-start(bf16[96,1536]{1,0:T(8,128)(2,1)S(1)} %slice.200), channel_id=1, source_target_pairs={{0,8},{8,0},{1,9},{9,1},{2,10},{10,2},{3,11},{11,3},{4,12},{12,4},... | collective-permute-start | bytes 884744 | tf_op jit(solution)/shard_map/ppermute | solution.py:180
  78.0 25.7 %collective-permute-start.23 = (bf16[2,192,1024]{2,1,0:T(8,128)(2,1)S(1)}, bf16[2,192,1024]{2,1,0:T(8,128)(2,1)}, u32[]{:S(2)}, u32[]{:S(2)}) collective-permute-start(bf16[2,192,1024]{2,1,0:T(8,128)(2,1)S(1)} %bitcast.245), channel_id=1, source_target_pairs={{0,8},{8,0},{1,9},{9,1},{2,10},{10,2},{3,11},{11,3},{4,12},{12,4},... | collective-permute-start | bytes 2359304 | tf_op jit(solution)/shard_map/ppermute | solution.py:180
  80.8 18.9 %collective-permute-start.20 = (bf16[192,1536]{1,0:T(8,128)(2,1)S(1)}, bf16[192,1536]{1,0:T(8,128)(2,1)S(1)}, u32[]{:S(2)}, u32[]{:S(2)}) collective-permute-start(bf16[192,1536]{1,0:T(8,128)(2,1)S(1)} %copy-done.6), channel_id=1, source_target_pairs={{0,4},{4,0},{1,5},{5,1},{2,6},{6,2},{3,7},{7,3},{8,12},{12,8},{9,1... | collective-permute-start | bytes 1769480 | tf_op jit(solution)/shard_map/ppermute | solution.py:180
  81.4 15.9 %collective-permute-start.17 = (bf16[96,1536]{1,0:T(8,128)(2,1)S(1)}, bf16[96,1536]{1,0:T(8,128)(2,1)S(1)}, u32[]{:S(2)}, u32[]{:S(2)}) collective-permute-start(bf16[96,1536]{1,0:T(8,128)(2,1)S(1)} %slice.201), channel_id=1, source_target_pairs={{0,16},{16,0},{1,17},{17,1},{2,18},{18,2},{3,19},{19,3},{4,20},{20... | collective-permute-start | bytes 884744 | tf_op jit(solution)/shard_map/ppermute | solution.py:180
  82.9 16.9 %collective-permute-start.19 = (bf16[192,1536]{1,0:T(8,128)(2,1)S(1)}, bf16[192,1536]{1,0:T(8,128)(2,1)S(1)}, u32[]{:S(2)}, u32[]{:S(2)}) collective-permute-start(bf16[192,1536]{1,0:T(8,128)(2,1)S(1)} %collective-permute-done.15.refs_1_), channel_id=1, source_target_pairs={{0,4},{4,0},{1,5},{5,1},{2,6},{6,2},{3,7},{7,3},{8,12},{12,8},{9,1... | collective-permute-start | bytes 1769480 | tf_op jit(solution)/shard_map/ppermute | solution.py:180
  87.6 12.1 %collective-permute-start.21 = (bf16[96,1536]{1,0:T(8,128)(2,1)S(1)}, bf16[96,1536]{1,0:T(8,128)(2,1)S(1)}, u32[]{:S(2)}, u32[]{:S(2)}) collective-permute-start(bf16[96,1536]{1,0:T(8,128)(2,1)S(1)} %collective-permute-done.16.refs_3_), channel_id=1, source_target_pairs={{0,4},{4,0},{1,5},{5,1},{2,6},{6,2},{3,7},{7,3},{8,12},{12,8},{9,1... | collective-permute-start | bytes 884744 | tf_op jit(solution)/shard_map/ppermute | solution.py:180
  122.5 11.9 %collective-permute-start.25 = (bf16[384,256]{1,0:T(8,128)(2,1)S(1)}, bf16[384,256]{1,0:T(8,128)(2,1)S(1)}, u32[]{:S(2)}, u32[]{:S(2)}) collective-permute-start(bf16[384,256]{1,0:T(8,128)(2,1)S(1)} %get-tuple-element.131), channel_id=1, source_target_pairs={{0,1},{1,0},{2,3},{3,2},{4,5},{5,4},{6,7},{7,6},{8,9},{9,8},{10,11... | collective-permute-start | bytes 589832 | tf_op jit(solution)/shard_map/ppermute | solution.py:180
  124.2 15.0 %collective-permute-start.26 = (bf16[384,256]{1,0:T(8,128)(2,1)S(1)}, bf16[384,256]{1,0:T(8,128)(2,1)S(1)}, u32[]{:S(2)}, u32[]{:S(2)}) collective-permute-start(bf16[384,256]{1,0:T(8,128)(2,1)S(1)} %get-tuple-element.130), channel_id=1, source_target_pairs={{0,2},{1,3},{2,0},{3,1},{4,6},{5,7},{6,4},{7,5},{8,10},{9,11},{10,... | collective-permute-start | bytes 589832 | tf_op jit(solution)/shard_map/ppermute | solution.py:180
  125.4 25.6 %collective-permute-start.27 = (bf16[384,256]{1,0:T(8,128)(2,1)S(1)}, bf16[384,256]{1,0:T(8,128)(2,1)S(1)}, u32[]{:S(2)}, u32[]{:S(2)}) collective-permute-start(bf16[384,256]{1,0:T(8,128)(2,1)S(1)} %get-tuple-element.129), channel_id=1, source_target_pairs={{0,3},{1,2},{2,1},{3,0},{4,7},{5,6},{6,5},{7,4},{8,11},{9,10},{10,... | collective-permute-start | bytes 589832 | tf_op jit(solution)/shard_map/ppermute | solution.py:180
  156.3 37.5 %collective-permute-start.29 = (bf16[256,1536]{1,0:T(8,128)(2,1)}, bf16[256,1536]{1,0:T(8,128)(2,1)}, u32[]{:S(2)}, u32[]{:S(2)}) collective-permute-start(bf16[256,1536]{1,0:T(8,128)(2,1)} %multiply_convert_fusion.1.h_ref.refs_0_), channel_id=1, source_target_pairs={{0,8},{8,0},{1,9},{9,1},{2,10},{10,2},{3,11},{11,3},{4,12},{12,4},... | collective-permute-start | bytes 2359304 | tf_op jit(solution)/shard_map/ppermute | solution.py:180
  206.2 19.8 %collective-permute-start.30 = (bf16[256,1536]{1,0:T(8,128)(2,1)}, bf16[256,1536]{1,0:T(8,128)(2,1)S(1)}, u32[]{:S(2)}, u32[]{:S(2)}) collective-permute-start(bf16[256,1536]{1,0:T(8,128)(2,1)} %get-tuple-element.60), channel_id=1, source_target_pairs={{0,8},{8,0},{1,9},{9,1},{2,10},{10,2},{3,11},{11,3},{4,12},{12,4},... | collective-permute-start | bytes 2359304 | tf_op jit(solution)/shard_map/ppermute | solution.py:180
  229.6 134.3 %reduce-scatter.5.cloned.1.call-start = ((), (), s32[]{:S(2)}) async-start(), calls=%async_computation.6 | async-start | bytes 1966080 | tf_op jit(solution)/shard_map/reduce_scatter | solution.py:625
  229.7 18.9 %collective-permute-start.31 = (bf16[256,1536]{1,0:T(8,128)(2,1)}, bf16[256,1536]{1,0:T(8,128)(2,1)S(1)}, u32[]{:S(2)}, u32[]{:S(2)}) collective-permute-start(bf16[256,1536]{1,0:T(8,128)(2,1)} %get-tuple-element.62.g_ref.refs_0_), channel_id=1, source_target_pairs={{0,8},{8,0},{1,9},{9,1},{2,10},{10,2},{3,11},{11,3},{4,12},{12,4},... | collective-permute-start | bytes 2359304 | tf_op jit(solution)/shard_map/ppermute | solution.py:180
  231.3 18.2 %collective-permute-start.37 = (bf16[256,1536]{1,0:T(8,128)(2,1)}, bf16[256,1536]{1,0:T(8,128)(2,1)}, u32[]{:S(2)}, u32[]{:S(2)}) collective-permute-start(bf16[256,1536]{1,0:T(8,128)(2,1)} %multiply_convert_fusion.1.h_ref.refs_0_), channel_id=1, source_target_pairs={{0,4},{4,0},{1,5},{5,1},{2,6},{6,2},{3,7},{7,3},{8,12},{12,8},{9,1... | collective-permute-start | bytes 2359304 | tf_op jit(solution)/shard_map/ppermute | solution.py:180
  231.3 30.4 %collective-permute-start.35 = (bf16[256,2048]{1,0:T(8,128)(2,1)S(1)}, bf16[256,2048]{1,0:T(8,128)(2,1)}, u32[]{:S(2)}, u32[]{:S(2)}) collective-permute-start(bf16[256,2048]{1,0:T(8,128)(2,1)S(1)} %copy-done.47), channel_id=1, source_target_pairs={{0,4},{4,0},{1,5},{5,1},{2,6},{6,2},{3,7},{7,3},{8,12},{12,8},{9,1... | collective-permute-start | bytes 3145736 | tf_op jit(solution)/shard_map/ppermute | solution.py:180
  231.8 30.5 %collective-permute-start.36 = (bf16[256,2048]{1,0:T(8,128)(2,1)}, bf16[256,2048]{1,0:T(8,128)(2,1)}, u32[]{:S(2)}, u32[]{:S(2)}) collective-permute-start(bf16[256,2048]{1,0:T(8,128)(2,1)} %get-tuple-element.69.refs_6_), channel_id=1, source_target_pairs={{0,4},{4,0},{1,5},{5,1},{2,6},{6,2},{3,7},{7,3},{8,12},{12,8},{9,1... | collective-permute-start | bytes 3145736 | tf_op jit(solution)/shard_map/ppermute | solution.py:180
  246.2 16.6 %collective-permute-start.39 = (bf16[256,2048]{1,0:T(8,128)(2,1)}, bf16[256,2048]{1,0:T(8,128)(2,1)}, u32[]{:S(2)}, u32[]{:S(2)}) collective-permute-start(bf16[256,2048]{1,0:T(8,128)(2,1)} %get-tuple-element.64.refs_1_.refs_0_), channel_id=1, source_target_pairs={{0,4},{4,0},{1,5},{5,1},{2,6},{6,2},{3,7},{7,3},{8,12},{12,8},{9,1... | collective-permute-start | bytes 3145736 | tf_op jit(solution)/shard_map/ppermute | solution.py:180
  248.6 13.8 %collective-permute-start.33 = (bf16[256,1536]{1,0:T(8,128)(2,1)S(1)}, bf16[256,1536]{1,0:T(8,128)(2,1)}, u32[]{:S(2)}, u32[]{:S(2)}) collective-permute-start(bf16[256,1536]{1,0:T(8,128)(2,1)S(1)} %copy-done.32), channel_id=1, source_target_pairs={{0,4},{4,0},{1,5},{5,1},{2,6},{6,2},{3,7},{7,3},{8,12},{12,8},{9,1... | collective-permute-start | bytes 2359304 | tf_op jit(solution)/shard_map/ppermute | solution.py:180
  249.5 14.0 %collective-permute-start.34 = (bf16[256,1536]{1,0:T(8,128)(2,1)}, bf16[256,1536]{1,0:T(8,128)(2,1)}, u32[]{:S(2)}, u32[]{:S(2)}) collective-permute-start(bf16[256,1536]{1,0:T(8,128)(2,1)} %after.39.g_ref.refs_2_), channel_id=1, source_target_pairs={{0,4},{4,0},{1,5},{5,1},{2,6},{6,2},{3,7},{7,3},{8,12},{12,8},{9,1... | collective-permute-start | bytes 2359304 | tf_op jit(solution)/shard_map/ppermute | solution.py:180
  261.7 12.5 %collective-permute-start.41 = (bf16[256,2048]{1,0:T(8,128)(2,1)}, bf16[256,2048]{1,0:T(8,128)(2,1)}, u32[]{:S(2)}, u32[]{:S(2)}) collective-permute-start(bf16[256,2048]{1,0:T(8,128)(2,1)} %get-tuple-element.65.refs_2_.refs_8_), channel_id=1, source_target_pairs={{0,4},{4,0},{1,5},{5,1},{2,6},{6,2},{3,7},{7,3},{8,12},{12,8},{9,1... | collective-permute-start | bytes 3145736 | tf_op jit(solution)/shard_map/ppermute | solution.py:180
  262.3 11.9 %collective-permute-start.40 = (bf16[256,2048]{1,0:T(8,128)(2,1)}, bf16[256,2048]{1,0:T(8,128)(2,1)}, u32[]{:S(2)}, u32[]{:S(2)}) collective-permute-start(bf16[256,2048]{1,0:T(8,128)(2,1)} %get-tuple-element.72.refs_6_), channel_id=1, source_target_pairs={{0,4},{4,0},{1,5},{5,1},{2,6},{6,2},{3,7},{7,3},{8,12},{12,8},{9,1... | collective-permute-start | bytes 3145736 | tf_op jit(solution)/shard_map/ppermute | solution.py:180
  262.4 11.8 %collective-permute-start.42 = (bf16[256,2048]{1,0:T(8,128)(2,1)}, bf16[256,2048]{1,0:T(8,128)(2,1)}, u32[]{:S(2)}, u32[]{:S(2)}) collective-permute-start(bf16[256,2048]{1,0:T(8,128)(2,1)} %get-tuple-element.73.refs_10_), channel_id=1, source_target_pairs={{0,4},{4,0},{1,5},{5,1},{2,6},{6,2},{3,7},{7,3},{8,12},{12,8},{9,1... | collective-permute-start | bytes 3145736 | tf_op jit(solution)/shard_map/ppermute | solution.py:180
  262.8 11.3 %collective-permute-start.38 = (bf16[256,1536]{1,0:T(8,128)(2,1)}, bf16[256,1536]{1,0:T(8,128)(2,1)}, u32[]{:S(2)}, u32[]{:S(2)}) collective-permute-start(bf16[256,1536]{1,0:T(8,128)(2,1)} %after.37.h_ref.refs_2_), channel_id=1, source_target_pairs={{0,4},{4,0},{1,5},{5,1},{2,6},{6,2},{3,7},{7,3},{8,12},{12,8},{9,1... | collective-permute-start | bytes 2359304 | tf_op jit(solution)/shard_map/ppermute | solution.py:180
  263.5 23.4 %collective-permute-start.32 = (bf16[256,1536]{1,0:T(8,128)(2,1)S(1)}, bf16[256,1536]{1,0:T(8,128)(2,1)S(1)}, u32[]{:S(2)}, u32[]{:S(2)}) collective-permute-start(bf16[256,1536]{1,0:T(8,128)(2,1)S(1)} %copy-done.69), channel_id=1, source_target_pairs={{0,8},{8,0},{1,9},{9,1},{2,10},{10,2},{3,11},{11,3},{4,12},{12,4},... | collective-permute-start | bytes 2359304 | tf_op jit(solution)/shard_map/ppermute | solution.py:180
  274.1 36.8 %collective-permute-start.46 = (bf16[4,384,512]{2,1,0:T(8,128)(2,1)}, bf16[4,384,512]{2,1,0:T(8,128)(2,1)}, u32[]{:S(2)}, u32[]{:S(2)}) collective-permute-start(bf16[4,384,512]{2,1,0:T(8,128)(2,1)} %get-tuple-element.70.refs_2_.refs_1_), channel_id=1, source_target_pairs={{0,16},{16,0},{1,17},{17,1},{2,18},{18,2},{3,19},{19,3},{4,20},{20... | collective-permute-start | bytes 4718600 | tf_op jit(solution)/shard_map/ppermute | solution.py:180
  299.0 12.0 %collective-permute-start.43 = (bf16[384,256]{1,0:T(8,128)(2,1)S(1)}, bf16[384,256]{1,0:T(8,128)(2,1)S(1)}, u32[]{:S(2)}, u32[]{:S(2)}) collective-permute-start(bf16[384,256]{1,0:T(8,128)(2,1)S(1)} %get-tuple-element.126), channel_id=1, source_target_pairs={{0,1},{1,0},{2,3},{3,2},{4,5},{5,4},{6,7},{7,6},{8,9},{9,8},{10,11... | collective-permute-start | bytes 589832 | tf_op jit(solution)/shard_map/ppermute | solution.py:180
  300.9 17.1 %collective-permute-start.44 = (bf16[384,256]{1,0:T(8,128)(2,1)S(1)}, bf16[384,256]{1,0:T(8,128)(2,1)S(1)}, u32[]{:S(2)}, u32[]{:S(2)}) collective-permute-start(bf16[384,256]{1,0:T(8,128)(2,1)S(1)} %get-tuple-element.125), channel_id=1, source_target_pairs={{0,2},{1,3},{2,0},{3,1},{4,6},{5,7},{6,4},{7,5},{8,10},{9,11},{10,... | collective-permute-start | bytes 589832 | tf_op jit(solution)/shard_map/ppermute | solution.py:180
  301.9 16.1 %collective-permute-start.45 = (bf16[384,256]{1,0:T(8,128)(2,1)S(1)}, bf16[384,256]{1,0:T(8,128)(2,1)S(1)}, u32[]{:S(2)}, u32[]{:S(2)}) collective-permute-start(bf16[384,256]{1,0:T(8,128)(2,1)S(1)} %get-tuple-element.124), channel_id=1, source_target_pairs={{0,3},{1,2},{2,1},{3,0},{4,7},{5,6},{6,5},{7,4},{8,11},{9,10},{10,... | collective-permute-start | bytes 589832 | tf_op jit(solution)/shard_map/ppermute | solution.py:180
  322.4 78.1 %reduce-scatter.7.cloned.1.call-start = ((), (), s32[]{:S(2)}) async-start(), calls=%async_computation.7 | async-start | bytes 1966080 | tf_op jit(solution)/shard_map/reduce_scatter | solution.py:625
  323.8 33.8 %collective-permute-start.48 = (bf16[4,384,512]{2,1,0:T(8,128)(2,1)S(1)}, bf16[4,384,512]{2,1,0:T(8,128)(2,1)}, u32[]{:S(2)}, u32[]{:S(2)}) collective-permute-start(bf16[4,384,512]{2,1,0:T(8,128)(2,1)S(1)} %copy-done.40), channel_id=1, source_target_pairs={{0,16},{16,0},{1,17},{17,1},{2,18},{18,2},{3,19},{19,3},{4,20},{20... | collective-permute-start | bytes 4718600 | tf_op jit(solution)/shard_map/ppermute | solution.py:180
  360.6 78.9 %reduce-scatter.9.cloned.1.call-start = ((), (), s32[]{:S(2)}) async-start(), calls=%async_computation.8 | async-start | bytes 1966080 | tf_op jit(solution)/shard_map/reduce_scatter | solution.py:625
  362.0 32.8 %collective-permute-start.50 = (bf16[4,384,512]{2,1,0:T(8,128)(2,1)S(1)}, bf16[4,384,512]{2,1,0:T(8,128)(2,1)S(1)}, u32[]{:S(2)}, u32[]{:S(2)}) collective-permute-start(bf16[4,384,512]{2,1,0:T(8,128)(2,1)S(1)} %copy-done.38), channel_id=1, source_target_pairs={{0,16},{16,0},{1,17},{17,1},{2,18},{18,2},{3,19},{19,3},{4,20},{20... | collective-permute-start | bytes 4718600 | tf_op jit(solution)/shard_map/ppermute | solution.py:180
  363.4 31.4 %collective-permute-start.49 = (bf16[2,96,1024]{2,1,0:T(8,128)(2,1)}, bf16[2,96,1024]{2,1,0:T(8,128)(2,1)S(1)}, u32[]{:S(2)}, u32[]{:S(2)}) collective-permute-start(bf16[2,96,1024]{2,1,0:T(8,128)(2,1)} %fusion.36.refs_1_), channel_id=1, source_target_pairs={{0,8},{8,0},{1,9},{9,1},{2,10},{10,2},{3,11},{11,3},{4,12},{12,4},... | collective-permute-start | bytes 1179656 | tf_op jit(solution)/shard_map/ppermute | solution.py:180
  400.4 102.2 %reduce-scatter.11.cloned.1.call-start = ((), (), s32[]{:S(2)}) async-start(), calls=%async_computation.9 | async-start | bytes 3932160 | tf_op jit(solution)/shard_map/reduce_scatter | solution.py:693
  404.0 11.2 %collective-permute-start.52 = (bf16[2,96,1024]{2,1,0:T(8,128)(2,1)S(1)}, bf16[2,96,1024]{2,1,0:T(8,128)(2,1)S(1)}, u32[]{:S(2)}, u32[]{:S(2)}) collective-permute-start(bf16[2,96,1024]{2,1,0:T(8,128)(2,1)S(1)} %fusion.37.refs_1_), channel_id=1, source_target_pairs={{0,8},{8,0},{1,9},{9,1},{2,10},{10,2},{3,11},{11,3},{4,12},{12,4},... | collective-permute-start | bytes 1179656 | tf_op jit(solution)/shard_map/ppermute | solution.py:180
  439.6 145.8 %all-gather.8.cloned.1.call-start = ((), (), s32[]{:S(2)}) async-start(), calls=%async_computation.10 | async-start | bytes 3932160 | tf_op jit(solution)/shard_map/all_gather | solution.py:707
  445.5 7.4 %collective-permute-start.53 = (bf16[2,2,192,1536]{3,2,1,0:T(8,128)(2,1)S(1)}, bf16[2,2,192,1536]{3,2,1,0:T(8,128)(2,1)}, u32[]{:S(2)}, u32[]{:S(2)}) collective-permute-start(bf16[2,2,192,1536]{3,2,1,0:T(8,128)(2,1)S(1)} %dynamic-slice_bitcast_fusion), channel_id=1, source_target_pairs={{0,4},{4,0},{1,5},{5,1},{2,6},{6,2},{3,7},{7,3},{8,12},{12,8},{9,1... | collective-permute-start | bytes 7077896 | tf_op jit(solution)/shard_map/ppermute | solution.py:180
  457.1 42.9 %collective-permute-start.54 = (bf16[2,192,1536]{2,1,0:T(8,128)(2,1)}, bf16[2,192,1536]{2,1,0:T(8,128)(2,1)}, u32[]{:S(2)}, u32[]{:S(2)}) collective-permute-start(bf16[2,192,1536]{2,1,0:T(8,128)(2,1)} %dynamic-slice_bitcast_fusion.2), channel_id=1, source_target_pairs={{0,16},{16,0},{1,17},{17,1},{2,18},{18,2},{3,19},{19,3},{4,20},{20... | collective-permute-start | bytes 3538952 | tf_op jit(solution)/shard_map/ppermute | solution.py:180
  460.9 37.1 %collective-permute-start.56 = (bf16[2,192,768]{2,1,0:T(8,128)(2,1)}, bf16[2,192,768]{2,1,0:T(8,128)(2,1)}, u32[]{:S(2)}, u32[]{:S(2)}) collective-permute-start(bf16[2,192,768]{2,1,0:T(8,128)(2,1)} %dynamic-slice_bitcast_fusion.4), channel_id=1, source_target_pairs={{0,16},{16,0},{1,17},{17,1},{2,18},{18,2},{3,19},{19,3},{4,20},{20... | collective-permute-start | bytes 1769480 | tf_op jit(solution)/shard_map/ppermute | solution.py:180
  516.1 7.7 %collective-permute-start.67 = (bf16[192,512]{1,0:T(8,128)(2,1)S(1)}, bf16[192,512]{1,0:T(8,128)(2,1)S(1)}, u32[]{:S(2)}, u32[]{:S(2)}) collective-permute-start(bf16[192,512]{1,0:T(8,128)(2,1)S(1)} %dynamic-slice_bitcast_fusion.8), channel_id=1, source_target_pairs={{0,8},{8,0},{1,9},{9,1},{2,10},{10,2},{3,11},{11,3},{4,12},{12,4},... | collective-permute-start | bytes 589832 | tf_op jit(solution)/shard_map/ppermute | solution.py:180
  526.9 10.1 %collective-permute-start.62 = (bf16[192,768]{1,0:T(8,128)(2,1)S(1)}, bf16[192,768]{1,0:T(8,128)(2,1)}, u32[]{:S(2)}, u32[]{:S(2)}) collective-permute-start(bf16[192,768]{1,0:T(8,128)(2,1)S(1)} %dynamic-slice_bitcast_fusion.5), channel_id=1, source_target_pairs={{0,8},{8,0},{1,9},{9,1},{2,10},{10,2},{3,11},{11,3},{4,12},{12,4},... | collective-permute-start | bytes 884744 | tf_op jit(solution)/shard_map/ppermute | solution.py:180
  528.0 18.7 %collective-permute-start.63 = (bf16[192,1536]{1,0:T(8,128)(2,1)S(1)}, bf16[192,1536]{1,0:T(8,128)(2,1)S(1)}, u32[]{:S(2)}, u32[]{:S(2)}) collective-permute-start(bf16[192,1536]{1,0:T(8,128)(2,1)S(1)} %dynamic-slice_bitcast_fusion.3), channel_id=1, source_target_pairs={{0,8},{8,0},{1,9},{9,1},{2,10},{10,2},{3,11},{11,3},{4,12},{12,4},... | collective-permute-start | bytes 1769480 | tf_op jit(solution)/shard_map/ppermute | solution.py:180
  529.8 8.3 %collective-permute-start.57 = (f32[3,1536]{1,0:T(4,128)}, f32[3,1536]{1,0:T(4,128)S(1)}, u32[]{:S(2)}, u32[]{:S(2)}) collective-permute-start(f32[3,1536]{1,0:T(4,128)} %after.56), channel_id=1, source_target_pairs={{0,16},{16,0},{1,17},{17,1},{2,18},{18,2},{3,19},{19,3},{4,20},{20... | collective-permute-start | bytes 55304 | tf_op jit(solution)/shard_map/ppermute | solution.py:180
  539.5 7.6 %collective-permute-start.58 = (f32[3,1536]{1,0:T(4,128)}, f32[3,1536]{1,0:T(4,128)}, u32[]{:S(2)}, u32[]{:S(2)}) collective-permute-start(f32[3,1536]{1,0:T(4,128)} %add.511), channel_id=1, source_target_pairs={{0,8},{8,0},{1,9},{9,1},{2,10},{10,2},{3,11},{11,3},{4,12},{12,4},... | collective-permute-start | bytes 55304 | tf_op jit(solution)/shard_map/ppermute | solution.py:180
  548.8 24.5 %collective-permute-start.64 = (bf16[192,384]{1,0:T(8,128)(2,1)S(1)}, bf16[192,384]{1,0:T(8,128)(2,1)S(1)}, u32[]{:S(2)}, u32[]{:S(2)}) collective-permute-start(bf16[192,384]{1,0:T(8,128)(2,1)S(1)} %bitcast.280), channel_id=1, source_target_pairs={{0,1},{1,0},{2,3},{3,2},{4,5},{5,4},{6,7},{7,6},{8,9},{9,8},{10,11... | collective-permute-start | bytes 442376 | tf_op jit(solution)/shard_map/ppermute | solution.py:180
  548.9 24.4 %collective-permute-start.65 = (bf16[192,384]{1,0:T(8,128)(2,1)S(1)}, bf16[192,384]{1,0:T(8,128)(2,1)S(1)}, u32[]{:S(2)}, u32[]{:S(2)}) collective-permute-start(bf16[192,384]{1,0:T(8,128)(2,1)S(1)} %bitcast.281), channel_id=1, source_target_pairs={{0,2},{1,3},{2,0},{3,1},{4,6},{5,7},{6,4},{7,5},{8,10},{9,11},{10,... | collective-permute-start | bytes 442376 | tf_op jit(solution)/shard_map/ppermute | solution.py:180
  550.5 22.8 %collective-permute-start.66 = (bf16[192,384]{1,0:T(8,128)(2,1)S(1)}, bf16[192,384]{1,0:T(8,128)(2,1)S(1)}, u32[]{:S(2)}, u32[]{:S(2)}) collective-permute-start(bf16[192,384]{1,0:T(8,128)(2,1)S(1)} %bitcast.282), channel_id=1, source_target_pairs={{0,3},{1,2},{2,1},{3,0},{4,7},{5,6},{6,5},{7,4},{8,11},{9,10},{10,... | collective-permute-start | bytes 442376 | tf_op jit(solution)/shard_map/ppermute | solution.py:180
  553.4 16.4 %collective-permute-start.60 = (f32[3,1536]{1,0:T(4,128)S(1)}, f32[3,1536]{1,0:T(4,128)S(1)}, u32[]{:S(2)}, u32[]{:S(2)}) collective-permute-start(f32[3,1536]{1,0:T(4,128)S(1)} %add.513), channel_id=1, source_target_pairs={{0,1},{1,0},{2,3},{3,2},{4,5},{5,4},{6,7},{7,6},{8,9},{9,8},{10,11... | collective-permute-start | bytes 55304 | tf_op jit(solution)/shard_map/ppermute | solution.py:180
  569.9 12.4 %collective-permute-start.61 = (f32[3,1536]{1,0:T(4,128)S(1)}, f32[3,1536]{1,0:T(4,128)S(1)}, u32[]{:S(2)}, u32[]{:S(2)}) collective-permute-start(f32[3,1536]{1,0:T(4,128)S(1)} %add.514), channel_id=1, source_target_pairs={{0,2},{1,3},{2,0},{3,1},{4,6},{5,7},{6,4},{7,5},{8,10},{9,11},{10,... | collective-permute-start | bytes 55304 | tf_op jit(solution)/shard_map/ppermute | solution.py:180
  (108 other events, 550.8 us)
Sparse Core Ops, SparseCore 0:
  57.9 111.3 all-gather.3
  229.8 62.8 all-gather.5
  322.5 36.2 reduce-scatter.4
  361.0 37.3 reduce-scatter.6
  401.1 38.4 reduce-scatter.8
  442.3 59.2 reduce-scatter.10
  510.0 75.3 all-gather.7

commit v5 on v4

--- a/solution.py
+++ b/solution.py
@@ -157,7 +157,7 @@
             out_specs=[pl.BlockSpec((group*HD, tq), lambda g,i,*_:(0,i))] + kv_out,
             scratch_shapes=[pltpu.VMEM((HD,N),BF), pltpu.VMEM((N,HD),BF), pltpu.VMEM((N,HD),BF), pltpu.VMEM((HD,N),F32), pltpu.VMEM((HD,N),F32), pltpu.VMEM((HD,group*tq),F32)]),
         compiler_params=pltpu.CompilerParams(vmem_limit_bytes=56*2**20),
-        cost_estimate=about(12),
+        cost_estimate=about(4),
         name="attend_back",
     )(bounds, place, qT, *kv_sources, start, qpos, gT, of, lse)
 
@@ -611,8 +611,11 @@
     def both_cores(parts):
         return [v for part in parts for v in everyone(part, "cc")]
 
-    def to_rows(parts):
-        return parts[0], parts[1:], [swap(parts[k], "fsdp", k) for k in range(1, nf)]
+    def to_rows(parts, *others):
+        own, sends = parts[0], list(parts[1:])
+        if others and sends:
+            sends = after(sends, *others)
+        return own, sends, [swap(sends[k - 1], "fsdp", k) for k in range(1, nf)]
 
     def scattered(own, given, hold):
         total = own.astype(F32)
@@ -648,8 +651,8 @@
     g_att = dot(out_weights, grad_attn, 0, 1).astype(BF).reshape(nz, q_cols, share)
     g_parts = [g_att[0]] + [swap(g_att[k], "tp", k) for k in range(1, nz)]
     down_total, down_done, shard_down_t = scattered(down_own, down_given, g_parts[1:])
-    gate_own, gate_sends, gate_given = to_rows(part_gate_up[:nf])
-    up_own, up_sends, up_given = to_rows(part_gate_up[nf:])
+    gate_own, gate_sends, gate_given = to_rows(part_gate_up[:nf], down_given)
+    up_own, up_sends, up_given = to_rows(part_gate_up[nf:], gate_given)
     grad_heads = jnp.concatenate(ordered(after(g_parts, down_total, gate_sends), z), axis=1)
 
     bounds = make_bounds(doc_start, first_row, rows, BWD_TQ, BWD_TK)

time: 609 us -> 610 us (level)
  waiting for transfers between devices: 234 us -> 225 us
  starting transfers between devices: 81.9 us -> 90.2 us
    ppermute x70, waiting for transfers between devices: 220 us -> 211 us  [swap(): return lax.ppermute(values, axis, [(i, i ^ step) for i in range(size)])]
    ppermute x70, starting transfers between devices: 81.4 us -> 89.7 us  [swap(): return lax.ppermute(values, axis, [(i, i ^ step) for i in range(size)])]
    unnamed x197 -> x191, local copies, waits for them, and re-layouts: 36 us -> 36.9 us
  transfers between devices with their start and end apart: 77 -> 77, of which waited for: 32 -> 30; matrix products, arithmetic and copies ran while one was open for 17% -> 17% of each run, Pallas kernels for 16% -> 16%
where the time goes in v5:
time: 610 us; the launch traced here: 604 us
  waiting for transfers between devices  225 us (37%)
  Pallas kernels  112 us (18%)
  starting transfers between devices  90.2 us (15%)
  other arithmetic  77.9 us (13%)
  local copies, waits for them, and re-layouts  55.9 us (9%)
  matrix products  25.4 us (4%)
  between operations  18.2 us (3%)
    ppermute x70, waiting for transfers between devices, swap(): return lax.ppermute(values, axis, [(i, i ^ step) for i in range(size)])  211 us
    ppermute x70, starting transfers between devices, swap(): return lax.ppermute(values, axis, [(i, i ^ step) for i in range(size)])  89.7 us
    unnamed x191, local copies, waits for them, and re-layouts  36.9 us
    pallas_call x2, Pallas kernels, ffn_backward(): pl.pallas_call(functools.partial(ffn_backward_kernel, dims), out_shape=(s...  26.9 us
    dot_general x7, matrix products, dot(): lax.dot_general(a, b, (((ca,), (cb,)), ((), ())), preferred_element_type=...  25.4 us
    pallas_call x2, Pallas kernels, ffn_forward(): pl.pallas_call(functools.partial(ffn_forward_kernel, dims), out_shape=(sh...  24.8 us
    pallas_call x2, Pallas kernels, weight_grad(): pl.pallas_call(functools.partial(weight_grad_kernel, dims, pieces, count)...  22 us
    pallas_call x2, Pallas kernels, attn_bwd(): pl.pallas_call(functools.partial(bwd_kernel, scale2, tq, tk, group, len(k...  21 us
  transfers between devices with their start and end apart: 77, of which 30 were waited for; matrix products, arithmetic and copies ran while one was open for 17% of the time, Pallas kernels for 16%

profile of v5, /device:TPU:0, one launch (start us, length us, event | category | flops | bytes accessed | tf_op | source)
XLA Modules:
  0.0 604.4 jit_solution(16554069803307191509)
XLA Ops:
  9.7 3.0 collective-permute-start
  15.8 2.6 collective-permute-start.5
  23.6 5.9 collective-permute-done.5.refs_3_
  34.0 2.4 pad_maximum_fusion.2.refs_0_
  36.4 2.0 constant_dynamic-slice_fusion.2
  39.5 2.6 fusion.2
  44.5 2.7 put_blocks.2
  48.5 5.4 collective-permute-done.28.refs_0_
  60.7 2.8 fusion.4.refs_0_
  72.6 3.9 fusion.9
  83.0 4.7 collective-permute-done.16.refs_3_
  87.7 9.6 %collective-permute-done.17.refs_4_ = bf16[96,1536]{1,0:T(8,128)(2,1)S(1)} collective-permute-done((bf16[96,1536]{1,0:T(8,128)(2,1)S(1)}, bf16[96,1536]{1,0:T(8,128)(2,1)S(1)}, u32[]{:S(2)}, u32[]{:S(2)}) %collective-permute-start.17) | collective-permute-done | bytes 294944 | tf_op jit(solution)/shard_map/ppermute | solution.py:180
  97.3 2.5 convert_reduce_fusion
  101.5 2.2 copy-done
  106.4 2.3 collective-permute-done.24.refs_1_
  108.8 12.0 %attend.1 = (bf16[384,1024]{1,0:T(8,128)(2,1)S(1)}, f32[384,1024]{1,0:T(8,128)S(1)}, f32[2,2,1024]{2,1,0:T(2,128)S(1)}) custom-call(s32[4,4]{1,0:T(4,128)S(1)} %pad_add_fusion.2.bounds, s32[4]{0:T(128)S(1)} %pad_add_fusion.4.place, bf16[384,1024]{1,0:T(8,128)(2,1)S(1)} %copy-done.1, bf16[2,2,192,1024]{3,2,1,0:T(8,128)(2,1)S(1)} %pad_maximum_fusion.refs_0_, ...), custom_call_target="tpu_custom_call" | custom-call | flops 12000000000 | bytes 1000000 | tf_op jit(solution)/shard_map/attend/pallas_call | solution.py:85
  127.0 7.4 %collective-permute-done.25 = bf16[384,256]{1,0:T(8,128)(2,1)S(1)} collective-permute-done((bf16[384,256]{1,0:T(8,128)(2,1)S(1)}, bf16[384,256]{1,0:T(8,128)(2,1)S(1)}, u32[]{:S(2)}, u32[]{:S(2)}) %collective-permute-start.25) | collective-permute-done | bytes 196640 | tf_op jit(solution)/shard_map/ppermute | solution.py:180
  134.4 4.9 collective-permute-done.26
  139.2 11.8 %collective-permute-done.27 = bf16[384,256]{1,0:T(8,128)(2,1)S(1)} collective-permute-done((bf16[384,256]{1,0:T(8,128)(2,1)S(1)}, bf16[384,256]{1,0:T(8,128)(2,1)S(1)}, u32[]{:S(2)}, u32[]{:S(2)}) %collective-permute-start.27) | collective-permute-done | bytes 196640 | tf_op jit(solution)/shard_map/ppermute | solution.py:180
  151.0 4.2 multiply_reduce_fusion.2
  156.3 15.8 %collective-permute-start.29 = (bf16[256,1536]{1,0:T(8,128)(2,1)}, bf16[256,1536]{1,0:T(8,128)(2,1)}, u32[]{:S(2)}, u32[]{:S(2)}) collective-permute-start(bf16[256,1536]{1,0:T(8,128)(2,1)} %multiply_convert_fusion.1.h_ref.refs_0_), channel_id=1, source_target_pairs={{0,8},{8,0},{1,9},{9,1},{2,10},{10,2},{3,11},{11,3},{4,12},{12,4},... | collective-permute-start | bytes 2359304 | tf_op jit(solution)/shard_map/ppermute | solution.py:180
  172.1 12.4 %feed_forward.2 = (f32[256,2048]{1,0:T(8,128)}, f32[256,2048]{1,0:T(8,128)}, bf16[256,2048]{1,0:T(8,128)(2,1)}, f32[256,1536]{1,0:T(8,128)}) custom-call(bf16[256,1536]{1,0:T(8,128)(2,1)} %multiply_convert_fusion.1.h_ref.refs_0_, bf16[4,4,3,384,512]{4,3,2,1,0:T(8,128)(2,1)} %bitcast.227, bf16[4,4,3,384,512]{4,3,2,1,0:T(8,128)(2,1)} %bitcast.228, ...), custom_call_target="tpu_custom_call" | custom-call | flops 6000000000 | bytes 1000000 | tf_op jit(solution)/shard_map/feed_forward/pallas_call | solution.py:394
  184.6 12.4 %feed_forward.3 = (f32[256,2048]{1,0:T(8,128)}, f32[256,2048]{1,0:T(8,128)}, bf16[256,2048]{1,0:T(8,128)(2,1)}, bf16[256,1536]{1,0:T(8,128)(2,1)}) custom-call(bf16[256,1536]{1,0:T(8,128)(2,1)} %after.39.h_ref.refs_2_, bf16[4,4,3,384,512]{4,3,2,1,0:T(8,128)(2,1)} %bitcast.230, bf16[4,4,3,384,512]{4,3,2,1,0:T(8,128)(2,1)} %bitcast.231, ...), custom_call_target="tpu_custom_call" | custom-call | flops 6000000000 | bytes 1000000 | tf_op jit(solution)/shard_map/feed_forward/pallas_call | solution.py:394
  197.7 16.4 %collective-permute-done.30 = bf16[256,1536]{1,0:T(8,128)(2,1)S(1)} collective-permute-done((bf16[256,1536]{1,0:T(8,128)(2,1)}, bf16[256,1536]{1,0:T(8,128)(2,1)S(1)}, u32[]{:S(2)}, u32[]{:S(2)}) %collective-permute-start.30) | collective-permute-done | bytes 786464 | tf_op jit(solution)/shard_map/ppermute | solution.py:180
  220.2 14.3 %feed_forward_back.2 = (bf16[256,2048]{1,0:T(8,128)(2,1)}, bf16[256,2048]{1,0:T(8,128)(2,1)}, f32[256,1536]{1,0:T(8,128)}) custom-call(bf16[256,1536]{1,0:T(8,128)(2,1)} %get-tuple-element.62.g_ref.refs_0_, bf16[4,4,3,384,512]{4,3,2,1,0:T(8,128)(2,1)} %bitcast.233, bf16[4,4,3,384,512]{4,3,2,1,0:T(8,128)(2,1)} %bitcast.234, ...), custom_call_target="tpu_custom_call" | custom-call | flops 6000000000 | bytes 1000000 | tf_op jit(solution)/shard_map/feed_forward_back/pallas_call | solution.py:430
  236.5 12.6 %feed_forward_back.3 = (bf16[256,2048]{1,0:T(8,128)(2,1)}, bf16[256,2048]{1,0:T(8,128)(2,1)}, bf16[256,1536]{1,0:T(8,128)(2,1)}) custom-call(bf16[256,1536]{1,0:T(8,128)(2,1)} %after.41.g_ref.refs_2_, bf16[4,4,3,384,512]{4,3,2,1,0:T(8,128)(2,1)} %bitcast.236, bf16[4,4,3,384,512]{4,3,2,1,0:T(8,128)(2,1)} %bitcast.237, bf16[4,4,3,384,512]{4,3,2,1,0:T(8,128)(2,1)} %bitcast.238, ...), custom_call_target="tpu_custom_call" | custom-call | flops 6000000000 | bytes 1000000 | tf_op jit(solution)/shard_map/feed_forward_back/pallas_call | solution.py:430
  252.6 9.3 %weight_grad.2 = (bf16[4,384,512]{2,1,0:T(8,128)(2,1)}, bf16[4,384,512]{2,1,0:T(8,128)(2,1)}) custom-call(s32[2]{0:T(128)} %pad_add_fusion.5.where, bf16[256,1536]{1,0:T(8,128)(2,1)} %get-tuple-element.62.g_ref.refs_0_, bf16[256,1536]{1,0:T(8,128)(2,1)} %collective-permute-done.33.refs_1_, bf16[256,1536]{1,0:T(8,128)(2,1)} %after.41.g_ref.refs_2_, ...), custom_call_target="tpu_custom_call" | custom-call | flops 5000000000 | bytes 1000000 | tf_op jit(solution)/shard_map/weight_grad/pallas_call | solution.py:480
  261.9 14.0 %collective-permute-start.46 = (bf16[4,384,512]{2,1,0:T(8,128)(2,1)}, bf16[4,384,512]{2,1,0:T(8,128)(2,1)S(1)}, u32[]{:S(2)}, u32[]{:S(2)}) collective-permute-start(bf16[4,384,512]{2,1,0:T(8,128)(2,1)} %get-tuple-element.70.refs_2_.refs_1_), channel_id=1, source_target_pairs={{0,16},{16,0},{1,17},{17,1},{2,18},{18,2},{3,19},{19,3},{4,20},{20... | collective-permute-start | bytes 4718600 | tf_op jit(solution)/shard_map/ppermute | solution.py:180
  276.0 12.7 %weight_grad.3 = (bf16[4,384,512]{2,1,0:T(8,128)(2,1)}, bf16[4,384,512]{2,1,0:T(8,128)(2,1)}, bf16[4,384,512]{2,1,0:T(8,128)(2,1)}, bf16[4,384,512]{2,1,0:T(8,128)(2,1)}) custom-call(s32[2]{0:T(128)} %pad_add_fusion.5.where, bf16[256,1536]{1,0:T(8,128)(2,1)} %multiply_convert_fusion.1.h_ref.refs_0_, bf16[256,1536]{1,0:T(8,128)(2,1)} %collective-permute-done.37.refs_1_, ...), custom_call_target="tpu_custom_call" | custom-call | flops 5000000000 | bytes 1000000 | tf_op jit(solution)/shard_map/weight_grad/pallas_call | solution.py:480
  288.7 2.3 multiply_reduce_fusion.1
  291.3 3.4 fusion.75
  294.7 4.0 convolution_convert_fusion.3
  304.0 6.9 %collective-permute-done.46.refs_0_.refs_1_ = bf16[4,384,512]{2,1,0:T(8,128)(2,1)S(1)} collective-permute-done((bf16[4,384,512]{2,1,0:T(8,128)(2,1)}, bf16[4,384,512]{2,1,0:T(8,128)(2,1)S(1)}, u32[]{:S(2)}, u32[]{:S(2)}) %collective-permute-start.46) | collective-permute-done | bytes 1572896 | tf_op jit(solution)/shard_map/ppermute | solution.py:180
  312.0 6.6 %collective-permute-done.44.refs_2_ = bf16[384,256]{1,0:T(8,128)(2,1)S(1)} collective-permute-done((bf16[384,256]{1,0:T(8,128)(2,1)}, bf16[384,256]{1,0:T(8,128)(2,1)S(1)}, u32[]{:S(2)}, u32[]{:S(2)}) %collective-permute-start.44) | collective-permute-done | bytes 196640 | tf_op jit(solution)/shard_map/ppermute | solution.py:180
  319.3 3.0 add_convert_fusion.2.refs_4_
  326.7 10.6 %attend_back.2 = (f32[192,1024]{1,0:T(8,128)}, bf16[2,2,96,1024]{3,2,1,0:T(8,128)(2,1)}, bf16[2,2,96,1024]{3,2,1,0:T(8,128)(2,1)}) custom-call(s32[4,4]{1,0:T(4,128)} %pad_add_fusion.3.bounds, s32[4]{0:T(128)} %copy-done.20, bf16[384,1024]{1,0:T(8,128)(2,1)} %after.35.refs_1_.q_ref, bf16[2,2,192,1024]{3,2,1,0:T(8,128)(2,1)} %copy-done.11, ...), custom_call_target="tpu_custom_call" | custom-call | flops 4000000000 | bytes 1000000 | tf_op jit(solution)/shard_map/attend_back/pallas_call | solution.py:152
  337.3 3.5 collective-permute-start.47
  340.8 16.2 %collective-permute-done.48.refs_0_.refs_1_ = bf16[4,384,512]{2,1,0:T(8,128)(2,1)S(1)} collective-permute-done((bf16[4,384,512]{2,1,0:T(8,128)(2,1)S(1)}, bf16[4,384,512]{2,1,0:T(8,128)(2,1)S(1)}, u32[]{:S(2)}, u32[]{:S(2)}) %collective-permute-start.48) | collective-permute-done | bytes 1572896 | tf_op jit(solution)/shard_map/ppermute | solution.py:180
  358.2 2.0 fusion.36.refs_1_
  361.6 3.0 add_convert_fusion.1.refs_2_
  367.3 10.4 %attend_back.3 = (f32[192,1024]{1,0:T(8,128)}, bf16[2,2,96,1024]{3,2,1,0:T(8,128)(2,1)}, bf16[2,2,96,1024]{3,2,1,0:T(8,128)(2,1)}) custom-call(s32[4,4]{1,0:T(4,128)} %pad_add_fusion.3.bounds, s32[4]{0:T(128)} %copy-done.20, bf16[384,1024]{1,0:T(8,128)(2,1)} %after.35.refs_1_.q_ref, bf16[2,2,192,1024]{3,2,1,0:T(8,128)(2,1)} %copy-done.11, ...), custom_call_target="tpu_custom_call" | custom-call | flops 4000000000 | bytes 1000000 | tf_op jit(solution)/shard_map/attend_back/pallas_call | solution.py:152
  377.7 20.9 %collective-permute-done.50.refs_0_ = bf16[4,384,512]{2,1,0:T(8,128)(2,1)S(1)} collective-permute-done((bf16[4,384,512]{2,1,0:T(8,128)(2,1)S(1)}, bf16[4,384,512]{2,1,0:T(8,128)(2,1)S(1)}, u32[]{:S(2)}, u32[]{:S(2)}) %collective-permute-start.50) | collective-permute-done | bytes 1572896 | tf_op jit(solution)/shard_map/ppermute | solution.py:180
  401.1 3.0 add_convert_fusion.refs_1_
  409.9 9.0 %collective-permute-done.52.refs_0_ = bf16[2,96,1024]{2,1,0:T(8,128)(2,1)S(1)} collective-permute-done((bf16[2,96,1024]{2,1,0:T(8,128)(2,1)S(1)}, bf16[2,96,1024]{2,1,0:T(8,128)(2,1)S(1)}, u32[]{:S(2)}, u32[]{:S(2)}) %collective-permute-start.52) | collective-permute-done | bytes 393248 | tf_op jit(solution)/shard_map/ppermute | solution.py:180
  425.5 4.1 convolution_convert_fusion.1.refs_0_
  429.6 13.4 %reduce-scatter.9.cloned.1.call-done = bf16[384,512]{1,0:T(8,128)(2,1)} async-done(((bf16[1536,512]{1,0:T(8,128)(2,1)}), bf16[384,512]{1,0:T(8,128)(2,1)}) %reduce-scatter.9.cloned.1.call-update) | async-done | bytes 393232 | tf_op jit(solution)/shard_map/reduce_scatter | solution.py:628
  444.3 2.6 convolution_convert_fusion
  447.1 2.0 copy-done.23
  449.1 5.2 convolution_convert_fusion.2
  456.5 3.0 fusion.7
  466.6 34.9 %collective-permute-done.56 = bf16[2,192,768]{2,1,0:T(8,128)(2,1)} collective-permute-done((bf16[2,192,768]{2,1,0:T(8,128)(2,1)}, bf16[2,192,768]{2,1,0:T(8,128)(2,1)}, u32[]{:S(2)}, u32[]{:S(2)}) %collective-permute-start.56) | collective-permute-done | bytes 589856 | tf_op jit(solution)/shard_map/ppermute | solution.py:180
  501.5 2.0 fusion.28.refs_2_
  503.6 2.6 fusion.14.refs_1_
  508.0 2.5 fusion.23
  510.5 2.8 fusion.21.refs_1_
  516.2 3.3 collective-permute-done.69
  523.1 4.2 collective-permute-done.67
  534.8 5.8 collective-permute-done.62
  544.0 6.3 %collective-permute-done.63 = bf16[192,1536]{1,0:T(8,128)(2,1)S(1)} collective-permute-done((bf16[192,1536]{1,0:T(8,128)(2,1)S(1)}, bf16[192,1536]{1,0:T(8,128)(2,1)S(1)}, u32[]{:S(2)}, u32[]{:S(2)}) %collective-permute-start.63) | collective-permute-done | bytes 589856 | tf_op jit(solution)/shard_map/ppermute | solution.py:180
  554.0 3.0 collective-permute-start.66
  558.6 14.8 %collective-permute-done.60 = f32[3,1536]{1,0:T(4,128)S(1)} collective-permute-done((f32[3,1536]{1,0:T(4,128)S(1)}, f32[3,1536]{1,0:T(4,128)S(1)}, u32[]{:S(2)}, u32[]{:S(2)}) %collective-permute-start.60) | collective-permute-done | bytes 18464 | tf_op jit(solution)/shard_map/ppermute | solution.py:180
  573.4 3.3 collective-permute-start.61
  577.5 8.3 %collective-permute-done.61 = f32[3,1536]{1,0:T(4,128)S(1)} collective-permute-done((f32[3,1536]{1,0:T(4,128)S(1)}, f32[3,1536]{1,0:T(4,128)S(1)}, u32[]{:S(2)}, u32[]{:S(2)}) %collective-permute-start.61) | collective-permute-done | bytes 18464 | tf_op jit(solution)/shard_map/ppermute | solution.py:180
  588.9 5.6 bitcast_convert_fusion
  (459 shorter events, 137.1 us)
Async XLA Ops:
  7.2 164.9 %all-gather.4.cloned.1.call-start = ((), (), s32[]{:S(2)}) async-start(), calls=%async_computation.4 | async-start | bytes 20054016 | tf_op jit(solution)/shard_map/all_gather | solution.py:535
  9.7 10.5 %collective-permute-start = (bf16[208,768]{1,0:T(8,128)(2,1)S(1)}, bf16[208,768]{1,0:T(8,128)(2,1)S(1)}, u32[]{:S(2)}, u32[]{:S(2)}) collective-permute-start(bf16[208,768]{1,0:T(8,128)(2,1)S(1)} %pad_maximum_fusion.14.refs_0_), channel_id=1, source_target_pairs={{0,8},{8,0},{1,9},{9,1},{2,10},{10,2},{3,11},{11,3},{4,12},{12,4},... | collective-permute-start | bytes 958472 | tf_op jit(solution)/shard_map/ppermute | solution.py:180
  12.7 9.4 %collective-permute-start.1 = (bf16[208,768]{1,0:T(8,128)(2,1)S(1)}, bf16[208,768]{1,0:T(8,128)(2,1)S(1)}, u32[]{:S(2)}, u32[]{:S(2)}) collective-permute-start(bf16[208,768]{1,0:T(8,128)(2,1)S(1)} %pad_maximum_fusion.14.refs_0_), channel_id=1, source_target_pairs={{0,16},{16,0},{1,17},{17,1},{2,18},{18,2},{3,19},{19,3},{4,20},{20... | collective-permute-start | bytes 958472 | tf_op jit(solution)/shard_map/ppermute | solution.py:180
  14.2 9.4 %collective-permute-start.4 = (bf16[192,384]{1,0:T(8,128)(2,1)}, bf16[192,384]{1,0:T(8,128)(2,1)S(1)}, u32[]{:S(2)}, u32[]{:S(2)}) collective-permute-start(bf16[192,384]{1,0:T(8,128)(2,1)} %bitcast.275), channel_id=1, source_target_pairs={{0,1},{1,0},{2,3},{3,2},{4,5},{5,4},{6,7},{7,6},{8,9},{9,8},{10,11... | collective-permute-start | bytes 442376 | tf_op jit(solution)/shard_map/ppermute | solution.py:180
  15.8 13.8 %collective-permute-start.5 = (bf16[192,384]{1,0:T(8,128)(2,1)}, bf16[192,384]{1,0:T(8,128)(2,1)S(1)}, u32[]{:S(2)}, u32[]{:S(2)}) collective-permute-start(bf16[192,384]{1,0:T(8,128)(2,1)} %bitcast.276), channel_id=1, source_target_pairs={{0,2},{1,3},{2,0},{3,1},{4,6},{5,7},{6,4},{7,5},{8,10},{9,11},{10,... | collective-permute-start | bytes 442376 | tf_op jit(solution)/shard_map/ppermute | solution.py:180
  18.4 11.2 %collective-permute-start.6 = (bf16[192,384]{1,0:T(8,128)(2,1)}, bf16[192,384]{1,0:T(8,128)(2,1)S(1)}, u32[]{:S(2)}, u32[]{:S(2)}) collective-permute-start(bf16[192,384]{1,0:T(8,128)(2,1)} %bitcast.277), channel_id=1, source_target_pairs={{0,3},{1,2},{2,1},{3,0},{4,7},{5,6},{6,5},{7,4},{8,11},{9,10},{10,... | collective-permute-start | bytes 442376 | tf_op jit(solution)/shard_map/ppermute | solution.py:180
  20.2 11.8 %collective-permute-start.3 = (bf16[112,768]{1,0:T(8,128)(2,1)S(1)}, bf16[112,768]{1,0:T(8,128)(2,1)S(1)}, u32[]{:S(2)}, u32[]{:S(2)}) collective-permute-start(bf16[112,768]{1,0:T(8,128)(2,1)S(1)} %slice.188), channel_id=1, source_target_pairs={{0,16},{16,0},{1,17},{17,1},{2,18},{18,2},{3,19},{19,3},{4,20},{20... | collective-permute-start | bytes 516104 | tf_op jit(solution)/shard_map/ppermute | solution.py:180
  22.1 10.0 %collective-permute-start.2 = (bf16[96,768]{1,0:T(8,128)(2,1)S(1)}, bf16[96,768]{1,0:T(8,128)(2,1)S(1)}, u32[]{:S(2)}, u32[]{:S(2)}) collective-permute-start(bf16[96,768]{1,0:T(8,128)(2,1)S(1)} %slice.187), channel_id=1, source_target_pairs={{0,8},{8,0},{1,9},{9,1},{2,10},{10,2},{3,11},{11,3},{4,12},{12,4},... | collective-permute-start | bytes 442376 | tf_op jit(solution)/shard_map/ppermute | solution.py:180
  30.7 11.5 %collective-permute-start.12 = (bf16[192,1536]{1,0:T(8,128)(2,1)S(1)}, bf16[192,1536]{1,0:T(8,128)(2,1)S(1)}, u32[]{:S(2)}, u32[]{:S(2)}) collective-permute-start(bf16[192,1536]{1,0:T(8,128)(2,1)S(1)} %pad_maximum_fusion.13.refs_0_), channel_id=1, source_target_pairs={{0,16},{16,0},{1,17},{17,1},{2,18},{18,2},{3,19},{19,3},{4,20},{20... | collective-permute-start | bytes 1769480 | tf_op jit(solution)/shard_map/ppermute | solution.py:180
  31.2 12.1 %collective-permute-start.7 = (bf16[208,768]{1,0:T(8,128)(2,1)S(1)}, bf16[208,768]{1,0:T(8,128)(2,1)S(1)}, u32[]{:S(2)}, u32[]{:S(2)}) collective-permute-start(bf16[208,768]{1,0:T(8,128)(2,1)S(1)} %pad_maximum_fusion.14.refs_0_), channel_id=1, source_target_pairs={{0,4},{4,0},{1,5},{5,1},{2,6},{6,2},{3,7},{7,3},{8,12},{12,8},{9,1... | collective-permute-start | bytes 958472 | tf_op jit(solution)/shard_map/ppermute | solution.py:180
  38.3 15.6 %collective-permute-start.28 = (bf16[3,192,512]{2,1,0:T(8,128)(2,1)}, bf16[3,192,512]{2,1,0:T(8,128)(2,1)}, u32[]{:S(2)}, u32[]{:S(2)}) collective-permute-start(bf16[3,192,512]{2,1,0:T(8,128)(2,1)} %constant_dynamic-slice_fusion.2), channel_id=1, source_target_pairs={{0,8},{8,0},{1,9},{9,1},{2,10},{10,2},{3,11},{11,3},{4,12},{12,4},... | collective-permute-start | bytes 1769480 | tf_op jit(solution)/shard_map/ppermute | solution.py:180
  57.8 236.9 %all-gather.6.cloned.1.call-start = ((), (), s32[]{:S(2)}) async-start(), calls=%async_computation.5 | async-start | bytes 3932160 | tf_op jit(solution)/shard_map/all_gather | solution.py:609
  60.0 21.4 %collective-permute-start.18 = (bf16[192,1536]{1,0:T(8,128)(2,1)S(1)}, bf16[192,1536]{1,0:T(8,128)(2,1)S(1)}, u32[]{:S(2)}, u32[]{:S(2)}) collective-permute-start(bf16[192,1536]{1,0:T(8,128)(2,1)S(1)} %pad_maximum_fusion.13.refs_0_), channel_id=1, source_target_pairs={{0,4},{4,0},{1,5},{5,1},{2,6},{6,2},{3,7},{7,3},{8,12},{12,8},{9,1... | collective-permute-start | bytes 1769480 | tf_op jit(solution)/shard_map/ppermute | solution.py:180
  60.0 20.9 %collective-permute-start.15 = (bf16[192,1536]{1,0:T(8,128)(2,1)}, bf16[192,1536]{1,0:T(8,128)(2,1)S(1)}, u32[]{:S(2)}, u32[]{:S(2)}) collective-permute-start(bf16[192,1536]{1,0:T(8,128)(2,1)} %after.34), channel_id=1, source_target_pairs={{0,8},{8,0},{1,9},{9,1},{2,10},{10,2},{3,11},{11,3},{4,12},{12,4},... | collective-permute-start | bytes 1769480 | tf_op jit(solution)/shard_map/ppermute | solution.py:180
  71.0 8.8 %collective-permute-start.13 = (s32[1,1024]{1,0:T(1,128)}, s32[1,1024]{1,0:T(1,128)S(1)}, u32[]{:S(2)}, u32[]{:S(2)}) collective-permute-start(s32[1,1024]{1,0:T(1,128)} %after.33), channel_id=1, source_target_pairs={{0,8},{8,0},{1,9},{9,1},{2,10},{10,2},{3,11},{11,3},{4,12},{12,4},... | collective-permute-start | bytes 12296 | tf_op jit(solution)/shard_map/ppermute | solution.py:180
  77.7 9.9 %collective-permute-start.16 = (bf16[96,1536]{1,0:T(8,128)(2,1)S(1)}, bf16[96,1536]{1,0:T(8,128)(2,1)S(1)}, u32[]{:S(2)}, u32[]{:S(2)}) collective-permute-start(bf16[96,1536]{1,0:T(8,128)(2,1)S(1)} %slice.200), channel_id=1, source_target_pairs={{0,8},{8,0},{1,9},{9,1},{2,10},{10,2},{3,11},{11,3},{4,12},{12,4},... | collective-permute-start | bytes 884744 | tf_op jit(solution)/shard_map/ppermute | solution.py:180
  78.0 25.7 %collective-permute-start.23 = (bf16[2,192,1024]{2,1,0:T(8,128)(2,1)S(1)}, bf16[2,192,1024]{2,1,0:T(8,128)(2,1)}, u32[]{:S(2)}, u32[]{:S(2)}) collective-permute-start(bf16[2,192,1024]{2,1,0:T(8,128)(2,1)S(1)} %bitcast.245), channel_id=1, source_target_pairs={{0,8},{8,0},{1,9},{9,1},{2,10},{10,2},{3,11},{11,3},{4,12},{12,4},... | collective-permute-start | bytes 2359304 | tf_op jit(solution)/shard_map/ppermute | solution.py:180
  80.9 18.9 %collective-permute-start.20 = (bf16[192,1536]{1,0:T(8,128)(2,1)S(1)}, bf16[192,1536]{1,0:T(8,128)(2,1)S(1)}, u32[]{:S(2)}, u32[]{:S(2)}) collective-permute-start(bf16[192,1536]{1,0:T(8,128)(2,1)S(1)} %copy-done.6), channel_id=1, source_target_pairs={{0,4},{4,0},{1,5},{5,1},{2,6},{6,2},{3,7},{7,3},{8,12},{12,8},{9,1... | collective-permute-start | bytes 1769480 | tf_op jit(solution)/shard_map/ppermute | solution.py:180
  81.4 15.9 %collective-permute-start.17 = (bf16[96,1536]{1,0:T(8,128)(2,1)S(1)}, bf16[96,1536]{1,0:T(8,128)(2,1)S(1)}, u32[]{:S(2)}, u32[]{:S(2)}) collective-permute-start(bf16[96,1536]{1,0:T(8,128)(2,1)S(1)} %slice.201), channel_id=1, source_target_pairs={{0,16},{16,0},{1,17},{17,1},{2,18},{18,2},{3,19},{19,3},{4,20},{20... | collective-permute-start | bytes 884744 | tf_op jit(solution)/shard_map/ppermute | solution.py:180
  82.9 16.9 %collective-permute-start.19 = (bf16[192,1536]{1,0:T(8,128)(2,1)S(1)}, bf16[192,1536]{1,0:T(8,128)(2,1)S(1)}, u32[]{:S(2)}, u32[]{:S(2)}) collective-permute-start(bf16[192,1536]{1,0:T(8,128)(2,1)S(1)} %collective-permute-done.15.refs_1_), channel_id=1, source_target_pairs={{0,4},{4,0},{1,5},{5,1},{2,6},{6,2},{3,7},{7,3},{8,12},{12,8},{9,1... | collective-permute-start | bytes 1769480 | tf_op jit(solution)/shard_map/ppermute | solution.py:180
  87.7 12.1 %collective-permute-start.21 = (bf16[96,1536]{1,0:T(8,128)(2,1)S(1)}, bf16[96,1536]{1,0:T(8,128)(2,1)S(1)}, u32[]{:S(2)}, u32[]{:S(2)}) collective-permute-start(bf16[96,1536]{1,0:T(8,128)(2,1)S(1)} %collective-permute-done.16.refs_3_), channel_id=1, source_target_pairs={{0,4},{4,0},{1,5},{5,1},{2,6},{6,2},{3,7},{7,3},{8,12},{12,8},{9,1... | collective-permute-start | bytes 884744 | tf_op jit(solution)/shard_map/ppermute | solution.py:180
  122.5 11.8 %collective-permute-start.25 = (bf16[384,256]{1,0:T(8,128)(2,1)S(1)}, bf16[384,256]{1,0:T(8,128)(2,1)S(1)}, u32[]{:S(2)}, u32[]{:S(2)}) collective-permute-start(bf16[384,256]{1,0:T(8,128)(2,1)S(1)} %get-tuple-element.131), channel_id=1, source_target_pairs={{0,1},{1,0},{2,3},{3,2},{4,5},{5,4},{6,7},{7,6},{8,9},{9,8},{10,11... | collective-permute-start | bytes 589832 | tf_op jit(solution)/shard_map/ppermute | solution.py:180
  124.3 15.0 %collective-permute-start.26 = (bf16[384,256]{1,0:T(8,128)(2,1)S(1)}, bf16[384,256]{1,0:T(8,128)(2,1)S(1)}, u32[]{:S(2)}, u32[]{:S(2)}) collective-permute-start(bf16[384,256]{1,0:T(8,128)(2,1)S(1)} %get-tuple-element.130), channel_id=1, source_target_pairs={{0,2},{1,3},{2,0},{3,1},{4,6},{5,7},{6,4},{7,5},{8,10},{9,11},{10,... | collective-permute-start | bytes 589832 | tf_op jit(solution)/shard_map/ppermute | solution.py:180
  125.5 25.6 %collective-permute-start.27 = (bf16[384,256]{1,0:T(8,128)(2,1)S(1)}, bf16[384,256]{1,0:T(8,128)(2,1)S(1)}, u32[]{:S(2)}, u32[]{:S(2)}) collective-permute-start(bf16[384,256]{1,0:T(8,128)(2,1)S(1)} %get-tuple-element.129), channel_id=1, source_target_pairs={{0,3},{1,2},{2,1},{3,0},{4,7},{5,6},{6,5},{7,4},{8,11},{9,10},{10,... | collective-permute-start | bytes 589832 | tf_op jit(solution)/shard_map/ppermute | solution.py:180
  156.3 28.2 %collective-permute-start.29 = (bf16[256,1536]{1,0:T(8,128)(2,1)}, bf16[256,1536]{1,0:T(8,128)(2,1)}, u32[]{:S(2)}, u32[]{:S(2)}) collective-permute-start(bf16[256,1536]{1,0:T(8,128)(2,1)} %multiply_convert_fusion.1.h_ref.refs_0_), channel_id=1, source_target_pairs={{0,8},{8,0},{1,9},{9,1},{2,10},{10,2},{3,11},{11,3},{4,12},{12,4},... | collective-permute-start | bytes 2359304 | tf_op jit(solution)/shard_map/ppermute | solution.py:180
  196.9 17.2 %collective-permute-start.30 = (bf16[256,1536]{1,0:T(8,128)(2,1)}, bf16[256,1536]{1,0:T(8,128)(2,1)S(1)}, u32[]{:S(2)}, u32[]{:S(2)}) collective-permute-start(bf16[256,1536]{1,0:T(8,128)(2,1)} %get-tuple-element.60), channel_id=1, source_target_pairs={{0,8},{8,0},{1,9},{9,1},{2,10},{10,2},{3,11},{11,3},{4,12},{12,4},... | collective-permute-start | bytes 2359304 | tf_op jit(solution)/shard_map/ppermute | solution.py:180
  218.0 149.3 %reduce-scatter.5.cloned.1.call-start = ((), (), s32[]{:S(2)}) async-start(), calls=%async_computation.6 | async-start | bytes 1966080 | tf_op jit(solution)/shard_map/reduce_scatter | solution.py:628
  218.1 17.4 %collective-permute-start.31 = (bf16[256,1536]{1,0:T(8,128)(2,1)}, bf16[256,1536]{1,0:T(8,128)(2,1)S(1)}, u32[]{:S(2)}, u32[]{:S(2)}) collective-permute-start(bf16[256,1536]{1,0:T(8,128)(2,1)} %get-tuple-element.62.g_ref.refs_0_), channel_id=1, source_target_pairs={{0,8},{8,0},{1,9},{9,1},{2,10},{10,2},{3,11},{11,3},{4,12},{12,4},... | collective-permute-start | bytes 2359304 | tf_op jit(solution)/shard_map/ppermute | solution.py:180
  219.6 16.9 %collective-permute-start.37 = (bf16[256,1536]{1,0:T(8,128)(2,1)}, bf16[256,1536]{1,0:T(8,128)(2,1)}, u32[]{:S(2)}, u32[]{:S(2)}) collective-permute-start(bf16[256,1536]{1,0:T(8,128)(2,1)} %multiply_convert_fusion.1.h_ref.refs_0_), channel_id=1, source_target_pairs={{0,4},{4,0},{1,5},{5,1},{2,6},{6,2},{3,7},{7,3},{8,12},{12,8},{9,1... | collective-permute-start | bytes 2359304 | tf_op jit(solution)/shard_map/ppermute | solution.py:180
  219.6 29.5 %collective-permute-start.35 = (bf16[256,2048]{1,0:T(8,128)(2,1)S(1)}, bf16[256,2048]{1,0:T(8,128)(2,1)}, u32[]{:S(2)}, u32[]{:S(2)}) collective-permute-start(bf16[256,2048]{1,0:T(8,128)(2,1)S(1)} %copy-done.47), channel_id=1, source_target_pairs={{0,4},{4,0},{1,5},{5,1},{2,6},{6,2},{3,7},{7,3},{8,12},{12,8},{9,1... | collective-permute-start | bytes 3145736 | tf_op jit(solution)/shard_map/ppermute | solution.py:180
  220.1 29.6 %collective-permute-start.36 = (bf16[256,2048]{1,0:T(8,128)(2,1)}, bf16[256,2048]{1,0:T(8,128)(2,1)}, u32[]{:S(2)}, u32[]{:S(2)}) collective-permute-start(bf16[256,2048]{1,0:T(8,128)(2,1)} %get-tuple-element.69.refs_6_), channel_id=1, source_target_pairs={{0,4},{4,0},{1,5},{5,1},{2,6},{6,2},{3,7},{7,3},{8,12},{12,8},{9,1... | collective-permute-start | bytes 3145736 | tf_op jit(solution)/shard_map/ppermute | solution.py:180
  234.5 15.7 %collective-permute-start.39 = (bf16[256,2048]{1,0:T(8,128)(2,1)}, bf16[256,2048]{1,0:T(8,128)(2,1)}, u32[]{:S(2)}, u32[]{:S(2)}) collective-permute-start(bf16[256,2048]{1,0:T(8,128)(2,1)} %get-tuple-element.64.refs_1_.refs_0_), channel_id=1, source_target_pairs={{0,4},{4,0},{1,5},{5,1},{2,6},{6,2},{3,7},{7,3},{8,12},{12,8},{9,1... | collective-permute-start | bytes 3145736 | tf_op jit(solution)/shard_map/ppermute | solution.py:180
  235.5 14.3 %collective-permute-start.33 = (bf16[256,1536]{1,0:T(8,128)(2,1)S(1)}, bf16[256,1536]{1,0:T(8,128)(2,1)}, u32[]{:S(2)}, u32[]{:S(2)}) collective-permute-start(bf16[256,1536]{1,0:T(8,128)(2,1)S(1)} %copy-done.36), channel_id=1, source_target_pairs={{0,4},{4,0},{1,5},{5,1},{2,6},{6,2},{3,7},{7,3},{8,12},{12,8},{9,1... | collective-permute-start | bytes 2359304 | tf_op jit(solution)/shard_map/ppermute | solution.py:180
  236.4 14.4 %collective-permute-start.34 = (bf16[256,1536]{1,0:T(8,128)(2,1)}, bf16[256,1536]{1,0:T(8,128)(2,1)}, u32[]{:S(2)}, u32[]{:S(2)}) collective-permute-start(bf16[256,1536]{1,0:T(8,128)(2,1)} %after.41.g_ref.refs_2_), channel_id=1, source_target_pairs={{0,4},{4,0},{1,5},{5,1},{2,6},{6,2},{3,7},{7,3},{8,12},{12,8},{9,1... | collective-permute-start | bytes 2359304 | tf_op jit(solution)/shard_map/ppermute | solution.py:180
  249.1 26.9 %collective-permute-start.41 = (bf16[256,2048]{1,0:T(8,128)(2,1)}, bf16[256,2048]{1,0:T(8,128)(2,1)}, u32[]{:S(2)}, u32[]{:S(2)}) collective-permute-start(bf16[256,2048]{1,0:T(8,128)(2,1)} %get-tuple-element.65.refs_2_.refs_8_), channel_id=1, source_target_pairs={{0,4},{4,0},{1,5},{5,1},{2,6},{6,2},{3,7},{7,3},{8,12},{12,8},{9,1... | collective-permute-start | bytes 3145736 | tf_op jit(solution)/shard_map/ppermute | solution.py:180
  249.7 26.3 %collective-permute-start.40 = (bf16[256,2048]{1,0:T(8,128)(2,1)}, bf16[256,2048]{1,0:T(8,128)(2,1)}, u32[]{:S(2)}, u32[]{:S(2)}) collective-permute-start(bf16[256,2048]{1,0:T(8,128)(2,1)} %get-tuple-element.72.refs_6_), channel_id=1, source_target_pairs={{0,4},{4,0},{1,5},{5,1},{2,6},{6,2},{3,7},{7,3},{8,12},{12,8},{9,1... | collective-permute-start | bytes 3145736 | tf_op jit(solution)/shard_map/ppermute | solution.py:180
  249.8 26.2 %collective-permute-start.42 = (bf16[256,2048]{1,0:T(8,128)(2,1)}, bf16[256,2048]{1,0:T(8,128)(2,1)}, u32[]{:S(2)}, u32[]{:S(2)}) collective-permute-start(bf16[256,2048]{1,0:T(8,128)(2,1)} %get-tuple-element.73.refs_10_), channel_id=1, source_target_pairs={{0,4},{4,0},{1,5},{5,1},{2,6},{6,2},{3,7},{7,3},{8,12},{12,8},{9,1... | collective-permute-start | bytes 3145736 | tf_op jit(solution)/shard_map/ppermute | solution.py:180
  250.2 11.7 %collective-permute-start.38 = (bf16[256,1536]{1,0:T(8,128)(2,1)}, bf16[256,1536]{1,0:T(8,128)(2,1)}, u32[]{:S(2)}, u32[]{:S(2)}) collective-permute-start(bf16[256,1536]{1,0:T(8,128)(2,1)} %after.39.h_ref.refs_2_), channel_id=1, source_target_pairs={{0,4},{4,0},{1,5},{5,1},{2,6},{6,2},{3,7},{7,3},{8,12},{12,8},{9,1... | collective-permute-start | bytes 2359304 | tf_op jit(solution)/shard_map/ppermute | solution.py:180
  250.9 37.8 %collective-permute-start.32 = (bf16[256,1536]{1,0:T(8,128)(2,1)}, bf16[256,1536]{1,0:T(8,128)(2,1)}, u32[]{:S(2)}, u32[]{:S(2)}) collective-permute-start(bf16[256,1536]{1,0:T(8,128)(2,1)} %get-tuple-element.68.refs_1_), channel_id=1, source_target_pairs={{0,8},{8,0},{1,9},{9,1},{2,10},{10,2},{3,11},{11,3},{4,12},{12,4},... | collective-permute-start | bytes 2359304 | tf_op jit(solution)/shard_map/ppermute | solution.py:180
  261.9 48.9 %collective-permute-start.46 = (bf16[4,384,512]{2,1,0:T(8,128)(2,1)}, bf16[4,384,512]{2,1,0:T(8,128)(2,1)S(1)}, u32[]{:S(2)}, u32[]{:S(2)}) collective-permute-start(bf16[4,384,512]{2,1,0:T(8,128)(2,1)} %get-tuple-element.70.refs_2_.refs_1_), channel_id=1, source_target_pairs={{0,16},{16,0},{1,17},{17,1},{2,18},{18,2},{3,19},{19,3},{4,20},{20... | collective-permute-start | bytes 4718600 | tf_op jit(solution)/shard_map/ppermute | solution.py:180
  299.6 12.5 %collective-permute-start.43 = (bf16[384,256]{1,0:T(8,128)(2,1)}, bf16[384,256]{1,0:T(8,128)(2,1)S(1)}, u32[]{:S(2)}, u32[]{:S(2)}) collective-permute-start(bf16[384,256]{1,0:T(8,128)(2,1)} %get-tuple-element.126), channel_id=1, source_target_pairs={{0,1},{1,0},{2,3},{3,2},{4,5},{5,4},{6,7},{7,6},{8,9},{9,8},{10,11... | collective-permute-start | bytes 589832 | tf_op jit(solution)/shard_map/ppermute | solution.py:180
  301.2 17.4 %collective-permute-start.44 = (bf16[384,256]{1,0:T(8,128)(2,1)}, bf16[384,256]{1,0:T(8,128)(2,1)S(1)}, u32[]{:S(2)}, u32[]{:S(2)}) collective-permute-start(bf16[384,256]{1,0:T(8,128)(2,1)} %get-tuple-element.125), channel_id=1, source_target_pairs={{0,2},{1,3},{2,0},{3,1},{4,6},{5,7},{6,4},{7,5},{8,10},{9,11},{10,... | collective-permute-start | bytes 589832 | tf_op jit(solution)/shard_map/ppermute | solution.py:180
  302.3 16.3 %collective-permute-start.45 = (bf16[384,256]{1,0:T(8,128)(2,1)}, bf16[384,256]{1,0:T(8,128)(2,1)}, u32[]{:S(2)}, u32[]{:S(2)}) collective-permute-start(bf16[384,256]{1,0:T(8,128)(2,1)} %get-tuple-element.124), channel_id=1, source_target_pairs={{0,3},{1,2},{2,1},{3,0},{4,7},{5,6},{6,5},{7,4},{8,11},{9,10},{10,... | collective-permute-start | bytes 589832 | tf_op jit(solution)/shard_map/ppermute | solution.py:180
  322.3 82.0 %reduce-scatter.7.cloned.1.call-start = ((), (), s32[]{:S(2)}) async-start(), calls=%async_computation.7 | async-start | bytes 1966080 | tf_op jit(solution)/shard_map/reduce_scatter | solution.py:628
  323.7 33.3 %collective-permute-start.48 = (bf16[4,384,512]{2,1,0:T(8,128)(2,1)S(1)}, bf16[4,384,512]{2,1,0:T(8,128)(2,1)S(1)}, u32[]{:S(2)}, u32[]{:S(2)}) collective-permute-start(bf16[4,384,512]{2,1,0:T(8,128)(2,1)S(1)} %copy-done.27), channel_id=1, source_target_pairs={{0,16},{16,0},{1,17},{17,1},{2,18},{18,2},{3,19},{19,3},{4,20},{20... | collective-permute-start | bytes 4718600 | tf_op jit(solution)/shard_map/ppermute | solution.py:180
  337.3 20.9 %collective-permute-start.47 = (bf16[2,2,96,1024]{3,2,1,0:T(8,128)(2,1)}, bf16[2,2,96,1024]{3,2,1,0:T(8,128)(2,1)}, u32[]{:S(2)}, u32[]{:S(2)}) collective-permute-start(bf16[2,2,96,1024]{3,2,1,0:T(8,128)(2,1)} %get-tuple-element.86), channel_id=1, source_target_pairs={{0,4},{4,0},{1,5},{5,1},{2,6},{6,2},{3,7},{7,3},{8,12},{12,8},{9,1... | collective-permute-start | bytes 2359304 | tf_op jit(solution)/shard_map/ppermute | solution.py:180
  364.7 78.4 %reduce-scatter.9.cloned.1.call-start = ((), (), s32[]{:S(2)}) async-start(), calls=%async_computation.8 | async-start | bytes 1966080 | tf_op jit(solution)/shard_map/reduce_scatter | solution.py:628
  366.0 32.6 %collective-permute-start.50 = (bf16[4,384,512]{2,1,0:T(8,128)(2,1)S(1)}, bf16[4,384,512]{2,1,0:T(8,128)(2,1)S(1)}, u32[]{:S(2)}, u32[]{:S(2)}) collective-permute-start(bf16[4,384,512]{2,1,0:T(8,128)(2,1)S(1)} %copy-done.25), channel_id=1, source_target_pairs={{0,16},{16,0},{1,17},{17,1},{2,18},{18,2},{3,19},{19,3},{4,20},{20... | collective-permute-start | bytes 4718600 | tf_op jit(solution)/shard_map/ppermute | solution.py:180
  366.7 11.1 %collective-permute-start.49 = (bf16[2,96,1024]{2,1,0:T(8,128)(2,1)}, bf16[2,96,1024]{2,1,0:T(8,128)(2,1)S(1)}, u32[]{:S(2)}, u32[]{:S(2)}) collective-permute-start(bf16[2,96,1024]{2,1,0:T(8,128)(2,1)} %fusion.36.refs_1_), channel_id=1, source_target_pairs={{0,8},{8,0},{1,9},{9,1},{2,10},{10,2},{3,11},{11,3},{4,12},{12,4},... | collective-permute-start | bytes 1179656 | tf_op jit(solution)/shard_map/ppermute | solution.py:180
  404.2 101.9 %reduce-scatter.11.cloned.1.call-start = ((), (), s32[]{:S(2)}) async-start(), calls=%async_computation.9 | async-start | bytes 3932160 | tf_op jit(solution)/shard_map/reduce_scatter | solution.py:696
  407.7 11.2 %collective-permute-start.52 = (bf16[2,96,1024]{2,1,0:T(8,128)(2,1)S(1)}, bf16[2,96,1024]{2,1,0:T(8,128)(2,1)S(1)}, u32[]{:S(2)}, u32[]{:S(2)}) collective-permute-start(bf16[2,96,1024]{2,1,0:T(8,128)(2,1)S(1)} %fusion.37.refs_1_), channel_id=1, source_target_pairs={{0,8},{8,0},{1,9},{9,1},{2,10},{10,2},{3,11},{11,3},{4,12},{12,4},... | collective-permute-start | bytes 1179656 | tf_op jit(solution)/shard_map/ppermute | solution.py:180
  443.1 145.8 %all-gather.8.cloned.1.call-start = ((), (), s32[]{:S(2)}) async-start(), calls=%async_computation.10 | async-start | bytes 3932160 | tf_op jit(solution)/shard_map/all_gather | solution.py:710
  460.6 42.9 %collective-permute-start.54 = (bf16[2,192,1536]{2,1,0:T(8,128)(2,1)}, bf16[2,192,1536]{2,1,0:T(8,128)(2,1)}, u32[]{:S(2)}, u32[]{:S(2)}) collective-permute-start(bf16[2,192,1536]{2,1,0:T(8,128)(2,1)} %dynamic-slice_bitcast_fusion.2), channel_id=1, source_target_pairs={{0,16},{16,0},{1,17},{17,1},{2,18},{18,2},{3,19},{19,3},{4,20},{20... | collective-permute-start | bytes 3538952 | tf_op jit(solution)/shard_map/ppermute | solution.py:180
  464.4 37.2 %collective-permute-start.56 = (bf16[2,192,768]{2,1,0:T(8,128)(2,1)}, bf16[2,192,768]{2,1,0:T(8,128)(2,1)}, u32[]{:S(2)}, u32[]{:S(2)}) collective-permute-start(bf16[2,192,768]{2,1,0:T(8,128)(2,1)} %dynamic-slice_bitcast_fusion.4), channel_id=1, source_target_pairs={{0,16},{16,0},{1,17},{17,1},{2,18},{18,2},{3,19},{19,3},{4,20},{20... | collective-permute-start | bytes 1769480 | tf_op jit(solution)/shard_map/ppermute | solution.py:180
  519.6 7.7 %collective-permute-start.67 = (bf16[192,512]{1,0:T(8,128)(2,1)S(1)}, bf16[192,512]{1,0:T(8,128)(2,1)S(1)}, u32[]{:S(2)}, u32[]{:S(2)}) collective-permute-start(bf16[192,512]{1,0:T(8,128)(2,1)S(1)} %dynamic-slice_bitcast_fusion.8), channel_id=1, source_target_pairs={{0,8},{8,0},{1,9},{9,1},{2,10},{10,2},{3,11},{11,3},{4,12},{12,4},... | collective-permute-start | bytes 589832 | tf_op jit(solution)/shard_map/ppermute | solution.py:180
  530.4 10.1 %collective-permute-start.62 = (bf16[192,768]{1,0:T(8,128)(2,1)S(1)}, bf16[192,768]{1,0:T(8,128)(2,1)}, u32[]{:S(2)}, u32[]{:S(2)}) collective-permute-start(bf16[192,768]{1,0:T(8,128)(2,1)S(1)} %dynamic-slice_bitcast_fusion.5), channel_id=1, source_target_pairs={{0,8},{8,0},{1,9},{9,1},{2,10},{10,2},{3,11},{11,3},{4,12},{12,4},... | collective-permute-start | bytes 884744 | tf_op jit(solution)/shard_map/ppermute | solution.py:180
  531.5 18.7 %collective-permute-start.63 = (bf16[192,1536]{1,0:T(8,128)(2,1)S(1)}, bf16[192,1536]{1,0:T(8,128)(2,1)S(1)}, u32[]{:S(2)}, u32[]{:S(2)}) collective-permute-start(bf16[192,1536]{1,0:T(8,128)(2,1)S(1)} %dynamic-slice_bitcast_fusion.3), channel_id=1, source_target_pairs={{0,8},{8,0},{1,9},{9,1},{2,10},{10,2},{3,11},{11,3},{4,12},{12,4},... | collective-permute-start | bytes 1769480 | tf_op jit(solution)/shard_map/ppermute | solution.py:180
  533.3 8.3 %collective-permute-start.57 = (f32[3,1536]{1,0:T(4,128)}, f32[3,1536]{1,0:T(4,128)S(1)}, u32[]{:S(2)}, u32[]{:S(2)}) collective-permute-start(f32[3,1536]{1,0:T(4,128)} %after.60), channel_id=1, source_target_pairs={{0,16},{16,0},{1,17},{17,1},{2,18},{18,2},{3,19},{19,3},{4,20},{20... | collective-permute-start | bytes 55304 | tf_op jit(solution)/shard_map/ppermute | solution.py:180
  543.0 7.6 %collective-permute-start.58 = (f32[3,1536]{1,0:T(4,128)}, f32[3,1536]{1,0:T(4,128)}, u32[]{:S(2)}, u32[]{:S(2)}) collective-permute-start(f32[3,1536]{1,0:T(4,128)} %add.511), channel_id=1, source_target_pairs={{0,8},{8,0},{1,9},{9,1},{2,10},{10,2},{3,11},{11,3},{4,12},{12,4},... | collective-permute-start | bytes 55304 | tf_op jit(solution)/shard_map/ppermute | solution.py:180
  552.3 24.4 %collective-permute-start.64 = (bf16[192,384]{1,0:T(8,128)(2,1)S(1)}, bf16[192,384]{1,0:T(8,128)(2,1)S(1)}, u32[]{:S(2)}, u32[]{:S(2)}) collective-permute-start(bf16[192,384]{1,0:T(8,128)(2,1)S(1)} %bitcast.279), channel_id=1, source_target_pairs={{0,1},{1,0},{2,3},{3,2},{4,5},{5,4},{6,7},{7,6},{8,9},{9,8},{10,11... | collective-permute-start | bytes 442376 | tf_op jit(solution)/shard_map/ppermute | solution.py:180
  552.4 24.3 %collective-permute-start.65 = (bf16[192,384]{1,0:T(8,128)(2,1)S(1)}, bf16[192,384]{1,0:T(8,128)(2,1)S(1)}, u32[]{:S(2)}, u32[]{:S(2)}) collective-permute-start(bf16[192,384]{1,0:T(8,128)(2,1)S(1)} %bitcast.280), channel_id=1, source_target_pairs={{0,2},{1,3},{2,0},{3,1},{4,6},{5,7},{6,4},{7,5},{8,10},{9,11},{10,... | collective-permute-start | bytes 442376 | tf_op jit(solution)/shard_map/ppermute | solution.py:180
  554.0 22.8 %collective-permute-start.66 = (bf16[192,384]{1,0:T(8,128)(2,1)S(1)}, bf16[192,384]{1,0:T(8,128)(2,1)S(1)}, u32[]{:S(2)}, u32[]{:S(2)}) collective-permute-start(bf16[192,384]{1,0:T(8,128)(2,1)S(1)} %bitcast.281), channel_id=1, source_target_pairs={{0,3},{1,2},{2,1},{3,0},{4,7},{5,6},{6,5},{7,4},{8,11},{9,10},{10,... | collective-permute-start | bytes 442376 | tf_op jit(solution)/shard_map/ppermute | solution.py:180
  557.0 16.4 %collective-permute-start.60 = (f32[3,1536]{1,0:T(4,128)S(1)}, f32[3,1536]{1,0:T(4,128)S(1)}, u32[]{:S(2)}, u32[]{:S(2)}) collective-permute-start(f32[3,1536]{1,0:T(4,128)S(1)} %add.513), channel_id=1, source_target_pairs={{0,1},{1,0},{2,3},{3,2},{4,5},{5,4},{6,7},{7,6},{8,9},{9,8},{10,11... | collective-permute-start | bytes 55304 | tf_op jit(solution)/shard_map/ppermute | solution.py:180
  573.4 12.5 %collective-permute-start.61 = (f32[3,1536]{1,0:T(4,128)S(1)}, f32[3,1536]{1,0:T(4,128)S(1)}, u32[]{:S(2)}, u32[]{:S(2)}) collective-permute-start(f32[3,1536]{1,0:T(4,128)S(1)} %add.514), channel_id=1, source_target_pairs={{0,2},{1,3},{2,0},{3,1},{4,6},{5,7},{6,4},{7,5},{8,10},{9,11},{10,... | collective-permute-start | bytes 55304 | tf_op jit(solution)/shard_map/ppermute | solution.py:180
  (105 other events, 542.0 us)
Sparse Core Ops, SparseCore 0:
  57.9 111.3 all-gather.3
  218.1 75.4 all-gather.5
  322.4 35.0 reduce-scatter.4
  364.8 36.8 reduce-scatter.6
  404.4 38.6 reduce-scatter.8
  445.8 59.2 reduce-scatter.10
  513.5 75.3 all-gather.7

commit v6 on v4

--- a/solution.py
+++ b/solution.py
@@ -363,8 +363,8 @@
     up = dot(hidden, whole_block(dims, wu_ref), 1, 0)
     sig = jax.nn.sigmoid(gate)
     act = gate * sig
-    slope_ref[...] = up * (sig * (1.0 + gate * (1.0 - sig)))
-    act_ref[...] = act
+    slope_ref[...] = (up * (sig * (1.0 + gate * (1.0 - sig)))).astype(BF)
+    act_ref[...] = act.astype(BF)
     inner = (act * up).astype(BF)
     inner_ref[...] = inner
     add_up(z, dot(inner, whole_block(dims, wd_ref), 1, 1), acc, out_ref)
@@ -394,8 +394,8 @@
     return pl.pallas_call(
         functools.partial(ffn_forward_kernel, dims),
         out_shape=(
-            shape((rows, nz * hs), F32),
-            shape((rows, nz * hs), F32),
+            shape((rows, nz * hs), BF),
+            shape((rows, nz * hs), BF),
             shape((rows, nz * hs), BF),
             shape((rows, width), kind),
         ),

time: 609 us -> 608 us (level)
  starting transfers between devices: 81.9 us -> 91 us
  waiting for transfers between devices: 234 us -> 226 us
    ppermute x70, starting transfers between devices: 81.4 us -> 90.5 us  [swap(): return lax.ppermute(values, axis, [(i, i ^ step) for i in range(size)])]
where the time goes in v6:
time: 608 us; the launch traced here: 601 us
  waiting for transfers between devices  226 us (37%)
  Pallas kernels  109 us (18%)
  starting transfers between devices  91 us (15%)
  other arithmetic  77 us (13%)
  local copies, waits for them, and re-layouts  54.8 us (9%)
  matrix products  25.3 us (4%)
  between operations  18.2 us (3%)
    ppermute x70, waiting for transfers between devices, swap(): return lax.ppermute(values, axis, [(i, i ^ step) for i in range(size)])  214 us
    ppermute x70, starting transfers between devices, swap(): return lax.ppermute(values, axis, [(i, i ^ step) for i in range(size)])  90.5 us
    unnamed x197, local copies, waits for them, and re-layouts  35.9 us
    pallas_call x2, Pallas kernels, ffn_backward(): pl.pallas_call(functools.partial(ffn_backward_kernel, dims), out_shape=(s...  25.5 us
    dot_general x7, matrix products, dot(): lax.dot_general(a, b, (((ca,), (cb,)), ((), ())), preferred_element_type=...  25.3 us
    pallas_call x2, Pallas kernels, ffn_forward(): pl.pallas_call(functools.partial(ffn_forward_kernel, dims), out_shape=(sh...  23.8 us
    pallas_call x2, Pallas kernels, weight_grad(): pl.pallas_call(functools.partial(weight_grad_kernel, dims, pieces, count)...  21.9 us
    pallas_call x2, Pallas kernels, attn_bwd(): pl.pallas_call(functools.partial(bwd_kernel, scale2, tq, tk, group, len(k...  20.7 us
  transfers between devices with their start and end apart: 77, of which 32 were waited for; matrix products, arithmetic and copies ran while one was open for 17% of the time, Pallas kernels for 16%

profile of v6, /device:TPU:0, one launch (start us, length us, event | category | flops | bytes accessed | tf_op | source)
XLA Modules:
  0.0 600.9 jit_solution(12714988777608357816)
XLA Ops:
  9.7 3.0 collective-permute-start
  15.8 2.6 collective-permute-start.5
  23.6 5.9 collective-permute-done.5.refs_3_
  34.0 2.4 pad_maximum_fusion.2.refs_0_
  39.5 2.6 fusion.2
  44.5 2.7 put_blocks.2
  48.5 5.4 collective-permute-done.28.refs_0_
  60.7 2.8 fusion.4.refs_0_
  72.7 3.9 fusion.9
  83.0 4.7 collective-permute-done.16.refs_3_
  87.7 9.6 %collective-permute-done.17.refs_4_ = bf16[96,1536]{1,0:T(8,128)(2,1)S(1)} collective-permute-done((bf16[96,1536]{1,0:T(8,128)(2,1)S(1)}, bf16[96,1536]{1,0:T(8,128)(2,1)S(1)}, u32[]{:S(2)}, u32[]{:S(2)}) %collective-permute-start.17) | collective-permute-done | bytes 294944 | tf_op jit(solution)/shard_map/ppermute | solution.py:180
  97.4 2.5 convert_reduce_fusion
  101.5 2.2 copy-done
  106.5 2.3 collective-permute-done.24.refs_1_
  108.8 11.9 %attend.1 = (bf16[384,1024]{1,0:T(8,128)(2,1)S(1)}, f32[384,1024]{1,0:T(8,128)S(1)}, f32[2,2,1024]{2,1,0:T(2,128)S(1)}) custom-call(s32[4,4]{1,0:T(4,128)S(1)} %pad_add_fusion.2.bounds, s32[4]{0:T(128)S(1)} %pad_add_fusion.4.place, bf16[384,1024]{1,0:T(8,128)(2,1)S(1)} %copy-done.1, bf16[2,2,192,1024]{3,2,1,0:T(8,128)(2,1)S(1)} %pad_maximum_fusion.refs_0_, ...), custom_call_target="tpu_custom_call" | custom-call | flops 12000000000 | bytes 1000000 | tf_op jit(solution)/shard_map/attend/pallas_call | solution.py:85
  127.0 7.4 %collective-permute-done.25 = bf16[384,256]{1,0:T(8,128)(2,1)S(1)} collective-permute-done((bf16[384,256]{1,0:T(8,128)(2,1)S(1)}, bf16[384,256]{1,0:T(8,128)(2,1)S(1)}, u32[]{:S(2)}, u32[]{:S(2)}) %collective-permute-start.25) | collective-permute-done | bytes 196640 | tf_op jit(solution)/shard_map/ppermute | solution.py:180
  134.5 4.8 collective-permute-done.26
  139.3 11.8 %collective-permute-done.27 = bf16[384,256]{1,0:T(8,128)(2,1)S(1)} collective-permute-done((bf16[384,256]{1,0:T(8,128)(2,1)S(1)}, bf16[384,256]{1,0:T(8,128)(2,1)S(1)}, u32[]{:S(2)}, u32[]{:S(2)}) %collective-permute-start.27) | collective-permute-done | bytes 196640 | tf_op jit(solution)/shard_map/ppermute | solution.py:180
  151.1 4.2 multiply_reduce_fusion.2
  156.3 17.0 %collective-permute-start.29 = (bf16[256,1536]{1,0:T(8,128)(2,1)}, bf16[256,1536]{1,0:T(8,128)(2,1)}, u32[]{:S(2)}, u32[]{:S(2)}) collective-permute-start(bf16[256,1536]{1,0:T(8,128)(2,1)} %multiply_convert_fusion.1.h_ref.refs_0_), channel_id=1, source_target_pairs={{0,8},{8,0},{1,9},{9,1},{2,10},{10,2},{3,11},{11,3},{4,12},{12,4},... | collective-permute-start | bytes 2359304 | tf_op jit(solution)/shard_map/ppermute | solution.py:180
  173.3 11.9 %feed_forward.2 = (bf16[256,2048]{1,0:T(8,128)(2,1)}, bf16[256,2048]{1,0:T(8,128)(2,1)}, bf16[256,2048]{1,0:T(8,128)(2,1)}, f32[256,1536]{1,0:T(8,128)}) custom-call(bf16[256,1536]{1,0:T(8,128)(2,1)} %multiply_convert_fusion.1.h_ref.refs_0_, bf16[4,4,3,384,512]{4,3,2,1,0:T(8,128)(2,1)} %bitcast.227, bf16[4,4,3,384,512]{4,3,2,1,0:T(8,128)(2,1)} %bitcast.228, ...), custom_call_target="tpu_custom_call" | custom-call | flops 6000000000 | bytes 1000000 | tf_op jit(solution)/shard_map/feed_forward/pallas_call | solution.py:394
  185.3 4.8 collective-permute-done.29.refs_0_
  190.1 11.8 %feed_forward.3 = (bf16[256,2048]{1,0:T(8,128)(2,1)}, bf16[256,2048]{1,0:T(8,128)(2,1)}, bf16[256,2048]{1,0:T(8,128)(2,1)}, bf16[256,1536]{1,0:T(8,128)(2,1)}) custom-call(bf16[256,1536]{1,0:T(8,128)(2,1)} %after.37.h_ref.refs_2_, bf16[4,4,3,384,512]{4,3,2,1,0:T(8,128)(2,1)} %bitcast.230, bf16[4,4,3,384,512]{4,3,2,1,0:T(8,128)(2,1)} %bitcast.231, ...), custom_call_target="tpu_custom_call" | custom-call | flops 6000000000 | bytes 1000000 | tf_op jit(solution)/shard_map/feed_forward/pallas_call | solution.py:394
  201.9 2.4 collective-permute-start.30
  205.0 17.1 %collective-permute-done.30 = bf16[256,1536]{1,0:T(8,128)(2,1)S(1)} collective-permute-done((bf16[256,1536]{1,0:T(8,128)(2,1)}, bf16[256,1536]{1,0:T(8,128)(2,1)S(1)}, u32[]{:S(2)}, u32[]{:S(2)}) %collective-permute-start.30) | collective-permute-done | bytes 786464 | tf_op jit(solution)/shard_map/ppermute | solution.py:180
  225.8 2.4 collective-permute-start.31
  228.8 13.7 %feed_forward_back.2 = (bf16[256,2048]{1,0:T(8,128)(2,1)}, bf16[256,2048]{1,0:T(8,128)(2,1)}, f32[256,1536]{1,0:T(8,128)}) custom-call(bf16[256,1536]{1,0:T(8,128)(2,1)} %get-tuple-element.62.g_ref.refs_0_, bf16[4,4,3,384,512]{4,3,2,1,0:T(8,128)(2,1)} %bitcast.233, bf16[4,4,3,384,512]{4,3,2,1,0:T(8,128)(2,1)} %bitcast.234, ...), custom_call_target="tpu_custom_call" | custom-call | flops 6000000000 | bytes 1000000 | tf_op jit(solution)/shard_map/feed_forward_back/pallas_call | solution.py:430
  243.0 3.4 collective-permute-done.31.refs_0_
  247.3 11.8 %feed_forward_back.3 = (bf16[256,2048]{1,0:T(8,128)(2,1)}, bf16[256,2048]{1,0:T(8,128)(2,1)}, bf16[256,1536]{1,0:T(8,128)(2,1)}) custom-call(bf16[256,1536]{1,0:T(8,128)(2,1)} %after.39.g_ref.refs_2_, bf16[4,4,3,384,512]{4,3,2,1,0:T(8,128)(2,1)} %bitcast.236, bf16[4,4,3,384,512]{4,3,2,1,0:T(8,128)(2,1)} %bitcast.237, bf16[4,4,3,384,512]{4,3,2,1,0:T(8,128)(2,1)} %bitcast.238, ...), custom_call_target="tpu_custom_call" | custom-call | flops 6000000000 | bytes 1000000 | tf_op jit(solution)/shard_map/feed_forward_back/pallas_call | solution.py:430
  262.6 9.3 %weight_grad.2 = (bf16[4,384,512]{2,1,0:T(8,128)(2,1)}, bf16[4,384,512]{2,1,0:T(8,128)(2,1)}) custom-call(s32[2]{0:T(128)} %pad_add_fusion.5.where, bf16[256,1536]{1,0:T(8,128)(2,1)} %get-tuple-element.62.g_ref.refs_0_, bf16[256,1536]{1,0:T(8,128)(2,1)} %collective-permute-done.33.refs_1_, bf16[256,1536]{1,0:T(8,128)(2,1)} %after.39.g_ref.refs_2_, ...), custom_call_target="tpu_custom_call" | custom-call | flops 5000000000 | bytes 1000000 | tf_op jit(solution)/shard_map/weight_grad/pallas_call | solution.py:480
  272.0 12.6 %weight_grad.3 = (bf16[4,384,512]{2,1,0:T(8,128)(2,1)}, bf16[4,384,512]{2,1,0:T(8,128)(2,1)}, bf16[4,384,512]{2,1,0:T(8,128)(2,1)}, bf16[4,384,512]{2,1,0:T(8,128)(2,1)}) custom-call(s32[2]{0:T(128)} %pad_add_fusion.5.where, bf16[256,1536]{1,0:T(8,128)(2,1)} %multiply_convert_fusion.1.h_ref.refs_0_, bf16[256,1536]{1,0:T(8,128)(2,1)} %collective-permute-done.37.refs_1_, ...), custom_call_target="tpu_custom_call" | custom-call | flops 5000000000 | bytes 1000000 | tf_op jit(solution)/shard_map/weight_grad/pallas_call | solution.py:480
  288.8 3.2 fusion.75
  292.0 4.0 convolution_convert_fusion.3
  298.4 2.7 collective-permute-start.45
  301.1 7.6 %collective-permute-done.46.refs_0_ = bf16[4,384,512]{2,1,0:T(8,128)(2,1)} collective-permute-done((bf16[4,384,512]{2,1,0:T(8,128)(2,1)}, bf16[4,384,512]{2,1,0:T(8,128)(2,1)}, u32[]{:S(2)}, u32[]{:S(2)}) %collective-permute-start.46) | collective-permute-done | bytes 1572896 | tf_op jit(solution)/shard_map/ppermute | solution.py:180
  308.7 5.1 collective-permute-done.44.refs_2_
  315.2 3.0 add_convert_fusion.2.refs_4_
  324.0 10.4 %attend_back.2 = (f32[192,1024]{1,0:T(8,128)}, bf16[2,2,96,1024]{3,2,1,0:T(8,128)(2,1)}, bf16[2,2,96,1024]{3,2,1,0:T(8,128)(2,1)}) custom-call(s32[4,4]{1,0:T(4,128)} %pad_add_fusion.3.bounds, s32[4]{0:T(128)} %copy-done.20, bf16[384,1024]{1,0:T(8,128)(2,1)} %after.33.refs_1_.q_ref, bf16[2,2,192,1024]{3,2,1,0:T(8,128)(2,1)} %copy-done.11, ...), custom_call_target="tpu_custom_call" | custom-call | flops 12000000000 | bytes 1000000 | tf_op jit(solution)/shard_map/attend_back/pallas_call | solution.py:152
  334.4 4.0 collective-permute-start.47
  343.2 11.3 %collective-permute-done.48.refs_0_ = bf16[4,384,512]{2,1,0:T(8,128)(2,1)} collective-permute-done((bf16[4,384,512]{2,1,0:T(8,128)(2,1)S(1)}, bf16[4,384,512]{2,1,0:T(8,128)(2,1)}, u32[]{:S(2)}, u32[]{:S(2)}) %collective-permute-start.48) | collective-permute-done | bytes 1572896 | tf_op jit(solution)/shard_map/ppermute | solution.py:180
  354.5 3.0 add_convert_fusion.1.refs_2_
  362.2 10.3 %attend_back.3 = (f32[192,1024]{1,0:T(8,128)}, bf16[2,2,96,1024]{3,2,1,0:T(8,128)(2,1)}, bf16[2,2,96,1024]{3,2,1,0:T(8,128)(2,1)}) custom-call(s32[4,4]{1,0:T(4,128)} %pad_add_fusion.3.bounds, s32[4]{0:T(128)} %copy-done.20, bf16[384,1024]{1,0:T(8,128)(2,1)} %after.33.refs_1_.q_ref, bf16[2,2,192,1024]{3,2,1,0:T(8,128)(2,1)} %copy-done.11, ...), custom_call_target="tpu_custom_call" | custom-call | flops 12000000000 | bytes 1000000 | tf_op jit(solution)/shard_map/attend_back/pallas_call | solution.py:152
  372.4 20.4 %collective-permute-done.50.refs_0_ = bf16[4,384,512]{2,1,0:T(8,128)(2,1)S(1)} collective-permute-done((bf16[4,384,512]{2,1,0:T(8,128)(2,1)S(1)}, bf16[4,384,512]{2,1,0:T(8,128)(2,1)S(1)}, u32[]{:S(2)}, u32[]{:S(2)}) %collective-permute-start.50) | collective-permute-done | bytes 1572896 | tf_op jit(solution)/shard_map/ppermute | solution.py:180
  395.5 3.0 add_convert_fusion.refs_1_
  402.1 6.0 collective-permute-start.52
  409.6 7.9 %collective-permute-done.52.refs_0_ = bf16[2,96,1024]{2,1,0:T(8,128)(2,1)S(1)} collective-permute-done((bf16[2,96,1024]{2,1,0:T(8,128)(2,1)S(1)}, bf16[2,96,1024]{2,1,0:T(8,128)(2,1)S(1)}, u32[]{:S(2)}, u32[]{:S(2)}) %collective-permute-start.52) | collective-permute-done | bytes 393248 | tf_op jit(solution)/shard_map/ppermute | solution.py:180
  424.1 4.1 convolution_convert_fusion.1.refs_0_
  428.2 11.3 %reduce-scatter.9.cloned.1.call-done = bf16[384,512]{1,0:T(8,128)(2,1)} async-done(((bf16[1536,512]{1,0:T(8,128)(2,1)}), bf16[384,512]{1,0:T(8,128)(2,1)}) %reduce-scatter.9.cloned.1.call-update) | async-done | bytes 393232 | tf_op jit(solution)/shard_map/reduce_scatter | solution.py:625
  440.8 2.6 convolution_convert_fusion
  445.6 5.2 convolution_convert_fusion.2
  453.0 3.0 fusion.7
  463.2 34.9 %collective-permute-done.56 = bf16[2,192,768]{2,1,0:T(8,128)(2,1)} collective-permute-done((bf16[2,192,768]{2,1,0:T(8,128)(2,1)}, bf16[2,192,768]{2,1,0:T(8,128)(2,1)}, u32[]{:S(2)}, u32[]{:S(2)}) %collective-permute-start.56) | collective-permute-done | bytes 589856 | tf_op jit(solution)/shard_map/ppermute | solution.py:180
  500.1 2.6 fusion.14.refs_1_
  504.5 2.5 fusion.23
  507.0 2.8 fusion.21.refs_1_
  512.6 3.5 collective-permute-done.69
  519.6 4.1 collective-permute-done.67
  531.3 5.7 collective-permute-done.62
  540.4 6.2 %collective-permute-done.63 = bf16[192,1536]{1,0:T(8,128)(2,1)S(1)} collective-permute-done((bf16[192,1536]{1,0:T(8,128)(2,1)S(1)}, bf16[192,1536]{1,0:T(8,128)(2,1)S(1)}, u32[]{:S(2)}, u32[]{:S(2)}) %collective-permute-start.63) | collective-permute-done | bytes 589856 | tf_op jit(solution)/shard_map/ppermute | solution.py:180
  550.5 2.9 collective-permute-start.66
  555.0 14.8 %collective-permute-done.60 = f32[3,1536]{1,0:T(4,128)S(1)} collective-permute-done((f32[3,1536]{1,0:T(4,128)S(1)}, f32[3,1536]{1,0:T(4,128)S(1)}, u32[]{:S(2)}, u32[]{:S(2)}) %collective-permute-start.60) | collective-permute-done | bytes 18464 | tf_op jit(solution)/shard_map/ppermute | solution.py:180
  569.9 3.4 collective-permute-start.61
  574.1 8.3 %collective-permute-done.61 = f32[3,1536]{1,0:T(4,128)S(1)} collective-permute-done((f32[3,1536]{1,0:T(4,128)S(1)}, f32[3,1536]{1,0:T(4,128)S(1)}, u32[]{:S(2)}, u32[]{:S(2)}) %collective-permute-start.61) | collective-permute-done | bytes 18464 | tf_op jit(solution)/shard_map/ppermute | solution.py:180
  585.4 5.6 bitcast_convert_fusion
  (463 shorter events, 146.6 us)
Async XLA Ops:
  7.2 166.2 %all-gather.4.cloned.1.call-start = ((), (), s32[]{:S(2)}) async-start(), calls=%async_computation.4 | async-start | bytes 20054016 | tf_op jit(solution)/shard_map/all_gather | solution.py:535
  9.7 10.5 %collective-permute-start = (bf16[208,768]{1,0:T(8,128)(2,1)S(1)}, bf16[208,768]{1,0:T(8,128)(2,1)S(1)}, u32[]{:S(2)}, u32[]{:S(2)}) collective-permute-start(bf16[208,768]{1,0:T(8,128)(2,1)S(1)} %pad_maximum_fusion.14.refs_0_), channel_id=1, source_target_pairs={{0,8},{8,0},{1,9},{9,1},{2,10},{10,2},{3,11},{11,3},{4,12},{12,4},... | collective-permute-start | bytes 958472 | tf_op jit(solution)/shard_map/ppermute | solution.py:180
  12.7 9.4 %collective-permute-start.1 = (bf16[208,768]{1,0:T(8,128)(2,1)S(1)}, bf16[208,768]{1,0:T(8,128)(2,1)S(1)}, u32[]{:S(2)}, u32[]{:S(2)}) collective-permute-start(bf16[208,768]{1,0:T(8,128)(2,1)S(1)} %pad_maximum_fusion.14.refs_0_), channel_id=1, source_target_pairs={{0,16},{16,0},{1,17},{17,1},{2,18},{18,2},{3,19},{19,3},{4,20},{20... | collective-permute-start | bytes 958472 | tf_op jit(solution)/shard_map/ppermute | solution.py:180
  14.2 9.4 %collective-permute-start.4 = (bf16[192,384]{1,0:T(8,128)(2,1)}, bf16[192,384]{1,0:T(8,128)(2,1)S(1)}, u32[]{:S(2)}, u32[]{:S(2)}) collective-permute-start(bf16[192,384]{1,0:T(8,128)(2,1)} %bitcast.276), channel_id=1, source_target_pairs={{0,1},{1,0},{2,3},{3,2},{4,5},{5,4},{6,7},{7,6},{8,9},{9,8},{10,11... | collective-permute-start | bytes 442376 | tf_op jit(solution)/shard_map/ppermute | solution.py:180
  15.8 13.8 %collective-permute-start.5 = (bf16[192,384]{1,0:T(8,128)(2,1)}, bf16[192,384]{1,0:T(8,128)(2,1)S(1)}, u32[]{:S(2)}, u32[]{:S(2)}) collective-permute-start(bf16[192,384]{1,0:T(8,128)(2,1)} %bitcast.277), channel_id=1, source_target_pairs={{0,2},{1,3},{2,0},{3,1},{4,6},{5,7},{6,4},{7,5},{8,10},{9,11},{10,... | collective-permute-start | bytes 442376 | tf_op jit(solution)/shard_map/ppermute | solution.py:180
  18.4 11.2 %collective-permute-start.6 = (bf16[192,384]{1,0:T(8,128)(2,1)}, bf16[192,384]{1,0:T(8,128)(2,1)S(1)}, u32[]{:S(2)}, u32[]{:S(2)}) collective-permute-start(bf16[192,384]{1,0:T(8,128)(2,1)} %bitcast.278), channel_id=1, source_target_pairs={{0,3},{1,2},{2,1},{3,0},{4,7},{5,6},{6,5},{7,4},{8,11},{9,10},{10,... | collective-permute-start | bytes 442376 | tf_op jit(solution)/shard_map/ppermute | solution.py:180
  20.2 11.8 %collective-permute-start.3 = (bf16[112,768]{1,0:T(8,128)(2,1)S(1)}, bf16[112,768]{1,0:T(8,128)(2,1)S(1)}, u32[]{:S(2)}, u32[]{:S(2)}) collective-permute-start(bf16[112,768]{1,0:T(8,128)(2,1)S(1)} %slice.188), channel_id=1, source_target_pairs={{0,16},{16,0},{1,17},{17,1},{2,18},{18,2},{3,19},{19,3},{4,20},{20... | collective-permute-start | bytes 516104 | tf_op jit(solution)/shard_map/ppermute | solution.py:180
  22.1 10.0 %collective-permute-start.2 = (bf16[96,768]{1,0:T(8,128)(2,1)S(1)}, bf16[96,768]{1,0:T(8,128)(2,1)S(1)}, u32[]{:S(2)}, u32[]{:S(2)}) collective-permute-start(bf16[96,768]{1,0:T(8,128)(2,1)S(1)} %slice.187), channel_id=1, source_target_pairs={{0,8},{8,0},{1,9},{9,1},{2,10},{10,2},{3,11},{11,3},{4,12},{12,4},... | collective-permute-start | bytes 442376 | tf_op jit(solution)/shard_map/ppermute | solution.py:180
  30.7 11.5 %collective-permute-start.12 = (bf16[192,1536]{1,0:T(8,128)(2,1)S(1)}, bf16[192,1536]{1,0:T(8,128)(2,1)S(1)}, u32[]{:S(2)}, u32[]{:S(2)}) collective-permute-start(bf16[192,1536]{1,0:T(8,128)(2,1)S(1)} %pad_maximum_fusion.13.refs_0_), channel_id=1, source_target_pairs={{0,16},{16,0},{1,17},{17,1},{2,18},{18,2},{3,19},{19,3},{4,20},{20... | collective-permute-start | bytes 1769480 | tf_op jit(solution)/shard_map/ppermute | solution.py:180
  31.2 12.1 %collective-permute-start.7 = (bf16[208,768]{1,0:T(8,128)(2,1)S(1)}, bf16[208,768]{1,0:T(8,128)(2,1)S(1)}, u32[]{:S(2)}, u32[]{:S(2)}) collective-permute-start(bf16[208,768]{1,0:T(8,128)(2,1)S(1)} %pad_maximum_fusion.14.refs_0_), channel_id=1, source_target_pairs={{0,4},{4,0},{1,5},{5,1},{2,6},{6,2},{3,7},{7,3},{8,12},{12,8},{9,1... | collective-permute-start | bytes 958472 | tf_op jit(solution)/shard_map/ppermute | solution.py:180
  38.3 15.6 %collective-permute-start.28 = (bf16[3,192,512]{2,1,0:T(8,128)(2,1)}, bf16[3,192,512]{2,1,0:T(8,128)(2,1)}, u32[]{:S(2)}, u32[]{:S(2)}) collective-permute-start(bf16[3,192,512]{2,1,0:T(8,128)(2,1)} %constant_dynamic-slice_fusion.2), channel_id=1, source_target_pairs={{0,8},{8,0},{1,9},{9,1},{2,10},{10,2},{3,11},{11,3},{4,12},{12,4},... | collective-permute-start | bytes 1769480 | tf_op jit(solution)/shard_map/ppermute | solution.py:180
  57.9 234.2 %all-gather.6.cloned.1.call-start = ((), (), s32[]{:S(2)}) async-start(), calls=%async_computation.5 | async-start | bytes 3932160 | tf_op jit(solution)/shard_map/all_gather | solution.py:609
  60.1 21.4 %collective-permute-start.18 = (bf16[192,1536]{1,0:T(8,128)(2,1)S(1)}, bf16[192,1536]{1,0:T(8,128)(2,1)S(1)}, u32[]{:S(2)}, u32[]{:S(2)}) collective-permute-start(bf16[192,1536]{1,0:T(8,128)(2,1)S(1)} %pad_maximum_fusion.13.refs_0_), channel_id=1, source_target_pairs={{0,4},{4,0},{1,5},{5,1},{2,6},{6,2},{3,7},{7,3},{8,12},{12,8},{9,1... | collective-permute-start | bytes 1769480 | tf_op jit(solution)/shard_map/ppermute | solution.py:180
  60.1 20.9 %collective-permute-start.15 = (bf16[192,1536]{1,0:T(8,128)(2,1)}, bf16[192,1536]{1,0:T(8,128)(2,1)S(1)}, u32[]{:S(2)}, u32[]{:S(2)}) collective-permute-start(bf16[192,1536]{1,0:T(8,128)(2,1)} %after.32), channel_id=1, source_target_pairs={{0,8},{8,0},{1,9},{9,1},{2,10},{10,2},{3,11},{11,3},{4,12},{12,4},... | collective-permute-start | bytes 1769480 | tf_op jit(solution)/shard_map/ppermute | solution.py:180
  71.1 8.8 %collective-permute-start.13 = (s32[1,1024]{1,0:T(1,128)}, s32[1,1024]{1,0:T(1,128)S(1)}, u32[]{:S(2)}, u32[]{:S(2)}) collective-permute-start(s32[1,1024]{1,0:T(1,128)} %after.31), channel_id=1, source_target_pairs={{0,8},{8,0},{1,9},{9,1},{2,10},{10,2},{3,11},{11,3},{4,12},{12,4},... | collective-permute-start | bytes 12296 | tf_op jit(solution)/shard_map/ppermute | solution.py:180
  77.8 9.9 %collective-permute-start.16 = (bf16[96,1536]{1,0:T(8,128)(2,1)S(1)}, bf16[96,1536]{1,0:T(8,128)(2,1)S(1)}, u32[]{:S(2)}, u32[]{:S(2)}) collective-permute-start(bf16[96,1536]{1,0:T(8,128)(2,1)S(1)} %slice.200), channel_id=1, source_target_pairs={{0,8},{8,0},{1,9},{9,1},{2,10},{10,2},{3,11},{11,3},{4,12},{12,4},... | collective-permute-start | bytes 884744 | tf_op jit(solution)/shard_map/ppermute | solution.py:180
  78.1 25.7 %collective-permute-start.23 = (bf16[2,192,1024]{2,1,0:T(8,128)(2,1)S(1)}, bf16[2,192,1024]{2,1,0:T(8,128)(2,1)}, u32[]{:S(2)}, u32[]{:S(2)}) collective-permute-start(bf16[2,192,1024]{2,1,0:T(8,128)(2,1)S(1)} %bitcast.245), channel_id=1, source_target_pairs={{0,8},{8,0},{1,9},{9,1},{2,10},{10,2},{3,11},{11,3},{4,12},{12,4},... | collective-permute-start | bytes 2359304 | tf_op jit(solution)/shard_map/ppermute | solution.py:180
  80.9 18.9 %collective-permute-start.20 = (bf16[192,1536]{1,0:T(8,128)(2,1)S(1)}, bf16[192,1536]{1,0:T(8,128)(2,1)S(1)}, u32[]{:S(2)}, u32[]{:S(2)}) collective-permute-start(bf16[192,1536]{1,0:T(8,128)(2,1)S(1)} %copy-done.6), channel_id=1, source_target_pairs={{0,4},{4,0},{1,5},{5,1},{2,6},{6,2},{3,7},{7,3},{8,12},{12,8},{9,1... | collective-permute-start | bytes 1769480 | tf_op jit(solution)/shard_map/ppermute | solution.py:180
  81.5 15.9 %collective-permute-start.17 = (bf16[96,1536]{1,0:T(8,128)(2,1)S(1)}, bf16[96,1536]{1,0:T(8,128)(2,1)S(1)}, u32[]{:S(2)}, u32[]{:S(2)}) collective-permute-start(bf16[96,1536]{1,0:T(8,128)(2,1)S(1)} %slice.201), channel_id=1, source_target_pairs={{0,16},{16,0},{1,17},{17,1},{2,18},{18,2},{3,19},{19,3},{4,20},{20... | collective-permute-start | bytes 884744 | tf_op jit(solution)/shard_map/ppermute | solution.py:180
  83.0 16.9 %collective-permute-start.19 = (bf16[192,1536]{1,0:T(8,128)(2,1)S(1)}, bf16[192,1536]{1,0:T(8,128)(2,1)S(1)}, u32[]{:S(2)}, u32[]{:S(2)}) collective-permute-start(bf16[192,1536]{1,0:T(8,128)(2,1)S(1)} %collective-permute-done.15.refs_1_), channel_id=1, source_target_pairs={{0,4},{4,0},{1,5},{5,1},{2,6},{6,2},{3,7},{7,3},{8,12},{12,8},{9,1... | collective-permute-start | bytes 1769480 | tf_op jit(solution)/shard_map/ppermute | solution.py:180
  87.7 12.1 %collective-permute-start.21 = (bf16[96,1536]{1,0:T(8,128)(2,1)S(1)}, bf16[96,1536]{1,0:T(8,128)(2,1)S(1)}, u32[]{:S(2)}, u32[]{:S(2)}) collective-permute-start(bf16[96,1536]{1,0:T(8,128)(2,1)S(1)} %collective-permute-done.16.refs_3_), channel_id=1, source_target_pairs={{0,4},{4,0},{1,5},{5,1},{2,6},{6,2},{3,7},{7,3},{8,12},{12,8},{9,1... | collective-permute-start | bytes 884744 | tf_op jit(solution)/shard_map/ppermute | solution.py:180
  122.6 11.9 %collective-permute-start.25 = (bf16[384,256]{1,0:T(8,128)(2,1)S(1)}, bf16[384,256]{1,0:T(8,128)(2,1)S(1)}, u32[]{:S(2)}, u32[]{:S(2)}) collective-permute-start(bf16[384,256]{1,0:T(8,128)(2,1)S(1)} %get-tuple-element.131), channel_id=1, source_target_pairs={{0,1},{1,0},{2,3},{3,2},{4,5},{5,4},{6,7},{7,6},{8,9},{9,8},{10,11... | collective-permute-start | bytes 589832 | tf_op jit(solution)/shard_map/ppermute | solution.py:180
  124.3 15.0 %collective-permute-start.26 = (bf16[384,256]{1,0:T(8,128)(2,1)S(1)}, bf16[384,256]{1,0:T(8,128)(2,1)S(1)}, u32[]{:S(2)}, u32[]{:S(2)}) collective-permute-start(bf16[384,256]{1,0:T(8,128)(2,1)S(1)} %get-tuple-element.130), channel_id=1, source_target_pairs={{0,2},{1,3},{2,0},{3,1},{4,6},{5,7},{6,4},{7,5},{8,10},{9,11},{10,... | collective-permute-start | bytes 589832 | tf_op jit(solution)/shard_map/ppermute | solution.py:180
  125.4 25.7 %collective-permute-start.27 = (bf16[384,256]{1,0:T(8,128)(2,1)S(1)}, bf16[384,256]{1,0:T(8,128)(2,1)S(1)}, u32[]{:S(2)}, u32[]{:S(2)}) collective-permute-start(bf16[384,256]{1,0:T(8,128)(2,1)S(1)} %get-tuple-element.129), channel_id=1, source_target_pairs={{0,3},{1,2},{2,1},{3,0},{4,7},{5,6},{6,5},{7,4},{8,11},{9,10},{10,... | collective-permute-start | bytes 589832 | tf_op jit(solution)/shard_map/ppermute | solution.py:180
  156.3 33.7 %collective-permute-start.29 = (bf16[256,1536]{1,0:T(8,128)(2,1)}, bf16[256,1536]{1,0:T(8,128)(2,1)}, u32[]{:S(2)}, u32[]{:S(2)}) collective-permute-start(bf16[256,1536]{1,0:T(8,128)(2,1)} %multiply_convert_fusion.1.h_ref.refs_0_), channel_id=1, source_target_pairs={{0,8},{8,0},{1,9},{9,1},{2,10},{10,2},{3,11},{11,3},{4,12},{12,4},... | collective-permute-start | bytes 2359304 | tf_op jit(solution)/shard_map/ppermute | solution.py:180
  201.9 20.2 %collective-permute-start.30 = (bf16[256,1536]{1,0:T(8,128)(2,1)}, bf16[256,1536]{1,0:T(8,128)(2,1)S(1)}, u32[]{:S(2)}, u32[]{:S(2)}) collective-permute-start(bf16[256,1536]{1,0:T(8,128)(2,1)} %get-tuple-element.60), channel_id=1, source_target_pairs={{0,8},{8,0},{1,9},{9,1},{2,10},{10,2},{3,11},{11,3},{4,12},{12,4},... | collective-permute-start | bytes 2359304 | tf_op jit(solution)/shard_map/ppermute | solution.py:180
  225.8 136.4 %reduce-scatter.5.cloned.1.call-start = ((), (), s32[]{:S(2)}) async-start(), calls=%async_computation.6 | async-start | bytes 1966080 | tf_op jit(solution)/shard_map/reduce_scatter | solution.py:625
  225.8 20.6 %collective-permute-start.31 = (bf16[256,1536]{1,0:T(8,128)(2,1)}, bf16[256,1536]{1,0:T(8,128)(2,1)S(1)}, u32[]{:S(2)}, u32[]{:S(2)}) collective-permute-start(bf16[256,1536]{1,0:T(8,128)(2,1)} %get-tuple-element.62.g_ref.refs_0_), channel_id=1, source_target_pairs={{0,8},{8,0},{1,9},{9,1},{2,10},{10,2},{3,11},{11,3},{4,12},{12,4},... | collective-permute-start | bytes 2359304 | tf_op jit(solution)/shard_map/ppermute | solution.py:180
  228.2 19.1 %collective-permute-start.37 = (bf16[256,1536]{1,0:T(8,128)(2,1)}, bf16[256,1536]{1,0:T(8,128)(2,1)}, u32[]{:S(2)}, u32[]{:S(2)}) collective-permute-start(bf16[256,1536]{1,0:T(8,128)(2,1)} %multiply_convert_fusion.1.h_ref.refs_0_), channel_id=1, source_target_pairs={{0,4},{4,0},{1,5},{5,1},{2,6},{6,2},{3,7},{7,3},{8,12},{12,8},{9,1... | collective-permute-start | bytes 2359304 | tf_op jit(solution)/shard_map/ppermute | solution.py:180
  228.2 30.9 %collective-permute-start.35 = (bf16[256,2048]{1,0:T(8,128)(2,1)S(1)}, bf16[256,2048]{1,0:T(8,128)(2,1)}, u32[]{:S(2)}, u32[]{:S(2)}) collective-permute-start(bf16[256,2048]{1,0:T(8,128)(2,1)S(1)} %copy-done.47), channel_id=1, source_target_pairs={{0,4},{4,0},{1,5},{5,1},{2,6},{6,2},{3,7},{7,3},{8,12},{12,8},{9,1... | collective-permute-start | bytes 3145736 | tf_op jit(solution)/shard_map/ppermute | solution.py:180
  228.7 31.0 %collective-permute-start.36 = (bf16[256,2048]{1,0:T(8,128)(2,1)}, bf16[256,2048]{1,0:T(8,128)(2,1)}, u32[]{:S(2)}, u32[]{:S(2)}) collective-permute-start(bf16[256,2048]{1,0:T(8,128)(2,1)} %get-tuple-element.69.refs_6_), channel_id=1, source_target_pairs={{0,4},{4,0},{1,5},{5,1},{2,6},{6,2},{3,7},{7,3},{8,12},{12,8},{9,1... | collective-permute-start | bytes 3145736 | tf_op jit(solution)/shard_map/ppermute | solution.py:180
  242.5 17.7 %collective-permute-start.39 = (bf16[256,2048]{1,0:T(8,128)(2,1)}, bf16[256,2048]{1,0:T(8,128)(2,1)}, u32[]{:S(2)}, u32[]{:S(2)}) collective-permute-start(bf16[256,2048]{1,0:T(8,128)(2,1)} %get-tuple-element.64.refs_1_.refs_0_), channel_id=1, source_target_pairs={{0,4},{4,0},{1,5},{5,1},{2,6},{6,2},{3,7},{7,3},{8,12},{12,8},{9,1... | collective-permute-start | bytes 3145736 | tf_op jit(solution)/shard_map/ppermute | solution.py:180
  246.4 13.4 %collective-permute-start.33 = (bf16[256,1536]{1,0:T(8,128)(2,1)S(1)}, bf16[256,1536]{1,0:T(8,128)(2,1)}, u32[]{:S(2)}, u32[]{:S(2)}) collective-permute-start(bf16[256,1536]{1,0:T(8,128)(2,1)S(1)} %copy-done.32), channel_id=1, source_target_pairs={{0,4},{4,0},{1,5},{5,1},{2,6},{6,2},{3,7},{7,3},{8,12},{12,8},{9,1... | collective-permute-start | bytes 2359304 | tf_op jit(solution)/shard_map/ppermute | solution.py:180
  247.3 13.6 %collective-permute-start.34 = (bf16[256,1536]{1,0:T(8,128)(2,1)}, bf16[256,1536]{1,0:T(8,128)(2,1)}, u32[]{:S(2)}, u32[]{:S(2)}) collective-permute-start(bf16[256,1536]{1,0:T(8,128)(2,1)} %after.39.g_ref.refs_2_), channel_id=1, source_target_pairs={{0,4},{4,0},{1,5},{5,1},{2,6},{6,2},{3,7},{7,3},{8,12},{12,8},{9,1... | collective-permute-start | bytes 2359304 | tf_op jit(solution)/shard_map/ppermute | solution.py:180
  259.2 12.8 %collective-permute-start.41 = (bf16[256,2048]{1,0:T(8,128)(2,1)}, bf16[256,2048]{1,0:T(8,128)(2,1)}, u32[]{:S(2)}, u32[]{:S(2)}) collective-permute-start(bf16[256,2048]{1,0:T(8,128)(2,1)} %get-tuple-element.65.refs_2_.refs_8_), channel_id=1, source_target_pairs={{0,4},{4,0},{1,5},{5,1},{2,6},{6,2},{3,7},{7,3},{8,12},{12,8},{9,1... | collective-permute-start | bytes 3145736 | tf_op jit(solution)/shard_map/ppermute | solution.py:180
  259.7 12.3 %collective-permute-start.40 = (bf16[256,2048]{1,0:T(8,128)(2,1)}, bf16[256,2048]{1,0:T(8,128)(2,1)}, u32[]{:S(2)}, u32[]{:S(2)}) collective-permute-start(bf16[256,2048]{1,0:T(8,128)(2,1)} %get-tuple-element.72.refs_6_), channel_id=1, source_target_pairs={{0,4},{4,0},{1,5},{5,1},{2,6},{6,2},{3,7},{7,3},{8,12},{12,8},{9,1... | collective-permute-start | bytes 3145736 | tf_op jit(solution)/shard_map/ppermute | solution.py:180
  259.8 12.2 %collective-permute-start.42 = (bf16[256,2048]{1,0:T(8,128)(2,1)}, bf16[256,2048]{1,0:T(8,128)(2,1)}, u32[]{:S(2)}, u32[]{:S(2)}) collective-permute-start(bf16[256,2048]{1,0:T(8,128)(2,1)} %get-tuple-element.73.refs_10_), channel_id=1, source_target_pairs={{0,4},{4,0},{1,5},{5,1},{2,6},{6,2},{3,7},{7,3},{8,12},{12,8},{9,1... | collective-permute-start | bytes 3145736 | tf_op jit(solution)/shard_map/ppermute | solution.py:180
  260.2 11.7 %collective-permute-start.38 = (bf16[256,1536]{1,0:T(8,128)(2,1)}, bf16[256,1536]{1,0:T(8,128)(2,1)}, u32[]{:S(2)}, u32[]{:S(2)}) collective-permute-start(bf16[256,1536]{1,0:T(8,128)(2,1)} %after.37.h_ref.refs_2_), channel_id=1, source_target_pairs={{0,4},{4,0},{1,5},{5,1},{2,6},{6,2},{3,7},{7,3},{8,12},{12,8},{9,1... | collective-permute-start | bytes 2359304 | tf_op jit(solution)/shard_map/ppermute | solution.py:180
  260.9 23.8 %collective-permute-start.32 = (bf16[256,1536]{1,0:T(8,128)(2,1)S(1)}, bf16[256,1536]{1,0:T(8,128)(2,1)S(1)}, u32[]{:S(2)}, u32[]{:S(2)}) collective-permute-start(bf16[256,1536]{1,0:T(8,128)(2,1)S(1)} %copy-done.69), channel_id=1, source_target_pairs={{0,8},{8,0},{1,9},{9,1},{2,10},{10,2},{3,11},{11,3},{4,12},{12,4},... | collective-permute-start | bytes 2359304 | tf_op jit(solution)/shard_map/ppermute | solution.py:180
  271.9 36.8 %collective-permute-start.46 = (bf16[4,384,512]{2,1,0:T(8,128)(2,1)}, bf16[4,384,512]{2,1,0:T(8,128)(2,1)}, u32[]{:S(2)}, u32[]{:S(2)}) collective-permute-start(bf16[4,384,512]{2,1,0:T(8,128)(2,1)} %get-tuple-element.70.refs_2_.refs_1_), channel_id=1, source_target_pairs={{0,16},{16,0},{1,17},{17,1},{2,18},{18,2},{3,19},{19,3},{4,20},{20... | collective-permute-start | bytes 4718600 | tf_op jit(solution)/shard_map/ppermute | solution.py:180
  296.7 12.0 %collective-permute-start.43 = (bf16[384,256]{1,0:T(8,128)(2,1)S(1)}, bf16[384,256]{1,0:T(8,128)(2,1)S(1)}, u32[]{:S(2)}, u32[]{:S(2)}) collective-permute-start(bf16[384,256]{1,0:T(8,128)(2,1)S(1)} %get-tuple-element.126), channel_id=1, source_target_pairs={{0,1},{1,0},{2,3},{3,2},{4,5},{5,4},{6,7},{7,6},{8,9},{9,8},{10,11... | collective-permute-start | bytes 589832 | tf_op jit(solution)/shard_map/ppermute | solution.py:180
  296.7 17.1 %collective-permute-start.44 = (bf16[384,256]{1,0:T(8,128)(2,1)S(1)}, bf16[384,256]{1,0:T(8,128)(2,1)S(1)}, u32[]{:S(2)}, u32[]{:S(2)}) collective-permute-start(bf16[384,256]{1,0:T(8,128)(2,1)S(1)} %get-tuple-element.125), channel_id=1, source_target_pairs={{0,2},{1,3},{2,0},{3,1},{4,6},{5,7},{6,4},{7,5},{8,10},{9,11},{10,... | collective-permute-start | bytes 589832 | tf_op jit(solution)/shard_map/ppermute | solution.py:180
  298.4 15.4 %collective-permute-start.45 = (bf16[384,256]{1,0:T(8,128)(2,1)S(1)}, bf16[384,256]{1,0:T(8,128)(2,1)S(1)}, u32[]{:S(2)}, u32[]{:S(2)}) collective-permute-start(bf16[384,256]{1,0:T(8,128)(2,1)S(1)} %get-tuple-element.124), channel_id=1, source_target_pairs={{0,3},{1,2},{2,1},{3,0},{4,7},{5,6},{6,5},{7,4},{8,11},{9,10},{10,... | collective-permute-start | bytes 589832 | tf_op jit(solution)/shard_map/ppermute | solution.py:180
  318.2 80.4 %reduce-scatter.7.cloned.1.call-start = ((), (), s32[]{:S(2)}) async-start(), calls=%async_computation.7 | async-start | bytes 1966080 | tf_op jit(solution)/shard_map/reduce_scatter | solution.py:625
  319.6 34.9 %collective-permute-start.48 = (bf16[4,384,512]{2,1,0:T(8,128)(2,1)S(1)}, bf16[4,384,512]{2,1,0:T(8,128)(2,1)}, u32[]{:S(2)}, u32[]{:S(2)}) collective-permute-start(bf16[4,384,512]{2,1,0:T(8,128)(2,1)S(1)} %copy-done.40), channel_id=1, source_target_pairs={{0,16},{16,0},{1,17},{17,1},{2,18},{18,2},{3,19},{19,3},{4,20},{20... | collective-permute-start | bytes 4718600 | tf_op jit(solution)/shard_map/ppermute | solution.py:180
  357.6 82.0 %reduce-scatter.9.cloned.1.call-start = ((), (), s32[]{:S(2)}) async-start(), calls=%async_computation.8 | async-start | bytes 1966080 | tf_op jit(solution)/shard_map/reduce_scatter | solution.py:625
  359.0 33.9 %collective-permute-start.50 = (bf16[4,384,512]{2,1,0:T(8,128)(2,1)S(1)}, bf16[4,384,512]{2,1,0:T(8,128)(2,1)S(1)}, u32[]{:S(2)}, u32[]{:S(2)}) collective-permute-start(bf16[4,384,512]{2,1,0:T(8,128)(2,1)S(1)} %copy-done.38), channel_id=1, source_target_pairs={{0,16},{16,0},{1,17},{17,1},{2,18},{18,2},{3,19},{19,3},{4,20},{20... | collective-permute-start | bytes 4718600 | tf_op jit(solution)/shard_map/ppermute | solution.py:180
  360.4 32.5 %collective-permute-start.49 = (bf16[2,96,1024]{2,1,0:T(8,128)(2,1)}, bf16[2,96,1024]{2,1,0:T(8,128)(2,1)S(1)}, u32[]{:S(2)}, u32[]{:S(2)}) collective-permute-start(bf16[2,96,1024]{2,1,0:T(8,128)(2,1)} %fusion.36.refs_1_), channel_id=1, source_target_pairs={{0,8},{8,0},{1,9},{9,1},{2,10},{10,2},{3,11},{11,3},{4,12},{12,4},... | collective-permute-start | bytes 1179656 | tf_op jit(solution)/shard_map/ppermute | solution.py:180
  398.6 104.1 %reduce-scatter.11.cloned.1.call-start = ((), (), s32[]{:S(2)}) async-start(), calls=%async_computation.9 | async-start | bytes 3932160 | tf_op jit(solution)/shard_map/reduce_scatter | solution.py:693
  402.1 15.4 %collective-permute-start.52 = (bf16[2,96,1024]{2,1,0:T(8,128)(2,1)S(1)}, bf16[2,96,1024]{2,1,0:T(8,128)(2,1)S(1)}, u32[]{:S(2)}, u32[]{:S(2)}) collective-permute-start(bf16[2,96,1024]{2,1,0:T(8,128)(2,1)S(1)} %fusion.37.refs_1_), channel_id=1, source_target_pairs={{0,8},{8,0},{1,9},{9,1},{2,10},{10,2},{3,11},{11,3},{4,12},{12,4},... | collective-permute-start | bytes 1179656 | tf_op jit(solution)/shard_map/ppermute | solution.py:180
  439.6 145.8 %all-gather.8.cloned.1.call-start = ((), (), s32[]{:S(2)}) async-start(), calls=%async_computation.10 | async-start | bytes 3932160 | tf_op jit(solution)/shard_map/all_gather | solution.py:707
  445.6 7.4 %collective-permute-start.53 = (bf16[2,2,192,1536]{3,2,1,0:T(8,128)(2,1)S(1)}, bf16[2,2,192,1536]{3,2,1,0:T(8,128)(2,1)}, u32[]{:S(2)}, u32[]{:S(2)}) collective-permute-start(bf16[2,2,192,1536]{3,2,1,0:T(8,128)(2,1)S(1)} %dynamic-slice_bitcast_fusion), channel_id=1, source_target_pairs={{0,4},{4,0},{1,5},{5,1},{2,6},{6,2},{3,7},{7,3},{8,12},{12,8},{9,1... | collective-permute-start | bytes 7077896 | tf_op jit(solution)/shard_map/ppermute | solution.py:180
  457.1 42.9 %collective-permute-start.54 = (bf16[2,192,1536]{2,1,0:T(8,128)(2,1)}, bf16[2,192,1536]{2,1,0:T(8,128)(2,1)}, u32[]{:S(2)}, u32[]{:S(2)}) collective-permute-start(bf16[2,192,1536]{2,1,0:T(8,128)(2,1)} %dynamic-slice_bitcast_fusion.2), channel_id=1, source_target_pairs={{0,16},{16,0},{1,17},{17,1},{2,18},{18,2},{3,19},{19,3},{4,20},{20... | collective-permute-start | bytes 3538952 | tf_op jit(solution)/shard_map/ppermute | solution.py:180
  460.9 37.1 %collective-permute-start.56 = (bf16[2,192,768]{2,1,0:T(8,128)(2,1)}, bf16[2,192,768]{2,1,0:T(8,128)(2,1)}, u32[]{:S(2)}, u32[]{:S(2)}) collective-permute-start(bf16[2,192,768]{2,1,0:T(8,128)(2,1)} %dynamic-slice_bitcast_fusion.4), channel_id=1, source_target_pairs={{0,16},{16,0},{1,17},{17,1},{2,18},{18,2},{3,19},{19,3},{4,20},{20... | collective-permute-start | bytes 1769480 | tf_op jit(solution)/shard_map/ppermute | solution.py:180
  516.1 7.6 %collective-permute-start.67 = (bf16[192,512]{1,0:T(8,128)(2,1)S(1)}, bf16[192,512]{1,0:T(8,128)(2,1)S(1)}, u32[]{:S(2)}, u32[]{:S(2)}) collective-permute-start(bf16[192,512]{1,0:T(8,128)(2,1)S(1)} %dynamic-slice_bitcast_fusion.8), channel_id=1, source_target_pairs={{0,8},{8,0},{1,9},{9,1},{2,10},{10,2},{3,11},{11,3},{4,12},{12,4},... | collective-permute-start | bytes 589832 | tf_op jit(solution)/shard_map/ppermute | solution.py:180
  526.9 10.1 %collective-permute-start.62 = (bf16[192,768]{1,0:T(8,128)(2,1)S(1)}, bf16[192,768]{1,0:T(8,128)(2,1)}, u32[]{:S(2)}, u32[]{:S(2)}) collective-permute-start(bf16[192,768]{1,0:T(8,128)(2,1)S(1)} %dynamic-slice_bitcast_fusion.5), channel_id=1, source_target_pairs={{0,8},{8,0},{1,9},{9,1},{2,10},{10,2},{3,11},{11,3},{4,12},{12,4},... | collective-permute-start | bytes 884744 | tf_op jit(solution)/shard_map/ppermute | solution.py:180
  528.0 18.7 %collective-permute-start.63 = (bf16[192,1536]{1,0:T(8,128)(2,1)S(1)}, bf16[192,1536]{1,0:T(8,128)(2,1)S(1)}, u32[]{:S(2)}, u32[]{:S(2)}) collective-permute-start(bf16[192,1536]{1,0:T(8,128)(2,1)S(1)} %dynamic-slice_bitcast_fusion.3), channel_id=1, source_target_pairs={{0,8},{8,0},{1,9},{9,1},{2,10},{10,2},{3,11},{11,3},{4,12},{12,4},... | collective-permute-start | bytes 1769480 | tf_op jit(solution)/shard_map/ppermute | solution.py:180
  529.8 8.3 %collective-permute-start.57 = (f32[3,1536]{1,0:T(4,128)}, f32[3,1536]{1,0:T(4,128)S(1)}, u32[]{:S(2)}, u32[]{:S(2)}) collective-permute-start(f32[3,1536]{1,0:T(4,128)} %after.56), channel_id=1, source_target_pairs={{0,16},{16,0},{1,17},{17,1},{2,18},{18,2},{3,19},{19,3},{4,20},{20... | collective-permute-start | bytes 55304 | tf_op jit(solution)/shard_map/ppermute | solution.py:180
  539.5 7.6 %collective-permute-start.58 = (f32[3,1536]{1,0:T(4,128)}, f32[3,1536]{1,0:T(4,128)}, u32[]{:S(2)}, u32[]{:S(2)}) collective-permute-start(f32[3,1536]{1,0:T(4,128)} %add.511), channel_id=1, source_target_pairs={{0,8},{8,0},{1,9},{9,1},{2,10},{10,2},{3,11},{11,3},{4,12},{12,4},... | collective-permute-start | bytes 55304 | tf_op jit(solution)/shard_map/ppermute | solution.py:180
  548.8 24.5 %collective-permute-start.64 = (bf16[192,384]{1,0:T(8,128)(2,1)S(1)}, bf16[192,384]{1,0:T(8,128)(2,1)S(1)}, u32[]{:S(2)}, u32[]{:S(2)}) collective-permute-start(bf16[192,384]{1,0:T(8,128)(2,1)S(1)} %bitcast.280), channel_id=1, source_target_pairs={{0,1},{1,0},{2,3},{3,2},{4,5},{5,4},{6,7},{7,6},{8,9},{9,8},{10,11... | collective-permute-start | bytes 442376 | tf_op jit(solution)/shard_map/ppermute | solution.py:180
  548.9 24.4 %collective-permute-start.65 = (bf16[192,384]{1,0:T(8,128)(2,1)S(1)}, bf16[192,384]{1,0:T(8,128)(2,1)S(1)}, u32[]{:S(2)}, u32[]{:S(2)}) collective-permute-start(bf16[192,384]{1,0:T(8,128)(2,1)S(1)} %bitcast.281), channel_id=1, source_target_pairs={{0,2},{1,3},{2,0},{3,1},{4,6},{5,7},{6,4},{7,5},{8,10},{9,11},{10,... | collective-permute-start | bytes 442376 | tf_op jit(solution)/shard_map/ppermute | solution.py:180
  550.5 22.8 %collective-permute-start.66 = (bf16[192,384]{1,0:T(8,128)(2,1)S(1)}, bf16[192,384]{1,0:T(8,128)(2,1)S(1)}, u32[]{:S(2)}, u32[]{:S(2)}) collective-permute-start(bf16[192,384]{1,0:T(8,128)(2,1)S(1)} %bitcast.282), channel_id=1, source_target_pairs={{0,3},{1,2},{2,1},{3,0},{4,7},{5,6},{6,5},{7,4},{8,11},{9,10},{10,... | collective-permute-start | bytes 442376 | tf_op jit(solution)/shard_map/ppermute | solution.py:180
  553.4 16.4 %collective-permute-start.60 = (f32[3,1536]{1,0:T(4,128)S(1)}, f32[3,1536]{1,0:T(4,128)S(1)}, u32[]{:S(2)}, u32[]{:S(2)}) collective-permute-start(f32[3,1536]{1,0:T(4,128)S(1)} %add.513), channel_id=1, source_target_pairs={{0,1},{1,0},{2,3},{3,2},{4,5},{5,4},{6,7},{7,6},{8,9},{9,8},{10,11... | collective-permute-start | bytes 55304 | tf_op jit(solution)/shard_map/ppermute | solution.py:180
  569.9 12.5 %collective-permute-start.61 = (f32[3,1536]{1,0:T(4,128)S(1)}, f32[3,1536]{1,0:T(4,128)S(1)}, u32[]{:S(2)}, u32[]{:S(2)}) collective-permute-start(f32[3,1536]{1,0:T(4,128)S(1)} %add.514), channel_id=1, source_target_pairs={{0,2},{1,3},{2,0},{3,1},{4,6},{5,7},{6,4},{7,5},{8,10},{9,11},{10,... | collective-permute-start | bytes 55304 | tf_op jit(solution)/shard_map/ppermute | solution.py:180
  (108 other events, 559.3 us)
Sparse Core Ops, SparseCore 0:
  58.0 111.3 all-gather.3
  225.9 62.4 all-gather.5
  318.3 35.5 reduce-scatter.4
  357.7 38.1 reduce-scatter.6
  398.7 40.8 reduce-scatter.8
  442.3 59.2 reduce-scatter.10
  510.0 75.3 all-gather.7
